TPU v7x, 32 devices: a whole 2x2x4 slice. The times are simulated.
32 devices in a mesh: seq: 4 (over z), fsdp: 8 (over y, x, core).
Axes of the slice: x: 2, y: 2, z: 4, core: 2. Of those that a mesh axis runs over, the one named last changes fastest.
Arguments:
- tokens: bfloat16 [8, 1024, 1536], P('fsdp', 'seq'), may hold values from -6 to 6
- gain_attn: bfloat16 [1536], P(('seq', 'fsdp')), may hold values from 0.5 to 1.5
- w_query: bfloat16 [1536, 1536], P(('seq', 'fsdp')), may hold values from -0.15625 to 0.15625
- key_weight: bfloat16 [1536, 768], P(('seq', 'fsdp')), may hold values from -0.15625 to 0.15625
- value_weight: bfloat16 [1536, 768], P(('seq', 'fsdp')), may hold values from -0.15625 to 0.15625
- w_out: bfloat16 [1536, 1536], P(('seq', 'fsdp')), may hold values from -0.625 to 0.625
- gain_mlp: bfloat16 [1536], P(('seq', 'fsdp')), may hold values from 0.5 to 1.5
- w_gate: bfloat16 [1536, 4096], P(('seq', 'fsdp')), may hold values from -0.15625 to 0.15625
- w_up: bfloat16 [1536, 4096], P(('seq', 'fsdp')), may hold values from -0.15625 to 0.15625
- w_down: bfloat16 [4096, 1536], P(('seq', 'fsdp')), may hold values from -0.09375 to 0.09375
- out_grad: bfloat16 [8, 1024, 1536], P('fsdp', 'seq'), may hold values from -6 to 6
- lengths: int32 [8, 4], P('fsdp'), may hold values from 1 to 640, 1024 in all within a row
- stretch_map: int32 [8, 8], P('fsdp'), may hold values from 0 to 7, as said below
Outputs:
- result: bfloat16 [8, 1024, 1536], P('fsdp', 'seq')
- input_grad: bfloat16 [8, 1024, 1536], P('fsdp', 'seq')
- grad_gain_attn: float32 [1536], P(('seq', 'fsdp'))
- grad_query: float32 [1536, 1536], P(('seq', 'fsdp'))
- grad_key: float32 [1536, 768], P(('seq', 'fsdp'))
- grad_value: float32 [1536, 768], P(('seq', 'fsdp'))
- grad_out: float32 [1536, 1536], P(('seq', 'fsdp'))
- grad_gain_mlp: float32 [1536], P(('seq', 'fsdp'))
- grad_gate: float32 [1536, 4096], P(('seq', 'fsdp'))
- grad_up: float32 [1536, 4096], P(('seq', 'fsdp'))
- grad_down: float32 [4096, 1536], P(('seq', 'fsdp'))
Inputs may be any that keep to these rules, and one draw needn't show every extreme that they name: stretch_map of a group holds every slot once; slot s is stored rows s * 128 to (s + 1) * 128 - 1 of the group; logical stretches whose difference is not a multiple of 4 lie in different blocks of 256 stored rows. Each group's lengths sum to 1024; the longest has exactly 640 tokens.
All inputs are finite; a program needn't handle non-finite values.
Results may differ from a plain program's by a relative error of at most 0.015.
Values may be sent and summed in bfloat16 or wider, within the bound.
No kernel may reach another device: no remote copies, remote signals or barrier semaphores. Data moves between devices by JAX's collectives and lax.ppermute only.
A program may use at most 320 MiB of HBM per device.

v0:
```python
import math

import jax
import jax.numpy as jnp
from jax import lax
from jax.sharding import PartitionSpec as P

QUERY_HEADS = 16
KEY_VALUE_HEADS = 8
HEAD_SIZE = 96
FF = 4096
STRETCH = 128


EPSILON = 1e-05
THETA = 100000.0


def layout(doc_lengths, slot_map):
    token_count = slot_map.shape[0]
    slots = jnp.arange(token_count, dtype=jnp.int32)
    logical = jnp.sum(jnp.where(slot_map[None, :] == slots[:, None], slots[None, :], 0), axis=1)
    position_list = (
        logical[:, None] * STRETCH + jnp.arange(STRETCH, dtype=jnp.int32)[None, :]
    ).reshape(-1)
    endings = jnp.cumsum(doc_lengths)
    passed = endings[None, :] <= position_list[:, None]
    document_index = jnp.sum(passed.astype(jnp.int32), axis=1)
    starts = jnp.sum(jnp.where(passed, doc_lengths[None, :], 0), axis=1)
    return (document_index, position_list - starts)


def apply_rotary(value_rows, position_list, direction):
    half = value_rows.shape[-1] // 2
    freqs = THETA ** (-2.0 * jnp.arange(half, dtype=jnp.float32) / value_rows.shape[-1])
    angles = position_list.astype(jnp.float32)[:, None] * freqs[None, :]
    cosine = jnp.cos(angles)[:, None, :]
    sine = direction * jnp.sin(angles)[:, None, :]
    first = value_rows[..., :half]
    second = value_rows[..., half:]
    return jnp.concatenate(
        [first * cosine - second * sine, second * cosine + first * sine], axis=-1
    )


def matrix_product(left, right):
    return jnp.dot(left, right, preferred_element_type=jnp.float32)


def over_rows(left, right):
    return lax.dot_general(
        left, right, (((0,), (0,)), ((), ())), preferred_element_type=jnp.float32
    )


def times_transposed(left, right):
    return lax.dot_general(
        left, right, (((1,), (1,)), ((), ())), preferred_element_type=jnp.float32
    )


def column_terms(left, right):
    return over_rows(left, right)


def norm_back(grad_normed, normalized_input, inverse, gain):
    gain_grad = jnp.sum(grad_normed * normalized_input, axis=0)
    scaled = grad_normed * gain
    input_part = inverse * (
        scaled - normalized_input * jnp.mean(scaled * normalized_input, axis=-1, keepdims=True)
    )
    return (gain_grad, input_part)


def on_device(
    tokens,
    gain_attn,
    w_query,
    key_weight,
    value_weight,
    w_out,
    gain_mlp,
    w_gate,
    w_up,
    w_down,
    out_grad,
    lengths,
    stretch_map,
):
    gain_one, query_w, key_matrix, value_matrix, out_w, gain_two, gate_w, up_w, down_w = (
        lax.all_gather(gain_attn, ("seq", "fsdp"), axis=0, tiled=True),
        lax.all_gather(w_query, ("seq", "fsdp"), axis=0, tiled=True),
        lax.all_gather(key_weight, ("seq", "fsdp"), axis=0, tiled=True),
        lax.all_gather(value_weight, ("seq", "fsdp"), axis=0, tiled=True),
        lax.all_gather(w_out, ("seq", "fsdp"), axis=0, tiled=True),
        lax.all_gather(gain_mlp, ("seq", "fsdp"), axis=0, tiled=True),
        lax.all_gather(w_gate, ("seq", "fsdp"), axis=0, tiled=True),
        lax.all_gather(w_up, ("seq", "fsdp"), axis=0, tiled=True),
        lax.all_gather(w_down, ("seq", "fsdp"), axis=0, tiled=True),
    )
    token_count = tokens.shape[1]
    group_ratio = QUERY_HEADS // KEY_VALUE_HEADS
    scale = 1.0 / math.sqrt(HEAD_SIZE)
    doc_all, place_all = layout(lengths[0], stretch_map[0])
    offset = lax.axis_index("seq") * token_count
    doc_mine = lax.dynamic_slice_in_dim(doc_all, offset, token_count)
    local_positions = lax.dynamic_slice_in_dim(place_all, offset, token_count)
    allowed = (doc_mine[:, None] == doc_all[None, :]) & (
        place_all[None, :] <= local_positions[:, None]
    )
    inputs = tokens[0].astype(jnp.float32)
    first_inverse = lax.rsqrt(jnp.mean(inputs * inputs, axis=-1, keepdims=True) + EPSILON)
    first_normed = inputs * first_inverse
    first_gain = gain_one.astype(jnp.float32)
    first_normalized = (first_normed * first_gain).astype(jnp.bfloat16)
    query_rows = apply_rotary(
        matrix_product(first_normalized, query_w).reshape(token_count, QUERY_HEADS, HEAD_SIZE),
        local_positions,
        1.0,
    ).astype(jnp.bfloat16)
    keys_mine = (
        apply_rotary(
            matrix_product(first_normalized, key_matrix).reshape(
                token_count, KEY_VALUE_HEADS, HEAD_SIZE
            ),
            local_positions,
            1.0,
        )
        .astype(jnp.bfloat16)
        .reshape(token_count, KEY_VALUE_HEADS * HEAD_SIZE)
    )
    values_mine = matrix_product(first_normalized, value_matrix).astype(jnp.bfloat16)
    gathered_keys, gathered_values = (
        lax.all_gather(keys_mine, "seq", axis=0, tiled=True),
        lax.all_gather(values_mine, "seq", axis=0, tiled=True),
    )
    token_span = gathered_keys.shape[0]
    query_head_rows = query_rows.reshape(
        token_count, KEY_VALUE_HEADS, group_ratio, HEAD_SIZE
    ).transpose(1, 2, 0, 3)
    key_head_rows = gathered_keys.reshape(token_span, KEY_VALUE_HEADS, HEAD_SIZE).transpose(1, 0, 2)
    value_head_rows = gathered_values.reshape(token_span, KEY_VALUE_HEADS, HEAD_SIZE).transpose(
        1, 0, 2
    )

    def head_forward(item):
        head_queries, head_keys, head_values = item
        scores = (
            jnp.einsum("rqd,kd->rqk", head_queries, head_keys, preferred_element_type=jnp.float32)
            * scale
        )
        scores = jnp.where(allowed[None], scores, -1e30)
        peak = jnp.max(scores, axis=-1, keepdims=True)
        weights = jnp.exp(scores - peak)
        totals = jnp.sum(weights, axis=-1, keepdims=True)
        probs = weights / totals
        mixed = jnp.einsum(
            "rqk,kd->rqd",
            probs.astype(jnp.bfloat16),
            head_values,
            preferred_element_type=jnp.float32,
        )
        return (mixed.astype(jnp.bfloat16), peak[..., 0] + jnp.log(totals[..., 0]))

    mixed_heads, log_totals = lax.map(
        head_forward, (query_head_rows, key_head_rows, value_head_rows)
    )
    attention_output = mixed_heads.transpose(2, 0, 1, 3).reshape(
        token_count, QUERY_HEADS * HEAD_SIZE
    )
    resid = inputs + matrix_product(attention_output, out_w)
    second_inverse = lax.rsqrt(jnp.mean(resid * resid, axis=-1, keepdims=True) + EPSILON)
    second_normed = resid * second_inverse
    second_gain = gain_two.astype(jnp.float32)
    normed_two = (second_normed * second_gain).astype(jnp.bfloat16)
    gate = matrix_product(normed_two, gate_w)
    upper = matrix_product(normed_two, up_w)
    sigmoid_gate = jax.nn.sigmoid(gate)
    silu_gate = gate * sigmoid_gate
    hidden = (silu_gate * upper).astype(jnp.bfloat16)
    output = resid + matrix_product(hidden, down_w)
    result = output.astype(jnp.bfloat16)
    gain_one, query_w, key_matrix, value_matrix, out_w, gain_two, gate_w, up_w, down_w = (
        lax.all_gather(gain_attn, ("seq", "fsdp"), axis=0, tiled=True),
        lax.all_gather(w_query, ("seq", "fsdp"), axis=0, tiled=True),
        lax.all_gather(key_weight, ("seq", "fsdp"), axis=0, tiled=True),
        lax.all_gather(value_weight, ("seq", "fsdp"), axis=0, tiled=True),
        lax.all_gather(w_out, ("seq", "fsdp"), axis=0, tiled=True),
        lax.all_gather(gain_mlp, ("seq", "fsdp"), axis=0, tiled=True),
        lax.all_gather(w_gate, ("seq", "fsdp"), axis=0, tiled=True),
        lax.all_gather(w_up, ("seq", "fsdp"), axis=0, tiled=True),
        lax.all_gather(w_down, ("seq", "fsdp"), axis=0, tiled=True),
    )
    grad_output = out_grad[0].astype(jnp.float32)
    grad_branch = grad_output.astype(jnp.bfloat16)
    grad_hidden = times_transposed(grad_branch, down_w)
    grad_gate_in = (
        grad_hidden * upper * sigmoid_gate * (1.0 + gate * (1.0 - sigmoid_gate))
    ).astype(jnp.bfloat16)
    grad_up_in = (grad_hidden * silu_gate).astype(jnp.bfloat16)
    grad_normed_two = times_transposed(grad_gate_in, gate_w) + times_transposed(grad_up_in, up_w)
    grad_gain_two, resid_part = norm_back(
        grad_normed_two, second_normed, second_inverse, second_gain
    )
    grad_resid = grad_output + resid_part
    grad_attn_out = grad_resid.astype(jnp.bfloat16)
    attention_gradient = times_transposed(grad_attn_out, out_w).astype(jnp.bfloat16)
    head_gradient = attention_gradient.reshape(
        token_count, KEY_VALUE_HEADS, group_ratio, HEAD_SIZE
    ).transpose(1, 2, 0, 3)

    def head_backward(item):
        head_queries, head_keys, head_values, head_grads, head_totals = item
        scores = (
            jnp.einsum("rqd,kd->rqk", head_queries, head_keys, preferred_element_type=jnp.float32)
            * scale
        )
        scores = jnp.where(allowed[None], scores, -1e30)
        probs = jnp.exp(scores - head_totals[..., None])
        grad_probs = jnp.einsum(
            "rqd,kd->rqk", head_grads, head_values, preferred_element_type=jnp.float32
        )
        centre = jnp.sum(probs * grad_probs, axis=-1, keepdims=True)
        grad_scores = (probs * (grad_probs - centre)).astype(jnp.bfloat16)
        grad_queries = (
            jnp.einsum("rqk,kd->rqd", grad_scores, head_keys, preferred_element_type=jnp.float32)
            * scale
        )
        grad_keys = (
            jnp.einsum("rqk,rqd->kd", grad_scores, head_queries, preferred_element_type=jnp.float32)
            * scale
        )
        grad_values = jnp.einsum(
            "rqk,rqd->kd",
            probs.astype(jnp.bfloat16),
            head_grads,
            preferred_element_type=jnp.float32,
        )
        return (grad_queries, grad_keys, grad_values)

    grad_query_heads, key_head_gradient, value_head_gradient = lax.map(
        head_backward, (query_head_rows, key_head_rows, value_head_rows, head_gradient, log_totals)
    )
    gathered_key_gradient = key_head_gradient.transpose(1, 0, 2).reshape(
        token_span, KEY_VALUE_HEADS * HEAD_SIZE
    )
    gathered_value_gradient = value_head_gradient.transpose(1, 0, 2).reshape(
        token_span, KEY_VALUE_HEADS * HEAD_SIZE
    )
    local_key_gradient, grad_values_mine = (
        lax.psum_scatter(
            gathered_key_gradient.astype(jnp.bfloat16), "seq", scatter_dimension=0, tiled=True
        ).astype(jnp.float32),
        lax.psum_scatter(
            gathered_value_gradient.astype(jnp.bfloat16), "seq", scatter_dimension=0, tiled=True
        ).astype(jnp.float32),
    )
    grad_query_raw = (
        apply_rotary(
            grad_query_heads.transpose(2, 0, 1, 3).reshape(token_count, QUERY_HEADS, HEAD_SIZE),
            local_positions,
            -1.0,
        )
        .reshape(token_count, QUERY_HEADS * HEAD_SIZE)
        .astype(jnp.bfloat16)
    )
    grad_key_raw = (
        apply_rotary(
            local_key_gradient.reshape(token_count, KEY_VALUE_HEADS, HEAD_SIZE),
            local_positions,
            -1.0,
        )
        .reshape(token_count, KEY_VALUE_HEADS * HEAD_SIZE)
        .astype(jnp.bfloat16)
    )
    grad_value_raw = grad_values_mine.astype(jnp.bfloat16)
    grad_normed_one = (
        times_transposed(grad_query_raw, query_w)
        + times_transposed(grad_key_raw, key_matrix)
        + times_transposed(grad_value_raw, value_matrix)
    )
    grad_gain_one, input_part = norm_back(grad_normed_one, first_normed, first_inverse, first_gain)
    input_grad = (grad_resid + input_part).astype(jnp.bfloat16)
    projected_grads = jnp.concatenate([grad_query_raw, grad_key_raw, grad_value_raw], axis=1)
    proj_owned = lax.psum_scatter(
        column_terms(first_normalized, projected_grads),
        ("seq", "fsdp"),
        scatter_dimension=0,
        tiled=True,
    )
    gate_up_owned = lax.psum_scatter(
        column_terms(normed_two, jnp.concatenate([grad_gate_in, grad_up_in], axis=1)),
        ("seq", "fsdp"),
        scatter_dimension=0,
        tiled=True,
    )
    down_owned = lax.psum_scatter(
        column_terms(hidden, grad_branch), ("seq", "fsdp"), scatter_dimension=0, tiled=True
    )
    out_owned = lax.psum_scatter(
        column_terms(attention_output, grad_attn_out),
        ("seq", "fsdp"),
        scatter_dimension=0,
        tiled=True,
    )
    later_owned = (gate_up_owned, down_owned, out_owned)
    gate_up_owned, down_owned, out_owned = later_owned
    gain_one_owned, gain_two_owned = (
        lax.psum_scatter(grad_gain_one, ("seq", "fsdp"), scatter_dimension=0, tiled=True),
        lax.psum_scatter(grad_gain_two, ("seq", "fsdp"), scatter_dimension=0, tiled=True),
    )
    query_cols = QUERY_HEADS * HEAD_SIZE
    pair_cols = KEY_VALUE_HEADS * HEAD_SIZE
    query_owned = proj_owned[:, :query_cols]
    key_owned = proj_owned[:, query_cols : query_cols + pair_cols]
    value_owned = proj_owned[:, query_cols + pair_cols :]
    gate_owned = gate_up_owned[:, :FF]
    up_owned = gate_up_owned[:, FF:]
    return (
        result[None],
        input_grad[None],
        gain_one_owned,
        query_owned,
        key_owned,
        value_owned,
        out_owned,
        gain_two_owned,
        gate_owned,
        up_owned,
        down_owned,
    )


def solution(mesh):
    in_specs = (
        P("fsdp", "seq", None),
        P(("seq", "fsdp")),
        P(("seq", "fsdp"), None),
        P(("seq", "fsdp"), None),
        P(("seq", "fsdp"), None),
        P(("seq", "fsdp"), None),
        P(("seq", "fsdp")),
        P(("seq", "fsdp"), None),
        P(("seq", "fsdp"), None),
        P(("seq", "fsdp"), None),
        P("fsdp", "seq", None),
        P("fsdp", None),
        P("fsdp", None),
    )
    out_specs = (
        P("fsdp", "seq", None),
        P("fsdp", "seq", None),
        P(("seq", "fsdp")),
        P(("seq", "fsdp"), None),
        P(("seq", "fsdp"), None),
        P(("seq", "fsdp"), None),
        P(("seq", "fsdp"), None),
        P(("seq", "fsdp")),
        P(("seq", "fsdp"), None),
        P(("seq", "fsdp"), None),
        P(("seq", "fsdp"), None),
    )
    return jax.shard_map(
        on_device, mesh=mesh, in_specs=in_specs, out_specs=out_specs, check_vma=False
    )
```

profile of v0, /device:TPU:0, one launch (start us, length us, event | category | flops | bytes accessed | tf_op | source)
XLA Modules:
  0.0 1870.8 jit_solution(12171304837192680013)
XLA Ops:
  10.4 42.1 %all-reduce.5 = (bf16[1536]{0:T(1024)(128)(2,1)S(1)}, bf16[1536]{0:T(1024)(128)(2,1)S(1)}) all-reduce(bf16[1536]{0:T(1024)(128)(2,1)S(1)} %dynamic-update-slice, bf16[1536]{0:T(1024)(128)(2,1)S(1)} %dynamic-update-slice.1), channel_id=1, replica_groups=mesh['seq'=4,'fsdp'=8] {'seq','fsdp'}, use_global_device_ids=true, to_apply=%add | all-reduce | flops 3072 | bytes 12288
  53.9 17.0 all-gather.16.cloned.1.call-done
  70.9 3.5 convolution_convert_fusion.2
  76.0 54.0 %all-gather.12.cloned.1.call-done = bf16[1536,768]{1,0:T(8,128)(2,1)} async-done(((bf16[48,768]{1,0:T(8,128)(2,1)}), bf16[1536,768]{1,0:T(8,128)(2,1)}) %all-gather.12.cloned.1.call-update) | async-done | bytes 2359312 | tf_op jit(solution)/shard_map/all_gather | solution.py:93
  130.0 2.9 copy.37
  138.2 29.9 %all-gather.18.cloned.1.call-done = bf16[1024,768]{1,0:T(8,128)(2,1)} async-done(((bf16[256,768]{1,0:T(8,128)(2,1)}), bf16[1024,768]{1,0:T(8,128)(2,1)}) %all-gather.18.cloned.1.call-update) | async-done | bytes 1572880 | tf_op jit(solution)/shard_map/all_gather | solution.py:135
  168.1 2.6 copy.38
  170.7 62.7 %all-gather.10.cloned.1.call-done = bf16[1536,1536]{1,0:T(8,128)(2,1)} async-done(((bf16[48,1536]{1,0:T(8,128)(2,1)}), bf16[1536,1536]{1,0:T(8,128)(2,1)}) %all-gather.10.cloned.1.call-update) | async-done | bytes 4718608 | tf_op jit(solution)/shard_map/all_gather | solution.py:92
  233.4 6.6 copy.36
  240.0 4.1 fusion.88
  244.4 27.6 %all-gather.14.cloned.1.call-done = bf16[1024,768]{0,1:T(8,128)(2,1)} async-done(((bf16[256,768]{0,1:T(8,128)(2,1)}), bf16[1024,768]{0,1:T(8,128)(2,1)}) %all-gather.14.cloned.1.call-update) | async-done | bytes 1572880 | tf_op jit(solution)/shard_map/all_gather | solution.py:134
  272.0 34.3 %while.28 = (s32[]{:T(128)}, bf16[8,2,256,96]{2,3,1,0:T(8,128)(2,1)S(1)}, f32[8,2,256]{2,1,0:T(2,128)S(1)}, bf16[8,2,256,96]{2,3,1,0:T(8,128)(2,1)S(1)}, bf16[8,...) while((s32[]{:T(128)}, ...), condition=%wide.region_8.9_spmd.clone, body=%wide.region_5.8_spmd.clone.sunk | while | flops 208453120 | bytes 7958649 | solution.py:165
  306.3 30.4 %all-gather.20.cloned.1.call-done = bf16[1536,1536]{1,0:T(8,128)(2,1)} async-done(((bf16[48,1536]{1,0:T(8,128)(2,1)}), bf16[1536,1536]{1,0:T(8,128)(2,1)}) %all-gather.20.cloned.1.call-update) | async-done | bytes 4718608 | tf_op jit(solution)/shard_map/all_gather | solution.py:95
  336.6 3.8 multiply_reduce_fusion.3
  341.5 92.7 %all-gather.22.cloned.1.call-done = bf16[1536,4096]{1,0:T(8,128)(2,1)} async-done(((bf16[48,4096]{1,0:T(8,128)(2,1)}), bf16[1536,4096]{1,0:T(8,128)(2,1)}) %all-gather.22.cloned.1.call-update) | async-done | bytes 12582928 | tf_op jit(solution)/shard_map/all_gather | solution.py:97
  434.2 10.3 fusion.100
  444.5 86.8 %all-gather.24.cloned.1.call-done = bf16[1536,4096]{1,0:T(8,128)(2,1)} async-done(((bf16[48,4096]{1,0:T(8,128)(2,1)}), bf16[1536,4096]{1,0:T(8,128)(2,1)}) %all-gather.24.cloned.1.call-update) | async-done | bytes 12582928 | tf_op jit(solution)/shard_map/all_gather | solution.py:98
  531.3 10.2 fusion.101
  541.6 86.9 %all-gather.26.cloned.1.call-done = bf16[4096,1536]{1,0:T(8,128)(2,1)} async-done(((bf16[128,1536]{1,0:T(8,128)(2,1)}), bf16[4096,1536]{1,0:T(8,128)(2,1)}) %all-gather.26.cloned.1.call-update) | async-done | bytes 12582928 | tf_op jit(solution)/shard_map/all_gather | solution.py:99
  628.5 11.2 multiply_convert_fusion.1
  639.7 10.7 fusion.102
  650.4 10.6 multiply_reduce_fusion.1
  664.0 2.3 convolution_convert_fusion.1
  666.4 2.3 copy.39
  668.6 78.5 %while.29 = (s32[]{:T(128)}, f32[8,2,256,96]{2,3,1,0:T(8,128)}, bf16[8,1024,96]{1,2,0:T(8,128)(2,1)}, bf16[8,1024,96]{1,2,0:T(8,128)(2,1)}, bf16[8,2,256,96]{2,3...) while((s32[]{:T(128)}, f32[8,2,256,96]{2,3,1,0:T(8,128)}, ...), condition=%wide.region_13.14_spmd.clone, body=%wide.region_11.13_spmd.clone.sunk | while | flops 508968448 | bytes 18244752 | solution.py:241
  682.6 2.1 fusion.163
  692.4 2.1 fusion.163
  702.2 2.1 fusion.163
  712.0 2.1 fusion.163
  721.7 2.1 fusion.163
  731.5 2.1 fusion.163
  741.3 2.1 fusion.163
  750.6 30.4 %reduce-scatter.7.cloned.1.call-done = bf16[256,768]{0,1:T(8,128)(2,1)} async-done(((bf16[1024,768]{0,1:T(8,128)(2,1)}), bf16[256,768]{0,1:T(8,128)(2,1)}) %reduce-scatter.7.cloned.1.call-update) | async-done | bytes 393232 | tf_op jit(solution)/shard_map/reduce_scatter | solution.py:251
  782.1 35.4 %reduce-scatter.9.cloned.1.call-done = bf16[256,768]{0,1:T(8,128)(2,1)} async-done(((bf16[1024,768]{0,1:T(8,128)(2,1)}), bf16[256,768]{0,1:T(8,128)(2,1)}) %reduce-scatter.9.cloned.1.call-update) | async-done | bytes 393232 | tf_op jit(solution)/shard_map/reduce_scatter | solution.py:254
  817.5 9.3 fusion.71
  826.9 26.1 %fusion.48 = f32[1536,8192]{1,0:T(8,128)} fusion(bf16[256,1536]{1,0:T(8,128)(2,1)} %multiply_convert_fusion.4, bf16[256,4096]{1,0:T(8,128)(2,1)} %copy-done.10, bf16[256,4096]{1,0:T(8,128)(2,1)} %get-tuple-element.229), kind=kOutput, calls=%fused_computation.60 | convolution fusion | flops 6450839552 | bytes 55312384 | tf_op jit(solution)/shard_map/dot_general | solution.py:51
  853.1 6.9 fusion.83
  861.2 13.9 fusion.79
  876.3 4.0 fusion.103
  880.3 7.6 fusion.54
  889.6 2.3 fusion.67
  891.9 42.4 %all-reduce.4 = (f32[1536]{0:T(1024)S(1)}, f32[1536]{0:T(1024)S(1)}) all-reduce(f32[1536]{0:T(1024)S(1)} %get-tuple-element.168, f32[1536]{0:T(1024)S(1)} %copy-done.12), channel_id=4, replica_groups=mesh['seq'=4,'fsdp'=8] {'seq','fsdp'}, use_global_device_ids=true, to_apply=%region_18.19.clone | all-reduce | flops 3072 | bytes 24576
  935.4 2.8 fusion.78
  938.3 95.4 %reduce-scatter.11.cloned.1.call-done = f32[48,3072]{1,0:T(8,128)} async-done(((f32[1536,3072]{1,0:T(8,128)}), f32[48,3072]{1,0:T(8,128)}) %reduce-scatter.11.cloned.1.call-update) | async-done | bytes 589840 | tf_op jit(solution)/shard_map/reduce_scatter | solution.py:285
  1037.1 433.6 %reduce-scatter.15.cloned.1.call-done = f32[48,8192]{1,0:T(8,128)} async-done(((f32[1536,8192]{1,0:T(8,128)}), f32[48,8192]{1,0:T(8,128)}) %reduce-scatter.15.cloned.1.call-update) | async-done | bytes 1572880 | tf_op jit(solution)/shard_map/reduce_scatter | solution.py:291
  1470.7 2.6 fusion.98
  1473.3 138.2 %reduce-scatter.13.cloned.1.call-done = f32[48,1536]{1,0:T(8,128)} async-done(((f32[1536,1536]{1,0:T(8,128)}), f32[48,1536]{1,0:T(8,128)}) %reduce-scatter.13.cloned.1.call-update) | async-done | bytes 294928 | tf_op jit(solution)/shard_map/reduce_scatter | solution.py:300
  1611.6 252.4 %reduce-scatter.17.cloned.1.call-done = f32[128,1536]{1,0:T(8,128)} async-done(((f32[4096,1536]{1,0:T(8,128)}), f32[128,1536]{1,0:T(8,128)}) %reduce-scatter.17.cloned.1.call-update) | async-done | bytes 786448 | tf_op jit(solution)/shard_map/reduce_scatter | solution.py:297
  (205 shorter events, 126.6 us)
Async XLA Ops:
  7.2 63.7 %all-gather.16.cloned.1.call-start = ((), (), s32[]{:S(2)}) async-start(), calls=%async_computation.9 | async-start | bytes 2433024 | tf_op jit(solution)/shard_map/all_gather | solution.py:94
  7.9 122.1 %all-gather.12.cloned.1.call-start = ((), (), s32[]{:S(2)}) async-start(), calls=%async_computation.7 | async-start | bytes 2433024 | tf_op jit(solution)/shard_map/all_gather | solution.py:93
  8.7 159.5 %all-gather.18.cloned.1.call-start = ((), (), s32[]{:S(2)}) async-start(), calls=%async_computation.10 | async-start | bytes 1966080 | tf_op jit(solution)/shard_map/all_gather | solution.py:135
  53.9 21.2 %copy-start.13 = (s32[1,4]{1,0:T(1,128)S(1)}, s32[1,4]{1,0:T(1,128)}, u32[]{:S(2)}) copy-start(s32[1,4]{1,0:T(1,128)} %param.28) | copy-start | bytes 52
  53.9 21.3 %copy-start.14 = (s32[1,8]{1,0:T(1,128)S(1)}, s32[1,8]{1,0:T(1,128)}, u32[]{:S(2)}) copy-start(s32[1,8]{1,0:T(1,128)} %param.29) | copy-start | bytes 100
  74.4 159.0 %all-gather.10.cloned.1.call-start = ((), (), s32[]{:S(2)}) async-start(), calls=%async_computation.6 | async-start | bytes 4866048 | tf_op jit(solution)/shard_map/all_gather | solution.py:92
  75.0 197.0 %all-gather.14.cloned.1.call-start = ((), (), s32[]{:S(2)}) async-start(), calls=%async_computation.8 | async-start | bytes 1966080 | tf_op jit(solution)/shard_map/all_gather | solution.py:134
  130.0 2.9 copy-start
  134.7 201.9 %all-gather.20.cloned.1.call-start = ((), (), s32[]{:S(2)}) async-start(), calls=%async_computation.11 | async-start | bytes 4866048 | tf_op jit(solution)/shard_map/all_gather | solution.py:95
  135.3 298.9 %all-gather.22.cloned.1.call-start = ((), (), s32[]{:S(2)}) async-start(), calls=%async_computation.12 | async-start | bytes 12976128 | tf_op jit(solution)/shard_map/all_gather | solution.py:97
  136.0 395.3 %all-gather.24.cloned.1.call-start = ((), (), s32[]{:S(2)}) async-start(), calls=%async_computation.13 | async-start | bytes 12976128 | tf_op jit(solution)/shard_map/all_gather | solution.py:98
  136.8 491.7 %all-gather.26.cloned.1.call-start = ((), (), s32[]{:S(2)}) async-start(), calls=%async_computation.14 | async-start | bytes 12976128 | tf_op jit(solution)/shard_map/all_gather | solution.py:99
  137.5 643.4 %reduce-scatter.7.cloned.1.call-start = ((), (), s32[]{:S(2)}) async-start(), calls=%async_computation.15 | async-start | bytes 1966080 | tf_op jit(solution)/shard_map/reduce_scatter | solution.py:251
  306.2 30.4 %copy-start.5 = (bf16[8,2,256,96]{2,3,1,0:T(8,128)(2,1)}, bf16[8,2,256,96]{2,3,1,0:T(8,128)(2,1)S(1)}, u32[]{:S(2)}) copy-start(bf16[8,2,256,96]{2,3,1,0:T(8,128)(2,1)S(1)} %get-tuple-element.500) | copy-start | bytes 2359300
  639.7 10.7 copy-start.10
  639.7 24.3 %slice-start = ((s8[4718592]{0:T(1024)(128)(4,1)}), s8[4194304]{0:T(1024)(128)(4,1)S(1)}, s32[]{:S(2)}) async-start(s8[4718592]{0:T(1024)(128)(4,1)} %bitcast.229), calls=%async_computation.21 | async-start | bytes 8388608
  650.4 10.6 copy-start.7
  650.4 13.7 slice-start.1
  662.8 1.2 copy-start.1
  747.2 70.3 %reduce-scatter.9.cloned.1.call-start = ((), (), s32[]{:S(2)}) async-start(), calls=%async_computation.16 | async-start | bytes 1966080 | tf_op jit(solution)/shard_map/reduce_scatter | solution.py:254
  747.9 285.8 %reduce-scatter.11.cloned.1.call-start = ((), (), s32[]{:S(2)}) async-start(), calls=%async_computation.17 | async-start | bytes 19464192 | tf_op jit(solution)/shard_map/reduce_scatter | solution.py:285
  826.8 643.9 %reduce-scatter.15.cloned.1.call-start = ((), (), s32[]{:S(2)}) async-start(), calls=%async_computation.19 | async-start | bytes 51904512 | tf_op jit(solution)/shard_map/reduce_scatter | solution.py:291
  853.1 758.5 %reduce-scatter.13.cloned.1.call-start = ((), (), s32[]{:S(2)}) async-start(), calls=%async_computation.18 | async-start | bytes 9732096 | tf_op jit(solution)/shard_map/reduce_scatter | solution.py:300
  860.0 1.2 copy-start.8
  860.0 1004.0 %reduce-scatter.17.cloned.1.call-start = ((), (), s32[]{:S(2)}) async-start(), calls=%async_computation.20 | async-start | bytes 25952256 | tf_op jit(solution)/shard_map/reduce_scatter | solution.py:297
  875.2 1.2 copy-start.6
  876.3 4.0 copy-start.4
  880.3 7.6 copy-start.3
  887.9 1.7 copy-start.9
  887.9 1.7 copy-start.11
  889.6 2.3 copy-start.12
  889.6 45.8 %copy-start.2 = (f32[256,1536]{1,0:T(8,128)S(1)}, f32[256,1536]{1,0:T(8,128)}, u32[]{:S(2)}) copy-start(f32[256,1536]{1,0:T(8,128)} %copy-done.1) | copy-start | bytes 4718596
Sparse Core Ops, SparseCore 0:
  10.9 59.9 all-gather.15
  73.8 56.1 all-gather.11
  132.1 35.9 all-gather.17
  170.9 62.4 all-gather.9
  235.4 36.5 all-gather.13
  274.7 61.8 all-gather.19
  339.5 94.7 all-gather.21
  437.1 94.2 all-gather.23
  534.2 94.2 all-gather.25
  747.3 33.5 reduce-scatter.6
  783.2 34.2 reduce-scatter.8
  827.0 206.7 reduce-scatter.10
  1040.1 430.5 reduce-scatter.14
  1477.1 134.4 reduce-scatter.12
  1619.6 244.3 reduce-scatter.16
where the time goes:
time: 1880 us; the launch traced here: 1870 us
  waiting for transfers between devices  1480 us (79%)
  matrix products  239 us (13%)
  blocking collectives  84.5 us (4%)
  local copies, waits for them, and re-layouts  27.8 us (1%)
  other arithmetic  24.9 us (1%)
    reduce_scatter x1, waiting for transfers between devices, on_device(): lax.psum_scatter(column_terms(normed_two, jnp.concatenate([grad_gate_in,...  434 us
    reduce_scatter x1, waiting for transfers between devices, on_device(): lax.psum_scatter(column_terms(hidden, grad_branch), ('seq', 'fsdp'), scat...  252 us
    reduce_scatter x1, waiting for transfers between devices, on_device(): lax.psum_scatter(column_terms(attention_output, grad_attn_out), ('seq', '...  138 us
    reduce_scatter x1, waiting for transfers between devices, on_device(): lax.psum_scatter(column_terms(first_normalized, projected_grads), ('seq',...  95.4 us
    all_gather x1, waiting for transfers between devices, on_device(): lax.all_gather(w_gate, ('seq', 'fsdp'), axis=0, tiled=True)  92.7 us
    all_gather x1, waiting for transfers between devices, on_device(): lax.all_gather(w_down, ('seq', 'fsdp'), axis=0, tiled=True)  86.9 us
    all_gather x1, waiting for transfers between devices, on_device(): lax.all_gather(w_up, ('seq', 'fsdp'), axis=0, tiled=True)  86.8 us
    unnamed x2, blocking collectives  84.5 us
  transfers between devices with their start and end apart: 15, of which 15 were waited for; matrix products, arithmetic and copies ran while one was open for 9% of the time, Pallas kernels for 0%

commit v1 on v0

v1 whole, which is shorter than its diff:
```python
import math

import jax
import jax.numpy as jnp
from jax import lax
from jax.sharding import Mesh
from jax.sharding import PartitionSpec as P

QUERY_HEADS = 16
KEY_VALUE_HEADS = 8
HEAD_SIZE = 96
FF = 4096
STRETCH = 128

EPSILON = 1e-05
THETA = 100000.0

BF = jnp.bfloat16
F32 = jnp.float32


def layout(doc_lengths, slot_map, slots):
    count = slot_map.shape[0]
    stretches = jnp.arange(count, dtype=jnp.int32)
    logical = jnp.sum(
        jnp.where(slot_map[None, :] == slots[:, None], stretches[None, :], 0), axis=1
    )
    places = (
        logical[:, None] * STRETCH + jnp.arange(STRETCH, dtype=jnp.int32)[None, :]
    ).reshape(-1)
    endings = jnp.cumsum(doc_lengths)
    passed = endings[None, :] <= places[:, None]
    document = jnp.sum(passed.astype(jnp.int32), axis=1)
    starts = jnp.sum(jnp.where(passed, doc_lengths[None, :], 0), axis=1)
    return document, places - starts


def rotary_tables(positions):
    half = HEAD_SIZE // 2
    freqs = THETA ** (-2.0 * jnp.arange(half, dtype=F32) / HEAD_SIZE)
    angles = positions.astype(F32)[:, None] * freqs[None, :]
    return jnp.cos(angles)[:, None, :], jnp.sin(angles)[:, None, :]


def apply_rotary(rows, cosine, sine):
    half = rows.shape[-1] // 2
    first, second = rows[..., :half], rows[..., half:]
    return jnp.concatenate(
        [first * cosine - second * sine, second * cosine + first * sine], axis=-1
    )


def product(left, right):
    return jnp.dot(left, right, preferred_element_type=F32)


def over_rows(left, right):
    return lax.dot_general(left, right, (((0,), (0,)), ((), ())), preferred_element_type=F32)


def times_transposed(left, right):
    return lax.dot_general(left, right, (((1,), (1,)), ((), ())), preferred_element_type=F32)


def on_device(n, m, *operands):
    (
        tokens,
        gain_attn,
        w_query,
        key_weight,
        value_weight,
        w_out,
        gain_mlp,
        w_gate,
        w_up,
        w_down,
        out_grad,
        lengths,
        stretch_map,
    ) = operands
    at_z, at_y = lax.axis_index("z"), lax.axis_index("y")
    at_x, at_c = lax.axis_index("x"), lax.axis_index("c")
    rank = at_x * 2 + at_c
    tp = 4

    def shift(a, axis, size, by):
        return lax.ppermute(a, axis, [(i, (i + by) % size) for i in range(size)])

    def across(a, delta):
        if delta == 1:
            return lax.ppermute(a, "c", [(0, 1), (1, 0)])
        if delta == 2:
            return lax.ppermute(a, "x", [(0, 1), (1, 0)])
        return lax.ppermute(a, ("x", "c"), [(i, i ^ delta) for i in range(tp)])

    def ring(a, axis, size):
        blocks = [a]
        for _ in range(size - 1):
            blocks.append(shift(blocks[-1], axis, size, 1))
        return blocks

    def ring_sum(block, axis, size):
        total = block(1)
        for step in range(1, size):
            arrived = shift(total, axis, size, 1)
            mine = block((step + 1) % size)
            total = arrived.astype(F32) + mine.astype(F32)
            if step < size - 1:
                total = total.astype(BF)
        return total

    def pick(a, index, axis):
        return lax.dynamic_index_in_dim(a, index, axis, keepdims=False)

    def put(a, piece, *index):
        index = index + (0,) * (a.ndim - len(index))
        return lax.dynamic_update_slice(a, piece, index)

    def stack_z(blocks):
        out = jnp.zeros((n,) + blocks[0].shape, blocks[0].dtype)
        for k, block in enumerate(blocks):
            out = put(out, block[None], (at_z - k) % n)
        return out

    def gather_all(shard):
        pieces = [(0, 0, 0, stack_z(ring(shard, "z", n)))]
        pieces = [(k, 0, 0, p) for k, p in enumerate(ring(pieces[0][3], "y", m))]
        pieces += [(k, 1, 0, across(p, 2)) for k, _, _, p in pieces]
        pieces += [(k, j, 1, across(p, 1)) for k, j, _, p in pieces]
        rows, cols = shard.shape
        out = jnp.zeros((n, m, 2, 2, rows, cols), shard.dtype)
        for k, j, i, p in pieces:
            out = put(out, p[:, None, None, None], 0, (at_y - k) % m, at_x ^ j, at_c ^ i)
        return out.reshape(n * m * tp * rows, cols)

    def gather_zy(shard):
        out = jnp.zeros((n, m) + shard.shape, shard.dtype)
        for k, block in enumerate(ring(shard, "z", n)):
            for j, piece in enumerate(ring(block, "y", m)):
                out = put(out, piece[None, None], (at_z - k) % n, (at_y - j) % m)
        return out.reshape((n * m * shard.shape[0],) + shard.shape[1:])

    def sum_zy(terms):
        terms = ring_sum(lambda k: pick(terms, (at_y - k) % m, 1), "y", m).astype(BF)
        return ring_sum(lambda k: pick(terms, (at_z - k) % n, 0), "z", n)

    def sum_all(terms):
        cols = terms.shape[1]
        terms = terms.reshape(n, m, 2, 2, -1, cols)
        terms = ring_sum(lambda k: pick(terms, at_c ^ k, 3), "c", 2).astype(BF)
        terms = ring_sum(lambda k: pick(terms, at_x ^ k, 2), "x", 2).astype(BF)
        return sum_zy(terms)

    def spread(rows):
        by_c, by_x = across(rows, 1), across(rows, 2)
        return jnp.concatenate([rows, by_c, by_x, across(by_x, 1)], axis=0)

    def collect(terms):
        near, far = jnp.split(terms.reshape(tp, -1, terms.shape[-1]), 2)
        by_c = across(jnp.stack([near[1], far[1]]).astype(BF), 1).astype(F32)
        by_x = across((far[0] + by_c[1]).astype(BF), 2).astype(F32)
        return near[0] + by_c[0] + by_x

    token_count, width = tokens.shape[1:]
    group_ratio = QUERY_HEADS // KEY_VALUE_HEADS
    scale = 1.0 / math.sqrt(HEAD_SIZE)
    shard_rows = w_query.shape[0]
    unit = w_down.shape[0]
    pair_cols = KEY_VALUE_HEADS * HEAD_SIZE
    gain_one = gain_attn.astype(F32)[:, None]
    gain_two = gain_mlp.astype(F32)[:, None]

    own = tokens[0]
    group_rows = jnp.concatenate(ring(own, "z", n), axis=0)
    span = group_rows.shape[0]

    def scaled(weight, gain):
        return (weight.astype(F32) * gain).astype(BF)

    kv_weight = gather_all(
        scaled(jnp.concatenate([key_weight, value_weight], axis=1), gain_one)
    )
    query_out = gather_all(jnp.concatenate([scaled(w_query, gain_one), w_out], axis=1))
    q_weight, out_weight = query_out[:, :width], query_out[:, width:]

    gate_up = jnp.stack([w_gate, w_up], axis=1).reshape(shard_rows, 2, n * m, tp, unit)
    gate_up = (gate_up.astype(F32) * gain_two[:, :, None, None, None]).astype(BF)
    ff_cols = 2 * n * m * unit
    mine = jnp.zeros((2, 2, shard_rows, ff_cols), BF)
    for delta in range(tp):
        part = pick(gate_up, rank ^ delta, 3).reshape(shard_rows, ff_cols)
        if delta:
            part = across(part, delta)
        mine = put(mine, part[None, None], at_x ^ (delta >> 1), at_c ^ (delta & 1))
    gu_weight = gather_zy(mine.reshape(tp * shard_rows, ff_cols))
    down_weight = gather_zy(w_down)
    grad_rows = spread(out_grad[0])

    slots_each = stretch_map.shape[1] // n
    slots = (
        ((at_z - jnp.arange(n, dtype=jnp.int32)) % n)[:, None] * slots_each
        + jnp.arange(slots_each, dtype=jnp.int32)[None, :]
    ).reshape(-1)
    doc_all, place_all = layout(lengths[0], stretch_map[0], slots)
    allowed = (doc_all[:token_count, None] == doc_all[None, :]) & (
        place_all[None, :] <= place_all[:token_count, None]
    )
    cosine, sine = rotary_tables(place_all)
    own_cosine, own_sine = cosine[:token_count], sine[:token_count]

    inputs = group_rows.astype(F32)
    inverse_all = lax.rsqrt(jnp.mean(inputs * inputs, axis=-1, keepdims=True) + EPSILON)
    normed_group = (inputs * inverse_all).astype(BF)
    inputs = own.astype(F32)
    first_inverse = inverse_all[:token_count]
    first_normed = inputs * first_inverse
    normed_one = normed_group[:token_count]

    keys_values = product(normed_group, kv_weight)
    keys = apply_rotary(
        keys_values[:, :pair_cols].reshape(span, KEY_VALUE_HEADS, HEAD_SIZE), cosine, sine
    ).astype(BF)
    values = keys_values[:, pair_cols:].reshape(span, KEY_VALUE_HEADS, HEAD_SIZE).astype(BF)
    queries = apply_rotary(
        product(normed_one, q_weight).reshape(token_count, QUERY_HEADS, HEAD_SIZE),
        own_cosine,
        own_sine,
    ).astype(BF)

    def by_head(rows):
        return rows.reshape(token_count, KEY_VALUE_HEADS, group_ratio, HEAD_SIZE).transpose(
            1, 2, 0, 3
        )

    query_heads = by_head(queries)
    key_heads = keys.transpose(1, 0, 2)
    value_heads = values.transpose(1, 0, 2)

    def head_scores(head_queries, head_keys):
        scores = (
            jnp.einsum("rqd,kd->rqk", head_queries, head_keys, preferred_element_type=F32) * scale
        )
        return jnp.where(allowed[None], scores, -1e30)

    def head_forward(item):
        head_queries, head_keys, head_values = item
        scores = head_scores(head_queries, head_keys)
        peak = jnp.max(scores, axis=-1, keepdims=True)
        weights = jnp.exp(scores - peak)
        totals = jnp.sum(weights, axis=-1, keepdims=True)
        probs = weights / totals
        mixed = jnp.einsum(
            "rqk,kd->rqd", probs.astype(BF), head_values, preferred_element_type=F32
        )
        return mixed.astype(BF), peak[..., 0] + jnp.log(totals[..., 0])

    mixed_heads, log_totals = lax.map(head_forward, (query_heads, key_heads, value_heads))
    attention_output = mixed_heads.transpose(2, 0, 1, 3).reshape(token_count, width)
    resid = inputs + product(attention_output, out_weight)

    second_inverse = lax.rsqrt(jnp.mean(resid * resid, axis=-1, keepdims=True) + EPSILON)
    second_normed = resid * second_inverse
    normed_two = spread(second_normed.astype(BF))
    gate_up_rows = product(normed_two, gu_weight)
    gate, upper = jnp.split(gate_up_rows, 2, axis=1)
    sigmoid_gate = jax.nn.sigmoid(gate)
    silu_gate = gate * sigmoid_gate
    hidden = (silu_gate * upper).astype(BF)
    down_terms = over_rows(hidden, grad_rows).astype(BF).reshape(n, m, unit, width)
    result = (resid + collect(product(hidden, down_weight))).astype(BF)

    grad_hidden = times_transposed(grad_rows, down_weight)
    grad_gate_in = (
        grad_hidden * upper * sigmoid_gate * (1.0 + gate * (1.0 - sigmoid_gate))
    ).astype(BF)
    grad_up_in = (grad_hidden * silu_gate).astype(BF)
    grad_gate_up = jnp.concatenate([grad_gate_in, grad_up_in], axis=1)
    scaled_two = collect(times_transposed(grad_gate_up, gu_weight))
    gate_up_terms = (
        over_rows(normed_two, grad_gate_up).astype(BF).reshape(n, m, tp * shard_rows, ff_cols)
    )

    def norm_back(scaled_grad, normed, inverse):
        return inverse * (
            scaled_grad - normed * jnp.mean(scaled_grad * normed, axis=-1, keepdims=True)
        )

    grad_resid = out_grad[0].astype(F32) + norm_back(scaled_two, second_normed, second_inverse)
    grad_attn_out = grad_resid.astype(BF)

    out_terms = over_rows(attention_output, grad_attn_out).astype(BF)
    head_gradient = by_head(times_transposed(grad_attn_out, out_weight).astype(BF))

    def head_backward(item):
        head_queries, head_keys, head_values, head_grads, head_totals = item
        probs = jnp.exp(head_scores(head_queries, head_keys) - head_totals[..., None])
        grad_probs = jnp.einsum(
            "rqd,kd->rqk", head_grads, head_values, preferred_element_type=F32
        )
        centre = jnp.sum(probs * grad_probs, axis=-1, keepdims=True)
        grad_scores = (probs * (grad_probs - centre)).astype(BF)
        grad_queries = (
            jnp.einsum("rqk,kd->rqd", grad_scores, head_keys, preferred_element_type=F32) * scale
        )
        grad_keys = (
            jnp.einsum("rqk,rqd->kd", grad_scores, head_queries, preferred_element_type=F32)
            * scale
        )
        grad_values = jnp.einsum(
            "rqk,rqd->kd", probs.astype(BF), head_grads, preferred_element_type=F32
        )
        return grad_queries, grad_keys, grad_values

    grad_query_heads, grad_key_heads, grad_value_heads = lax.map(
        head_backward, (query_heads, key_heads, value_heads, head_gradient, log_totals)
    )
    grad_key_rows = apply_rotary(grad_key_heads.transpose(1, 0, 2), cosine, -sine)
    grad_kv = jnp.concatenate(
        [
            grad_key_rows.reshape(span, pair_cols).astype(BF),
            grad_value_heads.transpose(1, 0, 2).reshape(span, pair_cols).astype(BF),
        ],
        axis=1,
    )
    grad_query_rows = (
        apply_rotary(
            grad_query_heads.transpose(2, 0, 1, 3).reshape(token_count, QUERY_HEADS, HEAD_SIZE),
            own_cosine,
            -own_sine,
        )
        .reshape(token_count, width)
        .astype(BF)
    )
    kv_terms = over_rows(normed_group, grad_kv).astype(BF)
    query_terms = over_rows(normed_one, grad_query_rows).astype(BF)
    by_block = grad_kv.reshape(n, token_count, 2 * pair_cols)
    own_kv = ring_sum(lambda k: by_block[k], "z", n).astype(BF)
    scaled_one = times_transposed(grad_query_rows, q_weight) + times_transposed(own_kv, kv_weight)
    input_grad = (grad_resid + norm_back(scaled_one, first_normed, first_inverse)).astype(BF)

    down_owned = sum_zy(down_terms)
    parts = sum_zy(gate_up_terms).astype(BF).reshape(tp, shard_rows, ff_cols)
    arrived = []
    for delta in range(tp):
        part = pick(parts, rank ^ delta, 0)
        arrived.append(across(part, delta) if delta else part)
    arrived = jnp.stack(arrived)
    gate_up_owned = jnp.stack([pick(arrived, rank ^ r, 0) for r in range(tp)], axis=1)
    gate_up_owned = (
        gate_up_owned.astype(F32)
        .reshape(shard_rows, tp, 2, n * m, unit)
        .transpose(2, 0, 3, 1, 4)
        .reshape(2, shard_rows, n * m * tp * unit)
    )
    out_owned = sum_all(out_terms)
    query_owned = sum_all(query_terms)
    kv_owned = sum_all(kv_terms)
    key_owned, value_owned = kv_owned[:, :pair_cols], kv_owned[:, pair_cols:]
    gate_owned, up_owned = gate_up_owned[0], gate_up_owned[1]

    def along(weight, grad):
        return jnp.sum(weight.astype(F32) * grad, axis=1)

    gain_one_owned = (
        along(w_query, query_owned)
        + along(key_weight, key_owned)
        + along(value_weight, value_owned)
    )
    gain_two_owned = along(w_gate, gate_owned) + along(w_up, up_owned)
    return (
        result[None],
        input_grad[None],
        gain_one_owned,
        query_owned * gain_one,
        key_owned * gain_one,
        value_owned * gain_one,
        out_owned,
        gain_two_owned,
        gate_owned * gain_two,
        up_owned * gain_two,
        down_owned,
    )


def solution(mesh):
    n, groups = mesh.shape["seq"], mesh.shape["fsdp"]
    m = groups // 4
    fine = Mesh(mesh.devices.reshape(n, m, 2, 2), ("z", "y", "x", "c"))
    fsdp = ("y", "x", "c")
    every = ("z", "y", "x", "c")
    rows, vector, matrix = P(fsdp, "z", None), P(every), P(every, None)
    in_specs = (
        rows,
        vector,
        matrix,
        matrix,
        matrix,
        matrix,
        vector,
        matrix,
        matrix,
        matrix,
        rows,
        P(fsdp, None),
        P(fsdp, None),
    )
    out_specs = (rows, rows, vector) + (matrix,) * 4 + (vector,) + (matrix,) * 3

    def step(*operands):
        return on_device(n, m, *operands)

    return jax.shard_map(
        step, mesh=fine, in_specs=in_specs, out_specs=out_specs, check_vma=False
    )
```

time: 1880 us -> 772 us (0.41)
  waiting for transfers between devices: 1480 us -> 364 us
  blocking collectives: 84.5 us -> 0 us
  matrix products: 239 us -> 179 us
  starting transfers between devices: 1.12 us -> 61.1 us
  local copies, waits for them, and re-layouts: 27.8 us -> 83.2 us
  other arithmetic: 24.9 us -> 72.7 us
    reduce_scatter x6 -> x0, waiting for transfers between devices: 985 us -> none  [the longest x1 434 us: on_device(): lax.psum_scatter(column_terms(normed_two, jnp.concatenate([grad_gate_in,...]
    all_gather x9 -> x0, waiting for transfers between devices: 488 us -> none  [the longest x1 92.7 us: on_device(): lax.all_gather(w_gate, ('seq', 'fsdp'), axis=0, tiled=True)]
    ppermute x0 -> x82, waiting for transfers between devices: none -> 364 us  [the longest x54 261 us: shift(): return lax.ppermute(a, axis, [(i, (i + by) % size) for i in range(size)])]
    unnamed x2 -> x0, blocking collectives: 84.5 us -> none
    ppermute x0 -> x82, starting transfers between devices: none -> 61.1 us  [the longest x54 45.1 us: shift(): return lax.ppermute(a, axis, [(i, (i + by) % size) for i in range(size)])]
    dynamic_update_slice x0 -> x42, local copies, waits for them, and re-layouts: none -> 31.6 us  [put(): return lax.dynamic_update_slice(a, piece, index)]
    convert_element_type x12 -> x43, other arithmetic: 3.19 us -> 31.2 us  [the longest x1 5.59 us: on_device(): normed_group = (inputs * inverse_all).astype(BF)]
    dot_general x4 -> x5, matrix products: 56.3 us -> 29.9 us  [over_rows(): lax.dot_general(left, right, (((0,), (0,)), ((), ())), preferred_element_...]
  transfers between devices with their start and end apart: 15 -> 82, of which waited for: 15 -> 45; matrix products, arithmetic and copies ran while one was open for 9% -> 40% of each run, Pallas kernels for 0% -> 0%
where the time goes in v1:
time: 772 us; the launch traced here: 763 us
  waiting for transfers between devices  364 us (47%)
  matrix products  179 us (23%)
  local copies, waits for them, and re-layouts  83.2 us (11%)
  other arithmetic  72.7 us (9%)
  starting transfers between devices  61.1 us (8%)
    ppermute x54, waiting for transfers between devices, shift(): return lax.ppermute(a, axis, [(i, (i + by) % size) for i in range(size)])  261 us
    ppermute x10, waiting for transfers between devices, across(): return lax.ppermute(a, 'x', [(0, 1), (1, 0)])  89.5 us
    ppermute x54, starting transfers between devices, shift(): return lax.ppermute(a, axis, [(i, (i + by) % size) for i in range(size)])  45.1 us
    dynamic_update_slice x42, local copies, waits for them, and re-layouts, put(): return lax.dynamic_update_slice(a, piece, index)  31.6 us
    dot_general x5, matrix products, product(): return jnp.dot(left, right, preferred_element_type=F32)  30.8 us
    dot_general x5, matrix products, over_rows(): lax.dot_general(left, right, (((0,), (0,)), ((), ())), preferred_element_...  29.9 us
    dot_general x5, matrix products, times_transposed(): lax.dot_general(left, right, (((1,), (1,)), ((), ())), preferred_element_...  25.1 us
    dot_general x16, matrix products, head_scores(): jnp.einsum('rqd,kd->rqk', head_queries, head_keys, preferred_element_type...  20.8 us
  transfers between devices with their start and end apart: 82, of which 45 were waited for; matrix products, arithmetic and copies ran while one was open for 40% of the time, Pallas kernels for 0%

profile of v1, /device:TPU:0, one launch (start us, length us, event | category | flops | bytes accessed | tf_op | source)
XLA Modules:
  0.0 762.9 jit_solution(6977610578685852118)
XLA Ops:
  30.2 5.8 collective-permute-done.27
  36.8 6.3 collective-permute-done.28
  49.1 4.0 collective-permute-done.14
  57.7 19.6 %collective-permute-done.15 = bf16[48,1536]{1,0:T(8,128)(2,1)S(1)} collective-permute-done((bf16[48,1536]{1,0:T(8,128)(2,1)S(1)}, bf16[48,1536]{1,0:T(8,128)(2,1)S(1)}, u32[]{:S(2)}, u32[]{:S(2)}) %collective-permute-start.15) | collective-permute-done | bytes 147488 | tf_op jit(solution)/shard_map/ppermute | solution.py:87
  79.7 6.4 collective-permute-done.4
  88.4 5.7 collective-permute-done.38
  94.2 10.9 %collective-permute-done.39 = bf16[128,1536]{1,0:T(8,128)(2,1)S(1)} collective-permute-done((bf16[128,1536]{1,0:T(8,128)(2,1)}, bf16[128,1536]{1,0:T(8,128)(2,1)S(1)}, u32[]{:S(2)}, u32[]{:S(2)}) %collective-permute-start.39) | collective-permute-done | bytes 393248 | tf_op jit(solution)/shard_map/ppermute | solution.py:87
  105.1 8.5 %collective-permute-done.5 = bf16[48,3072]{1,0:T(8,128)(2,1)S(1)} collective-permute-done((bf16[48,3072]{1,0:T(8,128)(2,1)S(1)}, bf16[48,3072]{1,0:T(8,128)(2,1)S(1)}, u32[]{:S(2)}, u32[]{:S(2)}) %collective-permute-start.5) | collective-permute-done | bytes 294944 | tf_op jit(solution)/shard_map/ppermute | solution.py:87
  128.8 6.3 collective-permute-done.40
  139.8 7.9 %collective-permute-done.42 = bf16[128,1536]{1,0:T(8,128)(2,1)S(1)} collective-permute-done((bf16[128,1536]{1,0:T(8,128)(2,1)S(1)}, bf16[128,1536]{1,0:T(8,128)(2,1)S(1)}, u32[]{:S(2)}, u32[]{:S(2)}) %collective-permute-start.42) | collective-permute-done | bytes 393248 | tf_op jit(solution)/shard_map/ppermute | solution.py:87
  153.1 35.9 %collective-permute-done.31 = bf16[192,2048]{1,0:T(8,128)(2,1)S(1)} collective-permute-done((bf16[192,2048]{1,0:T(8,128)(2,1)}, bf16[192,2048]{1,0:T(8,128)(2,1)S(1)}, u32[]{:S(2)}, u32[]{:S(2)}) %collective-permute-start.31) | collective-permute-done | bytes 786464 | tf_op jit(solution)/shard_map/ppermute | solution.py:87
  192.3 20.2 %collective-permute-done.7 = bf16[4,48,3072]{2,1,0:T(8,128)(2,1)S(1)} collective-permute-done((bf16[4,48,3072]{2,1,0:T(8,128)(2,1)}, bf16[4,48,3072]{2,1,0:T(8,128)(2,1)S(1)}, u32[]{:S(2)}, u32[]{:S(2)}) %collective-permute-start.7) | collective-permute-done | bytes 1179680 | tf_op jit(solution)/shard_map/ppermute | solution.py:93
  215.2 8.8 %collective-permute-done.2 = bf16[256,1536]{1,0:T(8,128)(2,1)S(1)} collective-permute-done((bf16[256,1536]{1,0:T(8,128)(2,1)S(1)}, bf16[256,1536]{1,0:T(8,128)(2,1)S(1)}, u32[]{:S(2)}, u32[]{:S(2)}) %collective-permute-start.2) | collective-permute-done | bytes 786464 | tf_op jit(solution)/shard_map/ppermute | solution.py:87
  226.3 5.6 fusion.49
  231.9 5.0 fusion.144
  255.8 4.5 fusion.61
  260.7 36.8 %while.28 = (s32[]{:T(128)}, bf16[8,2,256,96]{2,3,1,0:T(8,128)(2,1)}, f32[8,2,256]{2,1,0:T(2,128)}, bf16[8,2,256,96]{2,3,1,0:T(8,128)(2,1)S(1)}, bf16[8,1024,96]...) while((s32[]{:T(128)}, ...), condition=%wide.region_8.9_spmd.clone, body=%wide.region_5.8_spmd.clone.sunk | while | flops 208453120 | bytes 7959149 | solution.py:257
  297.5 4.9 multiply_reduce_fusion.2
  308.5 13.8 %collective-permute-done.24 = bf16[256,1536]{1,0:T(8,128)(2,1)S(1)} collective-permute-done((bf16[256,1536]{1,0:T(8,128)(2,1)S(1)}, bf16[256,1536]{1,0:T(8,128)(2,1)S(1)}, u32[]{:S(2)}, u32[]{:S(2)}) %collective-permute-start.24) | collective-permute-done | bytes 786464 | tf_op jit(solution)/shard_map/ppermute | solution.py:93
  326.5 10.9 %fusion.113 = f32[1024,2048]{1,0:T(8,128)} fusion(bf16[1536,2048]{1,0:T(8,128)(2,1)S(1)} %bitcast.538, bf16[256,1536]{1,0:T(8,128)(2,1)S(1)} %collective-permute-done.25, bf16[256,1536]{1,0:T(8,128)(2,1)S(1)} %collective-permute-done.24, bf16[256,1536]{1,0:T(8,128)(2,1)S(1)} %collective-permute-done.23, bf16[256,1536]{1,0:T(8,128)(2,1)S(1)} %multiply_convert_fusion.5), kind=kOutput, calls=%fused_computation.233 | convolution fusion | flops 6455033856 | bytes 17825792 | tf_op jit(solution)/shard_map/dot_general | solution.py:54
  337.4 10.0 %multiply_convert_fusion.2 = (bf16[1024,1024]{1,0:T(8,128)(2,1)}, bf16[1024,1024]{1,0:T(8,128)(2,1)}, bf16[1024,1024]{1,0:T(8,128)(2,1)S(1)}) fusion(f32[1024,2048]{1,0:T(8,128)} %fusion.113, bf16[1024,1536]{1,0:T(8,128)(2,1)S(1)} %bitcast.553, bf16[256,1536]{1,0:T(8,128)(2,1)} %collective-permute-done.47, bf16[256,1536]{1,0:T(8,128)(2,1)} %collective-permute-done.46, ...), kind=kOutput, calls=%fused_computation.87 | convolution fusion | flops 3249537024 | bytes 20971520 | tf_op jit(solution)/shard_map/dot_general | solution.py:62
  347.5 5.4 fusion.143
  352.9 5.4 convolution_convert_fusion.5
  359.3 9.7 %fusion.142 = (bf16[1024,1536]{1,0:T(8,128)(2,1)}, f32[1024,1536]{1,0:T(8,128)S(1)}) fusion(bf16[1536,2048]{1,0:T(8,128)(2,1)S(1)} %bitcast.539, bf16[1024,1024]{1,0:T(8,128)(2,1)} %get-tuple-element.223, bf16[1024,1024]{1,0:T(8,128)(2,1)} %get-tuple-element.222), kind=kOutput, calls=%fused_computation.341 | convolution fusion | flops 6452412416 | bytes 19922944 | tf_op jit(solution)/shard_map/dot_general | solution.py:62
  373.4 9.7 %convolution_convert_fusion.2 = bf16[1536,2048]{1,0:T(8,128)(2,1)S(1)} fusion(bf16[1024,1024]{1,0:T(8,128)(2,1)} %get-tuple-element.223, bf16[1024,1024]{1,0:T(8,128)(2,1)} %get-tuple-element.222, bf16[256,1536]{1,0:T(8,128)(2,1)} %copy-done.60, bf16[256,1536]{1,0:T(8,128)(2,1)} %copy-done.58, bf16[256,1536]{1,0:T(8,128)(2,1)} %copy-done.59, ...), kind=kOutput, calls=%fused_computation.63 | convolution fusion | flops 6466568192 | bytes 13631488 | tf_op jit(solution)/shard_map/dot_general | solution.py:58
  388.3 7.4 collective-permute-done.78
  406.7 10.8 %collective-permute-done.49 = bf16[256,1536]{1,0:T(8,128)(2,1)S(1)} collective-permute-done((bf16[256,1536]{1,0:T(8,128)(2,1)S(1)}, bf16[256,1536]{1,0:T(8,128)(2,1)S(1)}, u32[]{:S(2)}, u32[]{:S(2)}) %collective-permute-start.49) | collective-permute-done | bytes 786464 | tf_op jit(solution)/shard_map/ppermute | solution.py:93
  418.1 11.3 %collective-permute-done.44 = bf16[256,1536]{1,0:T(8,128)(2,1)S(1)} collective-permute-done((bf16[256,1536]{1,0:T(8,128)(2,1)S(1)}, bf16[256,1536]{1,0:T(8,128)(2,1)S(1)}, u32[]{:S(2)}, u32[]{:S(2)}) %collective-permute-start.44) | collective-permute-done | bytes 786464 | tf_op jit(solution)/shard_map/ppermute | solution.py:93
  429.4 3.9 multiply_add_fusion
  435.7 4.7 convolution_convert_fusion.3
  445.1 78.9 %while.29 = (s32[]{:T(128)}, f32[8,2,256,96]{2,3,1,0:T(8,128)}, f32[8,1024,96]{1,2,0:T(8,128)}, bf16[8,1024,96]{1,2,0:T(8,128)(2,1)S(1)}, bf16[8,2,256,96]{2,3,1...) while((s32[]{:T(128)}, f32[8,2,256,96]{2,3,1,0:T(8,128)}, ...), condition=%wide.region_13.14_spmd.clone, body=%wide.region_11.13_spmd.clone.sunk | while | flops 508968448 | bytes 18244744 | solution.py:314
  528.2 7.4 convolution_convert_fusion.1
  535.7 5.4 constant_dynamic-slice_fusion.2
  542.8 4.2 collective-permute-start.50
  557.1 8.0 %collective-permute-done.50 = bf16[256,1536]{0,1:T(8,128)(2,1)S(1)} collective-permute-done((bf16[256,1536]{0,1:T(8,128)(2,1)S(1)}, bf16[256,1536]{0,1:T(8,128)(2,1)S(1)}, u32[]{:S(2)}, u32[]{:S(2)}) %collective-permute-start.50) | collective-permute-done | bytes 786464 | tf_op jit(solution)/shard_map/ppermute | solution.py:87
  565.4 16.4 %collective-permute-done.72 = bf16[192,2048]{1,0:T(8,128)(2,1)S(1)} collective-permute-done((bf16[192,2048]{1,0:T(8,128)(2,1)S(1)}, bf16[192,2048]{1,0:T(8,128)(2,1)S(1)}, u32[]{:S(2)}, u32[]{:S(2)}) %collective-permute-start.72) | collective-permute-done | bytes 786464 | tf_op jit(solution)/shard_map/ppermute | solution.py:87
  586.9 17.2 %collective-permute-done.51 = bf16[256,1536]{0,1:T(8,128)(2,1)S(1)} collective-permute-done((bf16[256,1536]{0,1:T(8,128)(2,1)S(1)}, bf16[256,1536]{0,1:T(8,128)(2,1)S(1)}, u32[]{:S(2)}, u32[]{:S(2)}) %collective-permute-start.51) | collective-permute-done | bytes 786464 | tf_op jit(solution)/shard_map/ppermute | solution.py:87
  604.8 16.2 %collective-permute-done.73 = bf16[192,2048]{1,0:T(8,128)(2,1)S(1)} collective-permute-done((bf16[192,2048]{1,0:T(8,128)(2,1)S(1)}, bf16[192,2048]{1,0:T(8,128)(2,1)S(1)}, u32[]{:S(2)}, u32[]{:S(2)}) %collective-permute-start.73) | collective-permute-done | bytes 786464 | tf_op jit(solution)/shard_map/ppermute | solution.py:87
  630.3 7.5 collective-permute-done.52
  641.0 12.6 %collective-permute-done.74 = bf16[192,2048]{1,0:T(8,128)(2,1)S(1)} collective-permute-done((bf16[192,2048]{1,0:T(8,128)(2,1)S(1)}, bf16[192,2048]{1,0:T(8,128)(2,1)S(1)}, u32[]{:S(2)}, u32[]{:S(2)}) %collective-permute-start.74) | collective-permute-done | bytes 786464 | tf_op jit(solution)/shard_map/ppermute | solution.py:87
  658.3 23.8 %collective-permute-done.76 = bf16[48,2048]{1,0:T(8,128)(2,1)S(1)} collective-permute-done((bf16[48,2048]{1,0:T(8,128)(2,1)S(1)}, bf16[48,2048]{1,0:T(8,128)(2,1)S(1)}, u32[]{:S(2)}, u32[]{:S(2)}) %collective-permute-start.76) | collective-permute-done | bytes 196640 | tf_op jit(solution)/shard_map/ppermute | solution.py:93
  694.9 13.5 %collective-permute-done.60 = bf16[4,2,48,1536]{3,2,0,1:T(8,128)(2,1)} collective-permute-done((bf16[4,2,48,1536]{3,2,0,1:T(8,128)(2,1)}, bf16[4,2,48,1536]{3,2,0,1:T(8,128)(2,1)}, u32[]{:S(2)}, u32[]{:S(2)}) %collective-permute-start.60) | collective-permute-done | bytes 1179680 | tf_op jit(solution)/shard_map/ppermute | solution.py:87
  711.6 8.0 %collective-permute-done.55 = bf16[4,48,1536]{2,1,0:T(8,128)(2,1)S(1)} collective-permute-done((bf16[4,48,1536]{2,1,0:T(8,128)(2,1)S(1)}, bf16[4,48,1536]{2,1,0:T(8,128)(2,1)S(1)}, u32[]{:S(2)}, u32[]{:S(2)}) %collective-permute-start.55) | collective-permute-done | bytes 589856 | tf_op jit(solution)/shard_map/ppermute | solution.py:87
  720.8 11.4 %collective-permute-done.61 = bf16[4,48,1536]{2,1,0:T(8,128)(2,1)S(1)} collective-permute-done((bf16[4,48,1536]{2,1,0:T(8,128)(2,1)S(1)}, bf16[4,48,1536]{2,1,0:T(8,128)(2,1)S(1)}, u32[]{:S(2)}, u32[]{:S(2)}) %collective-permute-start.61) | collective-permute-done | bytes 589856 | tf_op jit(solution)/shard_map/ppermute | solution.py:87
  733.9 3.9 collective-permute-start.57
  737.8 3.3 collective-permute-done.62
  744.4 6.2 collective-permute-done.63
  751.5 7.4 collective-permute-done.64
  (574 shorter events, 317.3 us)
Async XLA Ops:
  0.7 53.6 %collective-permute-start.36 = (bf16[128,1536]{1,0:T(8,128)(2,1)}, bf16[128,1536]{1,0:T(8,128)(2,1)}, u32[]{:S(2)}, u32[]{:S(2)}) collective-permute-start(bf16[128,1536]{1,0:T(8,128)(2,1)} %param.26), channel_id=1, source_target_pairs={{0,4},{4,0},{1,5},{5,1},{2,6},{6,2},{3,7},{7,3},{8,12},{12,8},{9,1... | collective-permute-start | bytes 1179656 | tf_op jit(solution)/shard_map/ppermute | solution.py:87
  3.7 51.6 %collective-permute-start.37 = (bf16[128,1536]{1,0:T(8,128)(2,1)}, bf16[128,1536]{1,0:T(8,128)(2,1)}, u32[]{:S(2)}, u32[]{:S(2)}) collective-permute-start(bf16[128,1536]{1,0:T(8,128)(2,1)} %param.26), channel_id=1, source_target_pairs={{0,8},{8,16},{16,24},{24,0},{1,9},{9,17},{17,25},{25,1},{2,10},{10... | collective-permute-start | bytes 1179656 | tf_op jit(solution)/shard_map/ppermute | solution.py:87
  9.3 143.1 %collective-permute-start = (bf16[256,1536]{1,0:T(8,128)(2,1)}, bf16[256,1536]{1,0:T(8,128)(2,1)S(1)}, u32[]{:S(2)}, u32[]{:S(2)}) collective-permute-start(bf16[256,1536]{1,0:T(8,128)(2,1)} %bitcast.533), channel_id=1, source_target_pairs={{0,8},{8,16},{16,24},{24,0},{1,9},{9,17},{17,25},{25,1},{2,10},{10... | collective-permute-start | bytes 2359304 | tf_op jit(solution)/shard_map/ppermute | solution.py:87
  12.5 33.0 %collective-permute-start.3 = (bf16[48,3072]{1,0:T(8,128)(2,1)}, bf16[48,3072]{1,0:T(8,128)(2,1)}, u32[]{:S(2)}, u32[]{:S(2)}) collective-permute-start(bf16[48,3072]{1,0:T(8,128)(2,1)} %pad_maximum_fusion.17), channel_id=1, source_target_pairs={{0,8},{8,16},{16,24},{24,0},{1,9},{9,17},{17,25},{25,1},{2,10},{10... | collective-permute-start | bytes 884744 | tf_op jit(solution)/shard_map/ppermute | solution.py:87
  43.2 109.3 %collective-permute-start.46 = (bf16[256,1536]{1,0:T(8,128)(2,1)}, bf16[256,1536]{1,0:T(8,128)(2,1)}, u32[]{:S(2)}, u32[]{:S(2)}) collective-permute-start(bf16[256,1536]{1,0:T(8,128)(2,1)} %bitcast.84), channel_id=1, source_target_pairs={{0,2},{2,0},{1,3},{3,1},{4,6},{6,4},{5,7},{7,5},{8,10},{10,8},{9,1... | collective-permute-start | bytes 2359304 | tf_op jit(solution)/shard_map/ppermute | solution.py:93
  53.1 65.4 %collective-permute-start.29 = (bf16[192,2048]{1,0:T(8,128)(2,1)S(1)}, bf16[192,2048]{1,0:T(8,128)(2,1)}, u32[]{:S(2)}, u32[]{:S(2)}) collective-permute-start(bf16[192,2048]{1,0:T(8,128)(2,1)S(1)} %bitcast.556), channel_id=1, source_target_pairs={{0,4},{4,0},{1,5},{5,1},{2,6},{6,2},{3,7},{7,3},{8,12},{12,8},{9,1... | collective-permute-start | bytes 2359304 | tf_op jit(solution)/shard_map/ppermute | solution.py:87
  54.3 67.1 %collective-permute-start.30 = (bf16[192,2048]{1,0:T(8,128)(2,1)S(1)}, bf16[192,2048]{1,0:T(8,128)(2,1)}, u32[]{:S(2)}, u32[]{:S(2)}) collective-permute-start(bf16[192,2048]{1,0:T(8,128)(2,1)S(1)} %bitcast.557), channel_id=1, source_target_pairs={{0,8},{8,16},{16,24},{24,0},{1,9},{9,17},{17,25},{25,1},{2,10},{10... | collective-permute-start | bytes 2359304 | tf_op jit(solution)/shard_map/ppermute | solution.py:87
  55.4 22.0 %collective-permute-start.15 = (bf16[48,1536]{1,0:T(8,128)(2,1)S(1)}, bf16[48,1536]{1,0:T(8,128)(2,1)S(1)}, u32[]{:S(2)}, u32[]{:S(2)}) collective-permute-start(bf16[48,1536]{1,0:T(8,128)(2,1)S(1)} %collective-permute-done.14), channel_id=1, source_target_pairs={{0,8},{8,16},{16,24},{24,0},{1,9},{9,17},{17,25},{25,1},{2,10},{10... | collective-permute-start | bytes 442376 | tf_op jit(solution)/shard_map/ppermute | solution.py:87
  121.4 28.5 %collective-permute-start.19 = (bf16[4,48,1536]{2,1,0:T(8,128)(2,1)}, bf16[4,48,1536]{2,1,0:T(8,128)(2,1)S(1)}, u32[]{:S(2)}, u32[]{:S(2)}) collective-permute-start(bf16[4,48,1536]{2,1,0:T(8,128)(2,1)} %bitcast_dynamic-update-slice_fusion.39), channel_id=1, source_target_pairs={{0,1},{1,0},{2,3},{3,2},{4,5},{5,4},{6,7},{7,6},{8,9},{9,8},{10,11... | collective-permute-start | bytes 1769480 | tf_op jit(solution)/shard_map/ppermute | solution.py:91
  147.7 42.9 %collective-permute-start.6 = (bf16[4,48,3072]{2,1,0:T(8,128)(2,1)}, bf16[4,48,3072]{2,1,0:T(8,128)(2,1)}, u32[]{:S(2)}, u32[]{:S(2)}) collective-permute-start(bf16[4,48,3072]{2,1,0:T(8,128)(2,1)} %bitcast_dynamic-update-slice_fusion.32), channel_id=1, source_target_pairs={{0,4},{4,0},{1,5},{5,1},{2,6},{6,2},{3,7},{7,3},{8,12},{12,8},{9,1... | collective-permute-start | bytes 3538952 | tf_op jit(solution)/shard_map/ppermute | solution.py:87
  152.1 36.9 %collective-permute-start.31 = (bf16[192,2048]{1,0:T(8,128)(2,1)}, bf16[192,2048]{1,0:T(8,128)(2,1)S(1)}, u32[]{:S(2)}, u32[]{:S(2)}) collective-permute-start(bf16[192,2048]{1,0:T(8,128)(2,1)} %collective-permute-done.30), channel_id=1, source_target_pairs={{0,4},{4,0},{1,5},{5,1},{2,6},{6,2},{3,7},{7,3},{8,12},{12,8},{9,1... | collective-permute-start | bytes 2359304 | tf_op jit(solution)/shard_map/ppermute | solution.py:87
  152.4 185.0 %collective-permute-start.45 = (bf16[256,1536]{1,0:T(8,128)(2,1)}, bf16[256,1536]{1,0:T(8,128)(2,1)}, u32[]{:S(2)}, u32[]{:S(2)}) collective-permute-start(bf16[256,1536]{1,0:T(8,128)(2,1)} %bitcast.84), channel_id=1, source_target_pairs={{0,1},{1,0},{2,3},{3,2},{4,5},{5,4},{6,7},{7,6},{8,9},{9,8},{10,11... | collective-permute-start | bytes 2359304 | tf_op jit(solution)/shard_map/ppermute | solution.py:91
  152.5 38.2 %collective-permute-start.1 = (bf16[256,1536]{1,0:T(8,128)(2,1)S(1)}, bf16[256,1536]{1,0:T(8,128)(2,1)S(1)}, u32[]{:S(2)}, u32[]{:S(2)}) collective-permute-start(bf16[256,1536]{1,0:T(8,128)(2,1)S(1)} %collective-permute-done), channel_id=1, source_target_pairs={{0,8},{8,16},{16,24},{24,0},{1,9},{9,17},{17,25},{25,1},{2,10},{10... | collective-permute-start | bytes 2359304 | tf_op jit(solution)/shard_map/ppermute | solution.py:87
  152.7 184.7 %collective-permute-start.47 = (bf16[256,1536]{1,0:T(8,128)(2,1)}, bf16[256,1536]{1,0:T(8,128)(2,1)}, u32[]{:S(2)}, u32[]{:S(2)}) collective-permute-start(bf16[256,1536]{1,0:T(8,128)(2,1)} %collective-permute-done.46), channel_id=1, source_target_pairs={{0,1},{1,0},{2,3},{3,2},{4,5},{5,4},{6,7},{7,6},{8,9},{9,8},{10,11... | collective-permute-start | bytes 2359304 | tf_op jit(solution)/shard_map/ppermute | solution.py:91
  189.0 23.5 %collective-permute-start.7 = (bf16[4,48,3072]{2,1,0:T(8,128)(2,1)}, bf16[4,48,3072]{2,1,0:T(8,128)(2,1)S(1)}, u32[]{:S(2)}, u32[]{:S(2)}) collective-permute-start(bf16[4,48,3072]{2,1,0:T(8,128)(2,1)} %bitcast_dynamic-update-slice_fusion.32), channel_id=1, source_target_pairs={{0,2},{2,0},{1,3},{3,1},{4,6},{6,4},{5,7},{7,5},{8,10},{10,8},{9,1... | collective-permute-start | bytes 3538952 | tf_op jit(solution)/shard_map/ppermute | solution.py:93
  190.7 22.6 %collective-permute-start.32 = (bf16[192,2048]{1,0:T(8,128)(2,1)}, bf16[192,2048]{1,0:T(8,128)(2,1)}, u32[]{:S(2)}, u32[]{:S(2)}) collective-permute-start(bf16[192,2048]{1,0:T(8,128)(2,1)} %collective-permute-done.30), channel_id=1, source_target_pairs={{0,8},{8,16},{16,24},{24,0},{1,9},{9,17},{17,25},{25,1},{2,10},{10... | collective-permute-start | bytes 2359304 | tf_op jit(solution)/shard_map/ppermute | solution.py:87
  190.7 33.4 %collective-permute-start.2 = (bf16[256,1536]{1,0:T(8,128)(2,1)S(1)}, bf16[256,1536]{1,0:T(8,128)(2,1)S(1)}, u32[]{:S(2)}, u32[]{:S(2)}) collective-permute-start(bf16[256,1536]{1,0:T(8,128)(2,1)S(1)} %collective-permute-done.1), channel_id=1, source_target_pairs={{0,8},{8,16},{16,24},{24,0},{1,9},{9,17},{17,25},{25,1},{2,10},{10... | collective-permute-start | bytes 2359304 | tf_op jit(solution)/shard_map/ppermute | solution.py:87
  213.2 35.5 %collective-permute-start.9 = (bf16[4,48,3072]{2,1,0:T(8,128)(2,1)}, bf16[4,48,3072]{2,1,0:T(8,128)(2,1)}, u32[]{:S(2)}, u32[]{:S(2)}) collective-permute-start(bf16[4,48,3072]{2,1,0:T(8,128)(2,1)} %bitcast_dynamic-update-slice_fusion.32), channel_id=1, source_target_pairs={{0,1},{1,0},{2,3},{3,2},{4,5},{5,4},{6,7},{7,6},{8,9},{9,8},{10,11... | collective-permute-start | bytes 3538952 | tf_op jit(solution)/shard_map/ppermute | solution.py:91
  214.6 92.6 %collective-permute-start.33 = (bf16[192,2048]{1,0:T(8,128)(2,1)}, bf16[192,2048]{1,0:T(8,128)(2,1)}, u32[]{:S(2)}, u32[]{:S(2)}) collective-permute-start(bf16[192,2048]{1,0:T(8,128)(2,1)} %collective-permute-done.32), channel_id=1, source_target_pairs={{0,4},{4,0},{1,5},{5,1},{2,6},{6,2},{3,7},{7,3},{8,12},{12,8},{9,1... | collective-permute-start | bytes 2359304 | tf_op jit(solution)/shard_map/ppermute | solution.py:87
  224.0 22.3 %collective-permute-start.8 = (bf16[4,48,3072]{2,1,0:T(8,128)(2,1)}, bf16[4,48,3072]{2,1,0:T(8,128)(2,1)}, u32[]{:S(2)}, u32[]{:S(2)}) collective-permute-start(bf16[4,48,3072]{2,1,0:T(8,128)(2,1)} %collective-permute-done.6), channel_id=1, source_target_pairs={{0,2},{2,0},{1,3},{3,1},{4,6},{6,4},{5,7},{7,5},{8,10},{10,8},{9,1... | collective-permute-start | bytes 3538952 | tf_op jit(solution)/shard_map/ppermute | solution.py:93
  252.8 54.0 %collective-permute-start.34 = (bf16[192,2048]{1,0:T(8,128)(2,1)}, bf16[192,2048]{1,0:T(8,128)(2,1)}, u32[]{:S(2)}, u32[]{:S(2)}) collective-permute-start(bf16[192,2048]{1,0:T(8,128)(2,1)} %collective-permute-done.32), channel_id=1, source_target_pairs={{0,8},{8,16},{16,24},{24,0},{1,9},{9,17},{17,25},{25,1},{2,10},{10... | collective-permute-start | bytes 2359304 | tf_op jit(solution)/shard_map/ppermute | solution.py:87
  302.6 19.7 %collective-permute-start.24 = (bf16[256,1536]{1,0:T(8,128)(2,1)S(1)}, bf16[256,1536]{1,0:T(8,128)(2,1)S(1)}, u32[]{:S(2)}, u32[]{:S(2)}) collective-permute-start(bf16[256,1536]{1,0:T(8,128)(2,1)S(1)} %multiply_convert_fusion.5), channel_id=1, source_target_pairs={{0,2},{2,0},{1,3},{3,1},{4,6},{6,4},{5,7},{7,5},{8,10},{10,8},{9,1... | collective-permute-start | bytes 2359304 | tf_op jit(solution)/shard_map/ppermute | solution.py:93
  358.4 37.4 %collective-permute-start.78 = (bf16[4,128,1536]{2,1,0:T(8,128)(2,1)S(1)}, bf16[4,128,1536]{2,1,0:T(8,128)(2,1)S(1)}, u32[]{:S(2)}, u32[]{:S(2)}) collective-permute-start(bf16[4,128,1536]{2,1,0:T(8,128)(2,1)S(1)} %dynamic-slice_bitcast_fusion.1), channel_id=1, source_target_pairs={{0,4},{4,0},{1,5},{5,1},{2,6},{6,2},{3,7},{7,3},{8,12},{12,8},{9,1... | collective-permute-start | bytes 4718600 | tf_op jit(solution)/shard_map/ppermute | solution.py:87
  359.3 38.3 %collective-permute-start.43 = (bf16[2,256,1536]{2,1,0:T(8,128)(2,1)S(1)}, bf16[2,256,1536]{2,1,0:T(8,128)(2,1)}, u32[]{:S(2)}, u32[]{:S(2)}) collective-permute-start(bf16[2,256,1536]{2,1,0:T(8,128)(2,1)S(1)} %pad_maximum_fusion.8), channel_id=1, source_target_pairs={{0,1},{1,0},{2,3},{3,2},{4,5},{5,4},{6,7},{7,6},{8,9},{9,8},{10,11... | collective-permute-start | bytes 4718600 | tf_op jit(solution)/shard_map/ppermute | solution.py:91
  373.0 23.3 %collective-permute-start.48 = (bf16[2,256,1536]{2,1,0:T(8,128)(2,1)}, bf16[2,256,1536]{2,1,0:T(8,128)(2,1)S(1)}, u32[]{:S(2)}, u32[]{:S(2)}) collective-permute-start(bf16[2,256,1536]{2,1,0:T(8,128)(2,1)} %pad_maximum_fusion.9), channel_id=1, source_target_pairs={{0,1},{1,0},{2,3},{3,2},{4,5},{5,4},{6,7},{7,6},{8,9},{9,8},{10,11... | collective-permute-start | bytes 4718600 | tf_op jit(solution)/shard_map/ppermute | solution.py:91
  386.9 163.2 %collective-permute-start.71 = (bf16[4,192,2048]{2,1,0:T(8,128)(2,1)}, bf16[4,192,2048]{2,1,0:T(8,128)(2,1)}, u32[]{:S(2)}, u32[]{:S(2)}) collective-permute-start(bf16[4,192,2048]{2,1,0:T(8,128)(2,1)} %dynamic-slice_bitcast_fusion), channel_id=1, source_target_pairs={{0,4},{4,0},{1,5},{5,1},{2,6},{6,2},{3,7},{7,3},{8,12},{12,8},{9,1... | collective-permute-start | bytes 9437192 | tf_op jit(solution)/shard_map/ppermute | solution.py:87
  397.0 20.5 %collective-permute-start.49 = (bf16[256,1536]{1,0:T(8,128)(2,1)S(1)}, bf16[256,1536]{1,0:T(8,128)(2,1)S(1)}, u32[]{:S(2)}, u32[]{:S(2)}) collective-permute-start(bf16[256,1536]{1,0:T(8,128)(2,1)S(1)} %fusion.85), channel_id=1, source_target_pairs={{0,2},{2,0},{1,3},{3,1},{4,6},{6,4},{5,7},{7,5},{8,10},{10,8},{9,1... | collective-permute-start | bytes 2359304 | tf_op jit(solution)/shard_map/ppermute | solution.py:93
  401.5 28.0 %collective-permute-start.44 = (bf16[256,1536]{1,0:T(8,128)(2,1)S(1)}, bf16[256,1536]{1,0:T(8,128)(2,1)S(1)}, u32[]{:S(2)}, u32[]{:S(2)}) collective-permute-start(bf16[256,1536]{1,0:T(8,128)(2,1)S(1)} %fusion.89), channel_id=1, source_target_pairs={{0,2},{2,0},{1,3},{3,1},{4,6},{6,4},{5,7},{7,5},{8,10},{10,8},{9,1... | collective-permute-start | bytes 2359304 | tf_op jit(solution)/shard_map/ppermute | solution.py:93
  406.7 33.7 %collective-permute-start.80 = (bf16[128,1536]{1,0:T(8,128)(2,1)}, bf16[128,1536]{1,0:T(8,128)(2,1)}, u32[]{:S(2)}, u32[]{:S(2)}) collective-permute-start(bf16[128,1536]{1,0:T(8,128)(2,1)} %fusion.109), channel_id=1, source_target_pairs={{0,8},{8,16},{16,24},{24,0},{1,9},{9,17},{17,25},{25,1},{2,10},{10... | collective-permute-start | bytes 1179656 | tf_op jit(solution)/shard_map/ppermute | solution.py:87
  442.4 141.9 %collective-permute-start.81 = (bf16[128,1536]{1,0:T(8,128)(2,1)}, bf16[128,1536]{1,0:T(8,128)(2,1)}, u32[]{:S(2)}, u32[]{:S(2)}) collective-permute-start(bf16[128,1536]{1,0:T(8,128)(2,1)} %fusion.108), channel_id=1, source_target_pairs={{0,8},{8,16},{16,24},{24,0},{1,9},{9,17},{17,25},{25,1},{2,10},{10... | collective-permute-start | bytes 1179656 | tf_op jit(solution)/shard_map/ppermute | solution.py:87
  542.7 78.9 %collective-permute-start.65 = (bf16[4,2,2,48,1536]{4,3,0,1,2:T(8,128)(2,1)}, bf16[4,2,2,48,1536]{4,3,0,1,2:T(8,128)(2,1)S(1)}, u32[]{:S(2)}, u32[]{:S(2)}) collective-permute-start(bf16[4,2,2,48,1536]{4,3,0,1,2:T(8,128)(2,1)} %bitcast.465), channel_id=1, source_target_pairs={{0,1},{1,0},{2,3},{3,2},{4,5},{5,4},{6,7},{7,6},{8,9},{9,8},{10,11... | collective-permute-start | bytes 7077896 | tf_op jit(solution)/shard_map/ppermute | solution.py:87
  542.8 22.3 %collective-permute-start.50 = (bf16[256,1536]{0,1:T(8,128)(2,1)S(1)}, bf16[256,1536]{0,1:T(8,128)(2,1)S(1)}, u32[]{:S(2)}, u32[]{:S(2)}) collective-permute-start(bf16[256,1536]{0,1:T(8,128)(2,1)S(1)} %fusion.103), channel_id=1, source_target_pairs={{0,8},{8,16},{16,24},{24,0},{1,9},{9,17},{17,25},{25,1},{2,10},{10... | collective-permute-start | bytes 2359304 | tf_op jit(solution)/shard_map/ppermute | solution.py:87
  553.5 28.2 %collective-permute-start.72 = (bf16[192,2048]{1,0:T(8,128)(2,1)S(1)}, bf16[192,2048]{1,0:T(8,128)(2,1)S(1)}, u32[]{:S(2)}, u32[]{:S(2)}) collective-permute-start(bf16[192,2048]{1,0:T(8,128)(2,1)S(1)} %dynamic-slice_bitcast_fusion.5), channel_id=1, source_target_pairs={{0,8},{8,16},{16,24},{24,0},{1,9},{9,17},{17,25},{25,1},{2,10},{10... | collective-permute-start | bytes 2359304 | tf_op jit(solution)/shard_map/ppermute | solution.py:87
  555.4 69.0 %collective-permute-start.53 = (bf16[4,2,2,48,1536]{4,3,0,1,2:T(8,128)(2,1)S(1)}, bf16[4,2,2,48,1536]{4,3,0,1,2:T(8,128)(2,1)S(1)}, u32[]{:S(2)}, u32[]{:S(2)}) collective-permute-start(bf16[4,2,2,48,1536]{4,3,0,1,2:T(8,128)(2,1)S(1)} %bitcast.559), channel_id=1, source_target_pairs={{0,1},{1,0},{2,3},{3,2},{4,5},{5,4},{6,7},{7,6},{8,9},{9,8},{10,11... | collective-permute-start | bytes 7077896 | tf_op jit(solution)/shard_map/ppermute | solution.py:87
  565.1 62.4 %collective-permute-start.59 = (bf16[4,2,2,48,1536]{4,3,0,1,2:T(8,128)(2,1)S(1)}, bf16[4,2,2,48,1536]{4,3,0,1,2:T(8,128)(2,1)S(1)}, u32[]{:S(2)}, u32[]{:S(2)}) collective-permute-start(bf16[4,2,2,48,1536]{4,3,0,1,2:T(8,128)(2,1)S(1)} %bitcast.558), channel_id=1, source_target_pairs={{0,1},{1,0},{2,3},{3,2},{4,5},{5,4},{6,7},{7,6},{8,9},{9,8},{10,11... | collective-permute-start | bytes 7077896 | tf_op jit(solution)/shard_map/ppermute | solution.py:87
  581.7 22.4 %collective-permute-start.51 = (bf16[256,1536]{0,1:T(8,128)(2,1)S(1)}, bf16[256,1536]{0,1:T(8,128)(2,1)S(1)}, u32[]{:S(2)}, u32[]{:S(2)}) collective-permute-start(bf16[256,1536]{0,1:T(8,128)(2,1)S(1)} %add_convert_fusion.2), channel_id=1, source_target_pairs={{0,8},{8,16},{16,24},{24,0},{1,9},{9,17},{17,25},{25,1},{2,10},{10... | collective-permute-start | bytes 2359304 | tf_op jit(solution)/shard_map/ppermute | solution.py:87
  584.3 36.7 %collective-permute-start.73 = (bf16[192,2048]{1,0:T(8,128)(2,1)S(1)}, bf16[192,2048]{1,0:T(8,128)(2,1)S(1)}, u32[]{:S(2)}, u32[]{:S(2)}) collective-permute-start(bf16[192,2048]{1,0:T(8,128)(2,1)S(1)} %fusion.96), channel_id=1, source_target_pairs={{0,8},{8,16},{16,24},{24,0},{1,9},{9,17},{17,25},{25,1},{2,10},{10... | collective-permute-start | bytes 2359304 | tf_op jit(solution)/shard_map/ppermute | solution.py:87
  604.4 33.4 %collective-permute-start.52 = (bf16[256,1536]{0,1:T(8,128)(2,1)S(1)}, bf16[256,1536]{0,1:T(8,128)(2,1)S(1)}, u32[]{:S(2)}, u32[]{:S(2)}) collective-permute-start(bf16[256,1536]{0,1:T(8,128)(2,1)S(1)} %add_convert_fusion.1), channel_id=1, source_target_pairs={{0,8},{8,16},{16,24},{24,0},{1,9},{9,17},{17,25},{25,1},{2,10},{10... | collective-permute-start | bytes 2359304 | tf_op jit(solution)/shard_map/ppermute | solution.py:87
  621.2 32.4 %collective-permute-start.74 = (bf16[192,2048]{1,0:T(8,128)(2,1)S(1)}, bf16[192,2048]{1,0:T(8,128)(2,1)S(1)}, u32[]{:S(2)}, u32[]{:S(2)}) collective-permute-start(bf16[192,2048]{1,0:T(8,128)(2,1)S(1)} %fusion.95), channel_id=1, source_target_pairs={{0,8},{8,16},{16,24},{24,0},{1,9},{9,17},{17,25},{25,1},{2,10},{10... | collective-permute-start | bytes 2359304 | tf_op jit(solution)/shard_map/ppermute | solution.py:87
  623.5 65.6 %collective-permute-start.66 = (bf16[4,2,48,1536]{3,2,0,1:T(8,128)(2,1)}, bf16[4,2,48,1536]{3,2,0,1:T(8,128)(2,1)}, u32[]{:S(2)}, u32[]{:S(2)}) collective-permute-start(bf16[4,2,48,1536]{3,2,0,1:T(8,128)(2,1)} %dynamic-slice_bitcast_fusion.2), channel_id=1, source_target_pairs={{0,2},{2,0},{1,3},{3,1},{4,6},{6,4},{5,7},{7,5},{8,10},{10,8},{9,1... | collective-permute-start | bytes 3538952 | tf_op jit(solution)/shard_map/ppermute | solution.py:87
  626.3 65.9 %collective-permute-start.54 = (bf16[4,2,48,1536]{3,2,0,1:T(8,128)(2,1)}, bf16[4,2,48,1536]{3,2,0,1:T(8,128)(2,1)}, u32[]{:S(2)}, u32[]{:S(2)}) collective-permute-start(bf16[4,2,48,1536]{3,2,0,1:T(8,128)(2,1)} %dynamic-slice_bitcast_fusion.4), channel_id=1, source_target_pairs={{0,2},{2,0},{1,3},{3,1},{4,6},{6,4},{5,7},{7,5},{8,10},{10,8},{9,1... | collective-permute-start | bytes 3538952 | tf_op jit(solution)/shard_map/ppermute | solution.py:87
  654.0 28.1 %collective-permute-start.76 = (bf16[48,2048]{1,0:T(8,128)(2,1)S(1)}, bf16[48,2048]{1,0:T(8,128)(2,1)S(1)}, u32[]{:S(2)}, u32[]{:S(2)}) collective-permute-start(bf16[48,2048]{1,0:T(8,128)(2,1)S(1)} %get-tuple-element.257), channel_id=1, source_target_pairs={{0,2},{2,0},{1,3},{3,1},{4,6},{6,4},{5,7},{7,5},{8,10},{10,8},{9,1... | collective-permute-start | bytes 589832 | tf_op jit(solution)/shard_map/ppermute | solution.py:93
  655.2 29.5 %collective-permute-start.77 = (bf16[48,2048]{1,0:T(8,128)(2,1)S(1)}, bf16[48,2048]{1,0:T(8,128)(2,1)S(1)}, u32[]{:S(2)}, u32[]{:S(2)}) collective-permute-start(bf16[48,2048]{1,0:T(8,128)(2,1)S(1)} %get-tuple-element.256), channel_id=1, source_target_pairs={{0,3},{1,2},{2,1},{3,0},{4,7},{5,6},{6,5},{7,4},{8,11},{9,10},{10,... | collective-permute-start | bytes 589832 | tf_op jit(solution)/shard_map/ppermute | solution.py:94
  657.2 51.2 %collective-permute-start.60 = (bf16[4,2,48,1536]{3,2,0,1:T(8,128)(2,1)}, bf16[4,2,48,1536]{3,2,0,1:T(8,128)(2,1)}, u32[]{:S(2)}, u32[]{:S(2)}) collective-permute-start(bf16[4,2,48,1536]{3,2,0,1:T(8,128)(2,1)} %dynamic-slice_bitcast_fusion.3), channel_id=1, source_target_pairs={{0,2},{2,0},{1,3},{3,1},{4,6},{6,4},{5,7},{7,5},{8,10},{10,8},{9,1... | collective-permute-start | bytes 3538952 | tf_op jit(solution)/shard_map/ppermute | solution.py:87
  691.1 20.2 %collective-permute-start.67 = (bf16[4,48,1536]{2,1,0:T(8,128)(2,1)S(1)}, bf16[4,48,1536]{2,1,0:T(8,128)(2,1)S(1)}, u32[]{:S(2)}, u32[]{:S(2)}) collective-permute-start(bf16[4,48,1536]{2,1,0:T(8,128)(2,1)S(1)} %dynamic-slice_bitcast_fusion.6), channel_id=1, source_target_pairs={{0,4},{4,0},{1,5},{5,1},{2,6},{6,2},{3,7},{7,3},{8,12},{12,8},{9,1... | collective-permute-start | bytes 1769480 | tf_op jit(solution)/shard_map/ppermute | solution.py:87
  693.9 25.8 %collective-permute-start.55 = (bf16[4,48,1536]{2,1,0:T(8,128)(2,1)S(1)}, bf16[4,48,1536]{2,1,0:T(8,128)(2,1)S(1)}, u32[]{:S(2)}, u32[]{:S(2)}) collective-permute-start(bf16[4,48,1536]{2,1,0:T(8,128)(2,1)S(1)} %dynamic-slice_bitcast_fusion.8), channel_id=1, source_target_pairs={{0,4},{4,0},{1,5},{5,1},{2,6},{6,2},{3,7},{7,3},{8,12},{12,8},{9,1... | collective-permute-start | bytes 1769480 | tf_op jit(solution)/shard_map/ppermute | solution.py:87
  710.1 22.2 %collective-permute-start.61 = (bf16[4,48,1536]{2,1,0:T(8,128)(2,1)S(1)}, bf16[4,48,1536]{2,1,0:T(8,128)(2,1)S(1)}, u32[]{:S(2)}, u32[]{:S(2)}) collective-permute-start(bf16[4,48,1536]{2,1,0:T(8,128)(2,1)S(1)} %dynamic-slice_bitcast_fusion.7), channel_id=1, source_target_pairs={{0,4},{4,0},{1,5},{5,1},{2,6},{6,2},{3,7},{7,3},{8,12},{12,8},{9,1... | collective-permute-start | bytes 1769480 | tf_op jit(solution)/shard_map/ppermute | solution.py:87
  711.5 21.9 %collective-permute-start.68 = (bf16[48,1536]{1,0:T(8,128)(2,1)S(1)}, bf16[48,1536]{1,0:T(8,128)(2,1)S(1)}, u32[]{:S(2)}, u32[]{:S(2)}) collective-permute-start(bf16[48,1536]{1,0:T(8,128)(2,1)S(1)} %dynamic-slice_bitcast_fusion.17), channel_id=1, source_target_pairs={{0,8},{8,16},{16,24},{24,0},{1,9},{9,17},{17,25},{25,1},{2,10},{10... | collective-permute-start | bytes 442376 | tf_op jit(solution)/shard_map/ppermute | solution.py:87
  (109 other events, 1309.1 us)

commit v2 on v1

v2 whole, which is shorter than its diff:
```python
import math

import jax
import jax.numpy as jnp
from jax import lax
from jax.experimental import pallas as pl
from jax.experimental.pallas import tpu as pltpu
from jax.sharding import Mesh
from jax.sharding import PartitionSpec as P

QUERY_HEADS = 16
KEY_VALUE_HEADS = 8
HEAD_SIZE = 96
FF = 4096
STRETCH = 128

EPSILON = 1e-05
THETA = 100000.0

BF = jnp.bfloat16
F32 = jnp.float32


def layout(doc_lengths, slot_map, slots):
    count = slot_map.shape[0]
    stretches = jnp.arange(count, dtype=jnp.int32)
    logical = jnp.sum(
        jnp.where(slot_map[None, :] == slots[:, None], stretches[None, :], 0), axis=1
    )
    places = (
        logical[:, None] * STRETCH + jnp.arange(STRETCH, dtype=jnp.int32)[None, :]
    ).reshape(-1)
    endings = jnp.cumsum(doc_lengths)
    passed = endings[None, :] <= places[:, None]
    document = jnp.sum(passed.astype(jnp.int32), axis=1)
    starts = jnp.sum(jnp.where(passed, doc_lengths[None, :], 0), axis=1)
    return document, places - starts


def rotary_tables(positions):
    half = HEAD_SIZE // 2
    freqs = THETA ** (-2.0 * jnp.arange(half, dtype=F32) / HEAD_SIZE)
    angles = positions.astype(F32)[:, None] * freqs[None, :]
    return jnp.cos(angles).T, jnp.sin(angles).T


def rotate(rows, cosine, sine):
    half = rows.shape[0] // 2
    first, second = rows[:half], rows[half:]
    return jnp.concatenate(
        [first * cosine - second * sine, second * cosine + first * sine], axis=0
    )


def contract(left, right, at_left, at_right):
    return lax.dot_general(
        left, right, (((at_left,), (at_right,)), ((), ())), preferred_element_type=F32
    )


RATIO = QUERY_HEADS // KEY_VALUE_HEADS
SCALE = 1.0 / math.sqrt(HEAD_SIZE)
VMEM_BYTES = 40 * 1024 * 1024
MOST_VMEM_BYTES = 60 * 1024 * 1024


def lasting(microseconds):
    return pl.CostEstimate(
        flops=int(microseconds * 1e9), bytes_accessed=int(microseconds * 3e6), transcendentals=0
    )


def forward_kernel(q_ref, k_ref, v_ref, bias_ref, out_ref, lse_ref):
    keys, values = k_ref[...], v_ref[...]
    for head in range(RATIO):
        rows = slice(head * HEAD_SIZE, (head + 1) * HEAD_SIZE)
        scores = contract(keys, q_ref[rows, :], 0, 0) * SCALE + bias_ref[...]
        peak = jnp.max(scores, axis=0, keepdims=True)
        weights = jnp.exp(scores - peak)
        totals = jnp.sum(weights, axis=0, keepdims=True)
        mixed = contract(values, weights.astype(BF), 1, 0)
        out_ref[rows, :] = (mixed / totals).astype(BF)
        lse_ref[0, head : head + 1, :] = peak + jnp.log(totals)


def backward_kernel(
    q_ref,
    k_ref,
    v_ref,
    grad_ref,
    lse_ref,
    cos_ref,
    sin_ref,
    bias_ref,
    token_ref,
    dq_ref,
    dkv_ref,
    *ring_refs,
):
    count = q_ref.shape[1]
    keys, values = k_ref[...], v_ref[...]
    cosine, sine = cos_ref[:, :count], sin_ref[:, :count]
    grad_keys = jnp.zeros(keys.shape, F32)
    grad_values = jnp.zeros(keys.shape, F32)
    for head in range(RATIO):
        rows = slice(head * HEAD_SIZE, (head + 1) * HEAD_SIZE)
        queries, grads = q_ref[rows, :], grad_ref[rows, :]
        scores = contract(keys, queries, 0, 0) * SCALE + bias_ref[...]
        probs = jnp.exp(scores - lse_ref[0, head : head + 1, :])
        grad_probs = contract(values, grads, 0, 0)
        centre = jnp.sum(probs * grad_probs, axis=0, keepdims=True)
        grad_scores = (probs * (grad_probs - centre)).astype(BF)
        grad_queries = contract(keys, grad_scores, 1, 0) * SCALE
        dq_ref[rows, :] = rotate(grad_queries, cosine, -sine).astype(BF)
        grad_keys += contract(queries, grad_scores, 1, 1)
        grad_values += contract(grads, probs.astype(BF), 1, 1)
    grad_keys = rotate(grad_keys * SCALE, cos_ref[...], -sin_ref[...]).astype(BF)
    grad_values = grad_values.astype(BF)
    dkv_ref[0] = grad_keys
    dkv_ref[1] = grad_values
    for block, ring_ref in enumerate(ring_refs):
        at = slice(block * count, (block + 1) * count)
        ring_ref[0] = grad_keys[:, at]
        ring_ref[1] = grad_values[:, at]


def attention_forward(queries, keys, values, bias):
    count, span = queries.shape[1], keys.shape[1]
    pair = RATIO * HEAD_SIZE
    mine = lambda rows, cols: pl.BlockSpec((rows, cols), lambda g: (g, 0))
    return pl.pallas_call(
        forward_kernel,
        grid=(KEY_VALUE_HEADS,),
        in_specs=[
            mine(pair, count),
            mine(HEAD_SIZE, span),
            mine(HEAD_SIZE, span),
            pl.BlockSpec(bias.shape, lambda g: (0, 0)),
        ],
        out_specs=[
            mine(pair, count),
            pl.BlockSpec((1, RATIO, count), lambda g: (g, 0, 0)),
        ],
        out_shape=[
            jax.ShapeDtypeStruct(queries.shape, BF),
            jax.ShapeDtypeStruct((KEY_VALUE_HEADS, RATIO, count), F32),
        ],
        compiler_params=pltpu.CompilerParams(vmem_limit_bytes=VMEM_BYTES),
        cost_estimate=lasting(0.1),
        name="attention_forward",
    )(queries, keys, values, bias)


def attention_backward(heads, queries, keys, values, grads, totals, cosine, sine, bias, token, blocks):
    count, span = queries.shape[1], keys.shape[1]
    pair = RATIO * HEAD_SIZE
    first, amount = heads.start, len(heads)
    whole = lambda a: pl.BlockSpec(a.shape, lambda g: (0,) * a.ndim)
    mine = lambda rows, cols: pl.BlockSpec((rows, cols), lambda g: (g + first, 0))
    rows = amount * HEAD_SIZE
    return pl.pallas_call(
        backward_kernel,
        grid=(amount,),
        in_specs=[
            mine(pair, count),
            mine(HEAD_SIZE, span),
            mine(HEAD_SIZE, span),
            mine(pair, count),
            pl.BlockSpec((1, RATIO, count), lambda g: (g + first, 0, 0)),
            whole(cosine),
            whole(sine),
            whole(bias),
            whole(token),
        ],
        out_specs=[
            pl.BlockSpec((pair, count), lambda g: (g, 0)),
            pl.BlockSpec((2, HEAD_SIZE, span), lambda g: (0, g, 0)),
        ]
        + [pl.BlockSpec((2, HEAD_SIZE, count), lambda g: (0, g, 0))] * blocks,
        out_shape=[
            jax.ShapeDtypeStruct((amount * pair, count), BF),
            jax.ShapeDtypeStruct((2, rows, span), BF),
        ]
        + [jax.ShapeDtypeStruct((2, rows, count), BF)] * blocks,
        compiler_params=pltpu.CompilerParams(vmem_limit_bytes=VMEM_BYTES),
        cost_estimate=lasting(0.1),
        name="attention_backward",
    )(queries, keys, values, grads, totals, cosine, sine, bias, token)


def product(left, right):
    return jnp.dot(left, right, preferred_element_type=F32)


def over_rows(left, right):
    return lax.dot_general(left, right, (((0,), (0,)), ((), ())), preferred_element_type=F32)


def times_transposed(left, right):
    return lax.dot_general(left, right, (((1,), (1,)), ((), ())), preferred_element_type=F32)


def blank(shape, dtype):
    return pl.pallas_call(
        lambda out_ref: None,
        out_shape=jax.ShapeDtypeStruct(shape, dtype),
        out_specs=pl.BlockSpec(memory_space=pl.ANY),
        name="blank",
    )()


def terms_kernel(steps, by_rows, owners_ref, left_ref, *refs):
    rights, (away_ref, mine_ref, total_ref) = refs[:-3], refs[-3:]
    step = pl.program_id(0)
    slots, n, rows, cols = away_ref.shape
    for right_ref, (first, last) in zip(rights, steps):

        @pl.when((step >= first) & (step < last))
        def _(right_ref=right_ref):
            if by_rows:
                right = right_ref[...]
                product = contract(left_ref[:, : right.shape[1]], right, 1, 1)
            else:
                product = contract(left_ref[...], right_ref[...], 1, 0)
            total_ref[...] = product.astype(BF)

    for slot in range(slots):
        for z in range(n):
            base = z * 2 * slots * rows
            for out_ref, at in ((mine_ref, slot), (away_ref, slots + slot)):
                start = pl.multiple_of(base + owners_ref[at] * rows, 16)
                out_ref[slot, z] = total_ref[pl.ds(start, rows), :]


def owned_terms(owners, n, left, rights, by_rows):
    tile = 256
    depth = left.shape[0] // (8 * n)
    steps, first = [], 0
    for right in rights:
        last = first + right.shape[0 if by_rows else 1] // tile
        steps.append((first, last))
        first = last
    specs = []
    for right, (start, stop) in zip(rights, steps):
        if by_rows:
            specs.append(
                pl.BlockSpec(
                    (tile, right.shape[1]),
                    lambda j, o, start=start, stop=stop: (jnp.clip(j, start, stop - 1) - start, 0),
                )
            )
        else:
            specs.append(pl.BlockSpec((right.shape[0], tile), lambda j, o: (0, j)))
    out = jax.ShapeDtypeStruct((4, n, depth, first * tile), BF)
    out_spec = pl.BlockSpec((4, n, depth, tile), lambda j, o: (0, 0, 0, j))
    return pl.pallas_call(
        lambda *refs: terms_kernel(steps, by_rows, *refs),
        grid_spec=pltpu.PrefetchScalarGridSpec(
            num_scalar_prefetch=1,
            grid=(first,),
            in_specs=[pl.BlockSpec(left.shape, lambda j, o: (0, 0))] + specs,
            out_specs=[out_spec, out_spec],
            scratch_shapes=[pltpu.VMEM((left.shape[0], tile), BF)],
        ),
        out_shape=[out, out],
        compiler_params=pltpu.CompilerParams(vmem_limit_bytes=VMEM_BYTES),
        cost_estimate=lasting(0.1),
        name="owned_terms",
    )(owners, left, *rights)


def project_kernel(n, count, starts_ref, *refs):
    parts, blocks, (cos_ref, sin_ref) = refs[:count], refs[count : count + n], refs[count + n : count + n + 2]
    refs = refs[count + n + 2 :]
    q_ref, k_ref, v_ref, normed_ref, weight_out, weight_ref, token_ref, part_sem, token_sem, out_sem = refs
    rows, (count, width) = parts[0].shape[1], blocks[0].shape
    token_copies = [
        pltpu.make_async_copy(block, token_ref.at[pl.ds(k * count, count)], token_sem.at[k])
        for k, block in enumerate(blocks)
    ]
    part_copies = []
    for part in parts:
        for j in range(part.shape[0]):
            k = len(part_copies)
            at = pl.multiple_of(starts_ref[k], 16)
            part_copies.append(
                pltpu.make_async_copy(part.at[j], weight_ref.at[pl.ds(at, rows)], part_sem.at[k])
            )
    for copy in token_copies + part_copies:
        copy.start()
    for k, copy in enumerate(token_copies):
        copy.wait()
        x = token_ref[k * count : (k + 1) * count, :].astype(F32)
        inverse = lax.rsqrt(jnp.mean(x * x, axis=-1, keepdims=True) + EPSILON)
        normed_ref[:, k * count : (k + 1) * count] = (x * inverse).astype(BF).T
    for copy in part_copies:
        copy.wait()
    out_copy = pltpu.make_async_copy(weight_ref, weight_out, out_sem)
    out_copy.start()
    pair_cols = k_ref.shape[0]
    tile = 4 * HEAD_SIZE
    for out_ref, base, rotated in ((q_ref, 0, True), (k_ref, width, True), (v_ref, width + pair_cols, False)):
        tokens = out_ref.shape[1]

        def step(j, carry, out_ref=out_ref, base=base, rotated=rotated, tokens=tokens):
            at = pl.multiple_of(j * tile, tile)
            columns = weight_ref[:, pl.ds(pl.multiple_of(base + at, 128), tile)]
            product = contract(columns, normed_ref[:, :tokens], 0, 0)
            for head in range(4):
                part = product[head * HEAD_SIZE : (head + 1) * HEAD_SIZE]
                if rotated:
                    part = rotate(part, cos_ref[:, :tokens], sin_ref[:, :tokens])
                start = pl.multiple_of(at + head * HEAD_SIZE, 16)
                out_ref[pl.ds(start, HEAD_SIZE), :] = part.astype(BF)
            return carry

        lax.fori_loop(0, out_ref.shape[0] // tile, step, 0)
    out_copy.wait()


def project(starts, parts, blocks, cosine, sine):
    rows, cols = parts[0].shape[1:]
    n, (count, width) = len(blocks), blocks[0].shape
    span, pair_cols = n * count, KEY_VALUE_HEADS * HEAD_SIZE
    every = pl.BlockSpec(memory_space=pl.ANY)
    vmem = pl.BlockSpec(memory_space=pltpu.VMEM)
    shape = (starts.shape[0] * rows, cols)
    return pl.pallas_call(
        lambda *refs: project_kernel(n, len(parts), *refs),
        in_specs=[pl.BlockSpec(memory_space=pltpu.SMEM)] + [every] * (len(parts) + n) + [vmem, vmem],
        out_specs=[vmem, vmem, vmem, vmem, every],
        out_shape=[
            jax.ShapeDtypeStruct((width, count), BF),
            jax.ShapeDtypeStruct((pair_cols, span), BF),
            jax.ShapeDtypeStruct((pair_cols, span), BF),
            jax.ShapeDtypeStruct((width, span), BF),
            jax.ShapeDtypeStruct(shape, BF),
        ],
        scratch_shapes=[
            pltpu.VMEM(shape, BF),
            pltpu.VMEM((span, width), BF),
            pltpu.SemaphoreType.DMA(starts.shape),
            pltpu.SemaphoreType.DMA((n,)),
            pltpu.SemaphoreType.DMA,
        ],
        compiler_params=pltpu.CompilerParams(vmem_limit_bytes=MOST_VMEM_BYTES),
        cost_estimate=lasting(0.1),
        name="project",
    )(starts, *parts, *blocks, cosine, sine)


def feed_kernel(count, first, *refs):
    parts, grads, blocks_ref = refs[:count], refs[count : 2 * count], refs[2 * count]
    refs = refs[2 * count + 1 :]
    if not first:
        earlier_ref, refs = refs[0], refs[1:]
    scaled_ref, hidden_ref, both_ref, sum_ref, down_ref = refs[:5]
    total_ref, part_ref, grad_ref, block_ref, weight_ref, part_sem, grad_sem, block_sem = refs[5:]
    step = pl.program_id(0)
    units = hidden_ref.shape[1]
    (n, rows, _), width = block_ref.shape, down_ref.shape[1]
    unit = units // n
    pieces = rows // unit
    piece = width // pieces

    def copies(k):
        return (
            pltpu.make_async_copy(parts[k], part_ref.at[k], part_sem.at[k]),
            pltpu.make_async_copy(grads[k], grad_ref.at[k], grad_sem.at[k]),
        )

    @pl.when(step == 0)
    def _():
        block_copies = [
            pltpu.make_async_copy(blocks_ref.at[k], block_ref.at[k], block_sem.at[k])
            for k in range(n)
        ]
        for copy in block_copies:
            copy.start()
        for k in range(count):
            for copy in copies(k):
                copy.start()
        for k, copy in enumerate(block_copies):
            copy.wait()
            weight_ref[k * rows : (k + 1) * rows, :] = block_ref[k, :, : 2 * units]
            for j in range(pieces):
                down_ref[k * unit : (k + 1) * unit, j * piece : (j + 1) * piece] = block_ref[
                    k, j * unit : (j + 1) * unit, 2 * units :
                ]
        total_ref[...] = jnp.zeros_like(total_ref) if first else earlier_ref[...]

    for k in range(count):

        @pl.when(step == k)
        def _(k=k):
            for copy in copies(k):
                copy.wait()

    part, grad = part_ref[step], grad_ref[step]
    gate = product(part, weight_ref[:, :units])
    upper = product(part, weight_ref[:, units:])
    sigmoid = jax.nn.sigmoid(gate)
    silu = gate * sigmoid
    hidden = (silu * upper).astype(BF)
    hidden_ref[...] = hidden
    grad_hidden = contract(grad, down_ref[...], 1, 1)
    grad_gate = (grad_hidden * upper * sigmoid * (1.0 + gate * (1.0 - sigmoid))).astype(BF)
    grad_up = (grad_hidden * silu).astype(BF)
    both_ref[:, :units] = grad_gate
    both_ref[:, units:] = grad_up
    scaled = contract(grad_gate, weight_ref[:, :units], 1, 1)
    scaled += contract(grad_up, weight_ref[:, units:], 1, 1)
    scaled_ref[...] = scaled.astype(BF)
    total_ref[...] += contract(hidden, grad, 0, 0)

    @pl.when(step == count - 1)
    def _():
        sum_ref[...] = total_ref[...].astype(sum_ref.dtype)


def feed_forward(parts, grads, blocks, units, earlier=None):
    count, n = len(parts), blocks.shape[0]
    rows, width = parts[0].shape
    every = pl.BlockSpec(memory_space=pl.ANY)
    part = lambda cols: pl.BlockSpec((rows, cols), lambda k: (k, 0))
    whole = pl.BlockSpec((units, width), lambda k: (0, 0))
    first = earlier is None
    return pl.pallas_call(
        lambda *refs: feed_kernel(count, first, *refs),
        grid=(count,),
        in_specs=[every] * (2 * count + 1) + ([] if first else [whole]),
        out_specs=[part(width), part(units), part(2 * units), whole, whole],
        out_shape=[
            jax.ShapeDtypeStruct((count * rows, width), BF),
            jax.ShapeDtypeStruct((count * rows, units), BF),
            jax.ShapeDtypeStruct((count * rows, 2 * units), BF),
            jax.ShapeDtypeStruct((units, width), F32 if first else BF),
            jax.ShapeDtypeStruct((units, width), BF),
        ],
        scratch_shapes=[
            pltpu.VMEM((units, width), F32),
            pltpu.VMEM((count, rows, width), BF),
            pltpu.VMEM((count, rows, width), BF),
            pltpu.VMEM(blocks.shape, BF),
            pltpu.VMEM((n * blocks.shape[1], 2 * units), BF),
            pltpu.SemaphoreType.DMA((count,)),
            pltpu.SemaphoreType.DMA((count,)),
            pltpu.SemaphoreType.DMA((n,)),
        ],
        compiler_params=pltpu.CompilerParams(vmem_limit_bytes=VMEM_BYTES),
        cost_estimate=lasting(30),
        name="feed_forward",
    )(*parts, *grads, blocks, *(() if first else (earlier,)))


def gate_up_kernel(count, *refs):
    parts, boths, out_ref, token_ref = refs[:count], refs[count:-2], refs[-2], refs[-1]
    token_ref[...] = jnp.zeros_like(token_ref)
    rows = parts[0].shape[0]
    each = boths[0].shape[0] // rows
    total = jnp.zeros(out_ref.shape, F32)
    for k, part in enumerate(parts):
        at = k % each * rows
        total += contract(part[...], boths[k // each][at : at + rows, :], 0, 0)
    out_ref[...] = total.astype(BF)


def gate_up_terms_of(parts, boths):
    rows, width = parts[0].shape
    cols = boths[0].shape[1]
    tile = 256
    return pl.pallas_call(
        lambda *refs: gate_up_kernel(len(parts), *refs),
        grid=(width // tile,),
        in_specs=[pl.BlockSpec((rows, tile), lambda j: (0, j))] * len(parts)
        + [pl.BlockSpec(both.shape, lambda j: (0, 0)) for both in boths],
        out_specs=[
            pl.BlockSpec((tile, cols), lambda j: (j, 0)),
            pl.BlockSpec((8, 128), lambda j: (0, 0)),
        ],
        out_shape=[
            jax.ShapeDtypeStruct((width, cols), BF),
            jax.ShapeDtypeStruct((8, 128), F32),
        ],
        compiler_params=pltpu.CompilerParams(vmem_limit_bytes=VMEM_BYTES),
        cost_estimate=lasting(15),
        name="gate_up_terms",
    )(*parts, *boths)


def on_device(n, ranks, *operands):
    (
        tokens,
        gain_attn,
        w_query,
        key_weight,
        value_weight,
        w_out,
        gain_mlp,
        w_gate,
        w_up,
        w_down,
        out_grad,
        lengths,
        stretch_map,
    ) = operands
    at_z, rank = lax.axis_index("z"), lax.axis_index("f")
    grid = ranks == 8
    turn = rank % 2
    first, second = 4 >> turn, 2 << turn
    scope = jax.named_scope

    def stage(*arrays):
        return lax.optimization_barrier(arrays)

    def shift(a, by):
        return lax.ppermute(a, "z", [(i, (i + by) % n) for i in range(n)])

    def swap_first(a):
        return lax.ppermute(a, "f", [(i, i ^ (4 >> i % 2)) for i in range(ranks)])

    def swap_second(a):
        return lax.ppermute(a, "f", [(i, i ^ (2 << i % 2)) for i in range(ranks)])

    def swap_core(a):
        return lax.ppermute(a, "f", [(i, i ^ 1) for i in range(ranks)])

    def pick(a, index, axis):
        return lax.dynamic_index_in_dim(a, index, axis, keepdims=False)

    def put(a, piece, *index):
        index = index + (0,) * (a.ndim - len(index))
        return lax.dynamic_update_slice(a, piece, index)

    def direct(a):
        return [a] + [shift(a, by) for by in range(1, n)]

    def stack_z(blocks):
        out = blank((n,) + blocks[0].shape, BF)
        for k, block in enumerate(blocks):
            out = put(out, block[None], (at_z - k) % n)
        return out

    def send_z(terms):
        sent = [shift(pick(terms, (at_z - by) % n, 0), -by) for by in range(1, n)]
        return [pick(terms, at_z, 0)] + sent

    def total(terms):
        return sum(term.astype(F32) for term in terms)

    def add(a, b):
        return (a.astype(F32) + b.astype(F32)).astype(BF)

    def spread_second(pair):
        return swap_second(pair) if grid else pair

    def spread_all(pair, other):
        if grid:
            return [pair, other, swap_core(pair), swap_core(other)]
        rows = lax.all_gather(pair, "f", tiled=True)
        return jnp.split(rows, rows.shape[0] // (2 * pair.shape[0]))

    def send_core(terms):
        return swap_core(terms) if grid else terms

    def add_halves(terms, arrived):
        half = terms.shape[0] // 2
        far = add(terms[half:], arrived[half:])
        return add(terms[:half], arrived[:half]), far

    if grid:
        owners = [rank, rank ^ first, rank ^ second, rank ^ 6]
        owners += [rank ^ 1, rank ^ 1 ^ second, rank ^ 1 ^ first, rank ^ 7]
        owners = jnp.stack(owners).astype(jnp.int32)

    def weight_terms(left, rights, by_rows):
        if grid:
            return owned_terms(owners, n, left, rights, by_rows)
        columns = [
            contract(left[:, : r.shape[1]], r, 1, 1) if by_rows else product(left, r)
            for r in rights
        ]
        terms = jnp.concatenate(columns, axis=1).astype(BF)
        return terms, terms

    def sum_f(mine):
        terms = mine.reshape(n, ranks, -1, mine.shape[1]).transpose(1, 0, 2, 3)
        return lax.psum_scatter(terms, "f", scatter_dimension=0, tiled=False)

    token_count, width = tokens.shape[1:]
    shard_rows = w_query.shape[0]
    unit = w_down.shape[0]
    hidden_units = n * unit
    pair_cols = KEY_VALUE_HEADS * HEAD_SIZE
    gain_one = gain_attn.astype(F32)[:, None]
    gain_two = gain_mlp.astype(F32)[:, None]

    def along(weight, grad):
        return jnp.sum(weight.astype(F32) * grad, axis=1)

    def scaled(weight, gain):
        return (weight.astype(F32) * gain).astype(BF)

    shard = jnp.concatenate([w_query, key_weight, value_weight], axis=1)
    shard = jnp.concatenate([scaled(shard, gain_one), w_out], axis=1)
    own = tokens[0]
    blocks = [own]
    grad_own = grad_first = out_grad[0]
    if grid:
        with scope("attention_weights_z"):
            behind = [shift(shard, by) for by in range(1, n)]
        with scope("attention_weights_own"):
            near = [shard, swap_first(shard), swap_second(shard)]
    with scope("gate_up_f"):
        gate_up = scaled(jnp.concatenate([w_gate, w_up], axis=1), gain_two)
        gate_up = gate_up.reshape(shard_rows, 2, n, ranks, unit).transpose(3, 0, 1, 2, 4)
        gate_up = gate_up.reshape(ranks, shard_rows, 2 * hidden_units)
        gate_up = lax.all_to_all(gate_up, "f", 0, 0, tiled=True)
        gate_up_rows = ranks * shard_rows
        gate_up = gate_up.reshape(gate_up_rows, 2 * hidden_units)
        pieces = gate_up_rows // unit
        down = w_down.reshape(unit, pieces, width // pieces).transpose(1, 0, 2)
        gate_up_down = jnp.concatenate(
            [gate_up, down.reshape(gate_up_rows, width // pieces)], axis=1
        )

    if grid:
        with scope("attention_weights_own"):
            near.append(swap_second(near[1]))
        *behind, near[2], near[3], gate_up_down = stage(*behind, near[2], near[3], gate_up_down)
        with scope("attention_weights_core"):
            near_core = [swap_core(part) for part in near]
        rest = [jnp.stack(behind)]
        with scope("attention_weights_first"):
            rest.append(swap_first(rest[0]))
        with scope("tokens_z"):
            blocks.append(shift(own, 1))
        rest[0], rest[1], blocks[1], *near_core = stage(rest[0], rest[1], blocks[1], *near_core)
        with scope("attention_weights_core"):
            rest_core = [swap_core(rest[0])]
        with scope("attention_weights_second"):
            rest.append(swap_second(rest[0]))
        with scope("tokens_z"):
            blocks.append(shift(blocks[1], 1))
        rest[1], rest[2], blocks[2], rest_core[0] = stage(
            rest[1], rest[2], blocks[2], rest_core[0]
        )
        with scope("attention_weights_core"):
            rest_core += [swap_core(rest[1]), swap_core(rest[2])]
        with scope("attention_weights_second"):
            rest.append(swap_second(rest[1]))
        with scope("out_grad_first"):
            grad_first = swap_first(grad_own)
        with scope("tokens_z"):
            while len(blocks) < n:
                blocks.append(shift(blocks[-1], 1))
        rest[3], blocks[-1], grad_first, *rest_core = stage(
            rest[3], blocks[-1], grad_first, *rest_core
        )
        with scope("attention_weights_core"):
            rest_core.append(swap_core(rest[3]))
    else:
        while len(blocks) < n:
            blocks.append(shift(blocks[-1], 1))
    with scope("gate_up_down_z"):
        gate_up_down, blocks[-1] = stage(gate_up_down, blocks[-1])
        gate_up_down = lax.all_gather(gate_up_down, "z")
    cuts = [width, width + pair_cols, width + 2 * pair_cols]

    slots_each = stretch_map.shape[1] // n
    slots = (
        ((at_z - jnp.arange(n, dtype=jnp.int32)) % n)[:, None] * slots_each
        + jnp.arange(slots_each, dtype=jnp.int32)[None, :]
    ).reshape(-1)
    doc_all, place_all = layout(lengths[0], stretch_map[0], slots)
    allowed = (doc_all[:, None] == doc_all[None, :token_count]) & (
        place_all[:, None] <= place_all[None, :token_count]
    )
    bias = jnp.where(allowed, 0.0, -1e30).astype(F32)
    cosine, sine = rotary_tables(place_all)

    inputs = own.astype(F32)
    first_inverse = lax.rsqrt(jnp.mean(inputs * inputs, axis=-1, keepdims=True) + EPSILON)
    first_normed = inputs * first_inverse
    if grid:
        parts, starts = [], []
        for near_parts, rest_parts, moves in (
            (near, rest, (0, first, second, 6)),
            (near_core, rest_core, (1, 1 ^ second, 1 ^ first, 7)),
        ):
            for near_part, rest_part, move in zip(near_parts, rest_parts, moves):
                parts += [near_part[None], rest_part]
                starts += [(at_z - k) % n * ranks + (rank ^ move) for k in range(n)]
        starts = jnp.stack(starts).astype(jnp.int32) * shard_rows
        queries, keys, values, normed_group, gathered = project(
            starts, parts, blocks, cosine, sine
        )
        q_weight, key_matrix, value_matrix, out_weight = jnp.split(gathered, cuts, axis=1)
    else:
        gathered = lax.all_gather(shard, ("z", "f"), tiled=True)
        q_weight, key_matrix, value_matrix, out_weight = jnp.split(gathered, cuts, axis=1)
        normed_group = jnp.concatenate(blocks, axis=0).astype(F32)
        inverse = lax.rsqrt(jnp.mean(normed_group * normed_group, axis=-1, keepdims=True) + EPSILON)
        normed_group = (normed_group * inverse).astype(BF).T

        def rotated(weight, tokens):
            rows = contract(weight, normed_group[:, :tokens], 0, 0)
            rows = rows.reshape(-1, HEAD_SIZE, tokens)
            turned = [rotate(r, cosine[:, :tokens], sine[:, :tokens]) for r in rows]
            return jnp.concatenate(turned, axis=0).astype(BF)

        queries, keys = rotated(q_weight, token_count), rotated(key_matrix, n * token_count)
        values = contract(value_matrix, normed_group, 0, 0).astype(BF)
    span = n * token_count

    with scope("out_grad_second"):
        grad_pair = jnp.concatenate([grad_own, grad_first], axis=0) if grid else grad_own
        grad_other = spread_second(grad_pair)

    attention_output, log_totals = attention_forward(queries, keys, values, bias)
    resid = inputs + contract(attention_output, out_weight, 0, 0)
    second_inverse = lax.rsqrt(jnp.mean(resid * resid, axis=-1, keepdims=True) + EPSILON)
    second_normed = resid * second_inverse
    normed_two = second_normed.astype(BF)
    normed_two, grad_other = stage(normed_two, grad_other)

    with scope("normed_first"):
        normed_first = swap_first(normed_two) if grid else normed_two
    with scope("out_grad_all"):
        grad_parts = spread_all(grad_pair, grad_other)
    with scope("normed_second"):
        (normed_first,) = stage(normed_first)
        normed_pair = normed_first
        if grid:
            normed_pair = jnp.concatenate([normed_two, normed_first], axis=0)
        normed_other = spread_second(normed_pair)
        normed_parts = spread_all(normed_pair, normed_other)
    half = len(normed_parts) // 2

    scaled_far, hidden_far, both_far, down_terms, down_weight = feed_forward(
        normed_parts[half:], grad_parts[half:], gate_up_down, hidden_units
    )
    with scope("scaled_core"):
        scaled_far = send_core(scaled_far)
    scaled_near, hidden_near, both_near, down_terms, _ = feed_forward(
        normed_parts[:half], grad_parts[:half], gate_up_down, hidden_units, down_terms
    )
    with scope("down_sum_z"):
        down_owned = lax.psum_scatter(down_terms, "z", scatter_dimension=0, tiled=True)

    def norm_back(scaled_grad, normed, inverse):
        return inverse * (
            scaled_grad - normed * jnp.mean(scaled_grad * normed, axis=-1, keepdims=True)
        )

    with scope("scaled_second"):
        if grid:
            scaled_near, far = add_halves(scaled_near, scaled_far)
            far, both_near = stage(far, both_near)
            far = swap_second(far)
        else:
            scaled_two = jnp.concatenate([scaled_near, scaled_far], axis=0)
            scaled_two = lax.psum_scatter(scaled_two, "f", scatter_dimension=0, tiled=True)
            scaled_two = far = scaled_two.astype(F32)
    with scope("gate_up_sum_z"):
        gate_up_terms, token = gate_up_terms_of(normed_parts, [both_near, both_far])
        gate_up_owned = lax.psum_scatter(gate_up_terms, "z", scatter_dimension=0, tiled=True)
    with scope("result_core"):
        hidden_far, token = stage(hidden_far, token)
        result_far = send_core(product(hidden_far, down_weight).astype(BF))
        result_near = product(hidden_near, down_weight).astype(BF)
        if grid:
            result_near, result_far = add_halves(result_near, result_far)
        else:
            result = jnp.concatenate([result_near, result_far], axis=0)
            result = lax.psum_scatter(result, "f", scatter_dimension=0, tiled=True)
            result_near = result_far = result
    far, result_far = stage(far, result_far)
    if grid:
        with scope("scaled_first"):
            scaled_near, far = add_halves(scaled_near, far)
            far, result_far = stage(swap_first(far), result_far)
            scaled_two = scaled_near.astype(F32) + far.astype(F32)
        with scope("result_second"):
            result_far = swap_second(result_far)
    grad_resid = out_grad[0].astype(F32) + norm_back(scaled_two, second_normed, second_inverse)
    grad_attn_out = grad_resid.astype(BF)

    with scope("out_core"):
        out_away, out_mine = weight_terms(attention_output, [grad_attn_out], False)
        out_away = send_core(out_away)
    grad_mixed = contract(out_weight, grad_attn_out, 1, 1).astype(BF)
    grad_mixed, out_away = stage(grad_mixed, out_away)
    with scope("out_second"):
        if grid:
            out_near, out_far = add_halves(out_mine, out_away)
            out_far = swap_second(out_far)
        else:
            out_near = out_far = sum_f(out_mine)
    grad_queries, grad_kv, *by_block = attention_backward(
        range(KEY_VALUE_HEADS),
        queries,
        keys,
        values,
        grad_mixed,
        log_totals,
        cosine,
        sine,
        bias,
        token,
        n,
    )
    grad_queries, result_far, down_owned = stage(grad_queries, result_far, down_owned)

    def pass_on(total):
        with scope("kv_grad_z"):
            return shift(total, 1)

    arrived = pass_on(by_block[1])
    if grid:
        with scope("result_first"):
            result_near, result_far = add_halves(result_near, result_far)
            result_far = swap_first(result_far)
    with scope("projected_core"):
        away, mine = weight_terms(
            normed_group, [grad_queries, grad_kv.reshape(2 * pair_cols, span)], True
        )
    away, arrived, out_far, result_far, gate_up_owned = stage(
        away, arrived, out_far, result_far, gate_up_owned
    )
    with scope("projected_core"):
        away = send_core(away)
    arrived = pass_on(add(arrived, by_block[2 % n]))
    if grid:
        result = result_near.astype(F32) + result_far.astype(F32)
        with scope("out_first"):
            out_near, out_far = add_halves(out_near, out_far)
            out_far = swap_first(out_far)
        with scope("projected_second"):
            near, far = add_halves(mine, away)
            far, out_far = stage(far, out_far)
            far = swap_second(far)
        out_near = add(out_near[0], out_far[0])
    else:
        result = result.astype(F32)
        near = far = sum_f(mine)
    result = (resid + result).astype(BF)
    with scope("out_z"):
        out_owned = total(send_z(out_near))
    arrived, far, out_owned = stage(arrived, far, out_owned)
    for step in range(3, n):
        arrived = pass_on(add(arrived, by_block[step]))
    if grid:
        with scope("projected_first"):
            near, far = add_halves(near, far)
            far = swap_first(far)
    far, gate_up_owned = stage(far, gate_up_owned)
    with scope("projected_z"):
        projected = send_z(add(near[0], far[0]) if grid else near)
    with scope("gate_up_sum_f"):
        gate_up_owned = lax.all_to_all(
            gate_up_owned.reshape(ranks, shard_rows, 2 * hidden_units), "f", 0, 0, tiled=True
        )
    kv_total = add(arrived, by_block[0])
    scaled_one = (
        contract(grad_queries, q_weight, 0, 1)
        + contract(kv_total[0], key_matrix, 0, 1)
        + contract(kv_total[1], value_matrix, 0, 1)
    )

    gate_up_owned = (
        gate_up_owned.astype(F32)
        .reshape(ranks, shard_rows, 2, n, unit)
        .transpose(2, 1, 3, 0, 4)
        .reshape(2, shard_rows, n * ranks * unit)
    )
    gate_owned, up_owned = gate_up_owned[0], gate_up_owned[1]
    gain_two_owned = along(w_gate, gate_owned) + along(w_up, up_owned)
    scaled_one, gain_two_owned, *projected = stage(scaled_one, gain_two_owned, *projected)
    input_grad = (grad_resid + norm_back(scaled_one, first_normed, first_inverse)).astype(BF)
    projected_owned = total(projected)
    query_owned, key_owned, value_owned = jnp.split(projected_owned, cuts[:2], axis=1)

    gain_one_owned = (
        along(w_query, query_owned)
        + along(key_weight, key_owned)
        + along(value_weight, value_owned)
    )
    return (
        result[None],
        input_grad[None],
        gain_one_owned,
        query_owned * gain_one,
        key_owned * gain_one,
        value_owned * gain_one,
        out_owned,
        gain_two_owned,
        gate_owned * gain_two,
        up_owned * gain_two,
        down_owned.astype(F32),
    )


def solution(mesh):
    n, ranks = mesh.shape["seq"], mesh.shape["fsdp"]
    named = Mesh(mesh.devices, ("z", "f"))
    every = ("z", "f")
    rows, vector, matrix = P("f", "z", None), P(every), P(every, None)
    in_specs = (
        rows,
        vector,
        matrix,
        matrix,
        matrix,
        matrix,
        vector,
        matrix,
        matrix,
        matrix,
        rows,
        P("f", None),
        P("f", None),
    )
    out_specs = (rows, rows, vector) + (matrix,) * 4 + (vector,) + (matrix,) * 3

    def step(*operands):
        return on_device(n, ranks, *operands)

    return jax.shard_map(
        step, mesh=named, in_specs=in_specs, out_specs=out_specs, check_vma=False
    )
```

time: 772 us -> 531 us (0.69)
  matrix products: 179 us -> 22.9 us
  waiting for transfers between devices: 364 us -> 212 us
  Pallas kernels: 0 us -> 107 us
  local copies, waits for them, and re-layouts: 83.2 us -> 40.4 us
  other arithmetic: 72.7 us -> 60 us
  between operations: 2.66 us -> 15.2 us
    ppermute x82 -> x49, waiting for transfers between devices: 364 us -> 188 us  [the longest x15 101 us: shift(): return lax.ppermute(a, 'z', [(i, (i + by) % n) for i in range(n)])]
    dot_general x66 -> x5, matrix products: 148 us -> 16.4 us  [contract(): lax.dot_general(left, right, (((at_left,), (at_right,)), ((), ())), prefe...]
    pallas_call x0 -> x8, Pallas kernels: none -> 107 us  [the longest x2 33.5 us: feed_forward(): pl.pallas_call(lambda *refs: feed_kernel(count, first, *refs), grid=(coun...]
    dynamic_update_slice x42 -> x0, local copies, waits for them, and re-layouts: 31.6 us -> none  [put(): return lax.dynamic_update_slice(a, piece, index)]
    unnamed x155 -> x181, local copies, waits for them, and re-layouts: 6.47 us -> 31.8 us
    dot_general x5 -> x2, matrix products: 30.8 us -> 6.48 us  [product(): return jnp.dot(left, right, preferred_element_type=F32)]
    reduce_scatter x0 -> x2, waiting for transfers between devices: none -> 14.7 us  [the longest x1 14.7 us: on_device(): lax.psum_scatter(gate_up_terms, 'z', scatter_dimension=0, tiled=True)]
    slice x10 -> x2, local copies, waits for them, and re-layouts: 12.8 us -> 0.01 us  [the longest x1 0.01 us: on_device(): place_all[None, :token_count]]
  transfers between devices with their start and end apart: 82 -> 54, of which waited for: 45 -> 21; matrix products, arithmetic and copies ran while one was open for 40% -> 14% of each run, Pallas kernels for 0% -> 16%
where the time goes in v2:
time: 531 us; the launch traced here: 524 us
  waiting for transfers between devices  212 us (40%)
  Pallas kernels  107 us (20%)
  starting transfers between devices  66.1 us (12%)
  other arithmetic  60 us (11%)
  local copies, waits for them, and re-layouts  40.4 us (8%)
  matrix products  22.9 us (4%)
  between operations  15.2 us (3%)
    ppermute x15, waiting for transfers between devices, shift(): return lax.ppermute(a, 'z', [(i, (i + by) % n) for i in range(n)])  101 us
    ppermute x8, waiting for transfers between devices, swap_first(): return lax.ppermute(a, 'f', [(i, i ^ 4 >> i % 2) for i in range(ranks)])  49.7 us
    pallas_call x2, Pallas kernels, feed_forward(): pl.pallas_call(lambda *refs: feed_kernel(count, first, *refs), grid=(coun...  33.5 us
    convert_element_type x13, other arithmetic, add(): return (a.astype(F32) + b.astype(F32)).astype(BF)  31.9 us
    unnamed x181, local copies, waits for them, and re-layouts  31.8 us
    ppermute x10, waiting for transfers between devices, swap_second(): return lax.ppermute(a, 'f', [(i, i ^ 2 << i % 2) for i in range(ranks)])  30.6 us
    ppermute x15, starting transfers between devices, shift(): return lax.ppermute(a, 'z', [(i, (i + by) % n) for i in range(n)])  30 us
    pallas_call x1, Pallas kernels, project(): pl.pallas_call(lambda *refs: project_kernel(n, len(parts), *refs), in_spe...  20 us
  transfers between devices with their start and end apart: 54, of which 21 were waited for; matrix products, arithmetic and copies ran while one was open for 14% of the time, Pallas kernels for 16%

profile of v2, /device:TPU:0, one launch (start us, length us, event | category | flops | bytes accessed | tf_op | source)
XLA Modules:
  0.0 523.7 jit_solution(1779714445735407286)
XLA Ops:
  11.3 5.3 %all-to-all-start = ((bf16[8,48,1024]{2,1,0:T(8,128)(2,1)}), bf16[8,48,1024]{2,1,0:T(8,128)(2,1)S(1)}, u32[]{:S(2)}, u32[]{:S(2)}) async-start(bf16[8,48,1024]{2,1,0:T(8,128)(2,1)} %reshape.212), calls=%async_computation | async-start | bytes 1572864 | tf_op jit(solution)/shard_map/gate_up_f/all_to_all | solution.py:618
  21.8 2.6 collective-permute-start.1
  27.2 9.4 %collective-permute-done.4 = bf16[48,4608]{1,0:T(8,128)(2,1)S(1)} collective-permute-done((bf16[48,4608]{1,0:T(8,128)(2,1)}, bf16[48,4608]{1,0:T(8,128)(2,1)S(1)}, u32[]{:S(2)}, u32[]{:S(2)}) %collective-permute-start.4) | collective-permute-done | bytes 442400 | tf_op jit(solution)/shard_map/attention_weights_own/ppermute | solution.py:520
  36.7 2.5 collective-permute-start.5
  40.7 12.8 %collective-permute-done.1 = bf16[48,4608]{1,0:T(8,128)(2,1)} collective-permute-done((bf16[48,4608]{1,0:T(8,128)(2,1)}, bf16[48,4608]{1,0:T(8,128)(2,1)}, u32[]{:S(2)}, u32[]{:S(2)}) %collective-permute-start.1) | collective-permute-done | bytes 442400 | tf_op jit(solution)/shard_map/attention_weights_z/ppermute | solution.py:517
  56.9 10.0 %collective-permute-start.7 = (bf16[256,1536]{1,0:T(8,128)(2,1)S(1)}, bf16[256,1536]{1,0:T(8,128)(2,1)S(1)}, u32[]{:S(2)}, u32[]{:S(2)}) collective-permute-start(bf16[256,1536]{1,0:T(8,128)(2,1)S(1)} %bitcast.130), channel_id=1, source_target_pairs={{0,8},{8,16},{16,24},{24,0},{1,9},{9,17},{17,25},{25,1},{2,10},{10... | collective-permute-start | bytes 2359304 | tf_op jit(solution)/shard_map/tokens_z/ppermute | solution.py:517
  67.7 18.2 %collective-permute-done.7.refs_18_ = bf16[256,1536]{1,0:T(8,128)(2,1)S(1)} collective-permute-done((bf16[256,1536]{1,0:T(8,128)(2,1)S(1)}, bf16[256,1536]{1,0:T(8,128)(2,1)S(1)}, u32[]{:S(2)}, u32[]{:S(2)}) %collective-permute-start.7) | collective-permute-done | bytes 786464 | tf_op jit(solution)/shard_map/tokens_z/ppermute | solution.py:517
  88.8 21.0 %collective-permute-done.13.refs_19_ = bf16[256,1536]{1,0:T(8,128)(2,1)S(1)} collective-permute-done((bf16[256,1536]{1,0:T(8,128)(2,1)S(1)}, bf16[256,1536]{1,0:T(8,128)(2,1)S(1)}, u32[]{:S(2)}, u32[]{:S(2)}) %collective-permute-start.13) | collective-permute-done | bytes 786464 | tf_op jit(solution)/shard_map/tokens_z/ppermute | solution.py:517
  113.1 18.8 %collective-permute-done.17 = bf16[256,1536]{1,0:T(8,128)(2,1)} collective-permute-done((bf16[256,1536]{1,0:T(8,128)(2,1)S(1)}, bf16[256,1536]{1,0:T(8,128)(2,1)}, u32[]{:S(2)}, u32[]{:S(2)}) %collective-permute-start.17) | collective-permute-done | bytes 786464 | tf_op jit(solution)/shard_map/out_grad_first/ppermute | solution.py:520
  133.6 2.6 collective-permute-done.15.refs_8_
  141.2 20.0 %project.1 = (bf16[1536,256]{1,0:T(8,128)(2,1)}, bf16[768,1024]{1,0:T(8,128)(2,1)}, bf16[768,1024]{1,0:T(8,128)(2,1)}, bf16[1536,1024]{1,0:T(8,128)(2,1)}, bf16[1536,4608]{1,0:T(8,128)(2,1)}) custom-call(s32[32]{0:T(128)} %broadcast_multiply_fusion.5.refs_0_, bf16[1,48,4608]{2,1,0:T(8,128)(2,1)} %get-tuple-element.219.refs_1_, ...), custom_call_target="tpu_custom_call" | custom-call | flops 100000000 | bytes 300000 | tf_op jit(solution)/shard_map/project/pallas_call | solution.py:328
  165.2 12.1 %attention_forward.1 = (bf16[1536,256]{1,0:T(8,128)(2,1)S(1)}, f32[8,2,256]{2,1,0:T(2,128)S(1)}) custom-call(bf16[1536,256]{1,0:T(8,128)(2,1)S(1)} %copy-done.8, bf16[768,1024]{1,0:T(8,128)(2,1)S(1)} %copy-done, bf16[768,1024]{1,0:T(8,128)(2,1)S(1)} %copy-done.2, f32[1024,256]{1,0:T(8,128)S(1)} %and_select_fusion.bias_ref), custom_call_target="tpu_custom_call" | custom-call | flops 100000000 | bytes 300000 | tf_op jit(solution)/shard_map/attention_forward/pallas_call | solution.py:131
  177.3 3.8 multiply_reduce_fusion.1
  182.6 10.7 %collective-permute-done.22 = bf16[256,1536]{1,0:T(8,128)(2,1)S(1)} collective-permute-done((bf16[256,1536]{1,0:T(8,128)(2,1)S(1)}, bf16[256,1536]{1,0:T(8,128)(2,1)S(1)}, u32[]{:S(2)}, u32[]{:S(2)}) %collective-permute-start.22) | collective-permute-done | bytes 786464 | tf_op jit(solution)/shard_map/normed_first/ppermute | solution.py:520
  196.5 17.4 %collective-permute-done.23.refs_1_ = bf16[512,1536]{1,0:T(8,128)(2,1)S(1)} collective-permute-done((bf16[512,1536]{1,0:T(8,128)(2,1)S(1)}, bf16[512,1536]{1,0:T(8,128)(2,1)S(1)}, u32[]{:S(2)}, u32[]{:S(2)}) %collective-permute-start.23) | collective-permute-done | bytes 1572896 | tf_op jit(solution)/shard_map/normed_second/ppermute | solution.py:523
  219.9 3.2 all-gather.3.cloned.1.call-done
  228.7 15.5 %feed_forward.2 = (bf16[1024,1536]{1,0:T(8,128)(2,1)S(1)}, bf16[1024,512]{1,0:T(8,128)(2,1)S(1)}, bf16[1024,1024]{1,0:T(8,128)(2,1)S(1)}, f32[512,1536]{1,0:T(8,128)}, bf16[512,1536]{1,0:T(8,128)(2,1)S(1)}) custom-call(bf16[512,1536]{1,0:T(8,128)(2,1)S(1)} %copy-done.21, bf16[512,1536]{1,0:T(8,128)(2,1)S(1)} %copy-done.24, bf16[512,1536]{1,0:T(8,128)(2,1)S(1)} %copy-done.27, ...), custom_call_target="tpu_custom_call" | custom-call | flops 30000001024 | bytes 90000000 | tf_op jit(solution)/shard_map/feed_forward/pallas_call | solution.py:428
  244.3 18.0 %feed_forward.3 = (bf16[1024,1536]{1,0:T(8,128)(2,1)}, bf16[1024,512]{1,0:T(8,128)(2,1)S(1)}, bf16[1024,1024]{1,0:T(8,128)(2,1)S(1)}, bf16[512,1536]{1,0:T(8,128)(2,1)}, bf16[512,1536]{1,0:T(8,128)(2,1)}) custom-call(bf16[512,1536]{1,0:T(8,128)(2,1)S(1)} %copy-done.14, bf16[512,1536]{1,0:T(8,128)(2,1)S(1)} %copy-done.19, ...), custom_call_target="tpu_custom_call" | custom-call | flops 30000001024 | bytes 90000000 | tf_op jit(solution)/shard_map/feed_forward/pallas_call | solution.py:428
  262.4 5.7 %add_convert_fusion.5 = (bf16[512,1536]{1,0:T(8,128)(2,1)}, bf16[512,1536]{1,0:T(8,128)(2,1)}) fusion(bf16[1024,1536]{1,0:T(8,128)(2,1)} %collective-permute-done.28, bf16[1024,1536]{1,0:T(8,128)(2,1)} %get-tuple-element.133), kind=kLoop, calls=%fused_computation.13 | loop fusion | flops 6291456 | bytes 9437184 | tf_op jit(solution)/shard_map/scaled_second/convert_element_type | solution.py:552
  268.1 8.1 %gate_up_terms.1 = (bf16[1536,1024]{1,0:T(8,128)(2,1)S(1)}, f32[8,128]{1,0:T(8,128)S(1)}) custom-call(bf16[512,1536]{1,0:T(8,128)(2,1)S(1)} %copy-done.14, bf16[512,1536]{1,0:T(8,128)(2,1)S(1)} %copy-done.19, bf16[512,1536]{1,0:T(8,128)(2,1)S(1)} %copy-done.22, bf16[512,1536]{1,0:T(8,128)(2,1)S(1)} %copy-done.25, ...), custom_call_target="tpu_custom_call" | custom-call | flops 15000000512 | bytes 45000000 | tf_op jit(solution)/shard_map/gate_up_sum_z/gate_up_terms/pallas_call | solution.py:472
  276.3 3.5 convolution_convert_fusion
  281.6 3.0 convolution_convert_fusion.1
  285.7 4.5 add_convert_fusion.4
  290.2 10.5 %collective-permute-done.30 = bf16[512,1536]{1,0:T(8,128)(2,1)S(1)} collective-permute-done((bf16[512,1536]{1,0:T(8,128)(2,1)}, bf16[512,1536]{1,0:T(8,128)(2,1)S(1)}, u32[]{:S(2)}, u32[]{:S(2)}) %collective-permute-start.30) | collective-permute-done | bytes 1572896 | tf_op jit(solution)/shard_map/scaled_second/ppermute | solution.py:523
  303.8 10.7 %collective-permute-done.31 = bf16[256,1536]{1,0:T(8,128)(2,1)} collective-permute-done((bf16[256,1536]{1,0:T(8,128)(2,1)}, bf16[256,1536]{1,0:T(8,128)(2,1)}, u32[]{:S(2)}, u32[]{:S(2)}) %collective-permute-start.31) | collective-permute-done | bytes 786464 | tf_op jit(solution)/shard_map/scaled_first/ppermute | solution.py:520
  316.6 3.2 fusion.41
  319.7 3.8 owned_terms.2
  326.7 3.8 fusion.15.grad_ref
  331.9 17.5 %attention_backward.1 = (bf16[1536,256]{1,0:T(8,128)(2,1)S(1)}, bf16[2,768,1024]{2,1,0:T(8,128)(2,1)S(1)}, bf16[2,768,256]{2,1,0:T(8,128)(2,1)S(1)}, bf16[2,768,...) custom-call(bf16[1536,256]{1,0:T(8,128)(2,1)S(1)} %copy-done.9, ...), custom_call_target="tpu_custom_call" | custom-call | flops 100000000 | bytes 300000 | tf_op jit(solution)/shard_map/attention_backward/pallas_call | solution.py:161
  352.9 4.6 add_convert_fusion.9
  358.3 2.4 add_convert_fusion.15
  362.3 12.2 %owned_terms.3 = (bf16[4,4,48,3072]{3,2,1,0:T(8,128)(2,1)S(1)}, bf16[4,4,48,3072]{3,2,1,0:T(8,128)(2,1)}) custom-call(s32[8]{0:T(128)S(1)} %stack.183.refs_0_, bf16[1536,1024]{1,0:T(8,128)(2,1)S(1)} %copy-done.4, bf16[1536,256]{1,0:T(8,128)(2,1)S(1)} %get-tuple-element.153.refs_2_, bf16[1536,1024]{1,0:T(8,128)(2,1)S(1)} %bitcast.128), custom_call_target="tpu_custom_call" | custom-call | flops 100000000 | bytes 300000 | tf_op jit(solution)/shard_map/projected_core/owned_terms/pallas_call | solution.py:256
  376.6 14.7 %reduce-scatter.5.cloned.1.call-done = bf16[384,1024]{1,0:T(8,128)(2,1)} async-done(((bf16[1536,1024]{1,0:T(8,128)(2,1)}), bf16[384,1024]{1,0:T(8,128)(2,1)}) %reduce-scatter.5.cloned.1.call-update) | async-done | bytes 786448 | tf_op jit(solution)/shard_map/gate_up_sum_z/reduce_scatter | solution.py:767
  395.1 5.1 collective-permute-done.38
  400.2 5.0 add_convert_fusion
  418.7 16.8 %collective-permute-done.43 = bf16[48,1536]{1,0:T(8,128)(2,1)S(1)} collective-permute-done((bf16[48,1536]{1,0:T(8,128)(2,1)S(1)}, bf16[48,1536]{1,0:T(8,128)(2,1)S(1)}, u32[]{:S(2)}, u32[]{:S(2)}) %collective-permute-start.43) | collective-permute-done | bytes 147488 | tf_op jit(solution)/shard_map/out_z/ppermute | solution.py:517
  435.5 5.4 %collective-permute-done.42 = bf16[48,1536]{1,0:T(8,128)(2,1)S(1)} collective-permute-done((bf16[48,1536]{1,0:T(8,128)(2,1)S(1)}, bf16[48,1536]{1,0:T(8,128)(2,1)S(1)}, u32[]{:S(2)}, u32[]{:S(2)}) %collective-permute-start.42) | collective-permute-done | bytes 147488 | tf_op jit(solution)/shard_map/out_z/ppermute | solution.py:517
  442.0 3.9 collective-permute-start.44
  445.9 2.4 fusion.31
  450.8 13.1 %collective-permute-done.44 = bf16[2,768,256]{2,1,0:T(8,128)(2,1)S(1)} collective-permute-done((bf16[2,768,256]{2,1,0:T(8,128)(2,1)S(1)}, bf16[2,768,256]{2,1,0:T(8,128)(2,1)S(1)}, u32[]{:S(2)}, u32[]{:S(2)}) %collective-permute-start.44) | collective-permute-done | bytes 786464 | tf_op jit(solution)/shard_map/kv_grad_z/ppermute | solution.py:517
  464.1 2.5 fusion.18
  466.6 2.5 fusion.20
  469.1 3.9 fusion.12
  473.9 4.4 all-to-all-start.1
  478.3 2.2 add_convert_fusion.6
  484.9 6.1 %all-to-all-done.1 = bf16[8,48,1024]{2,1,0:T(8,128)(2,1)} async-done(((bf16[8,48,1024]{2,1,0:T(8,128)(2,1)}), bf16[8,48,1024]{2,1,0:T(8,128)(2,1)}, u32[]{:S(2)}, u32[]{:S(2)}) %all-to-all-start.1) | async-done | bytes 786464 | tf_op jit(solution)/shard_map/gate_up_sum_f/all_to_all | solution.py:861
  496.2 2.6 broadcast_multiply_fusion
  499.5 11.6 %collective-permute-done.47 = bf16[48,3072]{1,0:T(8,128)(2,1)} collective-permute-done((bf16[48,3072]{1,0:T(8,128)(2,1)}, bf16[48,3072]{1,0:T(8,128)(2,1)}, u32[]{:S(2)}, u32[]{:S(2)}) %collective-permute-start.47) | collective-permute-done | bytes 294944 | tf_op jit(solution)/shard_map/projected_z/ppermute | solution.py:517
  (328 shorter events, 108.8 us)
Async XLA Ops:
  11.3 28.3 %all-to-all-start = ((bf16[8,48,1024]{2,1,0:T(8,128)(2,1)}), bf16[8,48,1024]{2,1,0:T(8,128)(2,1)S(1)}, u32[]{:S(2)}, u32[]{:S(2)}) async-start(bf16[8,48,1024]{2,1,0:T(8,128)(2,1)} %reshape.212), calls=%async_computation | async-start | bytes 1572864 | tf_op jit(solution)/shard_map/gate_up_f/all_to_all | solution.py:618
  16.6 206.4 %all-gather.3.cloned.1.call-start = ((), (), s32[]{:S(2)}) async-start(), calls=%async_computation.6 | async-start | bytes 5898240 | tf_op jit(solution)/shard_map/gate_up_down_z/all_gather | solution.py:667
  18.3 18.4 %collective-permute-start.4 = (bf16[48,4608]{1,0:T(8,128)(2,1)}, bf16[48,4608]{1,0:T(8,128)(2,1)S(1)}, u32[]{:S(2)}, u32[]{:S(2)}) collective-permute-start(bf16[48,4608]{1,0:T(8,128)(2,1)} %get-tuple-element.218), channel_id=1, source_target_pairs={{0,4},{1,3},{2,6},{3,1},{4,0},{5,7},{6,2},{7,5},{8,12},{9,11},{10,... | collective-permute-start | bytes 1327112 | tf_op jit(solution)/shard_map/attention_weights_own/ppermute | solution.py:520
  20.2 20.5 %collective-permute-start = (bf16[48,4608]{1,0:T(8,128)(2,1)}, bf16[48,4608]{1,0:T(8,128)(2,1)}, u32[]{:S(2)}, u32[]{:S(2)}) collective-permute-start(bf16[48,4608]{1,0:T(8,128)(2,1)} %get-tuple-element.218), channel_id=1, source_target_pairs={{0,8},{8,16},{16,24},{24,0},{1,9},{9,17},{17,25},{25,1},{2,10},{10... | collective-permute-start | bytes 1327112 | tf_op jit(solution)/shard_map/attention_weights_z/ppermute | solution.py:517
  21.8 31.7 %collective-permute-start.1 = (bf16[48,4608]{1,0:T(8,128)(2,1)}, bf16[48,4608]{1,0:T(8,128)(2,1)}, u32[]{:S(2)}, u32[]{:S(2)}) collective-permute-start(bf16[48,4608]{1,0:T(8,128)(2,1)} %get-tuple-element.218), channel_id=1, source_target_pairs={{0,16},{8,24},{16,0},{24,8},{1,17},{9,25},{17,1},{25,9},{2,18},{10... | collective-permute-start | bytes 1327112 | tf_op jit(solution)/shard_map/attention_weights_z/ppermute | solution.py:517
  24.4 29.1 %collective-permute-start.2 = (bf16[48,4608]{1,0:T(8,128)(2,1)}, bf16[48,4608]{1,0:T(8,128)(2,1)}, u32[]{:S(2)}, u32[]{:S(2)}) collective-permute-start(bf16[48,4608]{1,0:T(8,128)(2,1)} %get-tuple-element.218), channel_id=1, source_target_pairs={{0,24},{8,0},{16,8},{24,16},{1,25},{9,1},{17,9},{25,17},{2,26},{10... | collective-permute-start | bytes 1327112 | tf_op jit(solution)/shard_map/attention_weights_z/ppermute | solution.py:517
  25.8 27.7 %collective-permute-start.3 = (bf16[48,4608]{1,0:T(8,128)(2,1)}, bf16[48,4608]{1,0:T(8,128)(2,1)S(1)}, u32[]{:S(2)}, u32[]{:S(2)}) collective-permute-start(bf16[48,4608]{1,0:T(8,128)(2,1)} %get-tuple-element.218), channel_id=1, source_target_pairs={{0,2},{1,5},{2,0},{3,7},{4,6},{5,1},{6,4},{7,3},{8,10},{9,13},{10,... | collective-permute-start | bytes 1327112 | tf_op jit(solution)/shard_map/attention_weights_own/ppermute | solution.py:523
  36.7 16.8 %collective-permute-start.5 = (bf16[48,4608]{1,0:T(8,128)(2,1)S(1)}, bf16[48,4608]{1,0:T(8,128)(2,1)S(1)}, u32[]{:S(2)}, u32[]{:S(2)}) collective-permute-start(bf16[48,4608]{1,0:T(8,128)(2,1)S(1)} %collective-permute-done.4), channel_id=1, source_target_pairs={{0,2},{1,5},{2,0},{3,7},{4,6},{5,1},{6,4},{7,3},{8,10},{9,13},{10,... | collective-permute-start | bytes 1327112 | tf_op jit(solution)/shard_map/attention_weights_own/ppermute | solution.py:523
  55.9 30.1 %collective-permute-start.6 = (bf16[3,48,4608]{2,1,0:T(8,128)(2,1)S(1)}, bf16[3,48,4608]{2,1,0:T(8,128)(2,1)S(1)}, u32[]{:S(2)}, u32[]{:S(2)}) collective-permute-start(bf16[3,48,4608]{2,1,0:T(8,128)(2,1)S(1)} %pad_maximum_fusion.2.refs_2_), channel_id=1, source_target_pairs={{0,4},{1,3},{2,6},{3,1},{4,0},{5,7},{6,2},{7,5},{8,12},{9,11},{10,... | collective-permute-start | bytes 3981320 | tf_op jit(solution)/shard_map/attention_weights_first/ppermute | solution.py:520
  56.9 29.0 %collective-permute-start.7 = (bf16[256,1536]{1,0:T(8,128)(2,1)S(1)}, bf16[256,1536]{1,0:T(8,128)(2,1)S(1)}, u32[]{:S(2)}, u32[]{:S(2)}) collective-permute-start(bf16[256,1536]{1,0:T(8,128)(2,1)S(1)} %bitcast.130), channel_id=1, source_target_pairs={{0,8},{8,16},{16,24},{24,0},{1,9},{9,17},{17,25},{25,1},{2,10},{10... | collective-permute-start | bytes 2359304 | tf_op jit(solution)/shard_map/tokens_z/ppermute | solution.py:517
  66.9 19.0 %collective-permute-start.9 = (bf16[48,4608]{1,0:T(8,128)(2,1)S(1)}, bf16[48,4608]{1,0:T(8,128)(2,1)S(1)}, u32[]{:S(2)}, u32[]{:S(2)}) collective-permute-start(bf16[48,4608]{1,0:T(8,128)(2,1)S(1)} %copy-done.67), channel_id=1, source_target_pairs={{0,1},{1,0},{2,3},{3,2},{4,5},{5,4},{6,7},{7,6},{8,9},{9,8},{10,11... | collective-permute-start | bytes 1327112 | tf_op jit(solution)/shard_map/attention_weights_core/ppermute | solution.py:526
  67.2 18.8 %collective-permute-start.10 = (bf16[48,4608]{1,0:T(8,128)(2,1)}, bf16[48,4608]{1,0:T(8,128)(2,1)S(1)}, u32[]{:S(2)}, u32[]{:S(2)}) collective-permute-start(bf16[48,4608]{1,0:T(8,128)(2,1)} %copy-done.68), channel_id=1, source_target_pairs={{0,1},{1,0},{2,3},{3,2},{4,5},{5,4},{6,7},{7,6},{8,9},{9,8},{10,11... | collective-permute-start | bytes 1327112 | tf_op jit(solution)/shard_map/attention_weights_core/ppermute | solution.py:526
  67.4 18.5 %collective-permute-start.11 = (bf16[48,4608]{1,0:T(8,128)(2,1)}, bf16[48,4608]{1,0:T(8,128)(2,1)S(1)}, u32[]{:S(2)}, u32[]{:S(2)}) collective-permute-start(bf16[48,4608]{1,0:T(8,128)(2,1)} %copy-done.69), channel_id=1, source_target_pairs={{0,1},{1,0},{2,3},{3,2},{4,5},{5,4},{6,7},{7,6},{8,9},{9,8},{10,11... | collective-permute-start | bytes 1327112 | tf_op jit(solution)/shard_map/attention_weights_core/ppermute | solution.py:526
  86.9 23.0 %collective-permute-start.12 = (bf16[3,48,4608]{2,1,0:T(8,128)(2,1)S(1)}, bf16[3,48,4608]{2,1,0:T(8,128)(2,1)}, u32[]{:S(2)}, u32[]{:S(2)}) collective-permute-start(bf16[3,48,4608]{2,1,0:T(8,128)(2,1)S(1)} %pad_maximum_fusion.2.refs_2_), channel_id=1, source_target_pairs={{0,2},{1,5},{2,0},{3,7},{4,6},{5,1},{6,4},{7,3},{8,10},{9,13},{10,... | collective-permute-start | bytes 3981320 | tf_op jit(solution)/shard_map/attention_weights_second/ppermute | solution.py:523
  88.1 21.8 %collective-permute-start.14 = (bf16[3,48,4608]{2,1,0:T(8,128)(2,1)S(1)}, bf16[3,48,4608]{2,1,0:T(8,128)(2,1)S(1)}, u32[]{:S(2)}, u32[]{:S(2)}) collective-permute-start(bf16[3,48,4608]{2,1,0:T(8,128)(2,1)S(1)} %pad_maximum_fusion.2.refs_2_), channel_id=1, source_target_pairs={{0,1},{1,0},{2,3},{3,2},{4,5},{5,4},{6,7},{7,6},{8,9},{9,8},{10,11... | collective-permute-start | bytes 3981320 | tf_op jit(solution)/shard_map/attention_weights_core/ppermute | solution.py:526
  88.1 21.8 %collective-permute-start.13 = (bf16[256,1536]{1,0:T(8,128)(2,1)S(1)}, bf16[256,1536]{1,0:T(8,128)(2,1)S(1)}, u32[]{:S(2)}, u32[]{:S(2)}) collective-permute-start(bf16[256,1536]{1,0:T(8,128)(2,1)S(1)} %collective-permute-done.7.refs_18_), channel_id=1, source_target_pairs={{0,8},{8,16},{16,24},{24,0},{1,9},{9,17},{17,25},{25,1},{2,10},{10... | collective-permute-start | bytes 2359304 | tf_op jit(solution)/shard_map/tokens_z/ppermute | solution.py:517
  109.8 26.4 %collective-permute-start.15 = (bf16[3,48,4608]{2,1,0:T(8,128)(2,1)S(1)}, bf16[3,48,4608]{2,1,0:T(8,128)(2,1)}, u32[]{:S(2)}, u32[]{:S(2)}) collective-permute-start(bf16[3,48,4608]{2,1,0:T(8,128)(2,1)S(1)} %collective-permute-done.6.refs_4_), channel_id=1, source_target_pairs={{0,2},{1,5},{2,0},{3,7},{4,6},{5,1},{6,4},{7,3},{8,10},{9,13},{10,... | collective-permute-start | bytes 3981320 | tf_op jit(solution)/shard_map/attention_weights_second/ppermute | solution.py:523
  110.7 25.5 %collective-permute-start.18 = (bf16[3,48,4608]{2,1,0:T(8,128)(2,1)S(1)}, bf16[3,48,4608]{2,1,0:T(8,128)(2,1)}, u32[]{:S(2)}, u32[]{:S(2)}) collective-permute-start(bf16[3,48,4608]{2,1,0:T(8,128)(2,1)S(1)} %collective-permute-done.6.refs_4_), channel_id=1, source_target_pairs={{0,1},{1,0},{2,3},{3,2},{4,5},{5,4},{6,7},{7,6},{8,9},{9,8},{10,11... | collective-permute-start | bytes 3981320 | tf_op jit(solution)/shard_map/attention_weights_core/ppermute | solution.py:526
  110.7 25.5 %collective-permute-start.19 = (bf16[3,48,4608]{2,1,0:T(8,128)(2,1)}, bf16[3,48,4608]{2,1,0:T(8,128)(2,1)}, u32[]{:S(2)}, u32[]{:S(2)}) collective-permute-start(bf16[3,48,4608]{2,1,0:T(8,128)(2,1)} %collective-permute-done.12.refs_6_), channel_id=1, source_target_pairs={{0,1},{1,0},{2,3},{3,2},{4,5},{5,4},{6,7},{7,6},{8,9},{9,8},{10,11... | collective-permute-start | bytes 3981320 | tf_op jit(solution)/shard_map/attention_weights_core/ppermute | solution.py:526
  111.2 20.6 %collective-permute-start.17 = (bf16[256,1536]{1,0:T(8,128)(2,1)S(1)}, bf16[256,1536]{1,0:T(8,128)(2,1)}, u32[]{:S(2)}, u32[]{:S(2)}) collective-permute-start(bf16[256,1536]{1,0:T(8,128)(2,1)S(1)} %bitcast.133), channel_id=1, source_target_pairs={{0,4},{1,3},{2,6},{3,1},{4,0},{5,7},{6,2},{7,5},{8,12},{9,11},{10,... | collective-permute-start | bytes 2359304 | tf_op jit(solution)/shard_map/out_grad_first/ppermute | solution.py:520
  112.5 21.1 %collective-permute-start.16 = (bf16[256,1536]{1,0:T(8,128)(2,1)S(1)}, bf16[256,1536]{1,0:T(8,128)(2,1)}, u32[]{:S(2)}, u32[]{:S(2)}) collective-permute-start(bf16[256,1536]{1,0:T(8,128)(2,1)S(1)} %collective-permute-done.13.refs_19_), channel_id=1, source_target_pairs={{0,8},{8,16},{16,24},{24,0},{1,9},{9,17},{17,25},{25,1},{2,10},{10... | collective-permute-start | bytes 2359304 | tf_op jit(solution)/shard_map/tokens_z/ppermute | solution.py:517
  136.2 216.6 %reduce-scatter.3.cloned.1.call-start = ((), (), s32[]{:S(2)}) async-start(), calls=%async_computation.4 | async-start | bytes 1966080 | tf_op jit(solution)/shard_map/down_sum_z/reduce_scatter | solution.py:749
  139.4 41.9 %collective-permute-start.21 = (bf16[512,1536]{1,0:T(8,128)(2,1)S(1)}, bf16[512,1536]{1,0:T(8,128)(2,1)}, u32[]{:S(2)}, u32[]{:S(2)}) collective-permute-start(bf16[512,1536]{1,0:T(8,128)(2,1)S(1)} %pad_maximum_fusion.refs_2_), channel_id=1, source_target_pairs={{0,2},{1,5},{2,0},{3,7},{4,6},{5,1},{6,4},{7,3},{8,10},{9,13},{10,... | collective-permute-start | bytes 4718600 | tf_op jit(solution)/shard_map/out_grad_second/ppermute | solution.py:523
  181.3 12.1 %collective-permute-start.22 = (bf16[256,1536]{1,0:T(8,128)(2,1)S(1)}, bf16[256,1536]{1,0:T(8,128)(2,1)S(1)}, u32[]{:S(2)}, u32[]{:S(2)}) collective-permute-start(bf16[256,1536]{1,0:T(8,128)(2,1)S(1)} %multiply_convert_fusion.1), channel_id=1, source_target_pairs={{0,4},{1,3},{2,6},{3,1},{4,0},{5,7},{6,2},{7,5},{8,12},{9,11},{10,... | collective-permute-start | bytes 2359304 | tf_op jit(solution)/shard_map/normed_first/ppermute | solution.py:520
  193.5 20.5 %collective-permute-start.23 = (bf16[512,1536]{1,0:T(8,128)(2,1)S(1)}, bf16[512,1536]{1,0:T(8,128)(2,1)S(1)}, u32[]{:S(2)}, u32[]{:S(2)}) collective-permute-start(bf16[512,1536]{1,0:T(8,128)(2,1)S(1)} %pad_maximum_fusion.1.refs_0_), channel_id=1, source_target_pairs={{0,2},{1,5},{2,0},{3,7},{4,6},{5,1},{6,4},{7,3},{8,10},{9,13},{10,... | collective-permute-start | bytes 4718600 | tf_op jit(solution)/shard_map/normed_second/ppermute | solution.py:523
  194.8 20.3 %collective-permute-start.26 = (bf16[512,1536]{1,0:T(8,128)(2,1)S(1)}, bf16[512,1536]{1,0:T(8,128)(2,1)S(1)}, u32[]{:S(2)}, u32[]{:S(2)}) collective-permute-start(bf16[512,1536]{1,0:T(8,128)(2,1)S(1)} %pad_maximum_fusion.refs_2_), channel_id=1, source_target_pairs={{0,1},{1,0},{2,3},{3,2},{4,5},{5,4},{6,7},{7,6},{8,9},{9,8},{10,11... | collective-permute-start | bytes 4718600 | tf_op jit(solution)/shard_map/out_grad_all/ppermute | solution.py:526
  194.8 21.5 %collective-permute-start.27 = (bf16[512,1536]{1,0:T(8,128)(2,1)}, bf16[512,1536]{1,0:T(8,128)(2,1)S(1)}, u32[]{:S(2)}, u32[]{:S(2)}) collective-permute-start(bf16[512,1536]{1,0:T(8,128)(2,1)} %collective-permute-done.21.refs_3_), channel_id=1, source_target_pairs={{0,1},{1,0},{2,3},{3,2},{4,5},{5,4},{6,7},{7,6},{8,9},{9,8},{10,11... | collective-permute-start | bytes 4718600 | tf_op jit(solution)/shard_map/out_grad_all/ppermute | solution.py:526
  195.3 22.2 %collective-permute-start.24 = (bf16[512,1536]{1,0:T(8,128)(2,1)S(1)}, bf16[512,1536]{1,0:T(8,128)(2,1)S(1)}, u32[]{:S(2)}, u32[]{:S(2)}) collective-permute-start(bf16[512,1536]{1,0:T(8,128)(2,1)S(1)} %pad_maximum_fusion.1.refs_0_), channel_id=1, source_target_pairs={{0,1},{1,0},{2,3},{3,2},{4,5},{5,4},{6,7},{7,6},{8,9},{9,8},{10,11... | collective-permute-start | bytes 4718600 | tf_op jit(solution)/shard_map/normed_second/ppermute | solution.py:526
  244.2 18.2 %collective-permute-start.28 = (bf16[1024,1536]{1,0:T(8,128)(2,1)S(1)}, bf16[1024,1536]{1,0:T(8,128)(2,1)}, u32[]{:S(2)}, u32[]{:S(2)}) collective-permute-start(bf16[1024,1536]{1,0:T(8,128)(2,1)S(1)} %get-tuple-element.134), channel_id=1, source_target_pairs={{0,1},{1,0},{2,3},{3,2},{4,5},{5,4},{6,7},{7,6},{8,9},{9,8},{10,11... | collective-permute-start | bytes 9437192 | tf_op jit(solution)/shard_map/scaled_core/ppermute | solution.py:526
  280.0 111.3 %reduce-scatter.5.cloned.1.call-start = ((), (), s32[]{:S(2)}) async-start(), calls=%async_computation.5 | async-start | bytes 3932160 | tf_op jit(solution)/shard_map/gate_up_sum_z/reduce_scatter | solution.py:767
  280.0 20.7 %collective-permute-start.30 = (bf16[512,1536]{1,0:T(8,128)(2,1)}, bf16[512,1536]{1,0:T(8,128)(2,1)S(1)}, u32[]{:S(2)}, u32[]{:S(2)}) collective-permute-start(bf16[512,1536]{1,0:T(8,128)(2,1)} %get-tuple-element.140), channel_id=1, source_target_pairs={{0,2},{1,5},{2,0},{3,7},{4,6},{5,1},{6,4},{7,3},{8,10},{9,13},{10,... | collective-permute-start | bytes 4718600 | tf_op jit(solution)/shard_map/scaled_second/ppermute | solution.py:523
  302.1 12.3 %collective-permute-start.31 = (bf16[256,1536]{1,0:T(8,128)(2,1)}, bf16[256,1536]{1,0:T(8,128)(2,1)}, u32[]{:S(2)}, u32[]{:S(2)}) collective-permute-start(bf16[256,1536]{1,0:T(8,128)(2,1)} %add_convert_fusion.17), channel_id=1, source_target_pairs={{0,4},{1,3},{2,6},{3,1},{4,0},{5,7},{6,2},{7,5},{8,12},{9,11},{10,... | collective-permute-start | bytes 2359304 | tf_op jit(solution)/shard_map/scaled_first/ppermute | solution.py:520
  325.1 27.7 %collective-permute-start.33 = (bf16[512,1536]{1,0:T(8,128)(2,1)}, bf16[512,1536]{1,0:T(8,128)(2,1)}, u32[]{:S(2)}, u32[]{:S(2)}) collective-permute-start(bf16[512,1536]{1,0:T(8,128)(2,1)} %get-tuple-element.149), channel_id=1, source_target_pairs={{0,2},{1,5},{2,0},{3,7},{4,6},{5,1},{6,4},{7,3},{8,10},{9,13},{10,... | collective-permute-start | bytes 4718600 | tf_op jit(solution)/shard_map/result_second/ppermute | solution.py:523
  352.8 39.2 %collective-permute-start.34 = (bf16[2,768,256]{2,1,0:T(8,128)(2,1)}, bf16[2,768,256]{2,1,0:T(8,128)(2,1)}, u32[]{:S(2)}, u32[]{:S(2)}) collective-permute-start(bf16[2,768,256]{2,1,0:T(8,128)(2,1)} %copy-done.30), channel_id=1, source_target_pairs={{0,8},{8,16},{16,24},{24,0},{1,9},{9,17},{17,25},{25,1},{2,10},{10... | collective-permute-start | bytes 2359304 | tf_op jit(solution)/shard_map/kv_grad_z/ppermute | solution.py:517
  357.5 34.5 %collective-permute-start.35 = (bf16[2,4,48,1536]{3,2,1,0:T(8,128)(2,1)}, bf16[2,4,48,1536]{3,2,1,0:T(8,128)(2,1)}, u32[]{:S(2)}, u32[]{:S(2)}) collective-permute-start(bf16[2,4,48,1536]{3,2,1,0:T(8,128)(2,1)} %get-tuple-element.198), channel_id=1, source_target_pairs={{0,2},{1,5},{2,0},{3,7},{4,6},{5,1},{6,4},{7,3},{8,10},{9,13},{10,... | collective-permute-start | bytes 3538952 | tf_op jit(solution)/shard_map/out_second/ppermute | solution.py:523
  360.8 31.3 %collective-permute-start.36 = (bf16[256,1536]{1,0:T(8,128)(2,1)}, bf16[256,1536]{1,0:T(8,128)(2,1)S(1)}, u32[]{:S(2)}, u32[]{:S(2)}) collective-permute-start(bf16[256,1536]{1,0:T(8,128)(2,1)} %add_convert_fusion.15), channel_id=1, source_target_pairs={{0,4},{1,3},{2,6},{3,1},{4,0},{5,7},{6,2},{7,5},{8,12},{9,11},{10,... | collective-permute-start | bytes 2359304 | tf_op jit(solution)/shard_map/result_first/ppermute | solution.py:520
  393.7 11.5 %collective-permute-start.39 = (bf16[1,4,48,1536]{3,2,1,0:T(8,128)(2,1)S(1)}, bf16[1,4,48,1536]{3,2,1,0:T(8,128)(2,1)S(1)}, u32[]{:S(2)}, u32[]{:S(2)}) collective-permute-start(bf16[1,4,48,1536]{3,2,1,0:T(8,128)(2,1)S(1)} %add_convert_fusion.21), channel_id=1, source_target_pairs={{0,4},{1,3},{2,6},{3,1},{4,0},{5,7},{6,2},{7,5},{8,12},{9,11},{10,... | collective-permute-start | bytes 1769480 | tf_op jit(solution)/shard_map/out_first/ppermute | solution.py:520
  406.0 35.7 %collective-permute-start.40 = (bf16[2,4,48,3072]{3,2,1,0:T(8,128)(2,1)}, bf16[2,4,48,3072]{3,2,1,0:T(8,128)(2,1)}, u32[]{:S(2)}, u32[]{:S(2)}) collective-permute-start(bf16[2,4,48,3072]{3,2,1,0:T(8,128)(2,1)} %get-tuple-element.166), channel_id=1, source_target_pairs={{0,2},{1,5},{2,0},{3,7},{4,6},{5,1},{6,4},{7,3},{8,10},{9,13},{10,... | collective-permute-start | bytes 7077896 | tf_op jit(solution)/shard_map/projected_second/ppermute | solution.py:523
  410.0 31.8 %collective-permute-start.37 = (bf16[2,768,256]{2,1,0:T(8,128)(2,1)S(1)}, bf16[2,768,256]{2,1,0:T(8,128)(2,1)S(1)}, u32[]{:S(2)}, u32[]{:S(2)}) collective-permute-start(bf16[2,768,256]{2,1,0:T(8,128)(2,1)S(1)} %add_convert_fusion.13), channel_id=1, source_target_pairs={{0,8},{8,16},{16,24},{24,0},{1,9},{9,17},{17,25},{25,1},{2,10},{10... | collective-permute-start | bytes 2359304 | tf_op jit(solution)/shard_map/kv_grad_z/ppermute | solution.py:517
  413.0 22.5 %collective-permute-start.43 = (bf16[48,1536]{1,0:T(8,128)(2,1)S(1)}, bf16[48,1536]{1,0:T(8,128)(2,1)S(1)}, u32[]{:S(2)}, u32[]{:S(2)}) collective-permute-start(bf16[48,1536]{1,0:T(8,128)(2,1)S(1)} %get-tuple-element.216), channel_id=1, source_target_pairs={{0,8},{8,16},{16,24},{24,0},{1,9},{9,17},{17,25},{25,1},{2,10},{10... | collective-permute-start | bytes 442376 | tf_op jit(solution)/shard_map/out_z/ppermute | solution.py:517
  414.9 26.0 %collective-permute-start.42 = (bf16[48,1536]{1,0:T(8,128)(2,1)S(1)}, bf16[48,1536]{1,0:T(8,128)(2,1)S(1)}, u32[]{:S(2)}, u32[]{:S(2)}) collective-permute-start(bf16[48,1536]{1,0:T(8,128)(2,1)S(1)} %get-tuple-element.217), channel_id=1, source_target_pairs={{0,16},{8,24},{16,0},{24,8},{1,17},{9,25},{17,1},{25,9},{2,18},{10... | collective-permute-start | bytes 442376 | tf_op jit(solution)/shard_map/out_z/ppermute | solution.py:517
  415.8 25.2 %collective-permute-start.41 = (bf16[48,1536]{1,0:T(8,128)(2,1)S(1)}, bf16[48,1536]{1,0:T(8,128)(2,1)S(1)}, u32[]{:S(2)}, u32[]{:S(2)}) collective-permute-start(bf16[48,1536]{1,0:T(8,128)(2,1)S(1)} %get-tuple-element.215), channel_id=1, source_target_pairs={{0,24},{8,0},{16,8},{24,16},{1,25},{9,1},{17,9},{25,17},{2,26},{10... | collective-permute-start | bytes 442376 | tf_op jit(solution)/shard_map/out_z/ppermute | solution.py:517
  442.0 21.9 %collective-permute-start.44 = (bf16[2,768,256]{2,1,0:T(8,128)(2,1)S(1)}, bf16[2,768,256]{2,1,0:T(8,128)(2,1)S(1)}, u32[]{:S(2)}, u32[]{:S(2)}) collective-permute-start(bf16[2,768,256]{2,1,0:T(8,128)(2,1)S(1)} %add_convert_fusion.12), channel_id=1, source_target_pairs={{0,8},{8,16},{16,24},{24,0},{1,9},{9,17},{17,25},{25,1},{2,10},{10... | collective-permute-start | bytes 2359304 | tf_op jit(solution)/shard_map/kv_grad_z/ppermute | solution.py:517
  450.0 22.9 %collective-permute-start.45 = (bf16[1,4,48,3072]{3,2,1,0:T(8,128)(2,1)S(1)}, bf16[1,4,48,3072]{3,2,1,0:T(8,128)(2,1)S(1)}, u32[]{:S(2)}, u32[]{:S(2)}) collective-permute-start(bf16[1,4,48,3072]{3,2,1,0:T(8,128)(2,1)S(1)} %add_convert_fusion.8), channel_id=1, source_target_pairs={{0,4},{1,3},{2,6},{3,1},{4,0},{5,7},{6,2},{7,5},{8,12},{9,11},{10,... | collective-permute-start | bytes 3538952 | tf_op jit(solution)/shard_map/projected_first/ppermute | solution.py:520
  473.9 17.0 %all-to-all-start.1 = ((bf16[8,48,1024]{2,1,0:T(8,128)(2,1)}), bf16[8,48,1024]{2,1,0:T(8,128)(2,1)}, u32[]{:S(2)}, u32[]{:S(2)}) async-start(bf16[8,48,1024]{2,1,0:T(8,128)(2,1)} %bitcast.141), calls=%async_computation.3 | async-start | bytes 1572864 | tf_op jit(solution)/shard_map/gate_up_sum_f/all_to_all | solution.py:861
  481.6 17.9 %collective-permute-start.46 = (bf16[48,3072]{1,0:T(8,128)(2,1)}, bf16[48,3072]{1,0:T(8,128)(2,1)}, u32[]{:S(2)}, u32[]{:S(2)}) collective-permute-start(bf16[48,3072]{1,0:T(8,128)(2,1)} %get-tuple-element.203), channel_id=1, source_target_pairs={{0,24},{8,0},{16,8},{24,16},{1,25},{9,1},{17,9},{25,17},{2,26},{10... | collective-permute-start | bytes 884744 | tf_op jit(solution)/shard_map/projected_z/ppermute | solution.py:517
  483.3 27.8 %collective-permute-start.47 = (bf16[48,3072]{1,0:T(8,128)(2,1)}, bf16[48,3072]{1,0:T(8,128)(2,1)}, u32[]{:S(2)}, u32[]{:S(2)}) collective-permute-start(bf16[48,3072]{1,0:T(8,128)(2,1)} %get-tuple-element.202), channel_id=1, source_target_pairs={{0,16},{8,24},{16,0},{24,8},{1,17},{9,25},{17,1},{25,9},{2,18},{10... | collective-permute-start | bytes 884744 | tf_op jit(solution)/shard_map/projected_z/ppermute | solution.py:517
  484.6 26.5 %collective-permute-start.48 = (bf16[48,3072]{1,0:T(8,128)(2,1)}, bf16[48,3072]{1,0:T(8,128)(2,1)}, u32[]{:S(2)}, u32[]{:S(2)}) collective-permute-start(bf16[48,3072]{1,0:T(8,128)(2,1)} %get-tuple-element.201), channel_id=1, source_target_pairs={{0,8},{8,16},{16,24},{24,0},{1,9},{9,17},{17,25},{25,1},{2,10},{10... | collective-permute-start | bytes 884744 | tf_op jit(solution)/shard_map/projected_z/ppermute | solution.py:517
  (95 other events, 1017.8 us)
Sparse Core Ops, SparseCore 0:
  136.4 86.6 all-gather.2
  280.1 33.7 reduce-scatter.2
  316.2 75.0 reduce-scatter.4

commit v3 on v2

--- a/solution.py
+++ b/solution.py
@@ -84,6 +84,7 @@
 
 
 def backward_kernel(
+    place_ref,
     q_ref,
     k_ref,
     v_ref,
@@ -95,7 +96,7 @@
     token_ref,
     dq_ref,
     dkv_ref,
-    *ring_refs,
+    block_ref,
 ):
     count = q_ref.shape[1]
     keys, values = k_ref[...], v_ref[...]
@@ -118,10 +119,12 @@
     grad_values = grad_values.astype(BF)
     dkv_ref[0] = grad_keys
     dkv_ref[1] = grad_values
-    for block, ring_ref in enumerate(ring_refs):
+    blocks = block_ref.shape[0]
+    for block in range(blocks):
         at = slice(block * count, (block + 1) * count)
-        ring_ref[0] = grad_keys[:, at]
-        ring_ref[1] = grad_values[:, at]
+        place = lax.rem(place_ref[0] - block + blocks, blocks)
+        block_ref[place, 0] = grad_keys[:, at]
+        block_ref[place, 1] = grad_values[:, at]
 
 
 def attention_forward(queries, keys, values, bias):
@@ -145,13 +148,13 @@
             jax.ShapeDtypeStruct(queries.shape, BF),
             jax.ShapeDtypeStruct((KEY_VALUE_HEADS, RATIO, count), F32),
         ],
-        compiler_params=pltpu.CompilerParams(vmem_limit_bytes=VMEM_BYTES),
+        compiler_params=pltpu.CompilerParams(vmem_limit_bytes=MOST_VMEM_BYTES),
         cost_estimate=lasting(0.1),
         name="attention_forward",
     )(queries, keys, values, bias)
 
 
-def attention_backward(heads, queries, keys, values, grads, totals, cosine, sine, bias, token, blocks):
+def attention_backward(place, heads, queries, keys, values, grads, totals, cosine, sine, bias, token, blocks):
     count, span = queries.shape[1], keys.shape[1]
     pair = RATIO * HEAD_SIZE
     first, amount = heads.start, len(heads)
@@ -162,6 +165,7 @@
         backward_kernel,
         grid=(amount,),
         in_specs=[
+            pl.BlockSpec(memory_space=pltpu.SMEM),
             mine(pair, count),
             mine(HEAD_SIZE, span),
             mine(HEAD_SIZE, span),
@@ -175,17 +179,17 @@
         out_specs=[
             pl.BlockSpec((pair, count), lambda g: (g, 0)),
             pl.BlockSpec((2, HEAD_SIZE, span), lambda g: (0, g, 0)),
-        ]
-        + [pl.BlockSpec((2, HEAD_SIZE, count), lambda g: (0, g, 0))] * blocks,
+            pl.BlockSpec((blocks, 2, HEAD_SIZE, count), lambda g: (0, 0, g, 0)),
+        ],
         out_shape=[
             jax.ShapeDtypeStruct((amount * pair, count), BF),
             jax.ShapeDtypeStruct((2, rows, span), BF),
-        ]
-        + [jax.ShapeDtypeStruct((2, rows, count), BF)] * blocks,
+            jax.ShapeDtypeStruct((blocks, 2, rows, count), BF),
+        ],
         compiler_params=pltpu.CompilerParams(vmem_limit_bytes=VMEM_BYTES),
         cost_estimate=lasting(0.1),
         name="attention_backward",
-    )(queries, keys, values, grads, totals, cosine, sine, bias, token)
+    )(place, queries, keys, values, grads, totals, cosine, sine, bias, token)
 
 
 def product(left, right):
@@ -355,10 +359,10 @@
     if not first:
         earlier_ref, refs = refs[0], refs[1:]
     scaled_ref, hidden_ref, both_ref, sum_ref, down_ref = refs[:5]
-    total_ref, part_ref, grad_ref, block_ref, weight_ref, part_sem, grad_sem, block_sem = refs[5:]
+    total_ref, part_ref, grad_ref, weight_ref, part_sem, grad_sem, block_sem = refs[5:]
     step = pl.program_id(0)
     units = hidden_ref.shape[1]
-    (n, rows, _), width = block_ref.shape, down_ref.shape[1]
+    (n, rows, _), width = blocks_ref.shape, down_ref.shape[1]
     unit = units // n
     pieces = rows // unit
     piece = width // pieces
@@ -372,21 +376,29 @@
     @pl.when(step == 0)
     def _():
         block_copies = [
-            pltpu.make_async_copy(blocks_ref.at[k], block_ref.at[k], block_sem.at[k])
+            pltpu.make_async_copy(
+                blocks_ref.at[k, :, : 2 * units],
+                weight_ref.at[pl.ds(k * rows, rows)],
+                block_sem.at[k * (1 + pieces)],
+            )
             for k in range(n)
+        ]
+        block_copies += [
+            pltpu.make_async_copy(
+                blocks_ref.at[k, pl.ds(j * unit, unit), 2 * units :],
+                down_ref.at[pl.ds(k * unit, unit), j * piece : (j + 1) * piece],
+                block_sem.at[k * (1 + pieces) + 1 + j],
+            )
+            for k in range(n)
+            for j in range(pieces)
         ]
         for copy in block_copies:
             copy.start()
         for k in range(count):
             for copy in copies(k):
                 copy.start()
-        for k, copy in enumerate(block_copies):
+        for copy in block_copies:
             copy.wait()
-            weight_ref[k * rows : (k + 1) * rows, :] = block_ref[k, :, : 2 * units]
-            for j in range(pieces):
-                down_ref[k * unit : (k + 1) * unit, j * piece : (j + 1) * piece] = block_ref[
-                    k, j * unit : (j + 1) * unit, 2 * units :
-                ]
         total_ref[...] = jnp.zeros_like(total_ref) if first else earlier_ref[...]
 
     for k in range(count):
@@ -441,51 +453,187 @@
             pltpu.VMEM((units, width), F32),
             pltpu.VMEM((count, rows, width), BF),
             pltpu.VMEM((count, rows, width), BF),
-            pltpu.VMEM(blocks.shape, BF),
             pltpu.VMEM((n * blocks.shape[1], 2 * units), BF),
             pltpu.SemaphoreType.DMA((count,)),
             pltpu.SemaphoreType.DMA((count,)),
-            pltpu.SemaphoreType.DMA((n,)),
-        ],
-        compiler_params=pltpu.CompilerParams(vmem_limit_bytes=VMEM_BYTES),
+            pltpu.SemaphoreType.DMA((n * (1 + blocks.shape[1] * n // units),)),
+        ],
+        compiler_params=pltpu.CompilerParams(vmem_limit_bytes=MOST_VMEM_BYTES),
         cost_estimate=lasting(30),
         name="feed_forward",
     )(*parts, *grads, blocks, *(() if first else (earlier,)))
 
 
-def gate_up_kernel(count, *refs):
-    parts, boths, out_ref, token_ref = refs[:count], refs[count:-2], refs[-2], refs[-1]
+def add_kernel(a_ref, b_ref, out_ref):
+    out_ref[...] = (a_ref[0].astype(F32) + b_ref[0].astype(F32)).astype(BF)
+
+
+def add_half(a, b, which):
+    cols = a.shape[-1]
+    both = [x.reshape(2, -1, cols) for x in (a, b)]
+    rows = both[0].shape[1]
+    tile = rows // 2 if rows % 32 == 0 else rows
+    out = pl.pallas_call(
+        add_kernel,
+        grid=(rows // tile,),
+        in_specs=[pl.BlockSpec((1, tile, cols), lambda j: (which, j, 0))] * 2,
+        out_specs=pl.BlockSpec((tile, cols), lambda j: (j, 0)),
+        out_shape=jax.ShapeDtypeStruct((rows, cols), BF),
+        compiler_params=pltpu.CompilerParams(vmem_limit_bytes=VMEM_BYTES),
+        cost_estimate=lasting(0.1),
+        name="add_half",
+    )(*both)
+    return out.reshape((a.shape[0] // 2,) + a.shape[1:])
+
+
+def feed_terms_kernel(count, *refs):
+    parts, (down_ref, *boths, out_ref, token_ref) = refs[:count], refs[count:]
     token_ref[...] = jnp.zeros_like(token_ref)
-    rows = parts[0].shape[0]
+    rows, cols = parts[0].shape[0], boths[0].shape[1]
+    unit, width = down_ref.shape
+    pieces = out_ref.shape[0] // unit
+    piece = width // pieces
     each = boths[0].shape[0] // rows
-    total = jnp.zeros(out_ref.shape, F32)
+    total = jnp.zeros((out_ref.shape[0], cols), F32)
     for k, part in enumerate(parts):
         at = k % each * rows
         total += contract(part[...], boths[k // each][at : at + rows, :], 0, 0)
-    out_ref[...] = total.astype(BF)
-
-
-def gate_up_terms_of(parts, boths):
+    out_ref[:, :cols] = total.astype(BF)
+    for j in range(pieces):
+        out_ref[j * unit : (j + 1) * unit, cols:] = down_ref[:, j * piece : (j + 1) * piece]
+
+
+def feed_terms(parts, down, boths, n):
     rows, width = parts[0].shape
-    cols = boths[0].shape[1]
-    tile = 256
+    tile, cols = width // n, boths[0].shape[1]
+    unit = down.shape[0] // n
+    more = width * unit // tile
     return pl.pallas_call(
-        lambda *refs: gate_up_kernel(len(parts), *refs),
-        grid=(width // tile,),
+        lambda *refs: feed_terms_kernel(len(parts), *refs),
+        grid=(n,),
         in_specs=[pl.BlockSpec((rows, tile), lambda j: (0, j))] * len(parts)
+        + [pl.BlockSpec((unit, width), lambda j: (j, 0))]
         + [pl.BlockSpec(both.shape, lambda j: (0, 0)) for both in boths],
         out_specs=[
-            pl.BlockSpec((tile, cols), lambda j: (j, 0)),
+            pl.BlockSpec((tile, cols + more), lambda j: (j, 0)),
             pl.BlockSpec((8, 128), lambda j: (0, 0)),
         ],
         out_shape=[
-            jax.ShapeDtypeStruct((width, cols), BF),
+            jax.ShapeDtypeStruct((width, cols + more), BF),
             jax.ShapeDtypeStruct((8, 128), F32),
         ],
         compiler_params=pltpu.CompilerParams(vmem_limit_bytes=VMEM_BYTES),
         cost_estimate=lasting(15),
-        name="gate_up_terms",
-    )(*parts, *boths)
+        name="feed_terms",
+    )(*parts, down, *boths)
+
+
+def feed_finish_kernel(
+    arrived_ref, gate_ref, up_ref, gain_ref, gate_out, up_out, gain_out
+):
+    ranks, rows, cols = arrived_ref.shape
+    units = cols // 2
+    n = gate_ref.shape[1] // (ranks * 128)
+    unit = units // n
+    gain = gain_ref[...]
+    total = jnp.zeros((rows, unit), F32)
+    for r in range(ranks):
+        for z in range(n):
+            at = slice((z * ranks + r) * unit, (z * ranks + r + 1) * unit)
+            for half, weight_ref, out_ref in ((0, gate_ref, gate_out), (units, up_ref, up_out)):
+                start = half + z * unit
+                grad = arrived_ref[r, :, start : start + unit].astype(F32)
+                out_ref[:, at] = grad * gain
+                total += grad * weight_ref[:, at].astype(F32)
+    gain_out[...] = jnp.sum(total, axis=1, keepdims=True)
+
+
+def feed_finish(arrived, gate, up, gain):
+    return pl.pallas_call(
+        feed_finish_kernel,
+        out_shape=[
+            jax.ShapeDtypeStruct(gate.shape, F32),
+            jax.ShapeDtypeStruct(up.shape, F32),
+            jax.ShapeDtypeStruct(gain.shape, F32),
+        ],
+        compiler_params=pltpu.CompilerParams(vmem_limit_bytes=VMEM_BYTES),
+        cost_estimate=lasting(0.1),
+        name="feed_finish",
+    )(arrived, gate, up, gain)
+
+
+def attention_finish_kernel(n, *refs):
+    projected, outs, weights = refs[:n], refs[n : 2 * n], refs[2 * n : 2 * n + 3]
+    gain_ref, *grad_refs, out_ref, gain_out = refs[2 * n + 3 :]
+    gain = gain_ref[...]
+    out_ref[...] = sum(ref[...].astype(F32) for ref in outs)
+    first = 0
+    total = jnp.zeros(gain.shape, F32)
+    for weight_ref, grad_ref in zip(weights, grad_refs):
+        at = slice(first, first + weight_ref.shape[1])
+        first = at.stop
+        grad = sum(ref[:, at].astype(F32) for ref in projected)
+        grad_ref[...] = grad * gain
+        total += jnp.sum(grad * weight_ref[...].astype(F32), axis=1, keepdims=True)
+    gain_out[...] = total
+
+
+def attention_finish(projected, outs, weights, gain):
+    shapes = [weight.shape for weight in weights] + [outs[0].shape, gain.shape]
+    return pl.pallas_call(
+        lambda *refs: attention_finish_kernel(len(outs), *refs),
+        out_shape=[jax.ShapeDtypeStruct(shape, F32) for shape in shapes],
+        compiler_params=pltpu.CompilerParams(vmem_limit_bytes=VMEM_BYTES),
+        cost_estimate=lasting(0.1),
+        name="attention_finish",
+    )(*projected, *outs, *weights, gain)
+
+
+def input_kernel(query_ref, pair_ref, weight_ref, own_ref, resid_ref, out_ref, left_ref, total_ref):
+    step = pl.program_id(0)
+    queries, tile = query_ref.shape[0], weight_ref.shape[0]
+
+    @pl.when(step == 0)
+    def _():
+        left_ref[:, :queries] = query_ref[...].T
+        left_ref[:, queries:] = pair_ref[...].T
+
+    at = pl.multiple_of(step * tile, tile)
+    total_ref[:, pl.ds(at, tile)] = contract(
+        left_ref[...], weight_ref[:, : left_ref.shape[1]], 1, 1
+    )
+
+    @pl.when(step == pl.num_programs(0) - 1)
+    def _():
+        x, scaled = own_ref[...].astype(F32), total_ref[...]
+        inverse = lax.rsqrt(jnp.mean(x * x, axis=-1, keepdims=True) + EPSILON)
+        normed = x * inverse
+        mean = jnp.mean(scaled * normed, axis=-1, keepdims=True)
+        out_ref[...] = (resid_ref[...] + inverse * (scaled - normed * mean)).astype(BF)
+
+
+def input_gradient(queries, pairs, weight, own, resid):
+    count, width = own.shape
+    tile = 256
+    whole = lambda a: pl.BlockSpec(a.shape, lambda j: (0, 0))
+    features = queries.shape[0] + pairs.shape[0]
+    return pl.pallas_call(
+        input_kernel,
+        grid=(width // tile,),
+        in_specs=[
+            whole(queries),
+            whole(pairs),
+            pl.BlockSpec((tile, weight.shape[1]), lambda j: (j, 0)),
+            whole(own),
+            whole(resid),
+        ],
+        out_specs=pl.BlockSpec((count, width), lambda j: (0, 0)),
+        out_shape=jax.ShapeDtypeStruct((count, width), BF),
+        scratch_shapes=[pltpu.VMEM((count, features), BF), pltpu.VMEM((count, width), F32)],
+        compiler_params=pltpu.CompilerParams(vmem_limit_bytes=VMEM_BYTES),
+        cost_estimate=lasting(0.1),
+        name="input_gradient",
+    )(queries, pairs, weight, own, resid)
 
 
 def on_device(n, ranks, *operands):
@@ -505,7 +653,7 @@
         stretch_map,
     ) = operands
     at_z, rank = lax.axis_index("z"), lax.axis_index("f")
-    grid = ranks == 8
+    grid = ranks == 8 and w_down.shape[0] % 128 == 0
     turn = rank % 2
     first, second = 4 >> turn, 2 << turn
     scope = jax.named_scope
@@ -564,9 +712,7 @@
         return swap_core(terms) if grid else terms
 
     def add_halves(terms, arrived):
-        half = terms.shape[0] // 2
-        far = add(terms[half:], arrived[half:])
-        return add(terms[:half], arrived[:half]), far
+        return add_half(terms, arrived, 0), add_half(terms, arrived, 1)
 
     if grid:
         owners = [rank, rank ^ first, rank ^ second, rank ^ 6]
@@ -598,75 +744,6 @@
     def along(weight, grad):
         return jnp.sum(weight.astype(F32) * grad, axis=1)
 
-    def scaled(weight, gain):
-        return (weight.astype(F32) * gain).astype(BF)
-
-    shard = jnp.concatenate([w_query, key_weight, value_weight], axis=1)
-    shard = jnp.concatenate([scaled(shard, gain_one), w_out], axis=1)
-    own = tokens[0]
-    blocks = [own]
-    grad_own = grad_first = out_grad[0]
-    if grid:
-        with scope("attention_weights_z"):
-            behind = [shift(shard, by) for by in range(1, n)]
-        with scope("attention_weights_own"):
-            near = [shard, swap_first(shard), swap_second(shard)]
-    with scope("gate_up_f"):
-        gate_up = scaled(jnp.concatenate([w_gate, w_up], axis=1), gain_two)
-        gate_up = gate_up.reshape(shard_rows, 2, n, ranks, unit).transpose(3, 0, 1, 2, 4)
-        gate_up = gate_up.reshape(ranks, shard_rows, 2 * hidden_units)
-        gate_up = lax.all_to_all(gate_up, "f", 0, 0, tiled=True)
-        gate_up_rows = ranks * shard_rows
-        gate_up = gate_up.reshape(gate_up_rows, 2 * hidden_units)
-        pieces = gate_up_rows // unit
-        down = w_down.reshape(unit, pieces, width // pieces).transpose(1, 0, 2)
-        gate_up_down = jnp.concatenate(
-            [gate_up, down.reshape(gate_up_rows, width // pieces)], axis=1
-        )
-
-    if grid:
-        with scope("attention_weights_own"):
-            near.append(swap_second(near[1]))
-        *behind, near[2], near[3], gate_up_down = stage(*behind, near[2], near[3], gate_up_down)
-        with scope("attention_weights_core"):
-            near_core = [swap_core(part) for part in near]
-        rest = [jnp.stack(behind)]
-        with scope("attention_weights_first"):
-            rest.append(swap_first(rest[0]))
-        with scope("tokens_z"):
-            blocks.append(shift(own, 1))
-        rest[0], rest[1], blocks[1], *near_core = stage(rest[0], rest[1], blocks[1], *near_core)
-        with scope("attention_weights_core"):
-            rest_core = [swap_core(rest[0])]
-        with scope("attention_weights_second"):
-            rest.append(swap_second(rest[0]))
-        with scope("tokens_z"):
-            blocks.append(shift(blocks[1], 1))
-        rest[1], rest[2], blocks[2], rest_core[0] = stage(
-            rest[1], rest[2], blocks[2], rest_core[0]
-        )
-        with scope("attention_weights_core"):
-            rest_core += [swap_core(rest[1]), swap_core(rest[2])]
-        with scope("attention_weights_second"):
-            rest.append(swap_second(rest[1]))
-        with scope("out_grad_first"):
-            grad_first = swap_first(grad_own)
-        with scope("tokens_z"):
-            while len(blocks) < n:
-                blocks.append(shift(blocks[-1], 1))
-        rest[3], blocks[-1], grad_first, *rest_core = stage(
-            rest[3], blocks[-1], grad_first, *rest_core
-        )
-        with scope("attention_weights_core"):
-            rest_core.append(swap_core(rest[3]))
-    else:
-        while len(blocks) < n:
-            blocks.append(shift(blocks[-1], 1))
-    with scope("gate_up_down_z"):
-        gate_up_down, blocks[-1] = stage(gate_up_down, blocks[-1])
-        gate_up_down = lax.all_gather(gate_up_down, "z")
-    cuts = [width, width + pair_cols, width + 2 * pair_cols]
-
     slots_each = stretch_map.shape[1] // n
     slots = (
         ((at_z - jnp.arange(n, dtype=jnp.int32)) % n)[:, None] * slots_each
@@ -679,9 +756,81 @@
     bias = jnp.where(allowed, 0.0, -1e30).astype(F32)
     cosine, sine = rotary_tables(place_all)
 
+    def scaled(weight, gain):
+        return (weight.astype(F32) * gain).astype(BF)
+
+    shard = jnp.concatenate([w_query, key_weight, value_weight], axis=1)
+    shard = jnp.concatenate([scaled(shard, gain_one), w_out], axis=1)
+    own = tokens[0]
+    blocks = [own]
+    gate_up = scaled(jnp.concatenate([w_gate, w_up], axis=1), gain_two)
+    gate_up = gate_up.reshape(shard_rows, 2, n, ranks, unit).transpose(3, 0, 1, 2, 4)
+    gate_up = gate_up.reshape(ranks, shard_rows, 2 * hidden_units)
+    grad_own = grad_first = out_grad[0]
+    if grid:
+        with scope("attention_weights_z"):
+            behind = [shift(shard, 1)]
+            while len(behind) < n - 1:
+                behind.append(shift(behind[-1], 1))
+        with scope("attention_weights_own"):
+            near = [shard, swap_first(shard), swap_second(shard)]
+    if grid:
+        with scope("attention_weights_own"):
+            near.append(swap_second(near[1]))
+        with scope("tokens_z"):
+            blocks.append(shift(own, 1))
+        with scope("out_grad_first"):
+            grad_first = swap_first(grad_own)
+        *behind, near[2], near[3], gate_up, blocks[1], grad_first = stage(
+            *behind, near[2], near[3], gate_up, blocks[1], grad_first
+        )
+        with scope("attention_weights_core"):
+            near_core = [swap_core(part) for part in near]
+        rest = [jnp.stack(behind)]
+        with scope("gate_up_f"):
+            gate_up = lax.all_to_all(gate_up, "f", 0, 0, tiled=True)
+            gate_up_rows = ranks * shard_rows
+            gate_up = gate_up.reshape(gate_up_rows, 2 * hidden_units)
+            pieces = gate_up_rows // unit
+            down = w_down.reshape(unit, pieces, width // pieces).transpose(1, 0, 2)
+            gate_up_down = jnp.concatenate(
+                [gate_up, down.reshape(gate_up_rows, width // pieces)], axis=1
+            )
+        with scope("attention_weights_first"):
+            rest.append(swap_first(rest[0]))
+        with scope("tokens_z"):
+            blocks.append(shift(blocks[1], 1))
+        rest[0], rest[1], blocks[2], cosine, sine, bias, gate_up_down, *near_core = stage(
+            rest[0], rest[1], blocks[2], cosine, sine, bias, gate_up_down, *near_core
+        )
+        with scope("attention_weights_core"):
+            rest_core = [swap_core(rest[0]), swap_core(rest[1])]
+        with scope("attention_weights_second"):
+            rest += [swap_second(rest[0]), swap_second(rest[1])]
+        with scope("tokens_z"):
+            while len(blocks) < n:
+                blocks.append(shift(blocks[-1], 1))
+        rest[2], rest[3], blocks[-1], *rest_core = stage(rest[2], rest[3], blocks[-1], *rest_core)
+        with scope("attention_weights_core"):
+            rest_core += [swap_core(rest[2]), swap_core(rest[3])]
+    else:
+        with scope("gate_up_f"):
+            gate_up = lax.all_to_all(gate_up, "f", 0, 0, tiled=True)
+            gate_up_rows = ranks * shard_rows
+            gate_up = gate_up.reshape(gate_up_rows, 2 * hidden_units)
+            pieces = gate_up_rows // unit
+            down = w_down.reshape(unit, pieces, width // pieces).transpose(1, 0, 2)
+            gate_up_down = jnp.concatenate(
+                [gate_up, down.reshape(gate_up_rows, width // pieces)], axis=1
+            )
+        while len(blocks) < n:
+            blocks.append(shift(blocks[-1], 1))
+    with scope("gate_up_down_z"):
+        gate_up_down, blocks[-1] = stage(gate_up_down, blocks[-1])
+        gate_up_down = lax.all_gather(gate_up_down, "z")
+    cuts = [width, width + pair_cols, width + 2 * pair_cols]
+
     inputs = own.astype(F32)
-    first_inverse = lax.rsqrt(jnp.mean(inputs * inputs, axis=-1, keepdims=True) + EPSILON)
-    first_normed = inputs * first_inverse
     if grid:
         parts, starts = [], []
         for near_parts, rest_parts, moves in (
@@ -745,9 +894,6 @@
     scaled_near, hidden_near, both_near, down_terms, _ = feed_forward(
         normed_parts[:half], grad_parts[:half], gate_up_down, hidden_units, down_terms
     )
-    with scope("down_sum_z"):
-        down_owned = lax.psum_scatter(down_terms, "z", scatter_dimension=0, tiled=True)
-
     def norm_back(scaled_grad, normed, inverse):
         return inverse * (
             scaled_grad - normed * jnp.mean(scaled_grad * normed, axis=-1, keepdims=True)
@@ -762,27 +908,27 @@
             scaled_two = jnp.concatenate([scaled_near, scaled_far], axis=0)
             scaled_two = lax.psum_scatter(scaled_two, "f", scatter_dimension=0, tiled=True)
             scaled_two = far = scaled_two.astype(F32)
-    with scope("gate_up_sum_z"):
-        gate_up_terms, token = gate_up_terms_of(normed_parts, [both_near, both_far])
-        gate_up_owned = lax.psum_scatter(gate_up_terms, "z", scatter_dimension=0, tiled=True)
-    with scope("result_core"):
-        hidden_far, token = stage(hidden_far, token)
-        result_far = send_core(product(hidden_far, down_weight).astype(BF))
-        result_near = product(hidden_near, down_weight).astype(BF)
+    with scope("feed_sum_z"):
         if grid:
-            result_near, result_far = add_halves(result_near, result_far)
+            terms, token = feed_terms(normed_parts, down_terms, [both_near, both_far], n)
         else:
-            result = jnp.concatenate([result_near, result_far], axis=0)
-            result = lax.psum_scatter(result, "f", scatter_dimension=0, tiled=True)
-            result_near = result_far = result
-    far, result_far = stage(far, result_far)
+            terms = over_rows(
+                jnp.concatenate(normed_parts, axis=0),
+                jnp.concatenate([both_near, both_far], axis=0),
+            ).astype(BF)
+            down_terms = down_terms.reshape(n, unit, pieces, width // pieces)
+            down_terms = down_terms.transpose(0, 2, 1, 3).reshape(width, width // pieces)
+            terms = jnp.concatenate([terms, down_terms], axis=1)
+            token = jnp.zeros((8, 128), F32)
+        feed_owned = lax.psum_scatter(terms, "z", scatter_dimension=0, tiled=True)
+    far, token = stage(far, token)
     if grid:
         with scope("scaled_first"):
             scaled_near, far = add_halves(scaled_near, far)
-            far, result_far = stage(swap_first(far), result_far)
-            scaled_two = scaled_near.astype(F32) + far.astype(F32)
-        with scope("result_second"):
-            result_far = swap_second(result_far)
+            far = swap_first(far)
+    if grid:
+        (far,) = stage(far)
+        scaled_two = scaled_near.astype(F32) + far.astype(F32)
     grad_resid = out_grad[0].astype(F32) + norm_back(scaled_two, second_normed, second_inverse)
     grad_attn_out = grad_resid.astype(BF)
 
@@ -797,7 +943,8 @@
             out_far = swap_second(out_far)
         else:
             out_near = out_far = sum_f(out_mine)
-    grad_queries, grad_kv, *by_block = attention_backward(
+    grad_queries, grad_kv, by_block = attention_backward(
+        at_z.astype(jnp.int32)[None],
         range(KEY_VALUE_HEADS),
         queries,
         keys,
@@ -810,94 +957,102 @@
         token,
         n,
     )
-    grad_queries, result_far, down_owned = stage(grad_queries, result_far, down_owned)
-
-    def pass_on(total):
-        with scope("kv_grad_z"):
-            return shift(total, 1)
-
-    arrived = pass_on(by_block[1])
-    if grid:
-        with scope("result_first"):
-            result_near, result_far = add_halves(result_near, result_far)
-            result_far = swap_first(result_far)
+    grad_queries, out_far = stage(grad_queries, out_far)
+
+    with scope("kv_grad_z"):
+        kv_total = lax.psum_scatter(by_block, "z", scatter_dimension=0, tiled=False)
     with scope("projected_core"):
         away, mine = weight_terms(
             normed_group, [grad_queries, grad_kv.reshape(2 * pair_cols, span)], True
         )
-    away, arrived, out_far, result_far, gate_up_owned = stage(
-        away, arrived, out_far, result_far, gate_up_owned
-    )
-    with scope("projected_core"):
-        away = send_core(away)
-    arrived = pass_on(add(arrived, by_block[2 % n]))
     if grid:
-        result = result_near.astype(F32) + result_far.astype(F32)
         with scope("out_first"):
             out_near, out_far = add_halves(out_near, out_far)
             out_far = swap_first(out_far)
+        away, out_far = stage(away, out_far)
+        with scope("projected_core"):
+            away = send_core(away)
+        away, hidden_far, hidden_near = stage(away, hidden_far, hidden_near)
         with scope("projected_second"):
             near, far = add_halves(mine, away)
-            far, out_far = stage(far, out_far)
             far = swap_second(far)
         out_near = add(out_near[0], out_far[0])
-    else:
-        result = result.astype(F32)
-        near = far = sum_f(mine)
-    result = (resid + result).astype(BF)
-    with scope("out_z"):
-        out_owned = total(send_z(out_near))
-    arrived, far, out_owned = stage(arrived, far, out_owned)
-    for step in range(3, n):
-        arrived = pass_on(add(arrived, by_block[step]))
+    with scope("result_core"):
+        result_far = send_core(product(hidden_far, down_weight).astype(BF))
+        result_near = product(hidden_near, down_weight).astype(BF)
+    def exchange(owned):
+        with scope("gate_up_sum_f"):
+            owned = owned[:, : 2 * hidden_units].reshape(ranks, shard_rows, -1)
+            return lax.all_to_all(owned, "f", 0, 0, tiled=True)
+
     if grid:
+        result_near, result_far = add_halves(result_near, result_far)
+        far, result_far = stage(far, result_far)
         with scope("projected_first"):
             near, far = add_halves(near, far)
             far = swap_first(far)
-    far, gate_up_owned = stage(far, gate_up_owned)
+        with scope("out_z"):
+            out_owned = send_z(out_near)
+        with scope("result_f"):
+            own_part, first_part = jnp.split(result_near, 2)
+            second_part, both_part = jnp.split(result_far, 2)
+            both_part = lax.ppermute(both_part, "f", [(i, i ^ 6) for i in range(ranks)])
+            first_part, second_part = swap_first(first_part), swap_second(second_part)
+        gate_up_owned = exchange(feed_owned)
+        far, kv_total, gate_up_owned, first_part, second_part, both_part, *out_owned = stage(
+            far, kv_total, gate_up_owned, first_part, second_part, both_part, *out_owned
+        )
+        result = own_part.astype(F32) + first_part.astype(F32)
+        result = result + second_part.astype(F32) + both_part.astype(F32)
+        near = add(near[0], far[0])
+    else:
+        near = sum_f(mine)
+        gate_up_owned = exchange(feed_owned)
+        result = jnp.concatenate([result_near, result_far], axis=0)
+        result = lax.psum_scatter(result, "f", scatter_dimension=0, tiled=True)
+        with scope("out_z"):
+            out_owned = send_z(out_near)
     with scope("projected_z"):
-        projected = send_z(add(near[0], far[0]) if grid else near)
-    with scope("gate_up_sum_f"):
-        gate_up_owned = lax.all_to_all(
-            gate_up_owned.reshape(ranks, shard_rows, 2 * hidden_units), "f", 0, 0, tiled=True
+        projected = send_z(near)
+    result = (resid + result.astype(F32)).astype(BF)
+
+    down_owned = feed_owned[:, 2 * hidden_units :].reshape(pieces, unit, width // pieces)
+    down_owned = down_owned.transpose(1, 0, 2).reshape(unit, width).astype(F32)
+    input_grad = input_gradient(
+        grad_queries, kv_total.reshape(2 * pair_cols, token_count), gathered, own, grad_resid
+    )
+    if grid:
+        gate_owned, up_owned, gain_two_owned = feed_finish(gate_up_owned, w_gate, w_up, gain_two)
+        input_grad, gain_two_owned, *projected = stage(input_grad, gain_two_owned, *projected)
+        query_owned, key_owned, value_owned, out_owned, gain_one_owned = attention_finish(
+            projected, out_owned, [w_query, key_weight, value_weight], gain_one
         )
-    kv_total = add(arrived, by_block[0])
-    scaled_one = (
-        contract(grad_queries, q_weight, 0, 1)
-        + contract(kv_total[0], key_matrix, 0, 1)
-        + contract(kv_total[1], value_matrix, 0, 1)
-    )
-
-    gate_up_owned = (
-        gate_up_owned.astype(F32)
-        .reshape(ranks, shard_rows, 2, n, unit)
-        .transpose(2, 1, 3, 0, 4)
-        .reshape(2, shard_rows, n * ranks * unit)
-    )
-    gate_owned, up_owned = gate_up_owned[0], gate_up_owned[1]
-    gain_two_owned = along(w_gate, gate_owned) + along(w_up, up_owned)
-    scaled_one, gain_two_owned, *projected = stage(scaled_one, gain_two_owned, *projected)
-    input_grad = (grad_resid + norm_back(scaled_one, first_normed, first_inverse)).astype(BF)
-    projected_owned = total(projected)
-    query_owned, key_owned, value_owned = jnp.split(projected_owned, cuts[:2], axis=1)
-
-    gain_one_owned = (
-        along(w_query, query_owned)
-        + along(key_weight, key_owned)
-        + along(value_weight, value_owned)
-    )
+    else:
+        gate_up_owned = (
+            gate_up_owned.astype(F32)
+            .reshape(ranks, shard_rows, 2, n, unit)
+            .transpose(2, 1, 3, 0, 4)
+            .reshape(2, shard_rows, n * ranks * unit)
+        )
+        gate_owned, up_owned = gate_up_owned[0], gate_up_owned[1]
+        gain_two_owned = along(w_gate, gate_owned) + along(w_up, up_owned)
+        gate_owned, up_owned = gate_owned * gain_two, up_owned * gain_two
+        out_owned, grads = total(out_owned), jnp.split(total(projected), cuts[:2], axis=1)
+        weights = (w_query, key_weight, value_weight)
+        gain_one_owned = sum(along(weight, grad) for weight, grad in zip(weights, grads))
+        query_owned, key_owned, value_owned = (grad * gain_one for grad in grads)
     return (
         result[None],
         input_grad[None],
-        gain_one_owned,
-        query_owned * gain_one,
-        key_owned * gain_one,
-        value_owned * gain_one,
+        gain_one_owned.reshape(-1),
+        query_owned,
+        key_owned,
+        value_owned,
         out_owned,
-        gain_two_owned,
-        gate_owned * gain_two,
-        up_owned * gain_two,
-        down_owned.astype(F32),
+        gain_two_owned.reshape(-1),
+        gate_owned,
+        up_owned,
+        down_owned,
     )
 
 

time: 531 us -> 490 us (0.923)
  Pallas kernels: 107 us -> 144 us
  other arithmetic: 60 us -> 24 us
  starting transfers between devices: 66.1 us -> 44.1 us
  matrix products: 22.9 us -> 15 us
  waiting for transfers between devices: 212 us -> 206 us
  local copies, waits for them, and re-layouts: 40.4 us -> 34.9 us
    pallas_call x2 -> x19, Pallas kernels: 25.6 us -> 57 us  [the longest x1 17.6 us: attention_backward(): pl.pallas_call(backward_kernel, grid=(amount,), in_specs=[pl.BlockSpec(me...]
    convert_element_type x13 -> x2, other arithmetic: 31.9 us -> 1.92 us  [add(): return (a.astype(F32) + b.astype(F32)).astype(BF)]
    ppermute x8, waiting for transfers between devices: 49.7 us -> 23.3 us  [swap_first(): return lax.ppermute(a, 'f', [(i, i ^ 4 >> i % 2) for i in range(ranks)])]
    ppermute x15 -> x12, starting transfers between devices: 30 us -> 8.24 us  [shift(): return lax.ppermute(a, 'z', [(i, (i + by) % n) for i in range(n)])]
    all_to_all x1, waiting for transfers between devices: 0.01 us -> 15.9 us  [on_device(): gate_up = lax.all_to_all(gate_up, 'f', 0, 0, tiled=True)]
    ppermute x10, waiting for transfers between devices: 30.6 us -> 44 us  [swap_second(): return lax.ppermute(a, 'f', [(i, i ^ 2 << i % 2) for i in range(ranks)])]
    reduce_scatter x2, waiting for transfers between devices: 14.7 us -> 3.02 us  [the longest x1 3.02 us: on_device(): feed_owned = lax.psum_scatter(terms, 'z', scatter_dimension=0, tiled=True)]
    dot_general x5 -> x2, matrix products: 16.4 us -> 7.94 us  [contract(): lax.dot_general(left, right, (((at_left,), (at_right,)), ((), ())), prefe...]
  transfers between devices with their start and end apart: 54 -> 52, of which waited for: 21 -> 22; matrix products, arithmetic and copies ran while one was open for 14% -> 9% of each run, Pallas kernels for 16% -> 25%
where the time goes in v3:
time: 490 us; the launch traced here: 483 us
  waiting for transfers between devices  206 us (42%)
  Pallas kernels  144 us (29%)
  starting transfers between devices  44.1 us (9%)
  local copies, waits for them, and re-layouts  34.9 us (7%)
  other arithmetic  24 us (5%)
  between operations  15.3 us (3%)
  matrix products  15 us (3%)
    ppermute x12, waiting for transfers between devices, shift(): return lax.ppermute(a, 'z', [(i, (i + by) % n) for i in range(n)])  103 us
    ppermute x10, waiting for transfers between devices, swap_second(): return lax.ppermute(a, 'f', [(i, i ^ 2 << i % 2) for i in range(ranks)])  44 us
    pallas_call x2, Pallas kernels, feed_forward(): pl.pallas_call(lambda *refs: feed_kernel(count, first, *refs), grid=(coun...  37 us
    unnamed x154, local copies, waits for them, and re-layouts  26 us
    ppermute x8, waiting for transfers between devices, swap_first(): return lax.ppermute(a, 'f', [(i, i ^ 4 >> i % 2) for i in range(ranks)])  23.3 us
    pallas_call x1, Pallas kernels, project(): pl.pallas_call(lambda *refs: project_kernel(n, len(parts), *refs), in_spe...  19.6 us
    pallas_call x1, Pallas kernels, attention_backward(): pl.pallas_call(backward_kernel, grid=(amount,), in_specs=[pl.BlockSpec(me...  17.6 us
    all_to_all x1, waiting for transfers between devices, on_device(): gate_up = lax.all_to_all(gate_up, 'f', 0, 0, tiled=True)  15.9 us
  transfers between devices with their start and end apart: 52, of which 22 were waited for; matrix products, arithmetic and copies ran while one was open for 9% of the time, Pallas kernels for 25%

profile of v3, /device:TPU:0, one launch (start us, length us, event | category | flops | bytes accessed | tf_op | source)
XLA Modules:
  0.0 483.2 jit_solution(238917966736267688)
XLA Ops:
  9.1 1.9 pad_maximum_fusion.4
  11.0 3.0 collective-permute-start
  19.6 7.7 %collective-permute-done = bf16[48,4608]{1,0:T(8,128)(2,1)} collective-permute-done((bf16[48,4608]{1,0:T(8,128)(2,1)}, bf16[48,4608]{1,0:T(8,128)(2,1)}, u32[]{:S(2)}, u32[]{:S(2)}) %collective-permute-start) | collective-permute-done | bytes 442400 | tf_op jit(solution)/shard_map/attention_weights_z/ppermute | solution.py:665
  29.7 23.2 %collective-permute-done.1 = bf16[48,4608]{1,0:T(8,128)(2,1)} collective-permute-done((bf16[48,4608]{1,0:T(8,128)(2,1)}, bf16[48,4608]{1,0:T(8,128)(2,1)}, u32[]{:S(2)}, u32[]{:S(2)}) %collective-permute-start.1) | collective-permute-done | bytes 442400 | tf_op jit(solution)/shard_map/attention_weights_z/ppermute | solution.py:665
  55.0 11.4 %collective-permute-done.2 = bf16[48,4608]{1,0:T(8,128)(2,1)} collective-permute-done((bf16[48,4608]{1,0:T(8,128)(2,1)}, bf16[48,4608]{1,0:T(8,128)(2,1)}, u32[]{:S(2)}, u32[]{:S(2)}) %collective-permute-start.2) | collective-permute-done | bytes 442400 | tf_op jit(solution)/shard_map/attention_weights_z/ppermute | solution.py:665
  69.3 3.6 all-to-all-start
  78.1 15.9 %all-to-all-done = bf16[8,48,1024]{2,1,0:T(8,128)(2,1)S(1)} async-done(((bf16[8,48,1024]{2,1,0:T(8,128)(2,1)}), bf16[8,48,1024]{2,1,0:T(8,128)(2,1)S(1)}, u32[]{:S(2)}, u32[]{:S(2)}) %all-to-all-start) | async-done | bytes 786464 | tf_op jit(solution)/shard_map/gate_up_f/all_to_all | solution.py:791
  97.8 21.5 %collective-permute-done.16.refs_20_ = bf16[256,1536]{1,0:T(8,128)(2,1)S(1)} collective-permute-done((bf16[256,1536]{1,0:T(8,128)(2,1)}, bf16[256,1536]{1,0:T(8,128)(2,1)S(1)}, u32[]{:S(2)}, u32[]{:S(2)}) %collective-permute-start.16) | collective-permute-done | bytes 786464 | tf_op jit(solution)/shard_map/tokens_z/ppermute | solution.py:665
  119.2 8.0 %collective-permute-done.15.refs_8_ = bf16[3,48,4608]{2,1,0:T(8,128)(2,1)S(1)} collective-permute-done((bf16[3,48,4608]{2,1,0:T(8,128)(2,1)}, bf16[3,48,4608]{2,1,0:T(8,128)(2,1)S(1)}, u32[]{:S(2)}, u32[]{:S(2)}) %collective-permute-start.15) | collective-permute-done | bytes 1327136 | tf_op jit(solution)/shard_map/attention_weights_second/ppermute | solution.py:671
  130.1 2.4 pad_maximum_fusion.refs_2_
  135.6 19.6 %project.1 = (bf16[1536,256]{1,0:T(8,128)(2,1)}, bf16[768,1024]{1,0:T(8,128)(2,1)}, bf16[768,1024]{1,0:T(8,128)(2,1)}, bf16[1536,1024]{1,0:T(8,128)(2,1)}, bf16[1536,4608]{1,0:T(8,128)(2,1)}) custom-call(s32[32]{0:T(128)} %broadcast_multiply_fusion.2.refs_0_, bf16[1,48,4608]{2,1,0:T(8,128)(2,1)} %get-tuple-element.245.refs_1_, ...), custom_call_target="tpu_custom_call" | custom-call | flops 100000000 | bytes 300000 | tf_op jit(solution)/shard_map/project/pallas_call | solution.py:332
  155.2 14.5 %attention_forward.1 = (bf16[1536,256]{1,0:T(8,128)(2,1)}, f32[8,2,256]{2,1,0:T(2,128)}) custom-call(bf16[1536,256]{1,0:T(8,128)(2,1)} %get-tuple-element.126.q_ref, bf16[768,1024]{1,0:T(8,128)(2,1)} %get-tuple-element.127.k_ref, bf16[768,1024]{1,0:T(8,128)(2,1)} %get-tuple-element.128.v_ref, f32[1024,256]{1,0:T(8,128)} %and_select_fusion.bias_ref), custom_call_target="tpu_custom_call" | custom-call | flops 100000000 | bytes 300000 | tf_op jit(solution)/shard_map/attention_forward/pallas_call | solution.py:134
  169.7 4.1 multiply_reduce_fusion.1
  175.5 10.4 %collective-permute-done.22 = bf16[256,1536]{1,0:T(8,128)(2,1)S(1)} collective-permute-done((bf16[256,1536]{1,0:T(8,128)(2,1)S(1)}, bf16[256,1536]{1,0:T(8,128)(2,1)S(1)}, u32[]{:S(2)}, u32[]{:S(2)}) %collective-permute-start.22) | collective-permute-done | bytes 786464 | tf_op jit(solution)/shard_map/normed_first/ppermute | solution.py:668
  187.7 18.9 %collective-permute-done.23.refs_1_ = bf16[512,1536]{1,0:T(8,128)(2,1)S(1)} collective-permute-done((bf16[512,1536]{1,0:T(8,128)(2,1)S(1)}, bf16[512,1536]{1,0:T(8,128)(2,1)S(1)}, u32[]{:S(2)}, u32[]{:S(2)}) %collective-permute-start.23) | collective-permute-done | bytes 1572896 | tf_op jit(solution)/shard_map/normed_second/ppermute | solution.py:671
  210.0 7.1 %all-gather.3.cloned.1.call-done = bf16[1536,1536]{1,0:T(8,128)(2,1)} async-done(((bf16[384,1536]{1,0:T(8,128)(2,1)}), bf16[1536,1536]{1,0:T(8,128)(2,1)}) %all-gather.3.cloned.1.call-update) | async-done | bytes 4718608 | tf_op jit(solution)/shard_map/gate_up_down_z/all_gather | solution.py:830
  217.1 17.7 %feed_forward.2 = (bf16[1024,1536]{1,0:T(8,128)(2,1)}, bf16[1024,512]{1,0:T(8,128)(2,1)}, bf16[1024,1024]{1,0:T(8,128)(2,1)}, f32[512,1536]{1,0:T(8,128)}, bf16[512,1536]{1,0:T(8,128)(2,1)}) custom-call(bf16[512,1536]{1,0:T(8,128)(2,1)} %copy-done.43, bf16[512,1536]{1,0:T(8,128)(2,1)} %copy-done.45, bf16[512,1536]{1,0:T(8,128)(2,1)} %copy-done.67, ...), custom_call_target="tpu_custom_call" | custom-call | flops 30000001024 | bytes 90000000 | tf_op jit(solution)/shard_map/feed_forward/pallas_call | solution.py:440
  234.9 19.3 %feed_forward.3 = (bf16[1024,1536]{1,0:T(8,128)(2,1)}, bf16[1024,512]{1,0:T(8,128)(2,1)}, bf16[1024,1024]{1,0:T(8,128)(2,1)}, bf16[512,1536]{1,0:T(8,128)(2,1)}, bf16[512,1536]{1,0:T(8,128)(2,1)}) custom-call(bf16[512,1536]{1,0:T(8,128)(2,1)} %copy-done.22, bf16[512,1536]{1,0:T(8,128)(2,1)} %copy-done.41, bf16[512,1536]{1,0:T(8,128)(2,1)} %pad_maximum_fusion.refs_2_, ...), custom_call_target="tpu_custom_call" | custom-call | flops 30000001024 | bytes 90000000 | tf_op jit(solution)/shard_map/feed_forward/pallas_call | solution.py:440
  254.2 3.0 copy-done.3
  266.0 9.1 %feed_terms.1 = (bf16[1536,1536]{1,0:T(8,128)(2,1)}, f32[8,128]{1,0:T(8,128)S(1)}) custom-call(bf16[512,1536]{1,0:T(8,128)(2,1)S(1)} %copy-done.23, bf16[512,1536]{1,0:T(8,128)(2,1)S(1)} %copy-done.42, bf16[512,1536]{1,0:T(8,128)(2,1)S(1)} %copy-done.44, bf16[512,1536]{1,0:T(8,128)(2,1)S(1)} %copy-done.46, bf16[512,1536]{1,0:T(8,128)(2,1)S(1)} %copy-done.49, ...), custom_call_target="tpu_custom_call" | custom-call | flops 15000000512 | bytes 45000000 | tf_op jit(solution)/shard_map/feed_sum_z/feed_terms/pallas_call | solution.py:511
  275.1 3.0 collective-permute-done.29
  281.3 10.1 %collective-permute-done.30 = bf16[256,1536]{1,0:T(8,128)(2,1)} collective-permute-done((bf16[256,1536]{1,0:T(8,128)(2,1)}, bf16[256,1536]{1,0:T(8,128)(2,1)}, u32[]{:S(2)}, u32[]{:S(2)}) %collective-permute-start.30) | collective-permute-done | bytes 786464 | tf_op jit(solution)/shard_map/scaled_first/ppermute | solution.py:668
  293.0 2.9 fusion.20
  295.9 3.6 owned_terms.2
  299.5 3.9 fusion.7.grad_ref
  306.9 17.6 %attention_backward.1 = (bf16[1536,256]{1,0:T(8,128)(2,1)S(1)}, bf16[2,768,1024]{2,1,0:T(8,128)(2,1)S(1)}, bf16[4,2,768,256]{3,2,1,0:T(8,128)(2,1)S(1)}) custom-call(s32[1]{0:T(128)} %bitcast.63.place_ref, bf16[1536,256]{1,0:T(8,128)(2,1)S(1)} %copy-done.19, bf16[768,1024]{1,0:T(8,128)(2,1)S(1)} %copy-done.6, bf16[768,1024]{1,0:T(8,128)(2,1)S(1)} %copy-done.7, ...), custom_call_target="tpu_custom_call" | custom-call | flops 100000000 | bytes 300000 | tf_op jit(solution)/shard_map/attention_backward/pallas_call | solution.py:164
  327.9 1.9 copy-done.17
  329.9 12.3 %owned_terms.3 = (bf16[4,4,48,3072]{3,2,1,0:T(8,128)(2,1)}, bf16[4,4,48,3072]{3,2,1,0:T(8,128)(2,1)}) custom-call(s32[8]{0:T(128)S(1)} %stack.183.refs_0_, bf16[1536,1024]{1,0:T(8,128)(2,1)S(1)} %copy-done.15, bf16[1536,256]{1,0:T(8,128)(2,1)S(1)} %get-tuple-element.154.refs_2_.query_ref, bf16[1536,1024]{1,0:T(8,128)(2,1)S(1)} %bitcast.177), custom_call_target="tpu_custom_call" | custom-call | flops 100000000 | bytes 300000 | tf_op jit(solution)/shard_map/projected_core/owned_terms/pallas_call | solution.py:260
  343.0 7.5 %collective-permute-done.34 = bf16[4,4,48,3072]{3,2,1,0:T(8,128)(2,1)} collective-permute-done((bf16[4,4,48,3072]{3,2,1,0:T(8,128)(2,1)}, bf16[4,4,48,3072]{3,2,1,0:T(8,128)(2,1)}, u32[]{:S(2)}, u32[]{:S(2)}) %collective-permute-start.34) | collective-permute-done | bytes 4718624 | tf_op jit(solution)/shard_map/projected_core/ppermute | solution.py:674
  350.6 5.3 %convolution_convert_fusion = bf16[1024,1536]{1,0:T(8,128)(2,1)} fusion(bf16[1024,512]{1,0:T(8,128)(2,1)} %get-tuple-element.163, bf16[512,1536]{1,0:T(8,128)(2,1)} %get-tuple-element.162), kind=kOutput, calls=%fused_computation.4 | convolution fusion | flops 1612185600 | bytes 5767168 | tf_op jit(solution)/shard_map/result_core/dot_general | solution.py:196
  356.0 2.9 add_half.23
  360.5 3.0 reduce-scatter.5.cloned.1.call-done
  363.6 2.1 slice.16
  365.6 4.2 all-to-all-start.1
  369.8 2.3 copy-done
  372.2 2.2 add_half.22
  378.2 14.1 %collective-permute-done.36 = bf16[2,4,48,3072]{3,2,1,0:T(8,128)(2,1)} collective-permute-done((bf16[2,4,48,3072]{3,2,1,0:T(8,128)(2,1)}, bf16[2,4,48,3072]{3,2,1,0:T(8,128)(2,1)}, u32[]{:S(2)}, u32[]{:S(2)}) %collective-permute-start.36) | collective-permute-done | bytes 2359328 | tf_op jit(solution)/shard_map/projected_second/ppermute | solution.py:671
  392.3 2.3 add_half.25
  404.6 12.3 %collective-permute-done.41.refs_5_ = bf16[48,1536]{1,0:T(8,128)(2,1)S(1)} collective-permute-done((bf16[48,1536]{1,0:T(8,128)(2,1)S(1)}, bf16[48,1536]{1,0:T(8,128)(2,1)S(1)}, u32[]{:S(2)}, u32[]{:S(2)}) %collective-permute-start.41) | collective-permute-done | bytes 147488 | tf_op jit(solution)/shard_map/out_z/ppermute | solution.py:665
  417.6 16.3 %collective-permute-done.42.refs_6_ = bf16[48,1536]{1,0:T(8,128)(2,1)S(1)} collective-permute-done((bf16[48,1536]{1,0:T(8,128)(2,1)S(1)}, bf16[48,1536]{1,0:T(8,128)(2,1)S(1)}, u32[]{:S(2)}, u32[]{:S(2)}) %collective-permute-start.42) | collective-permute-done | bytes 147488 | tf_op jit(solution)/shard_map/out_z/ppermute | solution.py:665
  438.9 3.2 collective-permute-done.43.refs_7_
  442.1 2.7 collective-permute-done.38
  447.6 2.0 collective-permute-start.46
  449.6 3.0 fusion.13
  452.7 9.9 %input_gradient.1 = bf16[256,1536]{1,0:T(8,128)(2,1)} custom-call(bf16[1536,256]{1,0:T(8,128)(2,1)S(1)} %copy-done.14, bf16[1536,256]{1,0:T(8,128)(2,1)S(1)} %bitcast.182, bf16[1536,4608]{1,0:T(8,128)(2,1)} %get-tuple-element.131.weight_ref, bf16[256,1536]{1,0:T(8,128)(2,1)S(1)} %bitcast.176, f32[256,1536]{1,0:T(8,128)S(1)} %copy-done.5), custom_call_target="tpu_custom_call" | custom-call | flops 100000000 | bytes 300000 | tf_op jit(solution)/shard_map/input_gradient/pallas_call | solution.py:620
  462.7 2.8 feed_finish.1
  465.5 7.3 %collective-permute-done.45.refs_2_ = bf16[48,3072]{1,0:T(8,128)(2,1)S(1)} collective-permute-done((bf16[48,3072]{1,0:T(8,128)(2,1)S(1)}, bf16[48,3072]{1,0:T(8,128)(2,1)S(1)}, u32[]{:S(2)}, u32[]{:S(2)}) %collective-permute-start.45) | collective-permute-done | bytes 294944 | tf_op jit(solution)/shard_map/projected_z/ppermute | solution.py:665
  472.8 2.1 attention_finish.1
  (293 shorter events, 82.9 us)
Async XLA Ops:
  11.0 16.4 %collective-permute-start = (bf16[48,4608]{1,0:T(8,128)(2,1)}, bf16[48,4608]{1,0:T(8,128)(2,1)}, u32[]{:S(2)}, u32[]{:S(2)}) collective-permute-start(bf16[48,4608]{1,0:T(8,128)(2,1)} %get-tuple-element.244), channel_id=1, source_target_pairs={{0,8},{8,16},{16,24},{24,0},{1,9},{9,17},{17,25},{25,1},{2,10},{10... | collective-permute-start | bytes 1327112 | tf_op jit(solution)/shard_map/attention_weights_z/ppermute | solution.py:665
  14.0 40.8 %collective-permute-start.3 = (bf16[48,4608]{1,0:T(8,128)(2,1)}, bf16[48,4608]{1,0:T(8,128)(2,1)S(1)}, u32[]{:S(2)}, u32[]{:S(2)}) collective-permute-start(bf16[48,4608]{1,0:T(8,128)(2,1)} %get-tuple-element.244), channel_id=1, source_target_pairs={{0,2},{1,5},{2,0},{3,7},{4,6},{5,1},{6,4},{7,3},{8,10},{9,13},{10,... | collective-permute-start | bytes 1327112 | tf_op jit(solution)/shard_map/attention_weights_own/ppermute | solution.py:671
  15.5 12.4 %collective-permute-start.4 = (bf16[48,4608]{1,0:T(8,128)(2,1)}, bf16[48,4608]{1,0:T(8,128)(2,1)S(1)}, u32[]{:S(2)}, u32[]{:S(2)}) collective-permute-start(bf16[48,4608]{1,0:T(8,128)(2,1)} %get-tuple-element.244), channel_id=1, source_target_pairs={{0,4},{1,3},{2,6},{3,1},{4,0},{5,7},{6,2},{7,5},{8,12},{9,11},{10,... | collective-permute-start | bytes 1327112 | tf_op jit(solution)/shard_map/attention_weights_own/ppermute | solution.py:668
  17.0 37.9 %collective-permute-start.6 = (bf16[256,1536]{1,0:T(8,128)(2,1)S(1)}, bf16[256,1536]{1,0:T(8,128)(2,1)}, u32[]{:S(2)}, u32[]{:S(2)}) collective-permute-start(bf16[256,1536]{1,0:T(8,128)(2,1)S(1)} %bitcast.175), channel_id=1, source_target_pairs={{0,8},{8,16},{16,24},{24,0},{1,9},{9,17},{17,25},{25,1},{2,10},{10... | collective-permute-start | bytes 2359304 | tf_op jit(solution)/shard_map/tokens_z/ppermute | solution.py:665
  18.6 36.3 %collective-permute-start.7 = (bf16[256,1536]{1,0:T(8,128)(2,1)}, bf16[256,1536]{1,0:T(8,128)(2,1)S(1)}, u32[]{:S(2)}, u32[]{:S(2)}) collective-permute-start(bf16[256,1536]{1,0:T(8,128)(2,1)} %bitcast.186), channel_id=1, source_target_pairs={{0,4},{1,3},{2,6},{3,1},{4,0},{5,7},{6,2},{7,5},{8,12},{9,11},{10,... | collective-permute-start | bytes 2359304 | tf_op jit(solution)/shard_map/out_grad_first/ppermute | solution.py:668
  27.4 25.5 %collective-permute-start.1 = (bf16[48,4608]{1,0:T(8,128)(2,1)}, bf16[48,4608]{1,0:T(8,128)(2,1)}, u32[]{:S(2)}, u32[]{:S(2)}) collective-permute-start(bf16[48,4608]{1,0:T(8,128)(2,1)} %collective-permute-done), channel_id=1, source_target_pairs={{0,8},{8,16},{16,24},{24,0},{1,9},{9,17},{17,25},{25,1},{2,10},{10... | collective-permute-start | bytes 1327112 | tf_op jit(solution)/shard_map/attention_weights_z/ppermute | solution.py:665
  27.9 27.1 %collective-permute-start.5 = (bf16[48,4608]{1,0:T(8,128)(2,1)S(1)}, bf16[48,4608]{1,0:T(8,128)(2,1)}, u32[]{:S(2)}, u32[]{:S(2)}) collective-permute-start(bf16[48,4608]{1,0:T(8,128)(2,1)S(1)} %collective-permute-done.4), channel_id=1, source_target_pairs={{0,2},{1,5},{2,0},{3,7},{4,6},{5,1},{6,4},{7,3},{8,10},{9,13},{10,... | collective-permute-start | bytes 1327112 | tf_op jit(solution)/shard_map/attention_weights_own/ppermute | solution.py:671
  52.9 13.5 %collective-permute-start.2 = (bf16[48,4608]{1,0:T(8,128)(2,1)}, bf16[48,4608]{1,0:T(8,128)(2,1)}, u32[]{:S(2)}, u32[]{:S(2)}) collective-permute-start(bf16[48,4608]{1,0:T(8,128)(2,1)} %collective-permute-done.1), channel_id=1, source_target_pairs={{0,8},{8,16},{16,24},{24,0},{1,9},{9,17},{17,25},{25,1},{2,10},{10... | collective-permute-start | bytes 1327112 | tf_op jit(solution)/shard_map/attention_weights_z/ppermute | solution.py:665
  54.8 21.4 %collective-permute-start.10 = (bf16[48,4608]{1,0:T(8,128)(2,1)}, bf16[48,4608]{1,0:T(8,128)(2,1)}, u32[]{:S(2)}, u32[]{:S(2)}) collective-permute-start(bf16[48,4608]{1,0:T(8,128)(2,1)} %get-tuple-element.244), channel_id=1, source_target_pairs={{0,1},{1,0},{2,3},{3,2},{4,5},{5,4},{6,7},{7,6},{8,9},{9,8},{10,11... | collective-permute-start | bytes 1327112 | tf_op jit(solution)/shard_map/attention_weights_core/ppermute | solution.py:674
  67.8 27.4 %collective-permute-start.8 = (bf16[3,48,4608]{2,1,0:T(8,128)(2,1)S(1)}, bf16[3,48,4608]{2,1,0:T(8,128)(2,1)}, u32[]{:S(2)}, u32[]{:S(2)}) collective-permute-start(bf16[3,48,4608]{2,1,0:T(8,128)(2,1)S(1)} %pad_maximum_fusion.2.refs_2_), channel_id=1, source_target_pairs={{0,4},{1,3},{2,6},{3,1},{4,0},{5,7},{6,2},{7,5},{8,12},{9,11},{10,... | collective-permute-start | bytes 3981320 | tf_op jit(solution)/shard_map/attention_weights_first/ppermute | solution.py:668
  69.3 24.7 %all-to-all-start = ((bf16[8,48,1024]{2,1,0:T(8,128)(2,1)}), bf16[8,48,1024]{2,1,0:T(8,128)(2,1)S(1)}, u32[]{:S(2)}, u32[]{:S(2)}) async-start(bf16[8,48,1024]{2,1,0:T(8,128)(2,1)} %reshape.257), calls=%async_computation | async-start | bytes 1572864 | tf_op jit(solution)/shard_map/gate_up_f/all_to_all | solution.py:791
  72.9 144.2 %all-gather.3.cloned.1.call-start = ((), (), s32[]{:S(2)}) async-start(), calls=%async_computation.6 | async-start | bytes 5898240 | tf_op jit(solution)/shard_map/gate_up_down_z/all_gather | solution.py:830
  73.0 22.2 %collective-permute-start.9 = (bf16[256,1536]{1,0:T(8,128)(2,1)}, bf16[256,1536]{1,0:T(8,128)(2,1)}, u32[]{:S(2)}, u32[]{:S(2)}) collective-permute-start(bf16[256,1536]{1,0:T(8,128)(2,1)} %collective-permute-done.6.refs_18_), channel_id=1, source_target_pairs={{0,8},{8,16},{16,24},{24,0},{1,9},{9,17},{17,25},{25,1},{2,10},{10... | collective-permute-start | bytes 2359304 | tf_op jit(solution)/shard_map/tokens_z/ppermute | solution.py:665
  75.7 19.4 %collective-permute-start.11 = (bf16[48,4608]{1,0:T(8,128)(2,1)}, bf16[48,4608]{1,0:T(8,128)(2,1)}, u32[]{:S(2)}, u32[]{:S(2)}) collective-permute-start(bf16[48,4608]{1,0:T(8,128)(2,1)} %copy-done.65), channel_id=1, source_target_pairs={{0,1},{1,0},{2,3},{3,2},{4,5},{5,4},{6,7},{7,6},{8,9},{9,8},{10,11... | collective-permute-start | bytes 1327112 | tf_op jit(solution)/shard_map/attention_weights_core/ppermute | solution.py:674
  76.1 19.1 %collective-permute-start.12 = (bf16[48,4608]{1,0:T(8,128)(2,1)}, bf16[48,4608]{1,0:T(8,128)(2,1)}, u32[]{:S(2)}, u32[]{:S(2)}) collective-permute-start(bf16[48,4608]{1,0:T(8,128)(2,1)} %copy-done.64), channel_id=1, source_target_pairs={{0,1},{1,0},{2,3},{3,2},{4,5},{5,4},{6,7},{7,6},{8,9},{9,8},{10,11... | collective-permute-start | bytes 1327112 | tf_op jit(solution)/shard_map/attention_weights_core/ppermute | solution.py:674
  76.3 18.9 %collective-permute-start.13 = (bf16[48,4608]{1,0:T(8,128)(2,1)}, bf16[48,4608]{1,0:T(8,128)(2,1)}, u32[]{:S(2)}, u32[]{:S(2)}) collective-permute-start(bf16[48,4608]{1,0:T(8,128)(2,1)} %collective-permute-done.5), channel_id=1, source_target_pairs={{0,1},{1,0},{2,3},{3,2},{4,5},{5,4},{6,7},{7,6},{8,9},{9,8},{10,11... | collective-permute-start | bytes 1327112 | tf_op jit(solution)/shard_map/attention_weights_core/ppermute | solution.py:674
  95.2 24.1 %collective-permute-start.14 = (bf16[3,48,4608]{2,1,0:T(8,128)(2,1)S(1)}, bf16[3,48,4608]{2,1,0:T(8,128)(2,1)S(1)}, u32[]{:S(2)}, u32[]{:S(2)}) collective-permute-start(bf16[3,48,4608]{2,1,0:T(8,128)(2,1)S(1)} %pad_maximum_fusion.2.refs_2_), channel_id=1, source_target_pairs={{0,2},{1,5},{2,0},{3,7},{4,6},{5,1},{6,4},{7,3},{8,10},{9,13},{10,... | collective-permute-start | bytes 3981320 | tf_op jit(solution)/shard_map/attention_weights_second/ppermute | solution.py:671
  96.6 30.7 %collective-permute-start.15 = (bf16[3,48,4608]{2,1,0:T(8,128)(2,1)}, bf16[3,48,4608]{2,1,0:T(8,128)(2,1)S(1)}, u32[]{:S(2)}, u32[]{:S(2)}) collective-permute-start(bf16[3,48,4608]{2,1,0:T(8,128)(2,1)} %collective-permute-done.8.refs_4_), channel_id=1, source_target_pairs={{0,2},{1,5},{2,0},{3,7},{4,6},{5,1},{6,4},{7,3},{8,10},{9,13},{10,... | collective-permute-start | bytes 3981320 | tf_op jit(solution)/shard_map/attention_weights_second/ppermute | solution.py:671
  97.3 30.0 %collective-permute-start.17 = (bf16[3,48,4608]{2,1,0:T(8,128)(2,1)S(1)}, bf16[3,48,4608]{2,1,0:T(8,128)(2,1)S(1)}, u32[]{:S(2)}, u32[]{:S(2)}) collective-permute-start(bf16[3,48,4608]{2,1,0:T(8,128)(2,1)S(1)} %pad_maximum_fusion.2.refs_2_), channel_id=1, source_target_pairs={{0,1},{1,0},{2,3},{3,2},{4,5},{5,4},{6,7},{7,6},{8,9},{9,8},{10,11... | collective-permute-start | bytes 3981320 | tf_op jit(solution)/shard_map/attention_weights_core/ppermute | solution.py:674
  97.3 32.2 %collective-permute-start.18 = (bf16[3,48,4608]{2,1,0:T(8,128)(2,1)}, bf16[3,48,4608]{2,1,0:T(8,128)(2,1)}, u32[]{:S(2)}, u32[]{:S(2)}) collective-permute-start(bf16[3,48,4608]{2,1,0:T(8,128)(2,1)} %collective-permute-done.8.refs_4_), channel_id=1, source_target_pairs={{0,1},{1,0},{2,3},{3,2},{4,5},{5,4},{6,7},{7,6},{8,9},{9,8},{10,11... | collective-permute-start | bytes 3981320 | tf_op jit(solution)/shard_map/attention_weights_core/ppermute | solution.py:674
  97.8 21.5 %collective-permute-start.16 = (bf16[256,1536]{1,0:T(8,128)(2,1)}, bf16[256,1536]{1,0:T(8,128)(2,1)S(1)}, u32[]{:S(2)}, u32[]{:S(2)}) collective-permute-start(bf16[256,1536]{1,0:T(8,128)(2,1)} %collective-permute-done.9.refs_19_), channel_id=1, source_target_pairs={{0,8},{8,16},{16,24},{24,0},{1,9},{9,17},{17,25},{25,1},{2,10},{10... | collective-permute-start | bytes 2359304 | tf_op jit(solution)/shard_map/tokens_z/ppermute | solution.py:665
  129.5 234.1 %reduce-scatter.5.cloned.1.call-start = ((), (), s32[]{:S(2)}) async-start(), calls=%async_computation.5 | async-start | bytes 5898240 | tf_op jit(solution)/shard_map/feed_sum_z/reduce_scatter | solution.py:923
  132.5 41.4 %collective-permute-start.21 = (bf16[512,1536]{1,0:T(8,128)(2,1)}, bf16[512,1536]{1,0:T(8,128)(2,1)}, u32[]{:S(2)}, u32[]{:S(2)}) collective-permute-start(bf16[512,1536]{1,0:T(8,128)(2,1)} %pad_maximum_fusion.refs_2_), channel_id=1, source_target_pairs={{0,2},{1,5},{2,0},{3,7},{4,6},{5,1},{6,4},{7,3},{8,10},{9,13},{10,... | collective-permute-start | bytes 4718600 | tf_op jit(solution)/shard_map/out_grad_second/ppermute | solution.py:671
  173.9 12.1 %collective-permute-start.22 = (bf16[256,1536]{1,0:T(8,128)(2,1)S(1)}, bf16[256,1536]{1,0:T(8,128)(2,1)S(1)}, u32[]{:S(2)}, u32[]{:S(2)}) collective-permute-start(bf16[256,1536]{1,0:T(8,128)(2,1)S(1)} %multiply_convert_fusion.1), channel_id=1, source_target_pairs={{0,4},{1,3},{2,6},{3,1},{4,0},{5,7},{6,2},{7,5},{8,12},{9,11},{10,... | collective-permute-start | bytes 2359304 | tf_op jit(solution)/shard_map/normed_first/ppermute | solution.py:668
  186.1 20.5 %collective-permute-start.23 = (bf16[512,1536]{1,0:T(8,128)(2,1)S(1)}, bf16[512,1536]{1,0:T(8,128)(2,1)S(1)}, u32[]{:S(2)}, u32[]{:S(2)}) collective-permute-start(bf16[512,1536]{1,0:T(8,128)(2,1)S(1)} %pad_maximum_fusion.1.refs_0_), channel_id=1, source_target_pairs={{0,2},{1,5},{2,0},{3,7},{4,6},{5,1},{6,4},{7,3},{8,10},{9,13},{10,... | collective-permute-start | bytes 4718600 | tf_op jit(solution)/shard_map/normed_second/ppermute | solution.py:671
  187.2 19.4 %collective-permute-start.26 = (bf16[512,1536]{1,0:T(8,128)(2,1)}, bf16[512,1536]{1,0:T(8,128)(2,1)S(1)}, u32[]{:S(2)}, u32[]{:S(2)}) collective-permute-start(bf16[512,1536]{1,0:T(8,128)(2,1)} %pad_maximum_fusion.refs_2_), channel_id=1, source_target_pairs={{0,1},{1,0},{2,3},{3,2},{4,5},{5,4},{6,7},{7,6},{8,9},{9,8},{10,11... | collective-permute-start | bytes 4718600 | tf_op jit(solution)/shard_map/out_grad_all/ppermute | solution.py:674
  187.2 19.4 %collective-permute-start.27 = (bf16[512,1536]{1,0:T(8,128)(2,1)}, bf16[512,1536]{1,0:T(8,128)(2,1)S(1)}, u32[]{:S(2)}, u32[]{:S(2)}) collective-permute-start(bf16[512,1536]{1,0:T(8,128)(2,1)} %collective-permute-done.21.refs_3_), channel_id=1, source_target_pairs={{0,1},{1,0},{2,3},{3,2},{4,5},{5,4},{6,7},{7,6},{8,9},{9,8},{10,11... | collective-permute-start | bytes 4718600 | tf_op jit(solution)/shard_map/out_grad_all/ppermute | solution.py:674
  187.7 18.9 %collective-permute-start.24 = (bf16[512,1536]{1,0:T(8,128)(2,1)S(1)}, bf16[512,1536]{1,0:T(8,128)(2,1)S(1)}, u32[]{:S(2)}, u32[]{:S(2)}) collective-permute-start(bf16[512,1536]{1,0:T(8,128)(2,1)S(1)} %pad_maximum_fusion.1.refs_0_), channel_id=1, source_target_pairs={{0,1},{1,0},{2,3},{3,2},{4,5},{5,4},{6,7},{7,6},{8,9},{9,8},{10,11... | collective-permute-start | bytes 4718600 | tf_op jit(solution)/shard_map/normed_second/ppermute | solution.py:674
  234.8 19.4 %collective-permute-start.28 = (bf16[1024,1536]{1,0:T(8,128)(2,1)}, bf16[1024,1536]{1,0:T(8,128)(2,1)S(1)}, u32[]{:S(2)}, u32[]{:S(2)}) collective-permute-start(bf16[1024,1536]{1,0:T(8,128)(2,1)} %get-tuple-element.139), channel_id=1, source_target_pairs={{0,1},{1,0},{2,3},{3,2},{4,5},{5,4},{6,7},{7,6},{8,9},{9,8},{10,11... | collective-permute-start | bytes 9437192 | tf_op jit(solution)/shard_map/scaled_core/ppermute | solution.py:674
  257.7 20.5 %collective-permute-start.29 = (bf16[512,1536]{1,0:T(8,128)(2,1)S(1)}, bf16[512,1536]{1,0:T(8,128)(2,1)S(1)}, u32[]{:S(2)}, u32[]{:S(2)}) collective-permute-start(bf16[512,1536]{1,0:T(8,128)(2,1)S(1)} %add_half.15), channel_id=1, source_target_pairs={{0,2},{1,5},{2,0},{3,7},{4,6},{5,1},{6,4},{7,3},{8,10},{9,13},{10,... | collective-permute-start | bytes 4718600 | tf_op jit(solution)/shard_map/scaled_second/ppermute | solution.py:671
  279.1 12.3 %collective-permute-start.30 = (bf16[256,1536]{1,0:T(8,128)(2,1)}, bf16[256,1536]{1,0:T(8,128)(2,1)}, u32[]{:S(2)}, u32[]{:S(2)}) collective-permute-start(bf16[256,1536]{1,0:T(8,128)(2,1)} %add_half.17), channel_id=1, source_target_pairs={{0,4},{1,3},{2,6},{3,1},{4,0},{5,7},{6,2},{7,5},{8,12},{9,11},{10,... | collective-permute-start | bytes 2359304 | tf_op jit(solution)/shard_map/scaled_first/ppermute | solution.py:668
  280.6 161.5 %reduce-scatter.3.cloned.1.call-start = ((), (), s32[]{:S(2)}) async-start(), calls=%async_computation.4 | async-start | bytes 3932160 | tf_op jit(solution)/shard_map/kv_grad_z/reduce_scatter | solution.py:963
  304.4 21.7 %collective-permute-start.32 = (bf16[2,4,48,1536]{3,2,1,0:T(8,128)(2,1)S(1)}, bf16[2,4,48,1536]{3,2,1,0:T(8,128)(2,1)S(1)}, u32[]{:S(2)}, u32[]{:S(2)}) collective-permute-start(bf16[2,4,48,1536]{3,2,1,0:T(8,128)(2,1)S(1)} %bitcast.181), channel_id=1, source_target_pairs={{0,2},{1,5},{2,0},{3,7},{4,6},{5,1},{6,4},{7,3},{8,10},{9,13},{10,... | collective-permute-start | bytes 3538952 | tf_op jit(solution)/shard_map/out_second/ppermute | solution.py:671
  326.4 15.9 %collective-permute-start.33 = (bf16[1,4,48,1536]{3,2,1,0:T(8,128)(2,1)S(1)}, bf16[1,4,48,1536]{3,2,1,0:T(8,128)(2,1)S(1)}, u32[]{:S(2)}, u32[]{:S(2)}) collective-permute-start(bf16[1,4,48,1536]{3,2,1,0:T(8,128)(2,1)S(1)} %bitcast.183), channel_id=1, source_target_pairs={{0,4},{1,3},{2,6},{3,1},{4,0},{5,7},{6,2},{7,5},{8,12},{9,11},{10,... | collective-permute-start | bytes 1769480 | tf_op jit(solution)/shard_map/out_first/ppermute | solution.py:668
  342.2 8.3 %collective-permute-start.34 = (bf16[4,4,48,3072]{3,2,1,0:T(8,128)(2,1)}, bf16[4,4,48,3072]{3,2,1,0:T(8,128)(2,1)}, u32[]{:S(2)}, u32[]{:S(2)}) collective-permute-start(bf16[4,4,48,3072]{3,2,1,0:T(8,128)(2,1)} %get-tuple-element.158), channel_id=1, source_target_pairs={{0,1},{1,0},{2,3},{3,2},{4,5},{5,4},{6,7},{7,6},{8,9},{9,8},{10,11... | collective-permute-start | bytes 14155784 | tf_op jit(solution)/shard_map/projected_core/ppermute | solution.py:674
  355.9 20.7 %collective-permute-start.35 = (bf16[1024,1536]{1,0:T(8,128)(2,1)}, bf16[1024,1536]{1,0:T(8,128)(2,1)}, u32[]{:S(2)}, u32[]{:S(2)}) collective-permute-start(bf16[1024,1536]{1,0:T(8,128)(2,1)} %convolution_convert_fusion), channel_id=1, source_target_pairs={{0,1},{1,0},{2,3},{3,2},{4,5},{5,4},{6,7},{7,6},{8,9},{9,8},{10,11... | collective-permute-start | bytes 9437192 | tf_op jit(solution)/shard_map/result_core/ppermute | solution.py:674
  358.9 33.4 %collective-permute-start.36 = (bf16[2,4,48,3072]{3,2,1,0:T(8,128)(2,1)}, bf16[2,4,48,3072]{3,2,1,0:T(8,128)(2,1)}, u32[]{:S(2)}, u32[]{:S(2)}) collective-permute-start(bf16[2,4,48,3072]{3,2,1,0:T(8,128)(2,1)} %bitcast.81), channel_id=1, source_target_pairs={{0,2},{1,5},{2,0},{3,7},{4,6},{5,1},{6,4},{7,3},{8,10},{9,13},{10,... | collective-permute-start | bytes 7077896 | tf_op jit(solution)/shard_map/projected_second/ppermute | solution.py:671
  365.6 76.5 %all-to-all-start.1 = ((bf16[8,48,1024]{2,1,0:T(8,128)(2,1)}), bf16[8,48,1024]{2,1,0:T(8,128)(2,1)}, u32[]{:S(2)}, u32[]{:S(2)}) async-start(bf16[8,48,1024]{2,1,0:T(8,128)(2,1)} %bitcast.85), calls=%async_computation.3 | async-start | bytes 1572864 | tf_op jit(solution)/shard_map/gate_up_sum_f/all_to_all | solution.py:986
  394.6 50.2 %collective-permute-start.37 = (bf16[1,4,48,3072]{3,2,1,0:T(8,128)(2,1)}, bf16[1,4,48,3072]{3,2,1,0:T(8,128)(2,1)}, u32[]{:S(2)}, u32[]{:S(2)}) collective-permute-start(bf16[1,4,48,3072]{3,2,1,0:T(8,128)(2,1)} %bitcast.83), channel_id=1, source_target_pairs={{0,4},{1,3},{2,6},{3,1},{4,0},{5,7},{6,2},{7,5},{8,12},{9,11},{10,... | collective-permute-start | bytes 3538952 | tf_op jit(solution)/shard_map/projected_first/ppermute | solution.py:668
  398.3 46.4 %collective-permute-start.38 = (bf16[256,1536]{1,0:T(8,128)(2,1)}, bf16[256,1536]{1,0:T(8,128)(2,1)}, u32[]{:S(2)}, u32[]{:S(2)}) collective-permute-start(bf16[256,1536]{1,0:T(8,128)(2,1)} %split.21), channel_id=1, source_target_pairs={{0,4},{1,3},{2,6},{3,1},{4,0},{5,7},{6,2},{7,5},{8,12},{9,11},{10,... | collective-permute-start | bytes 2359304 | tf_op jit(solution)/shard_map/result_f/ppermute | solution.py:668
  400.4 44.4 %collective-permute-start.39 = (bf16[256,1536]{1,0:T(8,128)(2,1)}, bf16[256,1536]{1,0:T(8,128)(2,1)}, u32[]{:S(2)}, u32[]{:S(2)}) collective-permute-start(bf16[256,1536]{1,0:T(8,128)(2,1)} %get-tuple-element.235), channel_id=1, source_target_pairs={{0,2},{1,5},{2,0},{3,7},{4,6},{5,1},{6,4},{7,3},{8,10},{9,13},{10,... | collective-permute-start | bytes 2359304 | tf_op jit(solution)/shard_map/result_f/ppermute | solution.py:671
  401.8 42.9 %collective-permute-start.40 = (bf16[256,1536]{1,0:T(8,128)(2,1)}, bf16[256,1536]{1,0:T(8,128)(2,1)}, u32[]{:S(2)}, u32[]{:S(2)}) collective-permute-start(bf16[256,1536]{1,0:T(8,128)(2,1)} %get-tuple-element.234), channel_id=1, source_target_pairs={{0,6},{1,7},{2,4},{3,5},{4,2},{5,3},{6,0},{7,1},{8,14},{9,15},{10,... | collective-permute-start | bytes 2359304 | tf_op jit(solution)/shard_map/result_f/ppermute | solution.py:999
  404.0 12.9 %collective-permute-start.41 = (bf16[48,1536]{1,0:T(8,128)(2,1)S(1)}, bf16[48,1536]{1,0:T(8,128)(2,1)S(1)}, u32[]{:S(2)}, u32[]{:S(2)}) collective-permute-start(bf16[48,1536]{1,0:T(8,128)(2,1)S(1)} %get-tuple-element.242), channel_id=1, source_target_pairs={{0,24},{8,0},{16,8},{24,16},{1,25},{9,1},{17,9},{25,17},{2,26},{10... | collective-permute-start | bytes 442376 | tf_op jit(solution)/shard_map/out_z/ppermute | solution.py:665
  417.6 16.3 %collective-permute-start.42 = (bf16[48,1536]{1,0:T(8,128)(2,1)S(1)}, bf16[48,1536]{1,0:T(8,128)(2,1)S(1)}, u32[]{:S(2)}, u32[]{:S(2)}) collective-permute-start(bf16[48,1536]{1,0:T(8,128)(2,1)S(1)} %get-tuple-element.241), channel_id=1, source_target_pairs={{0,16},{8,24},{16,0},{24,8},{1,17},{9,25},{17,1},{25,9},{2,18},{10... | collective-permute-start | bytes 442376 | tf_op jit(solution)/shard_map/out_z/ppermute | solution.py:665
  434.5 7.6 %collective-permute-start.43 = (bf16[48,1536]{1,0:T(8,128)(2,1)}, bf16[48,1536]{1,0:T(8,128)(2,1)}, u32[]{:S(2)}, u32[]{:S(2)}) collective-permute-start(bf16[48,1536]{1,0:T(8,128)(2,1)} %get-tuple-element.240), channel_id=1, source_target_pairs={{0,8},{8,16},{16,24},{24,0},{1,9},{9,17},{17,25},{25,1},{2,10},{10... | collective-permute-start | bytes 442376 | tf_op jit(solution)/shard_map/out_z/ppermute | solution.py:665
  446.7 18.8 %collective-permute-start.44 = (bf16[48,3072]{1,0:T(8,128)(2,1)S(1)}, bf16[48,3072]{1,0:T(8,128)(2,1)S(1)}, u32[]{:S(2)}, u32[]{:S(2)}) collective-permute-start(bf16[48,3072]{1,0:T(8,128)(2,1)S(1)} %get-tuple-element.238), channel_id=1, source_target_pairs={{0,24},{8,0},{16,8},{24,16},{1,25},{9,1},{17,9},{25,17},{2,26},{10... | collective-permute-start | bytes 884744 | tf_op jit(solution)/shard_map/projected_z/ppermute | solution.py:665
  447.4 25.3 %collective-permute-start.45 = (bf16[48,3072]{1,0:T(8,128)(2,1)S(1)}, bf16[48,3072]{1,0:T(8,128)(2,1)S(1)}, u32[]{:S(2)}, u32[]{:S(2)}) collective-permute-start(bf16[48,3072]{1,0:T(8,128)(2,1)S(1)} %get-tuple-element.237), channel_id=1, source_target_pairs={{0,16},{8,24},{16,0},{24,8},{1,17},{9,25},{17,1},{25,9},{2,18},{10... | collective-permute-start | bytes 884744 | tf_op jit(solution)/shard_map/projected_z/ppermute | solution.py:665
  447.6 25.1 %collective-permute-start.46 = (bf16[48,3072]{1,0:T(8,128)(2,1)S(1)}, bf16[48,3072]{1,0:T(8,128)(2,1)S(1)}, u32[]{:S(2)}, u32[]{:S(2)}) collective-permute-start(bf16[48,3072]{1,0:T(8,128)(2,1)S(1)} %get-tuple-element.236), channel_id=1, source_target_pairs={{0,8},{8,16},{16,24},{24,0},{1,9},{9,17},{17,25},{25,1},{2,10},{10... | collective-permute-start | bytes 884744 | tf_op jit(solution)/shard_map/projected_z/ppermute | solution.py:665
  (80 other events, 636.2 us)
Sparse Core Ops, SparseCore 0:
  129.6 87.4 all-gather.2
  280.8 82.7 reduce-scatter.4
  365.9 66.9 reduce-scatter.2

commit v4 on v3

--- a/solution.py
+++ b/solution.py
@@ -353,11 +353,9 @@
     )(starts, *parts, *blocks, cosine, sine)
 
 
-def feed_kernel(count, first, *refs):
+def feed_kernel(count, *refs):
     parts, grads, blocks_ref = refs[:count], refs[count : 2 * count], refs[2 * count]
     refs = refs[2 * count + 1 :]
-    if not first:
-        earlier_ref, refs = refs[0], refs[1:]
     scaled_ref, hidden_ref, both_ref, sum_ref, down_ref = refs[:5]
     total_ref, part_ref, grad_ref, weight_ref, part_sem, grad_sem, block_sem = refs[5:]
     step = pl.program_id(0)
@@ -399,7 +397,7 @@
                 copy.start()
         for copy in block_copies:
             copy.wait()
-        total_ref[...] = jnp.zeros_like(total_ref) if first else earlier_ref[...]
+        total_ref[...] = jnp.zeros_like(total_ref)
 
     for k in range(count):
 
@@ -427,26 +425,25 @@
 
     @pl.when(step == count - 1)
     def _():
-        sum_ref[...] = total_ref[...].astype(sum_ref.dtype)
-
-
-def feed_forward(parts, grads, blocks, units, earlier=None):
+        sum_ref[...] = total_ref[...].astype(BF)
+
+
+def feed_forward(parts, grads, blocks, units):
     count, n = len(parts), blocks.shape[0]
     rows, width = parts[0].shape
     every = pl.BlockSpec(memory_space=pl.ANY)
     part = lambda cols: pl.BlockSpec((rows, cols), lambda k: (k, 0))
     whole = pl.BlockSpec((units, width), lambda k: (0, 0))
-    first = earlier is None
     return pl.pallas_call(
-        lambda *refs: feed_kernel(count, first, *refs),
+        lambda *refs: feed_kernel(count, *refs),
         grid=(count,),
-        in_specs=[every] * (2 * count + 1) + ([] if first else [whole]),
+        in_specs=[every] * (2 * count + 1),
         out_specs=[part(width), part(units), part(2 * units), whole, whole],
         out_shape=[
             jax.ShapeDtypeStruct((count * rows, width), BF),
             jax.ShapeDtypeStruct((count * rows, units), BF),
             jax.ShapeDtypeStruct((count * rows, 2 * units), BF),
-            jax.ShapeDtypeStruct((units, width), F32 if first else BF),
+            jax.ShapeDtypeStruct((units, width), BF),
             jax.ShapeDtypeStruct((units, width), BF),
         ],
         scratch_shapes=[
@@ -461,7 +458,7 @@
         compiler_params=pltpu.CompilerParams(vmem_limit_bytes=MOST_VMEM_BYTES),
         cost_estimate=lasting(30),
         name="feed_forward",
-    )(*parts, *grads, blocks, *(() if first else (earlier,)))
+    )(*parts, *grads, blocks)
 
 
 def add_kernel(a_ref, b_ref, out_ref):
@@ -487,10 +484,10 @@
 
 
 def feed_terms_kernel(count, *refs):
-    parts, (down_ref, *boths, out_ref, token_ref) = refs[:count], refs[count:]
+    parts, (far_ref, near_ref, *boths, out_ref, token_ref) = refs[:count], refs[count:]
     token_ref[...] = jnp.zeros_like(token_ref)
     rows, cols = parts[0].shape[0], boths[0].shape[1]
-    unit, width = down_ref.shape
+    unit, width = far_ref.shape
     pieces = out_ref.shape[0] // unit
     piece = width // pieces
     each = boths[0].shape[0] // rows
@@ -499,20 +496,21 @@
         at = k % each * rows
         total += contract(part[...], boths[k // each][at : at + rows, :], 0, 0)
     out_ref[:, :cols] = total.astype(BF)
+    down = (far_ref[...].astype(F32) + near_ref[...].astype(F32)).astype(BF)
     for j in range(pieces):
-        out_ref[j * unit : (j + 1) * unit, cols:] = down_ref[:, j * piece : (j + 1) * piece]
-
-
-def feed_terms(parts, down, boths, n):
+        out_ref[j * unit : (j + 1) * unit, cols:] = down[:, j * piece : (j + 1) * piece]
+
+
+def feed_terms(parts, downs, boths, n):
     rows, width = parts[0].shape
     tile, cols = width // n, boths[0].shape[1]
-    unit = down.shape[0] // n
+    unit = downs[0].shape[0] // n
     more = width * unit // tile
     return pl.pallas_call(
         lambda *refs: feed_terms_kernel(len(parts), *refs),
         grid=(n,),
         in_specs=[pl.BlockSpec((rows, tile), lambda j: (0, j))] * len(parts)
-        + [pl.BlockSpec((unit, width), lambda j: (j, 0))]
+        + [pl.BlockSpec((unit, width), lambda j: (j, 0))] * 2
         + [pl.BlockSpec(both.shape, lambda j: (0, 0)) for both in boths],
         out_specs=[
             pl.BlockSpec((tile, cols + more), lambda j: (j, 0)),
@@ -525,7 +523,7 @@
         compiler_params=pltpu.CompilerParams(vmem_limit_bytes=VMEM_BYTES),
         cost_estimate=lasting(15),
         name="feed_terms",
-    )(*parts, down, *boths)
+    )(*parts, *downs, *boths)
 
 
 def feed_finish_kernel(
@@ -587,6 +585,42 @@
         cost_estimate=lasting(0.1),
         name="attention_finish",
     )(*projected, *outs, *weights, gain)
+
+
+def middle_kernel(near_ref, far_ref, resid_ref, grad_ref, weight_ref, total_ref, round_ref, mixed_ref):
+    @pl.when(pl.program_id(0) == 0)
+    def _():
+        resid = resid_ref[...]
+        scaled = near_ref[...].astype(F32) + far_ref[...].astype(F32)
+        inverse = lax.rsqrt(jnp.mean(resid * resid, axis=-1, keepdims=True) + EPSILON)
+        normed = resid * inverse
+        mean = jnp.mean(scaled * normed, axis=-1, keepdims=True)
+        total = grad_ref[...].astype(F32) + inverse * (scaled - normed * mean)
+        total_ref[...] = total
+        round_ref[...] = total.astype(BF)
+
+    mixed_ref[...] = contract(weight_ref[...], round_ref[...], 1, 1).astype(BF)
+
+
+def middle_gradient(near, far, resid, grad, weight):
+    count, width = resid.shape
+    tile = 256
+    last = weight.shape[1] // width - 1
+    whole = pl.BlockSpec((count, width), lambda j: (0, 0))
+    return pl.pallas_call(
+        middle_kernel,
+        grid=(width // tile,),
+        in_specs=[whole] * 4 + [pl.BlockSpec((tile, width), lambda j: (j, last))],
+        out_specs=[whole, whole, pl.BlockSpec((tile, count), lambda j: (j, 0))],
+        out_shape=[
+            jax.ShapeDtypeStruct((count, width), F32),
+            jax.ShapeDtypeStruct((count, width), BF),
+            jax.ShapeDtypeStruct((width, count), BF),
+        ],
+        compiler_params=pltpu.CompilerParams(vmem_limit_bytes=VMEM_BYTES),
+        cost_estimate=lasting(0.1),
+        name="middle_gradient",
+    )(near, far, resid, grad, weight)
 
 
 def input_kernel(query_ref, pair_ref, weight_ref, own_ref, resid_ref, out_ref, left_ref, total_ref):
@@ -766,7 +800,17 @@
     gate_up = scaled(jnp.concatenate([w_gate, w_up], axis=1), gain_two)
     gate_up = gate_up.reshape(shard_rows, 2, n, ranks, unit).transpose(3, 0, 1, 2, 4)
     gate_up = gate_up.reshape(ranks, shard_rows, 2 * hidden_units)
+    with scope("gate_up_f"):
+        gate_up = lax.all_to_all(gate_up, "f", 0, 0, tiled=True)
+    gate_up_rows = ranks * shard_rows
+    pieces = gate_up_rows // unit
     grad_own = grad_first = out_grad[0]
+
+    def beside_down(gate_up):
+        gate_up = gate_up.reshape(gate_up_rows, 2 * hidden_units)
+        down = w_down.reshape(unit, pieces, width // pieces).transpose(1, 0, 2)
+        return jnp.concatenate([gate_up, down.reshape(gate_up_rows, width // pieces)], axis=1)
+
     if grid:
         with scope("attention_weights_z"):
             behind = [shift(shard, 1)]
@@ -774,8 +818,6 @@
                 behind.append(shift(behind[-1], 1))
         with scope("attention_weights_own"):
             near = [shard, swap_first(shard), swap_second(shard)]
-    if grid:
-        with scope("attention_weights_own"):
             near.append(swap_second(near[1]))
         with scope("tokens_z"):
             blocks.append(shift(own, 1))
@@ -784,49 +826,35 @@
         *behind, near[2], near[3], gate_up, blocks[1], grad_first = stage(
             *behind, near[2], near[3], gate_up, blocks[1], grad_first
         )
+        gate_up_down = beside_down(gate_up)
         with scope("attention_weights_core"):
             near_core = [swap_core(part) for part in near]
         rest = [jnp.stack(behind)]
-        with scope("gate_up_f"):
-            gate_up = lax.all_to_all(gate_up, "f", 0, 0, tiled=True)
-            gate_up_rows = ranks * shard_rows
-            gate_up = gate_up.reshape(gate_up_rows, 2 * hidden_units)
-            pieces = gate_up_rows // unit
-            down = w_down.reshape(unit, pieces, width // pieces).transpose(1, 0, 2)
-            gate_up_down = jnp.concatenate(
-                [gate_up, down.reshape(gate_up_rows, width // pieces)], axis=1
-            )
         with scope("attention_weights_first"):
             rest.append(swap_first(rest[0]))
+        with scope("attention_weights_second"):
+            rest.append(swap_second(rest[0]))
         with scope("tokens_z"):
             blocks.append(shift(blocks[1], 1))
-        rest[0], rest[1], blocks[2], cosine, sine, bias, gate_up_down, *near_core = stage(
-            rest[0], rest[1], blocks[2], cosine, sine, bias, gate_up_down, *near_core
+        rest[1], rest[2], blocks[2], cosine, sine, bias, gate_up_down, *near_core = stage(
+            rest[1], rest[2], blocks[2], cosine, sine, bias, gate_up_down, *near_core
         )
         with scope("attention_weights_core"):
-            rest_core = [swap_core(rest[0]), swap_core(rest[1])]
+            rest_core = [swap_core(part) for part in rest]
         with scope("attention_weights_second"):
-            rest += [swap_second(rest[0]), swap_second(rest[1])]
+            rest.append(swap_second(rest[1]))
         with scope("tokens_z"):
             while len(blocks) < n:
                 blocks.append(shift(blocks[-1], 1))
-        rest[2], rest[3], blocks[-1], *rest_core = stage(rest[2], rest[3], blocks[-1], *rest_core)
+        gate_up_down, blocks[-1] = stage(gate_up_down, blocks[-1])
+        rest[3], blocks[-1], *rest_core = stage(rest[3], blocks[-1], *rest_core)
         with scope("attention_weights_core"):
-            rest_core += [swap_core(rest[2]), swap_core(rest[3])]
+            rest_core.append(swap_core(rest[3]))
     else:
-        with scope("gate_up_f"):
-            gate_up = lax.all_to_all(gate_up, "f", 0, 0, tiled=True)
-            gate_up_rows = ranks * shard_rows
-            gate_up = gate_up.reshape(gate_up_rows, 2 * hidden_units)
-            pieces = gate_up_rows // unit
-            down = w_down.reshape(unit, pieces, width // pieces).transpose(1, 0, 2)
-            gate_up_down = jnp.concatenate(
-                [gate_up, down.reshape(gate_up_rows, width // pieces)], axis=1
-            )
+        gate_up_down = beside_down(gate_up)
         while len(blocks) < n:
             blocks.append(shift(blocks[-1], 1))
     with scope("gate_up_down_z"):
-        gate_up_down, blocks[-1] = stage(gate_up_down, blocks[-1])
         gate_up_down = lax.all_gather(gate_up_down, "z")
     cuts = [width, width + pair_cols, width + 2 * pair_cols]
 
@@ -862,6 +890,7 @@
         values = contract(value_matrix, normed_group, 0, 0).astype(BF)
     span = n * token_count
 
+    queries, grad_first = stage(queries, grad_first)
     with scope("out_grad_second"):
         grad_pair = jnp.concatenate([grad_own, grad_first], axis=0) if grid else grad_own
         grad_other = spread_second(grad_pair)
@@ -883,22 +912,18 @@
         if grid:
             normed_pair = jnp.concatenate([normed_two, normed_first], axis=0)
         normed_other = spread_second(normed_pair)
+        normed_other, gate_up_down = stage(normed_other, gate_up_down)
         normed_parts = spread_all(normed_pair, normed_other)
     half = len(normed_parts) // 2
 
-    scaled_far, hidden_far, both_far, down_terms, down_weight = feed_forward(
+    scaled_far, hidden_far, both_far, down_far, down_weight = feed_forward(
         normed_parts[half:], grad_parts[half:], gate_up_down, hidden_units
     )
     with scope("scaled_core"):
         scaled_far = send_core(scaled_far)
-    scaled_near, hidden_near, both_near, down_terms, _ = feed_forward(
-        normed_parts[:half], grad_parts[:half], gate_up_down, hidden_units, down_terms
-    )
-    def norm_back(scaled_grad, normed, inverse):
-        return inverse * (
-            scaled_grad - normed * jnp.mean(scaled_grad * normed, axis=-1, keepdims=True)
-        )
-
+    scaled_near, hidden_near, both_near, down_near, _ = feed_forward(
+        normed_parts[:half], grad_parts[:half], gate_up_down, hidden_units
+    )
     with scope("scaled_second"):
         if grid:
             scaled_near, far = add_halves(scaled_near, scaled_far)
@@ -910,13 +935,13 @@
             scaled_two = far = scaled_two.astype(F32)
     with scope("feed_sum_z"):
         if grid:
-            terms, token = feed_terms(normed_parts, down_terms, [both_near, both_far], n)
+            terms, token = feed_terms(normed_parts, [down_far, down_near], [both_near, both_far], n)
         else:
             terms = over_rows(
                 jnp.concatenate(normed_parts, axis=0),
                 jnp.concatenate([both_near, both_far], axis=0),
             ).astype(BF)
-            down_terms = down_terms.reshape(n, unit, pieces, width // pieces)
+            down_terms = add(down_far, down_near).reshape(n, unit, pieces, width // pieces)
             down_terms = down_terms.transpose(0, 2, 1, 3).reshape(width, width // pieces)
             terms = jnp.concatenate([terms, down_terms], axis=1)
             token = jnp.zeros((8, 128), F32)
@@ -928,14 +953,15 @@
             far = swap_first(far)
     if grid:
         (far,) = stage(far)
-        scaled_two = scaled_near.astype(F32) + far.astype(F32)
-    grad_resid = out_grad[0].astype(F32) + norm_back(scaled_two, second_normed, second_inverse)
-    grad_attn_out = grad_resid.astype(BF)
+    else:
+        far, scaled_near = scaled_two.astype(BF), jnp.zeros_like(scaled_two, BF)
+    grad_resid, grad_attn_out, grad_mixed = middle_gradient(
+        scaled_near, far, resid, out_grad[0], gathered
+    )
 
     with scope("out_core"):
         out_away, out_mine = weight_terms(attention_output, [grad_attn_out], False)
         out_away = send_core(out_away)
-    grad_mixed = contract(out_weight, grad_attn_out, 1, 1).astype(BF)
     grad_mixed, out_away = stage(grad_mixed, out_away)
     with scope("out_second"):
         if grid:
@@ -993,17 +1019,15 @@
             far = swap_first(far)
         with scope("out_z"):
             out_owned = send_z(out_near)
-        with scope("result_f"):
-            own_part, first_part = jnp.split(result_near, 2)
-            second_part, both_part = jnp.split(result_far, 2)
-            both_part = lax.ppermute(both_part, "f", [(i, i ^ 6) for i in range(ranks)])
-            first_part, second_part = swap_first(first_part), swap_second(second_part)
         gate_up_owned = exchange(feed_owned)
-        far, kv_total, gate_up_owned, first_part, second_part, both_part, *out_owned = stage(
-            far, kv_total, gate_up_owned, first_part, second_part, both_part, *out_owned
+        with scope("result_second"):
+            result_far = swap_second(result_far)
+        far, kv_total, gate_up_owned, result_far, *out_owned = stage(
+            far, kv_total, gate_up_owned, result_far, *out_owned
         )
-        result = own_part.astype(F32) + first_part.astype(F32)
-        result = result + second_part.astype(F32) + both_part.astype(F32)
+        with scope("result_first"):
+            result_near, result_far = add_halves(result_near, result_far)
+            result = result_near.astype(F32) + swap_first(result_far).astype(F32)
         near = add(near[0], far[0])
     else:
         near = sum_f(mine)
@@ -1023,7 +1047,9 @@
     )
     if grid:
         gate_owned, up_owned, gain_two_owned = feed_finish(gate_up_owned, w_gate, w_up, gain_two)
-        input_grad, gain_two_owned, *projected = stage(input_grad, gain_two_owned, *projected)
+        input_grad, gain_two_owned, down_owned, result, *projected = stage(
+            input_grad, gain_two_owned, down_owned, result, *projected
+        )
         query_owned, key_owned, value_owned, out_owned, gain_one_owned = attention_finish(
             projected, out_owned, [w_query, key_weight, value_weight], gain_one
         )

time: 490 us -> 472 us (0.963)
  waiting for transfers between devices: 206 us -> 188 us
  Pallas kernels: 144 us -> 152 us
  matrix products: 15 us -> 9.03 us
    ppermute x12, waiting for transfers between devices: 103 us -> 86.6 us  [shift(): return lax.ppermute(a, 'z', [(i, (i + by) % n) for i in range(n)])]
    all_to_all x1, waiting for transfers between devices: 15.9 us -> 0.01 us  [on_device(): gate_up = lax.all_to_all(gate_up, 'f', 0, 0, tiled=True)]
    ppermute x16, waiting for transfers between devices: 9.82 us -> 19.3 us  [swap_core(): return lax.ppermute(a, 'f', [(i, i ^ 1) for i in range(ranks)])]
    pallas_call x2 -> x3, Pallas kernels: 37 us -> 40.7 us  [the longest x2 34.6 us: feed_forward(): pl.pallas_call(lambda *refs: feed_kernel(count, *refs), grid=(count,), in...]
    pallas_call x14 -> x16, Pallas kernels: 15.4 us -> 18.9 us  [add_half(): pl.pallas_call(add_kernel, grid=(rows // tile,), in_specs=[pl.BlockSpec((...]
    unnamed x154 -> x144, local copies, waits for them, and re-layouts: 26 us -> 26.5 us
  transfers between devices with their start and end apart: 52 -> 51, of which waited for: 22 -> 23; matrix products, arithmetic and copies ran while one was open for 9% -> 8% of each run, Pallas kernels for 25% -> 28%
where the time goes in v4:
time: 472 us; the launch traced here: 465 us
  waiting for transfers between devices  188 us (40%)
  Pallas kernels  152 us (32%)
  starting transfers between devices  44 us (9%)
  local copies, waits for them, and re-layouts  35.8 us (8%)
  other arithmetic  20.5 us (4%)
  between operations  15.2 us (3%)
  matrix products  9.03 us (2%)
    ppermute x12, waiting for transfers between devices, shift(): return lax.ppermute(a, 'z', [(i, (i + by) % n) for i in range(n)])  86.6 us
    ppermute x10, waiting for transfers between devices, swap_second(): return lax.ppermute(a, 'f', [(i, i ^ 2 << i % 2) for i in range(ranks)])  48.8 us
    pallas_call x2, Pallas kernels, feed_forward(): pl.pallas_call(lambda *refs: feed_kernel(count, *refs), grid=(count,), in...  34.6 us
    unnamed x144, local copies, waits for them, and re-layouts  26.5 us
    ppermute x8, waiting for transfers between devices, swap_first(): return lax.ppermute(a, 'f', [(i, i ^ 4 >> i % 2) for i in range(ranks)])  24.7 us
    pallas_call x1, Pallas kernels, project(): pl.pallas_call(lambda *refs: project_kernel(n, len(parts), *refs), in_spe...  19.7 us
    ppermute x16, waiting for transfers between devices, swap_core(): return lax.ppermute(a, 'f', [(i, i ^ 1) for i in range(ranks)])  19.3 us
    pallas_call x16, Pallas kernels, add_half(): pl.pallas_call(add_kernel, grid=(rows // tile,), in_specs=[pl.BlockSpec((...  18.9 us
  transfers between devices with their start and end apart: 51, of which 23 were waited for; matrix products, arithmetic and copies ran while one was open for 8% of the time, Pallas kernels for 28%

profile of v4, /device:TPU:0, one launch (start us, length us, event | category | flops | bytes accessed | tf_op | source)
XLA Modules:
  0.0 465.0 jit_solution(8946365653177707673)
XLA Ops:
  9.7 1.9 pad_maximum_fusion.4
  11.6 3.0 collective-permute-start
  18.2 9.7 %collective-permute-done = bf16[48,4608]{1,0:T(8,128)(2,1)} collective-permute-done((bf16[48,4608]{1,0:T(8,128)(2,1)}, bf16[48,4608]{1,0:T(8,128)(2,1)}, u32[]{:S(2)}, u32[]{:S(2)}) %collective-permute-start) | collective-permute-done | bytes 442400 | tf_op jit(solution)/shard_map/attention_weights_z/ppermute | solution.py:699
  32.0 3.9 all-to-all-start
  36.0 2.0 collective-permute-start.3
  38.1 15.3 %collective-permute-done.1 = bf16[48,4608]{1,0:T(8,128)(2,1)} collective-permute-done((bf16[48,4608]{1,0:T(8,128)(2,1)}, bf16[48,4608]{1,0:T(8,128)(2,1)}, u32[]{:S(2)}, u32[]{:S(2)}) %collective-permute-start.1) | collective-permute-done | bytes 442400 | tf_op jit(solution)/shard_map/attention_weights_z/ppermute | solution.py:699
  54.6 2.6 collective-permute-done.5
  57.2 9.7 %collective-permute-done.2 = bf16[48,4608]{1,0:T(8,128)(2,1)} collective-permute-done((bf16[48,4608]{1,0:T(8,128)(2,1)}, bf16[48,4608]{1,0:T(8,128)(2,1)}, u32[]{:S(2)}, u32[]{:S(2)}) %collective-permute-start.2) | collective-permute-done | bytes 442400 | tf_op jit(solution)/shard_map/attention_weights_z/ppermute | solution.py:699
  74.7 2.0 and_select_fusion.bias_ref
  79.9 13.6 %collective-permute-done.10.refs_19_ = bf16[256,1536]{1,0:T(8,128)(2,1)} collective-permute-done((bf16[256,1536]{1,0:T(8,128)(2,1)}, bf16[256,1536]{1,0:T(8,128)(2,1)}, u32[]{:S(2)}, u32[]{:S(2)}) %collective-permute-start.10) | collective-permute-done | bytes 786464 | tf_op jit(solution)/shard_map/tokens_z/ppermute | solution.py:699
  93.6 5.1 %collective-permute-done.8.refs_4_ = bf16[3,48,4608]{2,1,0:T(8,128)(2,1)} collective-permute-done((bf16[3,48,4608]{2,1,0:T(8,128)(2,1)S(1)}, bf16[3,48,4608]{2,1,0:T(8,128)(2,1)}, u32[]{:S(2)}, u32[]{:S(2)}) %collective-permute-start.8) | collective-permute-done | bytes 1327136 | tf_op jit(solution)/shard_map/attention_weights_first/ppermute | solution.py:702
  100.5 17.8 %collective-permute-done.16.refs_20_ = bf16[256,1536]{1,0:T(8,128)(2,1)S(1)} collective-permute-done((bf16[256,1536]{1,0:T(8,128)(2,1)}, bf16[256,1536]{1,0:T(8,128)(2,1)S(1)}, u32[]{:S(2)}, u32[]{:S(2)}) %collective-permute-start.16) | collective-permute-done | bytes 786464 | tf_op jit(solution)/shard_map/tokens_z/ppermute | solution.py:699
  119.8 2.6 collective-permute-done.20.refs_16_
  123.5 19.7 %project.1 = (bf16[1536,256]{1,0:T(8,128)(2,1)}, bf16[768,1024]{1,0:T(8,128)(2,1)}, bf16[768,1024]{1,0:T(8,128)(2,1)}, bf16[1536,1024]{1,0:T(8,128)(2,1)}, bf16[1536,4608]{1,0:T(8,128)(2,1)}) custom-call(s32[32]{0:T(128)} %broadcast_multiply_fusion.1.refs_0_, bf16[1,48,4608]{2,1,0:T(8,128)(2,1)} %get-tuple-element.255.refs_1_, ...), custom_call_target="tpu_custom_call" | custom-call | flops 100000000 | bytes 300000 | tf_op jit(solution)/shard_map/project/pallas_call | solution.py:332
  145.5 14.4 %attention_forward.1 = (bf16[1536,256]{1,0:T(8,128)(2,1)}, f32[8,2,256]{2,1,0:T(2,128)}) custom-call(bf16[1536,256]{1,0:T(8,128)(2,1)} %get-tuple-element.135.q_ref, bf16[768,1024]{1,0:T(8,128)(2,1)} %get-tuple-element.136.k_ref, bf16[768,1024]{1,0:T(8,128)(2,1)} %get-tuple-element.137.v_ref, f32[1024,256]{1,0:T(8,128)} %and_select_fusion.bias_ref), custom_call_target="tpu_custom_call" | custom-call | flops 100000000 | bytes 300000 | tf_op jit(solution)/shard_map/attention_forward/pallas_call | solution.py:134
  159.9 4.1 multiply_reduce_fusion
  167.0 10.2 %collective-permute-done.22 = bf16[256,1536]{1,0:T(8,128)(2,1)S(1)} collective-permute-done((bf16[256,1536]{1,0:T(8,128)(2,1)S(1)}, bf16[256,1536]{1,0:T(8,128)(2,1)S(1)}, u32[]{:S(2)}, u32[]{:S(2)}) %collective-permute-start.22) | collective-permute-done | bytes 786464 | tf_op jit(solution)/shard_map/normed_first/ppermute | solution.py:702
  178.9 19.0 %collective-permute-done.23.refs_1_ = bf16[512,1536]{1,0:T(8,128)(2,1)} collective-permute-done((bf16[512,1536]{1,0:T(8,128)(2,1)S(1)}, bf16[512,1536]{1,0:T(8,128)(2,1)}, u32[]{:S(2)}, u32[]{:S(2)}) %collective-permute-start.23) | collective-permute-done | bytes 1572896 | tf_op jit(solution)/shard_map/normed_second/ppermute | solution.py:705
  197.9 7.5 %all-gather.3.cloned.1.call-done = bf16[1536,1536]{1,0:T(8,128)(2,1)} async-done(((bf16[384,1536]{1,0:T(8,128)(2,1)}), bf16[1536,1536]{1,0:T(8,128)(2,1)}) %all-gather.3.cloned.1.call-update) | async-done | bytes 4718608 | tf_op jit(solution)/shard_map/gate_up_down_z/all_gather | solution.py:858
  205.4 3.7 collective-permute-done.25.refs_1_.refs_3_
  209.1 17.2 %feed_forward.3 = (bf16[1024,1536]{1,0:T(8,128)(2,1)}, bf16[1024,512]{1,0:T(8,128)(2,1)}, bf16[1024,1024]{1,0:T(8,128)(2,1)}, bf16[512,1536]{1,0:T(8,128)(2,1)}, bf16[512,1536]{1,0:T(8,128)(2,1)}) custom-call(bf16[512,1536]{1,0:T(8,128)(2,1)} %collective-permute-done.24.refs_0_.refs_2_, bf16[512,1536]{1,0:T(8,128)(2,1)} %collective-permute-done.25.refs_1_.refs_3_, ...), custom_call_target="tpu_custom_call" | custom-call | flops 30000001024 | bytes 90000000 | tf_op jit(solution)/shard_map/feed_forward/pallas_call | solution.py:437
  226.6 17.3 %feed_forward.2 = (bf16[1024,1536]{1,0:T(8,128)(2,1)}, bf16[1024,512]{1,0:T(8,128)(2,1)}, bf16[1024,1024]{1,0:T(8,128)(2,1)}, bf16[512,1536]{1,0:T(8,128)(2,1)}, bf16[512,1536]{1,0:T(8,128)(2,1)}) custom-call(bf16[512,1536]{1,0:T(8,128)(2,1)} %copy-done.33, bf16[512,1536]{1,0:T(8,128)(2,1)} %collective-permute-done.23.refs_1_, ...), custom_call_target="tpu_custom_call" | custom-call | flops 30000001024 | bytes 90000000 | tf_op jit(solution)/shard_map/feed_forward/pallas_call | solution.py:437
  245.9 2.6 add_half.17
  251.4 10.2 %feed_terms.1 = (bf16[1536,1536]{1,0:T(8,128)(2,1)}, f32[8,128]{1,0:T(8,128)S(1)}) custom-call(bf16[512,1536]{1,0:T(8,128)(2,1)S(1)} %copy-done.34, bf16[512,1536]{1,0:T(8,128)(2,1)} %collective-permute-done.23.refs_1_, bf16[512,1536]{1,0:T(8,128)(2,1)} %collective-permute-done.24.refs_0_.refs_2_, bf16[512,1536]{1,0:T(8,128)(2,1)} %collective-permute-done.25.refs_1_.refs_3_, ...), custom_call_target="tpu_custom_call" | custom-call | flops 15000000512 | bytes 45000000 | tf_op jit(solution)/shard_map/feed_sum_z/feed_terms/pallas_call | solution.py:509
  265.4 3.8 collective-permute-done.29
  269.2 2.0 add_half.19
  274.1 9.4 %collective-permute-done.30.far_ref = bf16[256,1536]{1,0:T(8,128)(2,1)} collective-permute-done((bf16[256,1536]{1,0:T(8,128)(2,1)}, bf16[256,1536]{1,0:T(8,128)(2,1)}, u32[]{:S(2)}, u32[]{:S(2)}) %collective-permute-start.30) | collective-permute-done | bytes 786464 | tf_op jit(solution)/shard_map/scaled_first/ppermute | solution.py:702
  283.5 6.2 %middle_gradient.1 = (f32[256,1536]{1,0:T(8,128)S(1)}, bf16[256,1536]{1,0:T(8,128)(2,1)S(1)}, bf16[1536,256]{1,0:T(8,128)(2,1)S(1)}) custom-call(bf16[256,1536]{1,0:T(8,128)(2,1)S(1)} %add_half.18.near_ref, bf16[256,1536]{1,0:T(8,128)(2,1)} %collective-permute-done.30.far_ref, f32[256,1536]{1,0:T(8,128)S(1)} %get-tuple-element.263.resid_ref, ...), custom_call_target="tpu_custom_call" | custom-call | flops 100000000 | bytes 300000 | tf_op jit(solution)/shard_map/middle_gradient/pallas_call | solution.py:610
  290.8 3.6 owned_terms.2
  294.5 4.5 collective-permute-done.31
  301.8 17.6 %attention_backward.1 = (bf16[1536,256]{1,0:T(8,128)(2,1)S(1)}, bf16[2,768,1024]{2,1,0:T(8,128)(2,1)S(1)}, bf16[4,2,768,256]{3,2,1,0:T(8,128)(2,1)S(1)}) custom-call(s32[1]{0:T(128)} %bitcast.place_ref, bf16[1536,256]{1,0:T(8,128)(2,1)S(1)} %copy-done.26, bf16[768,1024]{1,0:T(8,128)(2,1)S(1)} %copy-done.13, bf16[768,1024]{1,0:T(8,128)(2,1)S(1)} %copy-done.14, ...), custom_call_target="tpu_custom_call" | custom-call | flops 100000000 | bytes 300000 | tf_op jit(solution)/shard_map/attention_backward/pallas_call | solution.py:164
  323.9 12.2 %owned_terms.3 = (bf16[4,4,48,3072]{3,2,1,0:T(8,128)(2,1)}, bf16[4,4,48,3072]{3,2,1,0:T(8,128)(2,1)}) custom-call(s32[8]{0:T(128)S(1)} %stack.183.refs_0_, bf16[1536,1024]{1,0:T(8,128)(2,1)S(1)} %copy-done.24, bf16[1536,256]{1,0:T(8,128)(2,1)S(1)} %get-tuple-element.166.refs_2_.query_ref, bf16[1536,1024]{1,0:T(8,128)(2,1)S(1)} %bitcast.180), custom_call_target="tpu_custom_call" | custom-call | flops 100000000 | bytes 300000 | tf_op jit(solution)/shard_map/projected_core/owned_terms/pallas_call | solution.py:260
  337.0 8.2 %collective-permute-done.34 = bf16[4,4,48,3072]{3,2,1,0:T(8,128)(2,1)} collective-permute-done((bf16[4,4,48,3072]{3,2,1,0:T(8,128)(2,1)}, bf16[4,4,48,3072]{3,2,1,0:T(8,128)(2,1)}, u32[]{:S(2)}, u32[]{:S(2)}) %collective-permute-start.34) | collective-permute-done | bytes 4718624 | tf_op jit(solution)/shard_map/projected_core/ppermute | solution.py:708
  345.2 3.2 convolution_convert_fusion
  348.6 2.0 add_half.24
  357.2 22.4 %collective-permute-done.35 = bf16[2,4,48,3072]{3,2,1,0:T(8,128)(2,1)S(1)} collective-permute-done((bf16[2,4,48,3072]{3,2,1,0:T(8,128)(2,1)S(1)}, bf16[2,4,48,3072]{3,2,1,0:T(8,128)(2,1)S(1)}, u32[]{:S(2)}, u32[]{:S(2)}) %collective-permute-start.35) | collective-permute-done | bytes 2359328 | tf_op jit(solution)/shard_map/projected_second/ppermute | solution.py:705
  381.0 1.9 add_half.23
  387.1 2.1 slice.16
  389.2 4.2 all-to-all-start.1
  396.4 2.0 collective-permute-start.41
  400.9 1.9 copy-done.5
  402.8 1.9 copy-done.7
  407.7 12.9 %collective-permute-done.40.refs_6_ = bf16[48,1536]{1,0:T(8,128)(2,1)} collective-permute-done((bf16[48,1536]{1,0:T(8,128)(2,1)}, bf16[48,1536]{1,0:T(8,128)(2,1)}, u32[]{:S(2)}, u32[]{:S(2)}) %collective-permute-start.40) | collective-permute-done | bytes 147488 | tf_op jit(solution)/shard_map/out_z/ppermute | solution.py:699
  428.4 2.0 collective-permute-start.45
  432.0 9.9 %input_gradient.1 = bf16[256,1536]{1,0:T(8,128)(2,1)} custom-call(bf16[1536,256]{1,0:T(8,128)(2,1)S(1)} %copy-done.21, bf16[1536,256]{1,0:T(8,128)(2,1)S(1)} %bitcast.186, bf16[1536,4608]{1,0:T(8,128)(2,1)} %get-tuple-element.140.weight_ref, bf16[256,1536]{1,0:T(8,128)(2,1)S(1)} %bitcast.176, f32[256,1536]{1,0:T(8,128)S(1)} %copy-done.32), custom_call_target="tpu_custom_call" | custom-call | flops 100000000 | bytes 300000 | tf_op jit(solution)/shard_map/input_gradient/pallas_call | solution.py:654
  441.9 2.8 feed_finish.1
  445.9 7.3 %collective-permute-done.44.refs_2_ = bf16[48,3072]{1,0:T(8,128)(2,1)S(1)} collective-permute-done((bf16[48,3072]{1,0:T(8,128)(2,1)S(1)}, bf16[48,3072]{1,0:T(8,128)(2,1)S(1)}, u32[]{:S(2)}, u32[]{:S(2)}) %collective-permute-start.44) | collective-permute-done | bytes 294944 | tf_op jit(solution)/shard_map/projected_z/ppermute | solution.py:699
  453.3 2.3 attention_finish.1
  (278 shorter events, 88.1 us)
Async XLA Ops:
  11.6 16.4 %collective-permute-start = (bf16[48,4608]{1,0:T(8,128)(2,1)}, bf16[48,4608]{1,0:T(8,128)(2,1)}, u32[]{:S(2)}, u32[]{:S(2)}) collective-permute-start(bf16[48,4608]{1,0:T(8,128)(2,1)} %get-tuple-element.254), channel_id=1, source_target_pairs={{0,8},{8,16},{16,24},{24,0},{1,9},{9,17},{17,25},{25,1},{2,10},{10... | collective-permute-start | bytes 1327112 | tf_op jit(solution)/shard_map/attention_weights_z/ppermute | solution.py:699
  14.6 23.4 %collective-permute-start.4 = (bf16[48,4608]{1,0:T(8,128)(2,1)}, bf16[48,4608]{1,0:T(8,128)(2,1)}, u32[]{:S(2)}, u32[]{:S(2)}) collective-permute-start(bf16[48,4608]{1,0:T(8,128)(2,1)} %get-tuple-element.254), channel_id=1, source_target_pairs={{0,4},{1,3},{2,6},{3,1},{4,0},{5,7},{6,2},{7,5},{8,12},{9,11},{10,... | collective-permute-start | bytes 1327112 | tf_op jit(solution)/shard_map/attention_weights_own/ppermute | solution.py:702
  16.1 38.5 %collective-permute-start.6 = (bf16[256,1536]{1,0:T(8,128)(2,1)S(1)}, bf16[256,1536]{1,0:T(8,128)(2,1)}, u32[]{:S(2)}, u32[]{:S(2)}) collective-permute-start(bf16[256,1536]{1,0:T(8,128)(2,1)S(1)} %bitcast.175), channel_id=1, source_target_pairs={{0,8},{8,16},{16,24},{24,0},{1,9},{9,17},{17,25},{25,1},{2,10},{10... | collective-permute-start | bytes 2359304 | tf_op jit(solution)/shard_map/tokens_z/ppermute | solution.py:699
  17.7 36.9 %collective-permute-start.7 = (bf16[256,1536]{1,0:T(8,128)(2,1)S(1)}, bf16[256,1536]{1,0:T(8,128)(2,1)S(1)}, u32[]{:S(2)}, u32[]{:S(2)}) collective-permute-start(bf16[256,1536]{1,0:T(8,128)(2,1)S(1)} %bitcast.177), channel_id=1, source_target_pairs={{0,4},{1,3},{2,6},{3,1},{4,0},{5,7},{6,2},{7,5},{8,12},{9,11},{10,... | collective-permute-start | bytes 2359304 | tf_op jit(solution)/shard_map/out_grad_first/ppermute | solution.py:702
  28.0 25.5 %collective-permute-start.1 = (bf16[48,4608]{1,0:T(8,128)(2,1)}, bf16[48,4608]{1,0:T(8,128)(2,1)}, u32[]{:S(2)}, u32[]{:S(2)}) collective-permute-start(bf16[48,4608]{1,0:T(8,128)(2,1)} %collective-permute-done), channel_id=1, source_target_pairs={{0,8},{8,16},{16,24},{24,0},{1,9},{9,17},{17,25},{25,1},{2,10},{10... | collective-permute-start | bytes 1327112 | tf_op jit(solution)/shard_map/attention_weights_z/ppermute | solution.py:699
  32.0 22.6 %all-to-all-start = ((bf16[8,48,1024]{2,1,0:T(8,128)(2,1)}), bf16[8,48,1024]{2,1,0:T(8,128)(2,1)S(1)}, u32[]{:S(2)}, u32[]{:S(2)}) async-start(bf16[8,48,1024]{2,1,0:T(8,128)(2,1)} %reshape.261), calls=%async_computation | async-start | bytes 1572864 | tf_op jit(solution)/shard_map/gate_up_f/all_to_all | solution.py:804
  35.9 169.5 %all-gather.3.cloned.1.call-start = ((), (), s32[]{:S(2)}) async-start(), calls=%async_computation.6 | async-start | bytes 5898240 | tf_op jit(solution)/shard_map/gate_up_down_z/all_gather | solution.py:858
  36.0 18.5 %collective-permute-start.3 = (bf16[48,4608]{1,0:T(8,128)(2,1)}, bf16[48,4608]{1,0:T(8,128)(2,1)}, u32[]{:S(2)}, u32[]{:S(2)}) collective-permute-start(bf16[48,4608]{1,0:T(8,128)(2,1)} %get-tuple-element.254), channel_id=1, source_target_pairs={{0,2},{1,5},{2,0},{3,7},{4,6},{5,1},{6,4},{7,3},{8,10},{9,13},{10,... | collective-permute-start | bytes 1327112 | tf_op jit(solution)/shard_map/attention_weights_own/ppermute | solution.py:705
  38.0 19.2 %collective-permute-start.5 = (bf16[48,4608]{1,0:T(8,128)(2,1)}, bf16[48,4608]{1,0:T(8,128)(2,1)}, u32[]{:S(2)}, u32[]{:S(2)}) collective-permute-start(bf16[48,4608]{1,0:T(8,128)(2,1)} %collective-permute-done.4), channel_id=1, source_target_pairs={{0,2},{1,5},{2,0},{3,7},{4,6},{5,1},{6,4},{7,3},{8,10},{9,13},{10,... | collective-permute-start | bytes 1327112 | tf_op jit(solution)/shard_map/attention_weights_own/ppermute | solution.py:705
  53.5 13.5 %collective-permute-start.2 = (bf16[48,4608]{1,0:T(8,128)(2,1)}, bf16[48,4608]{1,0:T(8,128)(2,1)}, u32[]{:S(2)}, u32[]{:S(2)}) collective-permute-start(bf16[48,4608]{1,0:T(8,128)(2,1)} %collective-permute-done.1), channel_id=1, source_target_pairs={{0,8},{8,16},{16,24},{24,0},{1,9},{9,17},{17,25},{25,1},{2,10},{10... | collective-permute-start | bytes 1327112 | tf_op jit(solution)/shard_map/attention_weights_z/ppermute | solution.py:699
  54.5 22.2 %collective-permute-start.11 = (bf16[48,4608]{1,0:T(8,128)(2,1)}, bf16[48,4608]{1,0:T(8,128)(2,1)}, u32[]{:S(2)}, u32[]{:S(2)}) collective-permute-start(bf16[48,4608]{1,0:T(8,128)(2,1)} %get-tuple-element.254), channel_id=1, source_target_pairs={{0,1},{1,0},{2,3},{3,2},{4,5},{5,4},{6,7},{7,6},{8,9},{9,8},{10,11... | collective-permute-start | bytes 1327112 | tf_op jit(solution)/shard_map/attention_weights_core/ppermute | solution.py:708
  68.4 30.3 %collective-permute-start.8 = (bf16[3,48,4608]{2,1,0:T(8,128)(2,1)S(1)}, bf16[3,48,4608]{2,1,0:T(8,128)(2,1)}, u32[]{:S(2)}, u32[]{:S(2)}) collective-permute-start(bf16[3,48,4608]{2,1,0:T(8,128)(2,1)S(1)} %pad_maximum_fusion.2.refs_2_), channel_id=1, source_target_pairs={{0,4},{1,3},{2,6},{3,1},{4,0},{5,7},{6,2},{7,5},{8,12},{9,11},{10,... | collective-permute-start | bytes 3981320 | tf_op jit(solution)/shard_map/attention_weights_first/ppermute | solution.py:702
  69.7 28.9 %collective-permute-start.9 = (bf16[3,48,4608]{2,1,0:T(8,128)(2,1)S(1)}, bf16[3,48,4608]{2,1,0:T(8,128)(2,1)}, u32[]{:S(2)}, u32[]{:S(2)}) collective-permute-start(bf16[3,48,4608]{2,1,0:T(8,128)(2,1)S(1)} %pad_maximum_fusion.2.refs_2_), channel_id=1, source_target_pairs={{0,2},{1,5},{2,0},{3,7},{4,6},{5,1},{6,4},{7,3},{8,10},{9,13},{10,... | collective-permute-start | bytes 3981320 | tf_op jit(solution)/shard_map/attention_weights_second/ppermute | solution.py:705
  71.4 5.8 %collective-permute-start.12 = (bf16[48,4608]{1,0:T(8,128)(2,1)}, bf16[48,4608]{1,0:T(8,128)(2,1)}, u32[]{:S(2)}, u32[]{:S(2)}) collective-permute-start(bf16[48,4608]{1,0:T(8,128)(2,1)} %collective-permute-done.4), channel_id=1, source_target_pairs={{0,1},{1,0},{2,3},{3,2},{4,5},{5,4},{6,7},{7,6},{8,9},{9,8},{10,11... | collective-permute-start | bytes 1327112 | tf_op jit(solution)/shard_map/attention_weights_core/ppermute | solution.py:708
  71.5 22.1 %collective-permute-start.10 = (bf16[256,1536]{1,0:T(8,128)(2,1)}, bf16[256,1536]{1,0:T(8,128)(2,1)}, u32[]{:S(2)}, u32[]{:S(2)}) collective-permute-start(bf16[256,1536]{1,0:T(8,128)(2,1)} %collective-permute-done.6.refs_18_), channel_id=1, source_target_pairs={{0,8},{8,16},{16,24},{24,0},{1,9},{9,17},{17,25},{25,1},{2,10},{10... | collective-permute-start | bytes 2359304 | tf_op jit(solution)/shard_map/tokens_z/ppermute | solution.py:699
  98.7 19.6 %collective-permute-start.16 = (bf16[256,1536]{1,0:T(8,128)(2,1)}, bf16[256,1536]{1,0:T(8,128)(2,1)S(1)}, u32[]{:S(2)}, u32[]{:S(2)}) collective-permute-start(bf16[256,1536]{1,0:T(8,128)(2,1)} %collective-permute-done.10.refs_19_), channel_id=1, source_target_pairs={{0,8},{8,16},{16,24},{24,0},{1,9},{9,17},{17,25},{25,1},{2,10},{10... | collective-permute-start | bytes 2359304 | tf_op jit(solution)/shard_map/tokens_z/ppermute | solution.py:699
  98.7 19.7 %collective-permute-start.17 = (bf16[3,48,4608]{2,1,0:T(8,128)(2,1)S(1)}, bf16[3,48,4608]{2,1,0:T(8,128)(2,1)}, u32[]{:S(2)}, u32[]{:S(2)}) collective-permute-start(bf16[3,48,4608]{2,1,0:T(8,128)(2,1)S(1)} %pad_maximum_fusion.2.refs_2_), channel_id=1, source_target_pairs={{0,1},{1,0},{2,3},{3,2},{4,5},{5,4},{6,7},{7,6},{8,9},{9,8},{10,11... | collective-permute-start | bytes 3981320 | tf_op jit(solution)/shard_map/attention_weights_core/ppermute | solution.py:708
  98.7 19.6 %collective-permute-start.15 = (bf16[3,48,4608]{2,1,0:T(8,128)(2,1)}, bf16[3,48,4608]{2,1,0:T(8,128)(2,1)}, u32[]{:S(2)}, u32[]{:S(2)}) collective-permute-start(bf16[3,48,4608]{2,1,0:T(8,128)(2,1)} %collective-permute-done.8.refs_4_), channel_id=1, source_target_pairs={{0,2},{1,5},{2,0},{3,7},{4,6},{5,1},{6,4},{7,3},{8,10},{9,13},{10,... | collective-permute-start | bytes 3981320 | tf_op jit(solution)/shard_map/attention_weights_second/ppermute | solution.py:705
  99.8 18.5 %collective-permute-start.18 = (bf16[3,48,4608]{2,1,0:T(8,128)(2,1)}, bf16[3,48,4608]{2,1,0:T(8,128)(2,1)}, u32[]{:S(2)}, u32[]{:S(2)}) collective-permute-start(bf16[3,48,4608]{2,1,0:T(8,128)(2,1)} %collective-permute-done.8.refs_4_), channel_id=1, source_target_pairs={{0,1},{1,0},{2,3},{3,2},{4,5},{5,4},{6,7},{7,6},{8,9},{9,8},{10,11... | collective-permute-start | bytes 3981320 | tf_op jit(solution)/shard_map/attention_weights_core/ppermute | solution.py:708
  100.5 18.7 %collective-permute-start.19 = (bf16[3,48,4608]{2,1,0:T(8,128)(2,1)}, bf16[3,48,4608]{2,1,0:T(8,128)(2,1)}, u32[]{:S(2)}, u32[]{:S(2)}) collective-permute-start(bf16[3,48,4608]{2,1,0:T(8,128)(2,1)} %collective-permute-done.9.refs_6_), channel_id=1, source_target_pairs={{0,1},{1,0},{2,3},{3,2},{4,5},{5,4},{6,7},{7,6},{8,9},{9,8},{10,11... | collective-permute-start | bytes 3981320 | tf_op jit(solution)/shard_map/attention_weights_core/ppermute | solution.py:708
  118.3 268.8 %reduce-scatter.5.cloned.1.call-start = ((), (), s32[]{:S(2)}) async-start(), calls=%async_computation.5 | async-start | bytes 5898240 | tf_op jit(solution)/shard_map/feed_sum_z/reduce_scatter | solution.py:948
  144.5 20.7 %collective-permute-start.21 = (bf16[512,1536]{1,0:T(8,128)(2,1)}, bf16[512,1536]{1,0:T(8,128)(2,1)}, u32[]{:S(2)}, u32[]{:S(2)}) collective-permute-start(bf16[512,1536]{1,0:T(8,128)(2,1)} %pad_maximum_fusion.refs_2_), channel_id=1, source_target_pairs={{0,2},{1,5},{2,0},{3,7},{4,6},{5,1},{6,4},{7,3},{8,10},{9,13},{10,... | collective-permute-start | bytes 4718600 | tf_op jit(solution)/shard_map/out_grad_second/ppermute | solution.py:705
  165.2 12.0 %collective-permute-start.22 = (bf16[256,1536]{1,0:T(8,128)(2,1)S(1)}, bf16[256,1536]{1,0:T(8,128)(2,1)S(1)}, u32[]{:S(2)}, u32[]{:S(2)}) collective-permute-start(bf16[256,1536]{1,0:T(8,128)(2,1)S(1)} %multiply_convert_fusion), channel_id=1, source_target_pairs={{0,4},{1,3},{2,6},{3,1},{4,0},{5,7},{6,2},{7,5},{8,12},{9,11},{10,... | collective-permute-start | bytes 2359304 | tf_op jit(solution)/shard_map/normed_first/ppermute | solution.py:702
  177.3 20.6 %collective-permute-start.23 = (bf16[512,1536]{1,0:T(8,128)(2,1)S(1)}, bf16[512,1536]{1,0:T(8,128)(2,1)}, u32[]{:S(2)}, u32[]{:S(2)}) collective-permute-start(bf16[512,1536]{1,0:T(8,128)(2,1)S(1)} %pad_maximum_fusion.1.refs_0_), channel_id=1, source_target_pairs={{0,2},{1,5},{2,0},{3,7},{4,6},{5,1},{6,4},{7,3},{8,10},{9,13},{10,... | collective-permute-start | bytes 4718600 | tf_op jit(solution)/shard_map/normed_second/ppermute | solution.py:705
  178.4 27.0 %collective-permute-start.26 = (bf16[512,1536]{1,0:T(8,128)(2,1)}, bf16[512,1536]{1,0:T(8,128)(2,1)}, u32[]{:S(2)}, u32[]{:S(2)}) collective-permute-start(bf16[512,1536]{1,0:T(8,128)(2,1)} %pad_maximum_fusion.refs_2_), channel_id=1, source_target_pairs={{0,1},{1,0},{2,3},{3,2},{4,5},{5,4},{6,7},{7,6},{8,9},{9,8},{10,11... | collective-permute-start | bytes 4718600 | tf_op jit(solution)/shard_map/out_grad_all/ppermute | solution.py:708
  178.4 27.0 %collective-permute-start.27 = (bf16[512,1536]{1,0:T(8,128)(2,1)}, bf16[512,1536]{1,0:T(8,128)(2,1)}, u32[]{:S(2)}, u32[]{:S(2)}) collective-permute-start(bf16[512,1536]{1,0:T(8,128)(2,1)} %collective-permute-done.21.refs_3_), channel_id=1, source_target_pairs={{0,1},{1,0},{2,3},{3,2},{4,5},{5,4},{6,7},{7,6},{8,9},{9,8},{10,11... | collective-permute-start | bytes 4718600 | tf_op jit(solution)/shard_map/out_grad_all/ppermute | solution.py:708
  178.9 26.5 %collective-permute-start.24 = (bf16[512,1536]{1,0:T(8,128)(2,1)S(1)}, bf16[512,1536]{1,0:T(8,128)(2,1)}, u32[]{:S(2)}, u32[]{:S(2)}) collective-permute-start(bf16[512,1536]{1,0:T(8,128)(2,1)S(1)} %pad_maximum_fusion.1.refs_0_), channel_id=1, source_target_pairs={{0,1},{1,0},{2,3},{3,2},{4,5},{5,4},{6,7},{7,6},{8,9},{9,8},{10,11... | collective-permute-start | bytes 4718600 | tf_op jit(solution)/shard_map/normed_second/ppermute | solution.py:708
  205.4 3.8 collective-permute-start.25
  226.4 17.6 %collective-permute-start.28 = (bf16[1024,1536]{1,0:T(8,128)(2,1)}, bf16[1024,1536]{1,0:T(8,128)(2,1)}, u32[]{:S(2)}, u32[]{:S(2)}) collective-permute-start(bf16[1024,1536]{1,0:T(8,128)(2,1)} %get-tuple-element.148), channel_id=1, source_target_pairs={{0,1},{1,0},{2,3},{3,2},{4,5},{5,4},{6,7},{7,6},{8,9},{9,8},{10,11... | collective-permute-start | bytes 9437192 | tf_op jit(solution)/shard_map/scaled_core/ppermute | solution.py:708
  248.5 20.7 %collective-permute-start.29 = (bf16[512,1536]{1,0:T(8,128)(2,1)}, bf16[512,1536]{1,0:T(8,128)(2,1)}, u32[]{:S(2)}, u32[]{:S(2)}) collective-permute-start(bf16[512,1536]{1,0:T(8,128)(2,1)} %add_half.17), channel_id=1, source_target_pairs={{0,2},{1,5},{2,0},{3,7},{4,6},{5,1},{6,4},{7,3},{8,10},{9,13},{10,... | collective-permute-start | bytes 4718600 | tf_op jit(solution)/shard_map/scaled_second/ppermute | solution.py:705
  261.7 160.3 %reduce-scatter.3.cloned.1.call-start = ((), (), s32[]{:S(2)}) async-start(), calls=%async_computation.4 | async-start | bytes 3932160 | tf_op jit(solution)/shard_map/kv_grad_z/reduce_scatter | solution.py:989
  271.2 12.3 %collective-permute-start.30 = (bf16[256,1536]{1,0:T(8,128)(2,1)}, bf16[256,1536]{1,0:T(8,128)(2,1)}, u32[]{:S(2)}, u32[]{:S(2)}) collective-permute-start(bf16[256,1536]{1,0:T(8,128)(2,1)} %add_half.19), channel_id=1, source_target_pairs={{0,4},{1,3},{2,6},{3,1},{4,0},{5,7},{6,2},{7,5},{8,12},{9,11},{10,... | collective-permute-start | bytes 2359304 | tf_op jit(solution)/shard_map/scaled_first/ppermute | solution.py:702
  294.4 4.6 collective-permute-start.31
  299.4 21.7 %collective-permute-start.32 = (bf16[2,4,48,1536]{3,2,1,0:T(8,128)(2,1)S(1)}, bf16[2,4,48,1536]{3,2,1,0:T(8,128)(2,1)S(1)}, u32[]{:S(2)}, u32[]{:S(2)}) collective-permute-start(bf16[2,4,48,1536]{3,2,1,0:T(8,128)(2,1)S(1)} %bitcast.185), channel_id=1, source_target_pairs={{0,2},{1,5},{2,0},{3,7},{4,6},{5,1},{6,4},{7,3},{8,10},{9,13},{10,... | collective-permute-start | bytes 3538952 | tf_op jit(solution)/shard_map/out_second/ppermute | solution.py:705
  322.4 13.7 %collective-permute-start.33 = (bf16[1,4,48,1536]{3,2,1,0:T(8,128)(2,1)S(1)}, bf16[1,4,48,1536]{3,2,1,0:T(8,128)(2,1)S(1)}, u32[]{:S(2)}, u32[]{:S(2)}) collective-permute-start(bf16[1,4,48,1536]{3,2,1,0:T(8,128)(2,1)S(1)} %bitcast.187), channel_id=1, source_target_pairs={{0,4},{1,3},{2,6},{3,1},{4,0},{5,7},{6,2},{7,5},{8,12},{9,11},{10,... | collective-permute-start | bytes 1769480 | tf_op jit(solution)/shard_map/out_first/ppermute | solution.py:702
  337.0 8.3 %collective-permute-start.34 = (bf16[4,4,48,3072]{3,2,1,0:T(8,128)(2,1)}, bf16[4,4,48,3072]{3,2,1,0:T(8,128)(2,1)}, u32[]{:S(2)}, u32[]{:S(2)}) collective-permute-start(bf16[4,4,48,3072]{3,2,1,0:T(8,128)(2,1)} %get-tuple-element.172), channel_id=1, source_target_pairs={{0,1},{1,0},{2,3},{3,2},{4,5},{5,4},{6,7},{7,6},{8,9},{9,8},{10,11... | collective-permute-start | bytes 14155784 | tf_op jit(solution)/shard_map/projected_core/ppermute | solution.py:708
  348.4 5.7 %collective-permute-start.36 = (bf16[1024,1536]{1,0:T(8,128)(2,1)S(1)}, bf16[1024,1536]{1,0:T(8,128)(2,1)S(1)}, u32[]{:S(2)}, u32[]{:S(2)}) collective-permute-start(bf16[1024,1536]{1,0:T(8,128)(2,1)S(1)} %convolution_convert_fusion), channel_id=1, source_target_pairs={{0,1},{1,0},{2,3},{3,2},{4,5},{5,4},{6,7},{7,6},{8,9},{9,8},{10,11... | collective-permute-start | bytes 9437192 | tf_op jit(solution)/shard_map/result_core/ppermute | solution.py:708
  350.6 28.9 %collective-permute-start.35 = (bf16[2,4,48,3072]{3,2,1,0:T(8,128)(2,1)S(1)}, bf16[2,4,48,3072]{3,2,1,0:T(8,128)(2,1)S(1)}, u32[]{:S(2)}, u32[]{:S(2)}) collective-permute-start(bf16[2,4,48,3072]{3,2,1,0:T(8,128)(2,1)S(1)} %bitcast.182), channel_id=1, source_target_pairs={{0,2},{1,5},{2,0},{3,7},{4,6},{5,1},{6,4},{7,3},{8,10},{9,13},{10,... | collective-permute-start | bytes 7077896 | tf_op jit(solution)/shard_map/projected_second/ppermute | solution.py:705
  379.5 42.4 %collective-permute-start.38 = (bf16[512,1536]{1,0:T(8,128)(2,1)}, bf16[512,1536]{1,0:T(8,128)(2,1)}, u32[]{:S(2)}, u32[]{:S(2)}) collective-permute-start(bf16[512,1536]{1,0:T(8,128)(2,1)} %add_half.25), channel_id=1, source_target_pairs={{0,2},{1,5},{2,0},{3,7},{4,6},{5,1},{6,4},{7,3},{8,10},{9,13},{10,... | collective-permute-start | bytes 4718600 | tf_op jit(solution)/shard_map/result_second/ppermute | solution.py:705
  384.2 37.8 %collective-permute-start.37 = (bf16[1,4,48,3072]{3,2,1,0:T(8,128)(2,1)}, bf16[1,4,48,3072]{3,2,1,0:T(8,128)(2,1)}, u32[]{:S(2)}, u32[]{:S(2)}) collective-permute-start(bf16[1,4,48,3072]{3,2,1,0:T(8,128)(2,1)} %bitcast.83), channel_id=1, source_target_pairs={{0,4},{1,3},{2,6},{3,1},{4,0},{5,7},{6,2},{7,5},{8,12},{9,11},{10,... | collective-permute-start | bytes 3538952 | tf_op jit(solution)/shard_map/projected_first/ppermute | solution.py:702
  389.2 32.8 %all-to-all-start.1 = ((bf16[8,48,1024]{2,1,0:T(8,128)(2,1)}), bf16[8,48,1024]{2,1,0:T(8,128)(2,1)}, u32[]{:S(2)}, u32[]{:S(2)}) async-start(bf16[8,48,1024]{2,1,0:T(8,128)(2,1)} %bitcast.189), calls=%async_computation.3 | async-start | bytes 1572864 | tf_op jit(solution)/shard_map/gate_up_sum_f/all_to_all | solution.py:1012
  395.5 12.2 %collective-permute-start.39 = (bf16[48,1536]{1,0:T(8,128)(2,1)}, bf16[48,1536]{1,0:T(8,128)(2,1)}, u32[]{:S(2)}, u32[]{:S(2)}) collective-permute-start(bf16[48,1536]{1,0:T(8,128)(2,1)} %get-tuple-element.252), channel_id=1, source_target_pairs={{0,24},{8,0},{16,8},{24,16},{1,25},{9,1},{17,9},{25,17},{2,26},{10... | collective-permute-start | bytes 442376 | tf_op jit(solution)/shard_map/out_z/ppermute | solution.py:699
  396.4 24.2 %collective-permute-start.40 = (bf16[48,1536]{1,0:T(8,128)(2,1)}, bf16[48,1536]{1,0:T(8,128)(2,1)}, u32[]{:S(2)}, u32[]{:S(2)}) collective-permute-start(bf16[48,1536]{1,0:T(8,128)(2,1)} %get-tuple-element.251), channel_id=1, source_target_pairs={{0,16},{8,24},{16,0},{24,8},{1,17},{9,25},{17,1},{25,9},{2,18},{10... | collective-permute-start | bytes 442376 | tf_op jit(solution)/shard_map/out_z/ppermute | solution.py:699
  396.4 24.2 %collective-permute-start.41 = (bf16[48,1536]{1,0:T(8,128)(2,1)}, bf16[48,1536]{1,0:T(8,128)(2,1)}, u32[]{:S(2)}, u32[]{:S(2)}) collective-permute-start(bf16[48,1536]{1,0:T(8,128)(2,1)} %get-tuple-element.250), channel_id=1, source_target_pairs={{0,8},{8,16},{16,24},{24,0},{1,9},{9,17},{17,25},{25,1},{2,10},{10... | collective-permute-start | bytes 442376 | tf_op jit(solution)/shard_map/out_z/ppermute | solution.py:699
  424.6 20.1 %collective-permute-start.42 = (bf16[256,1536]{1,0:T(8,128)(2,1)S(1)}, bf16[256,1536]{1,0:T(8,128)(2,1)S(1)}, u32[]{:S(2)}, u32[]{:S(2)}) collective-permute-start(bf16[256,1536]{1,0:T(8,128)(2,1)S(1)} %add_half.30), channel_id=1, source_target_pairs={{0,4},{1,3},{2,6},{3,1},{4,0},{5,7},{6,2},{7,5},{8,12},{9,11},{10,... | collective-permute-start | bytes 2359304 | tf_op jit(solution)/shard_map/result_first/ppermute | solution.py:702
  427.3 18.6 %collective-permute-start.43 = (bf16[48,3072]{1,0:T(8,128)(2,1)S(1)}, bf16[48,3072]{1,0:T(8,128)(2,1)S(1)}, u32[]{:S(2)}, u32[]{:S(2)}) collective-permute-start(bf16[48,3072]{1,0:T(8,128)(2,1)S(1)} %get-tuple-element.248), channel_id=1, source_target_pairs={{0,24},{8,0},{16,8},{24,16},{1,25},{9,1},{17,9},{25,17},{2,26},{10... | collective-permute-start | bytes 884744 | tf_op jit(solution)/shard_map/projected_z/ppermute | solution.py:699
  428.3 25.0 %collective-permute-start.44 = (bf16[48,3072]{1,0:T(8,128)(2,1)S(1)}, bf16[48,3072]{1,0:T(8,128)(2,1)S(1)}, u32[]{:S(2)}, u32[]{:S(2)}) collective-permute-start(bf16[48,3072]{1,0:T(8,128)(2,1)S(1)} %get-tuple-element.247), channel_id=1, source_target_pairs={{0,16},{8,24},{16,0},{24,8},{1,17},{9,25},{17,1},{25,9},{2,18},{10... | collective-permute-start | bytes 884744 | tf_op jit(solution)/shard_map/projected_z/ppermute | solution.py:699
  428.4 24.8 %collective-permute-start.45 = (bf16[48,3072]{1,0:T(8,128)(2,1)S(1)}, bf16[48,3072]{1,0:T(8,128)(2,1)S(1)}, u32[]{:S(2)}, u32[]{:S(2)}) collective-permute-start(bf16[48,3072]{1,0:T(8,128)(2,1)S(1)} %get-tuple-element.246), channel_id=1, source_target_pairs={{0,8},{8,16},{16,24},{24,0},{1,9},{9,17},{17,25},{25,1},{2,10},{10... | collective-permute-start | bytes 884744 | tf_op jit(solution)/shard_map/projected_z/ppermute | solution.py:699
  (74 other events, 688.0 us)
Sparse Core Ops, SparseCore 0:
  118.4 86.9 all-gather.2
  261.8 83.7 reduce-scatter.4
  347.9 68.6 reduce-scatter.2

commit v5 on v4

--- a/solution.py
+++ b/solution.py
@@ -282,26 +282,32 @@
         pltpu.make_async_copy(block, token_ref.at[pl.ds(k * count, count)], token_sem.at[k])
         for k, block in enumerate(blocks)
     ]
-    part_copies = []
+    pair_cols = k_ref.shape[0]
+    middle, cols = width + 2 * pair_cols, weight_ref.shape[1]
+    early, late = [], []
     for part in parts:
         for j in range(part.shape[0]):
-            k = len(part_copies)
+            k = len(early)
             at = pl.multiple_of(starts_ref[k], 16)
-            part_copies.append(
-                pltpu.make_async_copy(part.at[j], weight_ref.at[pl.ds(at, rows)], part_sem.at[k])
-            )
-    for copy in token_copies + part_copies:
+            for copies, columns, sem in (
+                (early, slice(0, middle), part_sem.at[0, k]),
+                (late, slice(middle, cols), part_sem.at[1, k]),
+            ):
+                copies.append(
+                    pltpu.make_async_copy(
+                        part.at[j, :, columns], weight_ref.at[pl.ds(at, rows), columns], sem
+                    )
+                )
+    for copy in token_copies + early + late:
         copy.start()
     for k, copy in enumerate(token_copies):
         copy.wait()
         x = token_ref[k * count : (k + 1) * count, :].astype(F32)
         inverse = lax.rsqrt(jnp.mean(x * x, axis=-1, keepdims=True) + EPSILON)
         normed_ref[:, k * count : (k + 1) * count] = (x * inverse).astype(BF).T
-    for copy in part_copies:
+    for copy in early:
         copy.wait()
     out_copy = pltpu.make_async_copy(weight_ref, weight_out, out_sem)
-    out_copy.start()
-    pair_cols = k_ref.shape[0]
     tile = 4 * HEAD_SIZE
     for out_ref, base, rotated in ((q_ref, 0, True), (k_ref, width, True), (v_ref, width + pair_cols, False)):
         tokens = out_ref.shape[1]
@@ -319,6 +325,10 @@
             return carry
 
         lax.fori_loop(0, out_ref.shape[0] // tile, step, 0)
+        if out_ref is q_ref:
+            for copy in late:
+                copy.wait()
+            out_copy.start()
     out_copy.wait()
 
 
@@ -343,7 +353,7 @@
         scratch_shapes=[
             pltpu.VMEM(shape, BF),
             pltpu.VMEM((span, width), BF),
-            pltpu.SemaphoreType.DMA(starts.shape),
+            pltpu.SemaphoreType.DMA((2,) + starts.shape),
             pltpu.SemaphoreType.DMA((n,)),
             pltpu.SemaphoreType.DMA,
         ],
@@ -819,26 +829,29 @@
         with scope("attention_weights_own"):
             near = [shard, swap_first(shard), swap_second(shard)]
             near.append(swap_second(near[1]))
+            mid = [behind[0], swap_first(behind[0]), swap_second(behind[0])]
+            mid.append(swap_second(mid[1]))
         with scope("tokens_z"):
             blocks.append(shift(own, 1))
         with scope("out_grad_first"):
             grad_first = swap_first(grad_own)
-        *behind, near[2], near[3], gate_up, blocks[1], grad_first = stage(
-            *behind, near[2], near[3], gate_up, blocks[1], grad_first
+        *behind, near[2], near[3], mid[2], mid[3], gate_up, blocks[1], grad_first = stage(
+            *behind, near[2], near[3], mid[2], mid[3], gate_up, blocks[1], grad_first
         )
         gate_up_down = beside_down(gate_up)
         with scope("attention_weights_core"):
-            near_core = [swap_core(part) for part in near]
-        rest = [jnp.stack(behind)]
+            cores = [swap_core(part) for part in near + mid]
+        rest = [jnp.stack(behind[1:])]
         with scope("attention_weights_first"):
             rest.append(swap_first(rest[0]))
         with scope("attention_weights_second"):
             rest.append(swap_second(rest[0]))
         with scope("tokens_z"):
             blocks.append(shift(blocks[1], 1))
-        rest[1], rest[2], blocks[2], cosine, sine, bias, gate_up_down, *near_core = stage(
-            rest[1], rest[2], blocks[2], cosine, sine, bias, gate_up_down, *near_core
+        rest[1], rest[2], blocks[2], cosine, sine, bias, gate_up_down, *cores = stage(
+            rest[1], rest[2], blocks[2], cosine, sine, bias, gate_up_down, *cores
         )
+        near_core, mid_core = cores[:4], cores[4:]
         with scope("attention_weights_core"):
             rest_core = [swap_core(part) for part in rest]
         with scope("attention_weights_second"):
@@ -846,8 +859,9 @@
         with scope("tokens_z"):
             while len(blocks) < n:
                 blocks.append(shift(blocks[-1], 1))
-        gate_up_down, blocks[-1] = stage(gate_up_down, blocks[-1])
-        rest[3], blocks[-1], *rest_core = stage(rest[3], blocks[-1], *rest_core)
+        rest[3], blocks[-1], gate_up_down, *rest_core = stage(
+            rest[3], blocks[-1], gate_up_down, *rest_core
+        )
         with scope("attention_weights_core"):
             rest_core.append(swap_core(rest[3]))
     else:
@@ -861,12 +875,12 @@
     inputs = own.astype(F32)
     if grid:
         parts, starts = [], []
-        for near_parts, rest_parts, moves in (
-            (near, rest, (0, first, second, 6)),
-            (near_core, rest_core, (1, 1 ^ second, 1 ^ first, 7)),
+        for *held, moves in (
+            (near, mid, rest, (0, first, second, 6)),
+            (near_core, mid_core, rest_core, (1, 1 ^ second, 1 ^ first, 7)),
         ):
-            for near_part, rest_part, move in zip(near_parts, rest_parts, moves):
-                parts += [near_part[None], rest_part]
+            for near_part, mid_part, rest_part, move in zip(*held, moves):
+                parts += [near_part[None], mid_part[None], rest_part]
                 starts += [(at_z - k) % n * ranks + (rank ^ move) for k in range(n)]
         starts = jnp.stack(starts).astype(jnp.int32) * shard_rows
         queries, keys, values, normed_group, gathered = project(
@@ -912,8 +926,8 @@
         if grid:
             normed_pair = jnp.concatenate([normed_two, normed_first], axis=0)
         normed_other = spread_second(normed_pair)
-        normed_other, gate_up_down = stage(normed_other, gate_up_down)
         normed_parts = spread_all(normed_pair, normed_other)
+        normed_parts[1], gate_up_down = stage(normed_parts[1], gate_up_down)
     half = len(normed_parts) // 2
 
     scaled_far, hidden_far, both_far, down_far, down_weight = feed_forward(

time: 472 us -> 467 us (0.989)
  waiting for transfers between devices: 188 us -> 177 us
  starting transfers between devices: 44 us -> 49.9 us
    ppermute x10 -> x12, waiting for transfers between devices: 48.8 us -> 43.7 us  [swap_second(): return lax.ppermute(a, 'f', [(i, i ^ 2 << i % 2) for i in range(ranks)])]
    ppermute x10 -> x12, starting transfers between devices: 12.9 us -> 17.8 us  [swap_second(): return lax.ppermute(a, 'f', [(i, i ^ 2 << i % 2) for i in range(ranks)])]
    ppermute x16 -> x20, waiting for transfers between devices: 19.3 us -> 14.5 us  [swap_core(): return lax.ppermute(a, 'f', [(i, i ^ 1) for i in range(ranks)])]
    ppermute x8 -> x9, waiting for transfers between devices: 24.7 us -> 28.3 us  [swap_first(): return lax.ppermute(a, 'f', [(i, i ^ 4 >> i % 2) for i in range(ranks)])]
    ppermute x8 -> x9, starting transfers between devices: 9.69 us -> 10.5 us  [swap_first(): return lax.ppermute(a, 'f', [(i, i ^ 4 >> i % 2) for i in range(ranks)])]
    unnamed x144 -> x140, local copies, waits for them, and re-layouts: 26.5 us -> 26.3 us
  transfers between devices with their start and end apart: 51 -> 58, of which waited for: 23 -> 21; matrix products, arithmetic and copies ran while one was open for 8% -> 7% of each run, Pallas kernels for 28% -> 28%
where the time goes in v5:
time: 467 us; the launch traced here: 459 us
  waiting for transfers between devices  177 us (38%)
  Pallas kernels  154 us (33%)
  starting transfers between devices  49.9 us (11%)
  local copies, waits for them, and re-layouts  34 us (7%)
  other arithmetic  18.7 us (4%)
  between operations  15.3 us (3%)
  matrix products  10.7 us (2%)
    ppermute x12, waiting for transfers between devices, shift(): return lax.ppermute(a, 'z', [(i, (i + by) % n) for i in range(n)])  82.2 us
    ppermute x12, waiting for transfers between devices, swap_second(): return lax.ppermute(a, 'f', [(i, i ^ 2 << i % 2) for i in range(ranks)])  43.7 us
    pallas_call x2, Pallas kernels, feed_forward(): pl.pallas_call(lambda *refs: feed_kernel(count, *refs), grid=(count,), in...  34.6 us
    ppermute x9, waiting for transfers between devices, swap_first(): return lax.ppermute(a, 'f', [(i, i ^ 4 >> i % 2) for i in range(ranks)])  28.3 us
    unnamed x140, local copies, waits for them, and re-layouts  26.3 us
    pallas_call x1, Pallas kernels, project(): pl.pallas_call(lambda *refs: project_kernel(n, len(parts), *refs), in_spe...  20.7 us
    pallas_call x16, Pallas kernels, add_half(): pl.pallas_call(add_kernel, grid=(rows // tile,), in_specs=[pl.BlockSpec((...  18.8 us
    pallas_call x1, Pallas kernels, attention_backward(): pl.pallas_call(backward_kernel, grid=(amount,), in_specs=[pl.BlockSpec(me...  17.8 us
  transfers between devices with their start and end apart: 58, of which 21 were waited for; matrix products, arithmetic and copies ran while one was open for 7% of the time, Pallas kernels for 28%

profile of v5, /device:TPU:0, one launch (start us, length us, event | category | flops | bytes accessed | tf_op | source)
XLA Modules:
  0.0 459.5 jit_solution(13297001156948404485)
XLA Ops:
  9.1 1.9 pad_maximum_fusion.4
  11.0 3.0 collective-permute-start
  21.0 3.5 all-to-all-start
  24.7 2.7 collective-permute-done
  31.6 12.6 %collective-permute-done.9.refs_26_ = bf16[256,1536]{1,0:T(8,128)(2,1)} collective-permute-done((bf16[256,1536]{1,0:T(8,128)(2,1)S(1)}, bf16[256,1536]{1,0:T(8,128)(2,1)}, u32[]{:S(2)}, u32[]{:S(2)}) %collective-permute-start.9) | collective-permute-done | bytes 786464 | tf_op jit(solution)/shard_map/tokens_z/ppermute | solution.py:709
  46.0 6.9 %collective-permute-done.1 = bf16[48,4608]{1,0:T(8,128)(2,1)} collective-permute-done((bf16[48,4608]{1,0:T(8,128)(2,1)}, bf16[48,4608]{1,0:T(8,128)(2,1)}, u32[]{:S(2)}, u32[]{:S(2)}) %collective-permute-start.1) | collective-permute-done | bytes 442400 | tf_op jit(solution)/shard_map/attention_weights_z/ppermute | solution.py:709
  54.7 7.9 %collective-permute-done.10 = bf16[256,1536]{1,0:T(8,128)(2,1)S(1)} collective-permute-done((bf16[256,1536]{1,0:T(8,128)(2,1)S(1)}, bf16[256,1536]{1,0:T(8,128)(2,1)S(1)}, u32[]{:S(2)}, u32[]{:S(2)}) %collective-permute-start.10) | collective-permute-done | bytes 786464 | tf_op jit(solution)/shard_map/out_grad_first/ppermute | solution.py:712
  63.2 3.1 collective-permute-done.2
  77.8 15.6 %collective-permute-done.13.refs_27_ = bf16[256,1536]{1,0:T(8,128)(2,1)} collective-permute-done((bf16[256,1536]{1,0:T(8,128)(2,1)}, bf16[256,1536]{1,0:T(8,128)(2,1)}, u32[]{:S(2)}, u32[]{:S(2)}) %collective-permute-start.13) | collective-permute-done | bytes 786464 | tf_op jit(solution)/shard_map/tokens_z/ppermute | solution.py:709
  94.5 21.4 %collective-permute-done.23.refs_28_ = bf16[256,1536]{1,0:T(8,128)(2,1)S(1)} collective-permute-done((bf16[256,1536]{1,0:T(8,128)(2,1)}, bf16[256,1536]{1,0:T(8,128)(2,1)S(1)}, u32[]{:S(2)}, u32[]{:S(2)}) %collective-permute-start.23) | collective-permute-done | bytes 786464 | tf_op jit(solution)/shard_map/tokens_z/ppermute | solution.py:709
  120.3 20.7 %project.1 = (bf16[1536,256]{1,0:T(8,128)(2,1)}, bf16[768,1024]{1,0:T(8,128)(2,1)}, bf16[768,1024]{1,0:T(8,128)(2,1)}, bf16[1536,1024]{1,0:T(8,128)(2,1)}, bf16[1536,4608]{1,0:T(8,128)(2,1)}) custom-call(s32[32]{0:T(128)} %broadcast_multiply_fusion.1.refs_0_, bf16[1,48,4608]{2,1,0:T(8,128)(2,1)} %get-tuple-element.263.refs_1_, ...), custom_call_target="tpu_custom_call" | custom-call | flops 100000000 | bytes 300000 | tf_op jit(solution)/shard_map/project/pallas_call | solution.py:342
  141.0 2.4 pad_maximum_fusion.refs_2_
  145.0 14.4 %attention_forward.1 = (bf16[1536,256]{1,0:T(8,128)(2,1)}, f32[8,2,256]{2,1,0:T(2,128)}) custom-call(bf16[1536,256]{1,0:T(8,128)(2,1)} %get-tuple-element.143.q_ref, bf16[768,1024]{1,0:T(8,128)(2,1)} %get-tuple-element.144.k_ref, bf16[768,1024]{1,0:T(8,128)(2,1)} %get-tuple-element.145.v_ref, f32[1024,256]{1,0:T(8,128)} %and_select_fusion.bias_ref), custom_call_target="tpu_custom_call" | custom-call | flops 100000000 | bytes 300000 | tf_op jit(solution)/shard_map/attention_forward/pallas_call | solution.py:134
  159.4 4.1 multiply_reduce_fusion
  165.1 11.0 %collective-permute-done.29 = bf16[256,1536]{1,0:T(8,128)(2,1)S(1)} collective-permute-done((bf16[256,1536]{1,0:T(8,128)(2,1)S(1)}, bf16[256,1536]{1,0:T(8,128)(2,1)S(1)}, u32[]{:S(2)}, u32[]{:S(2)}) %collective-permute-start.29) | collective-permute-done | bytes 786464 | tf_op jit(solution)/shard_map/normed_first/ppermute | solution.py:712
  178.4 18.4 %collective-permute-done.30.refs_1_ = bf16[512,1536]{1,0:T(8,128)(2,1)} collective-permute-done((bf16[512,1536]{1,0:T(8,128)(2,1)S(1)}, bf16[512,1536]{1,0:T(8,128)(2,1)}, u32[]{:S(2)}, u32[]{:S(2)}) %collective-permute-start.30) | collective-permute-done | bytes 1572896 | tf_op jit(solution)/shard_map/normed_second/ppermute | solution.py:715
  196.8 6.8 %all-gather.3.cloned.1.call-done = bf16[1536,1536]{1,0:T(8,128)(2,1)} async-done(((bf16[384,1536]{1,0:T(8,128)(2,1)}), bf16[1536,1536]{1,0:T(8,128)(2,1)}) %all-gather.3.cloned.1.call-update) | async-done | bytes 4718608 | tf_op jit(solution)/shard_map/gate_up_down_z/all_gather | solution.py:872
  203.7 17.2 %feed_forward.3 = (bf16[1024,1536]{1,0:T(8,128)(2,1)}, bf16[1024,512]{1,0:T(8,128)(2,1)}, bf16[1024,1024]{1,0:T(8,128)(2,1)}, bf16[512,1536]{1,0:T(8,128)(2,1)}, bf16[512,1536]{1,0:T(8,128)(2,1)}) custom-call(bf16[512,1536]{1,0:T(8,128)(2,1)} %collective-permute-done.31.refs_0_.refs_2_, bf16[512,1536]{1,0:T(8,128)(2,1)} %collective-permute-done.32.refs_1_.refs_3_, ...), custom_call_target="tpu_custom_call" | custom-call | flops 30000001024 | bytes 90000000 | tf_op jit(solution)/shard_map/feed_forward/pallas_call | solution.py:447
  221.0 17.4 %feed_forward.2 = (bf16[1024,1536]{1,0:T(8,128)(2,1)}, bf16[1024,512]{1,0:T(8,128)(2,1)}, bf16[1024,1024]{1,0:T(8,128)(2,1)}, bf16[512,1536]{1,0:T(8,128)(2,1)}, bf16[512,1536]{1,0:T(8,128)(2,1)}) custom-call(bf16[512,1536]{1,0:T(8,128)(2,1)} %copy-done.33, bf16[512,1536]{1,0:T(8,128)(2,1)} %collective-permute-done.30.refs_1_, ...), custom_call_target="tpu_custom_call" | custom-call | flops 30000001024 | bytes 90000000 | tf_op jit(solution)/shard_map/feed_forward/pallas_call | solution.py:447
  238.4 1.9 copy-done.8
  240.3 2.6 add_half.17
  245.9 10.2 %feed_terms.1 = (bf16[1536,1536]{1,0:T(8,128)(2,1)}, f32[8,128]{1,0:T(8,128)S(1)}) custom-call(bf16[512,1536]{1,0:T(8,128)(2,1)S(1)} %copy-done.34, bf16[512,1536]{1,0:T(8,128)(2,1)} %collective-permute-done.30.refs_1_, bf16[512,1536]{1,0:T(8,128)(2,1)} %collective-permute-done.31.refs_0_.refs_2_, bf16[512,1536]{1,0:T(8,128)(2,1)} %collective-permute-done.32.refs_1_.refs_3_, ...), custom_call_target="tpu_custom_call" | custom-call | flops 15000000512 | bytes 45000000 | tf_op jit(solution)/shard_map/feed_sum_z/feed_terms/pallas_call | solution.py:519
  256.2 1.9 copy-done.9
  259.9 3.8 collective-permute-done.36
  263.7 2.0 add_half.19
  268.5 9.4 %collective-permute-done.37.far_ref = bf16[256,1536]{1,0:T(8,128)(2,1)} collective-permute-done((bf16[256,1536]{1,0:T(8,128)(2,1)}, bf16[256,1536]{1,0:T(8,128)(2,1)}, u32[]{:S(2)}, u32[]{:S(2)}) %collective-permute-start.37) | collective-permute-done | bytes 786464 | tf_op jit(solution)/shard_map/scaled_first/ppermute | solution.py:712
  277.9 6.2 %middle_gradient.1 = (f32[256,1536]{1,0:T(8,128)S(1)}, bf16[256,1536]{1,0:T(8,128)(2,1)S(1)}, bf16[1536,256]{1,0:T(8,128)(2,1)S(1)}) custom-call(bf16[256,1536]{1,0:T(8,128)(2,1)S(1)} %add_half.18.near_ref, bf16[256,1536]{1,0:T(8,128)(2,1)} %collective-permute-done.37.far_ref, f32[256,1536]{1,0:T(8,128)S(1)} %get-tuple-element.271.resid_ref, ...), custom_call_target="tpu_custom_call" | custom-call | flops 100000000 | bytes 300000 | tf_op jit(solution)/shard_map/middle_gradient/pallas_call | solution.py:620
  285.3 3.6 owned_terms.2
  289.0 4.5 collective-permute-done.38
  296.3 17.8 %attention_backward.1 = (bf16[1536,256]{1,0:T(8,128)(2,1)S(1)}, bf16[2,768,1024]{2,1,0:T(8,128)(2,1)S(1)}, bf16[4,2,768,256]{3,2,1,0:T(8,128)(2,1)S(1)}) custom-call(s32[1]{0:T(128)} %bitcast.place_ref, bf16[1536,256]{1,0:T(8,128)(2,1)S(1)} %copy-done.26, bf16[768,1024]{1,0:T(8,128)(2,1)S(1)} %copy-done.13, bf16[768,1024]{1,0:T(8,128)(2,1)S(1)} %copy-done.14, ...), custom_call_target="tpu_custom_call" | custom-call | flops 100000000 | bytes 300000 | tf_op jit(solution)/shard_map/attention_backward/pallas_call | solution.py:164
  318.4 12.4 %owned_terms.3 = (bf16[4,4,48,3072]{3,2,1,0:T(8,128)(2,1)}, bf16[4,4,48,3072]{3,2,1,0:T(8,128)(2,1)}) custom-call(s32[8]{0:T(128)S(1)} %stack.179.refs_0_, bf16[1536,1024]{1,0:T(8,128)(2,1)S(1)} %copy-done.24, bf16[1536,256]{1,0:T(8,128)(2,1)S(1)} %get-tuple-element.174.refs_2_.query_ref, bf16[1536,1024]{1,0:T(8,128)(2,1)S(1)} %bitcast.187), custom_call_target="tpu_custom_call" | custom-call | flops 100000000 | bytes 300000 | tf_op jit(solution)/shard_map/projected_core/owned_terms/pallas_call | solution.py:260
  331.6 8.2 %collective-permute-done.41 = bf16[4,4,48,3072]{3,2,1,0:T(8,128)(2,1)} collective-permute-done((bf16[4,4,48,3072]{3,2,1,0:T(8,128)(2,1)}, bf16[4,4,48,3072]{3,2,1,0:T(8,128)(2,1)}, u32[]{:S(2)}, u32[]{:S(2)}) %collective-permute-start.41) | collective-permute-done | bytes 4718624 | tf_op jit(solution)/shard_map/projected_core/ppermute | solution.py:718
  339.8 3.3 convolution_convert_fusion
  343.4 2.0 add_half.24
  346.9 3.2 convolution_convert_fusion.1
  353.2 21.0 %collective-permute-done.42 = bf16[2,4,48,3072]{3,2,1,0:T(8,128)(2,1)S(1)} collective-permute-done((bf16[2,4,48,3072]{3,2,1,0:T(8,128)(2,1)S(1)}, bf16[2,4,48,3072]{3,2,1,0:T(8,128)(2,1)S(1)}, u32[]{:S(2)}, u32[]{:S(2)}) %collective-permute-start.42) | collective-permute-done | bytes 2359328 | tf_op jit(solution)/shard_map/projected_second/ppermute | solution.py:715
  375.7 1.9 add_half.23
  381.9 2.1 slice.16
  384.0 4.2 all-to-all-start.1
  391.3 2.0 collective-permute-start.48
  395.7 1.9 copy-done.5
  397.6 1.9 copy-done.7
  402.5 12.7 %collective-permute-done.47.refs_6_ = bf16[48,1536]{1,0:T(8,128)(2,1)} collective-permute-done((bf16[48,1536]{1,0:T(8,128)(2,1)}, bf16[48,1536]{1,0:T(8,128)(2,1)}, u32[]{:S(2)}, u32[]{:S(2)}) %collective-permute-start.47) | collective-permute-done | bytes 147488 | tf_op jit(solution)/shard_map/out_z/ppermute | solution.py:709
  423.2 2.0 collective-permute-start.52
  426.8 9.9 %input_gradient.1 = bf16[256,1536]{1,0:T(8,128)(2,1)} custom-call(bf16[1536,256]{1,0:T(8,128)(2,1)S(1)} %copy-done.21, bf16[1536,256]{1,0:T(8,128)(2,1)S(1)} %bitcast.193, bf16[1536,4608]{1,0:T(8,128)(2,1)} %get-tuple-element.148.weight_ref, bf16[256,1536]{1,0:T(8,128)(2,1)S(1)} %bitcast.183, f32[256,1536]{1,0:T(8,128)S(1)} %copy-done.32), custom_call_target="tpu_custom_call" | custom-call | flops 100000000 | bytes 300000 | tf_op jit(solution)/shard_map/input_gradient/pallas_call | solution.py:664
  436.7 2.8 feed_finish.1
  440.7 7.0 %collective-permute-done.51.refs_2_ = bf16[48,3072]{1,0:T(8,128)(2,1)S(1)} collective-permute-done((bf16[48,3072]{1,0:T(8,128)(2,1)S(1)}, bf16[48,3072]{1,0:T(8,128)(2,1)S(1)}, u32[]{:S(2)}, u32[]{:S(2)}) %collective-permute-start.51) | collective-permute-done | bytes 294944 | tf_op jit(solution)/shard_map/projected_z/ppermute | solution.py:709
  447.7 2.3 attention_finish.1
  (288 shorter events, 88.1 us)
Async XLA Ops:
  11.0 16.4 %collective-permute-start = (bf16[48,4608]{1,0:T(8,128)(2,1)}, bf16[48,4608]{1,0:T(8,128)(2,1)}, u32[]{:S(2)}, u32[]{:S(2)}) collective-permute-start(bf16[48,4608]{1,0:T(8,128)(2,1)} %get-tuple-element.262), channel_id=1, source_target_pairs={{0,8},{8,16},{16,24},{24,0},{1,9},{9,17},{17,25},{25,1},{2,10},{10... | collective-permute-start | bytes 1327112 | tf_op jit(solution)/shard_map/attention_weights_z/ppermute | solution.py:709
  14.0 15.1 %collective-permute-start.3 = (bf16[48,4608]{1,0:T(8,128)(2,1)}, bf16[48,4608]{1,0:T(8,128)(2,1)}, u32[]{:S(2)}, u32[]{:S(2)}) collective-permute-start(bf16[48,4608]{1,0:T(8,128)(2,1)} %get-tuple-element.262), channel_id=1, source_target_pairs={{0,2},{1,5},{2,0},{3,7},{4,6},{5,1},{6,4},{7,3},{8,10},{9,13},{10,... | collective-permute-start | bytes 1327112 | tf_op jit(solution)/shard_map/attention_weights_own/ppermute | solution.py:715
  15.5 14.3 %collective-permute-start.4 = (bf16[48,4608]{1,0:T(8,128)(2,1)}, bf16[48,4608]{1,0:T(8,128)(2,1)}, u32[]{:S(2)}, u32[]{:S(2)}) collective-permute-start(bf16[48,4608]{1,0:T(8,128)(2,1)} %get-tuple-element.262), channel_id=1, source_target_pairs={{0,4},{1,3},{2,6},{3,1},{4,0},{5,7},{6,2},{7,5},{8,12},{9,11},{10,... | collective-permute-start | bytes 1327112 | tf_op jit(solution)/shard_map/attention_weights_own/ppermute | solution.py:712
  17.0 27.2 %collective-permute-start.9 = (bf16[256,1536]{1,0:T(8,128)(2,1)S(1)}, bf16[256,1536]{1,0:T(8,128)(2,1)}, u32[]{:S(2)}, u32[]{:S(2)}) collective-permute-start(bf16[256,1536]{1,0:T(8,128)(2,1)S(1)} %bitcast.182), channel_id=1, source_target_pairs={{0,8},{8,16},{16,24},{24,0},{1,9},{9,17},{17,25},{25,1},{2,10},{10... | collective-permute-start | bytes 2359304 | tf_op jit(solution)/shard_map/tokens_z/ppermute | solution.py:709
  21.0 45.3 %all-to-all-start = ((bf16[8,48,1024]{2,1,0:T(8,128)(2,1)}), bf16[8,48,1024]{2,1,0:T(8,128)(2,1)S(1)}, u32[]{:S(2)}, u32[]{:S(2)}) async-start(bf16[8,48,1024]{2,1,0:T(8,128)(2,1)} %reshape.261), calls=%async_computation | async-start | bytes 1572864 | tf_op jit(solution)/shard_map/gate_up_f/all_to_all | solution.py:814
  24.6 179.1 %all-gather.3.cloned.1.call-start = ((), (), s32[]{:S(2)}) async-start(), calls=%async_computation.6 | async-start | bytes 5898240 | tf_op jit(solution)/shard_map/gate_up_down_z/all_gather | solution.py:872
  27.4 25.5 %collective-permute-start.1 = (bf16[48,4608]{1,0:T(8,128)(2,1)}, bf16[48,4608]{1,0:T(8,128)(2,1)}, u32[]{:S(2)}, u32[]{:S(2)}) collective-permute-start(bf16[48,4608]{1,0:T(8,128)(2,1)} %collective-permute-done), channel_id=1, source_target_pairs={{0,8},{8,16},{16,24},{24,0},{1,9},{9,17},{17,25},{25,1},{2,10},{10... | collective-permute-start | bytes 1327112 | tf_op jit(solution)/shard_map/attention_weights_z/ppermute | solution.py:709
  27.4 25.5 %collective-permute-start.7 = (bf16[48,4608]{1,0:T(8,128)(2,1)}, bf16[48,4608]{1,0:T(8,128)(2,1)}, u32[]{:S(2)}, u32[]{:S(2)}) collective-permute-start(bf16[48,4608]{1,0:T(8,128)(2,1)} %collective-permute-done), channel_id=1, source_target_pairs={{0,4},{1,3},{2,6},{3,1},{4,0},{5,7},{6,2},{7,5},{8,12},{9,11},{10,... | collective-permute-start | bytes 1327112 | tf_op jit(solution)/shard_map/attention_weights_own/ppermute | solution.py:712
  29.2 33.5 %collective-permute-start.10 = (bf16[256,1536]{1,0:T(8,128)(2,1)S(1)}, bf16[256,1536]{1,0:T(8,128)(2,1)S(1)}, u32[]{:S(2)}, u32[]{:S(2)}) collective-permute-start(bf16[256,1536]{1,0:T(8,128)(2,1)S(1)} %bitcast.184), channel_id=1, source_target_pairs={{0,4},{1,3},{2,6},{3,1},{4,0},{5,7},{6,2},{7,5},{8,12},{9,11},{10,... | collective-permute-start | bytes 2359304 | tf_op jit(solution)/shard_map/out_grad_first/ppermute | solution.py:712
  29.9 33.3 %collective-permute-start.6 = (bf16[48,4608]{1,0:T(8,128)(2,1)}, bf16[48,4608]{1,0:T(8,128)(2,1)}, u32[]{:S(2)}, u32[]{:S(2)}) collective-permute-start(bf16[48,4608]{1,0:T(8,128)(2,1)} %collective-permute-done), channel_id=1, source_target_pairs={{0,2},{1,5},{2,0},{3,7},{4,6},{5,1},{6,4},{7,3},{8,10},{9,13},{10,... | collective-permute-start | bytes 1327112 | tf_op jit(solution)/shard_map/attention_weights_own/ppermute | solution.py:715
  44.2 18.4 %collective-permute-start.5 = (bf16[48,4608]{1,0:T(8,128)(2,1)}, bf16[48,4608]{1,0:T(8,128)(2,1)}, u32[]{:S(2)}, u32[]{:S(2)}) collective-permute-start(bf16[48,4608]{1,0:T(8,128)(2,1)} %collective-permute-done.4), channel_id=1, source_target_pairs={{0,2},{1,5},{2,0},{3,7},{4,6},{5,1},{6,4},{7,3},{8,10},{9,13},{10,... | collective-permute-start | bytes 1327112 | tf_op jit(solution)/shard_map/attention_weights_own/ppermute | solution.py:715
  52.9 13.5 %collective-permute-start.2 = (bf16[48,4608]{1,0:T(8,128)(2,1)}, bf16[48,4608]{1,0:T(8,128)(2,1)}, u32[]{:S(2)}, u32[]{:S(2)}) collective-permute-start(bf16[48,4608]{1,0:T(8,128)(2,1)} %collective-permute-done.1), channel_id=1, source_target_pairs={{0,8},{8,16},{16,24},{24,0},{1,9},{9,17},{17,25},{25,1},{2,10},{10... | collective-permute-start | bytes 1327112 | tf_op jit(solution)/shard_map/attention_weights_z/ppermute | solution.py:709
  52.9 13.5 %collective-permute-start.8 = (bf16[48,4608]{1,0:T(8,128)(2,1)}, bf16[48,4608]{1,0:T(8,128)(2,1)S(1)}, u32[]{:S(2)}, u32[]{:S(2)}) collective-permute-start(bf16[48,4608]{1,0:T(8,128)(2,1)} %collective-permute-done.7), channel_id=1, source_target_pairs={{0,2},{1,5},{2,0},{3,7},{4,6},{5,1},{6,4},{7,3},{8,10},{9,13},{10,... | collective-permute-start | bytes 1327112 | tf_op jit(solution)/shard_map/attention_weights_own/ppermute | solution.py:715
  62.6 8.6 %collective-permute-start.15 = (bf16[48,4608]{1,0:T(8,128)(2,1)}, bf16[48,4608]{1,0:T(8,128)(2,1)}, u32[]{:S(2)}, u32[]{:S(2)}) collective-permute-start(bf16[48,4608]{1,0:T(8,128)(2,1)} %collective-permute-done.4), channel_id=1, source_target_pairs={{0,1},{1,0},{2,3},{3,2},{4,5},{5,4},{6,7},{7,6},{8,9},{9,8},{10,11... | collective-permute-start | bytes 1327112 | tf_op jit(solution)/shard_map/attention_weights_core/ppermute | solution.py:718
  63.1 8.1 %collective-permute-start.18 = (bf16[48,4608]{1,0:T(8,128)(2,1)}, bf16[48,4608]{1,0:T(8,128)(2,1)}, u32[]{:S(2)}, u32[]{:S(2)}) collective-permute-start(bf16[48,4608]{1,0:T(8,128)(2,1)} %collective-permute-done), channel_id=1, source_target_pairs={{0,1},{1,0},{2,3},{3,2},{4,5},{5,4},{6,7},{7,6},{8,9},{9,8},{10,11... | collective-permute-start | bytes 1327112 | tf_op jit(solution)/shard_map/attention_weights_core/ppermute | solution.py:718
  68.4 25.1 %collective-permute-start.11 = (bf16[2,48,4608]{2,1,0:T(8,128)(2,1)S(1)}, bf16[2,48,4608]{2,1,0:T(8,128)(2,1)}, u32[]{:S(2)}, u32[]{:S(2)}) collective-permute-start(bf16[2,48,4608]{2,1,0:T(8,128)(2,1)S(1)} %pad_maximum_fusion.3.refs_3_), channel_id=1, source_target_pairs={{0,4},{1,3},{2,6},{3,1},{4,0},{5,7},{6,2},{7,5},{8,12},{9,11},{10,... | collective-permute-start | bytes 2654216 | tf_op jit(solution)/shard_map/attention_weights_first/ppermute | solution.py:712
  69.7 23.7 %collective-permute-start.12 = (bf16[2,48,4608]{2,1,0:T(8,128)(2,1)S(1)}, bf16[2,48,4608]{2,1,0:T(8,128)(2,1)}, u32[]{:S(2)}, u32[]{:S(2)}) collective-permute-start(bf16[2,48,4608]{2,1,0:T(8,128)(2,1)S(1)} %pad_maximum_fusion.3.refs_3_), channel_id=1, source_target_pairs={{0,2},{1,5},{2,0},{3,7},{4,6},{5,1},{6,4},{7,3},{8,10},{9,13},{10,... | collective-permute-start | bytes 2654216 | tf_op jit(solution)/shard_map/attention_weights_second/ppermute | solution.py:715
  71.8 21.6 %collective-permute-start.13 = (bf16[256,1536]{1,0:T(8,128)(2,1)}, bf16[256,1536]{1,0:T(8,128)(2,1)}, u32[]{:S(2)}, u32[]{:S(2)}) collective-permute-start(bf16[256,1536]{1,0:T(8,128)(2,1)} %collective-permute-done.9.refs_26_), channel_id=1, source_target_pairs={{0,8},{8,16},{16,24},{24,0},{1,9},{9,17},{17,25},{25,1},{2,10},{10... | collective-permute-start | bytes 2359304 | tf_op jit(solution)/shard_map/tokens_z/ppermute | solution.py:709
  77.7 16.7 %collective-permute-start.24 = (bf16[2,48,4608]{2,1,0:T(8,128)(2,1)S(1)}, bf16[2,48,4608]{2,1,0:T(8,128)(2,1)S(1)}, u32[]{:S(2)}, u32[]{:S(2)}) collective-permute-start(bf16[2,48,4608]{2,1,0:T(8,128)(2,1)S(1)} %pad_maximum_fusion.3.refs_3_), channel_id=1, source_target_pairs={{0,1},{1,0},{2,3},{3,2},{4,5},{5,4},{6,7},{7,6},{8,9},{9,8},{10,11... | collective-permute-start | bytes 2654216 | tf_op jit(solution)/shard_map/attention_weights_core/ppermute | solution.py:718
  93.4 22.5 %collective-permute-start.22 = (bf16[2,48,4608]{2,1,0:T(8,128)(2,1)}, bf16[2,48,4608]{2,1,0:T(8,128)(2,1)S(1)}, u32[]{:S(2)}, u32[]{:S(2)}) collective-permute-start(bf16[2,48,4608]{2,1,0:T(8,128)(2,1)} %collective-permute-done.11.refs_6_), channel_id=1, source_target_pairs={{0,2},{1,5},{2,0},{3,7},{4,6},{5,1},{6,4},{7,3},{8,10},{9,13},{10,... | collective-permute-start | bytes 2654216 | tf_op jit(solution)/shard_map/attention_weights_second/ppermute | solution.py:715
  94.0 22.9 %collective-permute-start.25 = (bf16[2,48,4608]{2,1,0:T(8,128)(2,1)}, bf16[2,48,4608]{2,1,0:T(8,128)(2,1)}, u32[]{:S(2)}, u32[]{:S(2)}) collective-permute-start(bf16[2,48,4608]{2,1,0:T(8,128)(2,1)} %collective-permute-done.11.refs_6_), channel_id=1, source_target_pairs={{0,1},{1,0},{2,3},{3,2},{4,5},{5,4},{6,7},{7,6},{8,9},{9,8},{10,11... | collective-permute-start | bytes 2654216 | tf_op jit(solution)/shard_map/attention_weights_core/ppermute | solution.py:718
  94.0 22.9 %collective-permute-start.26 = (bf16[2,48,4608]{2,1,0:T(8,128)(2,1)}, bf16[2,48,4608]{2,1,0:T(8,128)(2,1)}, u32[]{:S(2)}, u32[]{:S(2)}) collective-permute-start(bf16[2,48,4608]{2,1,0:T(8,128)(2,1)} %collective-permute-done.12.refs_9_), channel_id=1, source_target_pairs={{0,1},{1,0},{2,3},{3,2},{4,5},{5,4},{6,7},{7,6},{8,9},{9,8},{10,11... | collective-permute-start | bytes 2654216 | tf_op jit(solution)/shard_map/attention_weights_core/ppermute | solution.py:718
  94.5 21.5 %collective-permute-start.23 = (bf16[256,1536]{1,0:T(8,128)(2,1)}, bf16[256,1536]{1,0:T(8,128)(2,1)S(1)}, u32[]{:S(2)}, u32[]{:S(2)}) collective-permute-start(bf16[256,1536]{1,0:T(8,128)(2,1)} %collective-permute-done.13.refs_27_), channel_id=1, source_target_pairs={{0,8},{8,16},{16,24},{24,0},{1,9},{9,17},{17,25},{25,1},{2,10},{10... | collective-permute-start | bytes 2359304 | tf_op jit(solution)/shard_map/tokens_z/ppermute | solution.py:709
  116.8 265.0 %reduce-scatter.5.cloned.1.call-start = ((), (), s32[]{:S(2)}) async-start(), calls=%async_computation.5 | async-start | bytes 5898240 | tf_op jit(solution)/shard_map/feed_sum_z/reduce_scatter | solution.py:962
  143.4 20.7 %collective-permute-start.28 = (bf16[512,1536]{1,0:T(8,128)(2,1)}, bf16[512,1536]{1,0:T(8,128)(2,1)}, u32[]{:S(2)}, u32[]{:S(2)}) collective-permute-start(bf16[512,1536]{1,0:T(8,128)(2,1)} %pad_maximum_fusion.refs_2_), channel_id=1, source_target_pairs={{0,2},{1,5},{2,0},{3,7},{4,6},{5,1},{6,4},{7,3},{8,10},{9,13},{10,... | collective-permute-start | bytes 4718600 | tf_op jit(solution)/shard_map/out_grad_second/ppermute | solution.py:715
  164.1 12.0 %collective-permute-start.29 = (bf16[256,1536]{1,0:T(8,128)(2,1)S(1)}, bf16[256,1536]{1,0:T(8,128)(2,1)S(1)}, u32[]{:S(2)}, u32[]{:S(2)}) collective-permute-start(bf16[256,1536]{1,0:T(8,128)(2,1)S(1)} %multiply_convert_fusion), channel_id=1, source_target_pairs={{0,4},{1,3},{2,6},{3,1},{4,0},{5,7},{6,2},{7,5},{8,12},{9,11},{10,... | collective-permute-start | bytes 2359304 | tf_op jit(solution)/shard_map/normed_first/ppermute | solution.py:712
  176.2 20.6 %collective-permute-start.30 = (bf16[512,1536]{1,0:T(8,128)(2,1)S(1)}, bf16[512,1536]{1,0:T(8,128)(2,1)}, u32[]{:S(2)}, u32[]{:S(2)}) collective-permute-start(bf16[512,1536]{1,0:T(8,128)(2,1)S(1)} %pad_maximum_fusion.1.refs_0_), channel_id=1, source_target_pairs={{0,2},{1,5},{2,0},{3,7},{4,6},{5,1},{6,4},{7,3},{8,10},{9,13},{10,... | collective-permute-start | bytes 4718600 | tf_op jit(solution)/shard_map/normed_second/ppermute | solution.py:715
  177.9 25.8 %collective-permute-start.33 = (bf16[512,1536]{1,0:T(8,128)(2,1)}, bf16[512,1536]{1,0:T(8,128)(2,1)}, u32[]{:S(2)}, u32[]{:S(2)}) collective-permute-start(bf16[512,1536]{1,0:T(8,128)(2,1)} %pad_maximum_fusion.refs_2_), channel_id=1, source_target_pairs={{0,1},{1,0},{2,3},{3,2},{4,5},{5,4},{6,7},{7,6},{8,9},{9,8},{10,11... | collective-permute-start | bytes 4718600 | tf_op jit(solution)/shard_map/out_grad_all/ppermute | solution.py:718
  177.9 25.8 %collective-permute-start.34 = (bf16[512,1536]{1,0:T(8,128)(2,1)}, bf16[512,1536]{1,0:T(8,128)(2,1)}, u32[]{:S(2)}, u32[]{:S(2)}) collective-permute-start(bf16[512,1536]{1,0:T(8,128)(2,1)} %collective-permute-done.28.refs_3_), channel_id=1, source_target_pairs={{0,1},{1,0},{2,3},{3,2},{4,5},{5,4},{6,7},{7,6},{8,9},{9,8},{10,11... | collective-permute-start | bytes 4718600 | tf_op jit(solution)/shard_map/out_grad_all/ppermute | solution.py:718
  178.4 25.3 %collective-permute-start.31 = (bf16[512,1536]{1,0:T(8,128)(2,1)S(1)}, bf16[512,1536]{1,0:T(8,128)(2,1)}, u32[]{:S(2)}, u32[]{:S(2)}) collective-permute-start(bf16[512,1536]{1,0:T(8,128)(2,1)S(1)} %pad_maximum_fusion.1.refs_0_), channel_id=1, source_target_pairs={{0,1},{1,0},{2,3},{3,2},{4,5},{5,4},{6,7},{7,6},{8,9},{9,8},{10,11... | collective-permute-start | bytes 4718600 | tf_op jit(solution)/shard_map/normed_second/ppermute | solution.py:718
  220.9 17.5 %collective-permute-start.35 = (bf16[1024,1536]{1,0:T(8,128)(2,1)}, bf16[1024,1536]{1,0:T(8,128)(2,1)}, u32[]{:S(2)}, u32[]{:S(2)}) collective-permute-start(bf16[1024,1536]{1,0:T(8,128)(2,1)} %get-tuple-element.156), channel_id=1, source_target_pairs={{0,1},{1,0},{2,3},{3,2},{4,5},{5,4},{6,7},{7,6},{8,9},{9,8},{10,11... | collective-permute-start | bytes 9437192 | tf_op jit(solution)/shard_map/scaled_core/ppermute | solution.py:718
  242.9 20.7 %collective-permute-start.36 = (bf16[512,1536]{1,0:T(8,128)(2,1)}, bf16[512,1536]{1,0:T(8,128)(2,1)}, u32[]{:S(2)}, u32[]{:S(2)}) collective-permute-start(bf16[512,1536]{1,0:T(8,128)(2,1)} %add_half.17), channel_id=1, source_target_pairs={{0,2},{1,5},{2,0},{3,7},{4,6},{5,1},{6,4},{7,3},{8,10},{9,13},{10,... | collective-permute-start | bytes 4718600 | tf_op jit(solution)/shard_map/scaled_second/ppermute | solution.py:715
  256.1 160.6 %reduce-scatter.3.cloned.1.call-start = ((), (), s32[]{:S(2)}) async-start(), calls=%async_computation.4 | async-start | bytes 3932160 | tf_op jit(solution)/shard_map/kv_grad_z/reduce_scatter | solution.py:1003
  265.6 12.3 %collective-permute-start.37 = (bf16[256,1536]{1,0:T(8,128)(2,1)}, bf16[256,1536]{1,0:T(8,128)(2,1)}, u32[]{:S(2)}, u32[]{:S(2)}) collective-permute-start(bf16[256,1536]{1,0:T(8,128)(2,1)} %add_half.19), channel_id=1, source_target_pairs={{0,4},{1,3},{2,6},{3,1},{4,0},{5,7},{6,2},{7,5},{8,12},{9,11},{10,... | collective-permute-start | bytes 2359304 | tf_op jit(solution)/shard_map/scaled_first/ppermute | solution.py:712
  293.9 20.3 %collective-permute-start.39 = (bf16[2,4,48,1536]{3,2,1,0:T(8,128)(2,1)S(1)}, bf16[2,4,48,1536]{3,2,1,0:T(8,128)(2,1)S(1)}, u32[]{:S(2)}, u32[]{:S(2)}) collective-permute-start(bf16[2,4,48,1536]{3,2,1,0:T(8,128)(2,1)S(1)} %bitcast.192), channel_id=1, source_target_pairs={{0,2},{1,5},{2,0},{3,7},{4,6},{5,1},{6,4},{7,3},{8,10},{9,13},{10,... | collective-permute-start | bytes 3538952 | tf_op jit(solution)/shard_map/out_second/ppermute | solution.py:715
  316.8 13.9 %collective-permute-start.40 = (bf16[1,4,48,1536]{3,2,1,0:T(8,128)(2,1)S(1)}, bf16[1,4,48,1536]{3,2,1,0:T(8,128)(2,1)S(1)}, u32[]{:S(2)}, u32[]{:S(2)}) collective-permute-start(bf16[1,4,48,1536]{3,2,1,0:T(8,128)(2,1)S(1)} %bitcast.194), channel_id=1, source_target_pairs={{0,4},{1,3},{2,6},{3,1},{4,0},{5,7},{6,2},{7,5},{8,12},{9,11},{10,... | collective-permute-start | bytes 1769480 | tf_op jit(solution)/shard_map/out_first/ppermute | solution.py:712
  331.5 8.3 %collective-permute-start.41 = (bf16[4,4,48,3072]{3,2,1,0:T(8,128)(2,1)}, bf16[4,4,48,3072]{3,2,1,0:T(8,128)(2,1)}, u32[]{:S(2)}, u32[]{:S(2)}) collective-permute-start(bf16[4,4,48,3072]{3,2,1,0:T(8,128)(2,1)} %get-tuple-element.180), channel_id=1, source_target_pairs={{0,1},{1,0},{2,3},{3,2},{4,5},{5,4},{6,7},{7,6},{8,9},{9,8},{10,11... | collective-permute-start | bytes 14155784 | tf_op jit(solution)/shard_map/projected_core/ppermute | solution.py:718
  345.4 28.9 %collective-permute-start.42 = (bf16[2,4,48,3072]{3,2,1,0:T(8,128)(2,1)S(1)}, bf16[2,4,48,3072]{3,2,1,0:T(8,128)(2,1)S(1)}, u32[]{:S(2)}, u32[]{:S(2)}) collective-permute-start(bf16[2,4,48,3072]{3,2,1,0:T(8,128)(2,1)S(1)} %bitcast.189), channel_id=1, source_target_pairs={{0,2},{1,5},{2,0},{3,7},{4,6},{5,1},{6,4},{7,3},{8,10},{9,13},{10,... | collective-permute-start | bytes 7077896 | tf_op jit(solution)/shard_map/projected_second/ppermute | solution.py:715
  374.3 42.5 %collective-permute-start.45 = (bf16[512,1536]{1,0:T(8,128)(2,1)}, bf16[512,1536]{1,0:T(8,128)(2,1)}, u32[]{:S(2)}, u32[]{:S(2)}) collective-permute-start(bf16[512,1536]{1,0:T(8,128)(2,1)} %add_half.25), channel_id=1, source_target_pairs={{0,2},{1,5},{2,0},{3,7},{4,6},{5,1},{6,4},{7,3},{8,10},{9,13},{10,... | collective-permute-start | bytes 4718600 | tf_op jit(solution)/shard_map/result_second/ppermute | solution.py:715
  378.9 37.8 %collective-permute-start.44 = (bf16[1,4,48,3072]{3,2,1,0:T(8,128)(2,1)}, bf16[1,4,48,3072]{3,2,1,0:T(8,128)(2,1)}, u32[]{:S(2)}, u32[]{:S(2)}) collective-permute-start(bf16[1,4,48,3072]{3,2,1,0:T(8,128)(2,1)} %bitcast.90), channel_id=1, source_target_pairs={{0,4},{1,3},{2,6},{3,1},{4,0},{5,7},{6,2},{7,5},{8,12},{9,11},{10,... | collective-permute-start | bytes 3538952 | tf_op jit(solution)/shard_map/projected_first/ppermute | solution.py:712
  384.0 32.7 %all-to-all-start.1 = ((bf16[8,48,1024]{2,1,0:T(8,128)(2,1)}), bf16[8,48,1024]{2,1,0:T(8,128)(2,1)}, u32[]{:S(2)}, u32[]{:S(2)}) async-start(bf16[8,48,1024]{2,1,0:T(8,128)(2,1)} %bitcast.196), calls=%async_computation.3 | async-start | bytes 1572864 | tf_op jit(solution)/shard_map/gate_up_sum_f/all_to_all | solution.py:1026
  390.3 12.1 %collective-permute-start.46 = (bf16[48,1536]{1,0:T(8,128)(2,1)}, bf16[48,1536]{1,0:T(8,128)(2,1)}, u32[]{:S(2)}, u32[]{:S(2)}) collective-permute-start(bf16[48,1536]{1,0:T(8,128)(2,1)} %get-tuple-element.260), channel_id=1, source_target_pairs={{0,24},{8,0},{16,8},{24,16},{1,25},{9,1},{17,9},{25,17},{2,26},{10... | collective-permute-start | bytes 442376 | tf_op jit(solution)/shard_map/out_z/ppermute | solution.py:709
  391.3 23.9 %collective-permute-start.47 = (bf16[48,1536]{1,0:T(8,128)(2,1)}, bf16[48,1536]{1,0:T(8,128)(2,1)}, u32[]{:S(2)}, u32[]{:S(2)}) collective-permute-start(bf16[48,1536]{1,0:T(8,128)(2,1)} %get-tuple-element.259), channel_id=1, source_target_pairs={{0,16},{8,24},{16,0},{24,8},{1,17},{9,25},{17,1},{25,9},{2,18},{10... | collective-permute-start | bytes 442376 | tf_op jit(solution)/shard_map/out_z/ppermute | solution.py:709
  391.3 23.9 %collective-permute-start.48 = (bf16[48,1536]{1,0:T(8,128)(2,1)}, bf16[48,1536]{1,0:T(8,128)(2,1)}, u32[]{:S(2)}, u32[]{:S(2)}) collective-permute-start(bf16[48,1536]{1,0:T(8,128)(2,1)} %get-tuple-element.258), channel_id=1, source_target_pairs={{0,8},{8,16},{16,24},{24,0},{1,9},{9,17},{17,25},{25,1},{2,10},{10... | collective-permute-start | bytes 442376 | tf_op jit(solution)/shard_map/out_z/ppermute | solution.py:709
  419.4 20.1 %collective-permute-start.49 = (bf16[256,1536]{1,0:T(8,128)(2,1)S(1)}, bf16[256,1536]{1,0:T(8,128)(2,1)S(1)}, u32[]{:S(2)}, u32[]{:S(2)}) collective-permute-start(bf16[256,1536]{1,0:T(8,128)(2,1)S(1)} %add_half.30), channel_id=1, source_target_pairs={{0,4},{1,3},{2,6},{3,1},{4,0},{5,7},{6,2},{7,5},{8,12},{9,11},{10,... | collective-permute-start | bytes 2359304 | tf_op jit(solution)/shard_map/result_first/ppermute | solution.py:712
  422.0 18.7 %collective-permute-start.50 = (bf16[48,3072]{1,0:T(8,128)(2,1)S(1)}, bf16[48,3072]{1,0:T(8,128)(2,1)S(1)}, u32[]{:S(2)}, u32[]{:S(2)}) collective-permute-start(bf16[48,3072]{1,0:T(8,128)(2,1)S(1)} %get-tuple-element.256), channel_id=1, source_target_pairs={{0,24},{8,0},{16,8},{24,16},{1,25},{9,1},{17,9},{25,17},{2,26},{10... | collective-permute-start | bytes 884744 | tf_op jit(solution)/shard_map/projected_z/ppermute | solution.py:709
  423.0 24.7 %collective-permute-start.51 = (bf16[48,3072]{1,0:T(8,128)(2,1)S(1)}, bf16[48,3072]{1,0:T(8,128)(2,1)S(1)}, u32[]{:S(2)}, u32[]{:S(2)}) collective-permute-start(bf16[48,3072]{1,0:T(8,128)(2,1)S(1)} %get-tuple-element.255), channel_id=1, source_target_pairs={{0,16},{8,24},{16,0},{24,8},{1,17},{9,25},{17,1},{25,9},{2,18},{10... | collective-permute-start | bytes 884744 | tf_op jit(solution)/shard_map/projected_z/ppermute | solution.py:709
  423.2 24.5 %collective-permute-start.52 = (bf16[48,3072]{1,0:T(8,128)(2,1)S(1)}, bf16[48,3072]{1,0:T(8,128)(2,1)S(1)}, u32[]{:S(2)}, u32[]{:S(2)}) collective-permute-start(bf16[48,3072]{1,0:T(8,128)(2,1)S(1)} %get-tuple-element.254), channel_id=1, source_target_pairs={{0,8},{8,16},{16,24},{24,0},{1,9},{9,17},{17,25},{25,1},{2,10},{10... | collective-permute-start | bytes 884744 | tf_op jit(solution)/shard_map/projected_z/ppermute | solution.py:709
  (79 other events, 617.5 us)
Sparse Core Ops, SparseCore 0:
  117.0 86.6 all-gather.2
  256.3 83.8 reduce-scatter.4
  342.4 68.4 reduce-scatter.2

commit v6 on v5

--- a/solution.py
+++ b/solution.py
@@ -595,6 +595,48 @@
         cost_estimate=lasting(0.1),
         name="attention_finish",
     )(*projected, *outs, *weights, gain)
+
+
+def out_kernel(mixed_ref, weight_ref, own_ref, resid_ref, normed_ref, left_ref):
+    step, tile = pl.program_id(0), weight_ref.shape[1]
+
+    @pl.when(step == 0)
+    def _():
+        left_ref[...] = mixed_ref[...].T
+
+    at = pl.ds(pl.multiple_of(step * tile, tile), tile)
+    resid_ref[:, at] = own_ref[:, at].astype(F32) + product(left_ref[...], weight_ref[...])
+
+    @pl.when(step == pl.num_programs(0) - 1)
+    def _():
+        resid = resid_ref[...]
+        inverse = lax.rsqrt(jnp.mean(resid * resid, axis=-1, keepdims=True) + EPSILON)
+        normed_ref[...] = (resid * inverse).astype(BF)
+
+
+def out_product(mixed, weight, own):
+    count, width = own.shape
+    tile = 256
+    first = (weight.shape[1] - width) // tile
+    whole = lambda a: pl.BlockSpec(a.shape, lambda j: (0, 0))
+    return pl.pallas_call(
+        out_kernel,
+        grid=(width // tile,),
+        in_specs=[
+            whole(mixed),
+            pl.BlockSpec((weight.shape[0], tile), lambda j: (0, j + first)),
+            whole(own),
+        ],
+        out_specs=[whole(own), whole(own)],
+        out_shape=[
+            jax.ShapeDtypeStruct((count, width), F32),
+            jax.ShapeDtypeStruct((count, width), BF),
+        ],
+        scratch_shapes=[pltpu.VMEM((count, mixed.shape[0]), BF)],
+        compiler_params=pltpu.CompilerParams(vmem_limit_bytes=VMEM_BYTES),
+        cost_estimate=lasting(0.1),
+        name="out_product",
+    )(mixed, weight, own)
 
 
 def middle_kernel(near_ref, far_ref, resid_ref, grad_ref, weight_ref, total_ref, round_ref, mixed_ref):
@@ -910,10 +952,7 @@
         grad_other = spread_second(grad_pair)
 
     attention_output, log_totals = attention_forward(queries, keys, values, bias)
-    resid = inputs + contract(attention_output, out_weight, 0, 0)
-    second_inverse = lax.rsqrt(jnp.mean(resid * resid, axis=-1, keepdims=True) + EPSILON)
-    second_normed = resid * second_inverse
-    normed_two = second_normed.astype(BF)
+    resid, normed_two = out_product(attention_output, gathered, own)
     normed_two, grad_other = stage(normed_two, grad_other)
 
     with scope("normed_first"):

time: 467 us -> 469 us (level)
  local copies, waits for them, and re-layouts: 34 us -> 39.2 us
    pallas_call x0 -> x1, Pallas kernels: none -> 5.53 us  [out_product(): pl.pallas_call(out_kernel, grid=(width // tile,), in_specs=[whole(mixed),...]
    unnamed x140 -> x150, local copies, waits for them, and re-layouts: 26.3 us -> 31.5 us
    ppermute x12, waiting for transfers between devices: 82.2 us -> 87.2 us  [shift(): return lax.ppermute(a, 'z', [(i, (i + by) % n) for i in range(n)])]
  transfers between devices with their start and end apart: 58 -> 58, of which waited for: 21 -> 19; matrix products, arithmetic and copies ran while one was open for 7% -> 6% of each run, Pallas kernels for 28% -> 29%
where the time goes in v6:
time: 469 us; the launch traced here: 462 us
  waiting for transfers between devices  178 us (38%)
  Pallas kernels  155 us (33%)
  starting transfers between devices  49.5 us (11%)
  local copies, waits for them, and re-layouts  39.2 us (8%)
  other arithmetic  18.7 us (4%)
  between operations  15.3 us (3%)
  matrix products  6.53 us (1%)
    ppermute x12, waiting for transfers between devices, shift(): return lax.ppermute(a, 'z', [(i, (i + by) % n) for i in range(n)])  87.2 us
    ppermute x12, waiting for transfers between devices, swap_second(): return lax.ppermute(a, 'f', [(i, i ^ 2 << i % 2) for i in range(ranks)])  41.2 us
    pallas_call x2, Pallas kernels, feed_forward(): pl.pallas_call(lambda *refs: feed_kernel(count, *refs), grid=(count,), in...  34.6 us
    unnamed x150, local copies, waits for them, and re-layouts  31.5 us
    ppermute x9, waiting for transfers between devices, swap_first(): return lax.ppermute(a, 'f', [(i, i ^ 4 >> i % 2) for i in range(ranks)])  29.7 us
    pallas_call x1, Pallas kernels, project(): pl.pallas_call(lambda *refs: project_kernel(n, len(parts), *refs), in_spe...  20.6 us
    pallas_call x1, Pallas kernels, attention_backward(): pl.pallas_call(backward_kernel, grid=(amount,), in_specs=[pl.BlockSpec(me...  17.8 us
    ppermute x12, starting transfers between devices, swap_second(): return lax.ppermute(a, 'f', [(i, i ^ 2 << i % 2) for i in range(ranks)])  16.7 us
  transfers between devices with their start and end apart: 58, of which 19 were waited for; matrix products, arithmetic and copies ran while one was open for 6% of the time, Pallas kernels for 29%

profile of v6, /device:TPU:0, one launch (start us, length us, event | category | flops | bytes accessed | tf_op | source)
XLA Modules:
  0.0 461.9 jit_solution(9438088424931731157)
XLA Ops:
  9.1 1.9 pad_maximum_fusion.4
  11.0 3.0 collective-permute-start
  21.0 3.5 all-to-all-start
  24.7 2.7 collective-permute-done
  29.9 1.8 collective-permute-start.6
  31.6 12.6 %collective-permute-done.9.refs_26_ = bf16[256,1536]{1,0:T(8,128)(2,1)} collective-permute-done((bf16[256,1536]{1,0:T(8,128)(2,1)S(1)}, bf16[256,1536]{1,0:T(8,128)(2,1)}, u32[]{:S(2)}, u32[]{:S(2)}) %collective-permute-start.9) | collective-permute-done | bytes 786464 | tf_op jit(solution)/shard_map/tokens_z/ppermute | solution.py:751
  46.0 6.9 %collective-permute-done.1 = bf16[48,4608]{1,0:T(8,128)(2,1)} collective-permute-done((bf16[48,4608]{1,0:T(8,128)(2,1)}, bf16[48,4608]{1,0:T(8,128)(2,1)}, u32[]{:S(2)}, u32[]{:S(2)}) %collective-permute-start.1) | collective-permute-done | bytes 442400 | tf_op jit(solution)/shard_map/attention_weights_z/ppermute | solution.py:751
  54.7 7.9 %collective-permute-done.10 = bf16[256,1536]{1,0:T(8,128)(2,1)S(1)} collective-permute-done((bf16[256,1536]{1,0:T(8,128)(2,1)S(1)}, bf16[256,1536]{1,0:T(8,128)(2,1)S(1)}, u32[]{:S(2)}, u32[]{:S(2)}) %collective-permute-start.10) | collective-permute-done | bytes 786464 | tf_op jit(solution)/shard_map/out_grad_first/ppermute | solution.py:754
  63.2 3.1 collective-permute-done.2
  77.2 15.6 %collective-permute-done.13.refs_27_ = bf16[256,1536]{1,0:T(8,128)(2,1)} collective-permute-done((bf16[256,1536]{1,0:T(8,128)(2,1)}, bf16[256,1536]{1,0:T(8,128)(2,1)}, u32[]{:S(2)}, u32[]{:S(2)}) %collective-permute-start.13) | collective-permute-done | bytes 786464 | tf_op jit(solution)/shard_map/tokens_z/ppermute | solution.py:751
  93.9 21.4 %collective-permute-done.23.refs_28_ = bf16[256,1536]{1,0:T(8,128)(2,1)S(1)} collective-permute-done((bf16[256,1536]{1,0:T(8,128)(2,1)}, bf16[256,1536]{1,0:T(8,128)(2,1)S(1)}, u32[]{:S(2)}, u32[]{:S(2)}) %collective-permute-start.23) | collective-permute-done | bytes 786464 | tf_op jit(solution)/shard_map/tokens_z/ppermute | solution.py:751
  116.2 1.9 collective-permute-done.27.refs_24_
  119.1 20.6 %project.1 = (bf16[1536,256]{1,0:T(8,128)(2,1)}, bf16[768,1024]{1,0:T(8,128)(2,1)}, bf16[768,1024]{1,0:T(8,128)(2,1)}, bf16[1536,1024]{1,0:T(8,128)(2,1)}, bf16[1536,4608]{1,0:T(8,128)(2,1)}) custom-call(s32[32]{0:T(128)} %broadcast_multiply_fusion.1.refs_0_, bf16[1,48,4608]{2,1,0:T(8,128)(2,1)} %get-tuple-element.267.refs_1_, ...), custom_call_target="tpu_custom_call" | custom-call | flops 100000000 | bytes 300000 | tf_op jit(solution)/shard_map/project/pallas_call | solution.py:342
  139.7 2.5 pad_maximum_fusion.refs_2_
  143.8 14.4 %attention_forward.1 = (bf16[1536,256]{1,0:T(8,128)(2,1)}, f32[8,2,256]{2,1,0:T(2,128)}) custom-call(bf16[1536,256]{1,0:T(8,128)(2,1)} %get-tuple-element.145.q_ref, bf16[768,1024]{1,0:T(8,128)(2,1)} %get-tuple-element.146.k_ref, bf16[768,1024]{1,0:T(8,128)(2,1)} %get-tuple-element.147.v_ref, f32[1024,256]{1,0:T(8,128)} %and_select_fusion.bias_ref), custom_call_target="tpu_custom_call" | custom-call | flops 100000000 | bytes 300000 | tf_op jit(solution)/shard_map/attention_forward/pallas_call | solution.py:134
  159.3 5.5 %out_product.1 = (f32[256,1536]{1,0:T(8,128)S(1)}, bf16[256,1536]{1,0:T(8,128)(2,1)S(1)}) custom-call(bf16[1536,256]{1,0:T(8,128)(2,1)S(1)} %copy-done.30, bf16[1536,4608]{1,0:T(8,128)(2,1)} %get-tuple-element.150.weight_ref, bf16[256,1536]{1,0:T(8,128)(2,1)S(1)} %bitcast.180), custom_call_target="tpu_custom_call" | custom-call | flops 100000000 | bytes 300000 | tf_op jit(solution)/shard_map/out_product/pallas_call | solution.py:622
  165.7 11.3 %collective-permute-done.29 = bf16[256,1536]{1,0:T(8,128)(2,1)S(1)} collective-permute-done((bf16[256,1536]{1,0:T(8,128)(2,1)S(1)}, bf16[256,1536]{1,0:T(8,128)(2,1)S(1)}, u32[]{:S(2)}, u32[]{:S(2)}) %collective-permute-start.29) | collective-permute-done | bytes 786464 | tf_op jit(solution)/shard_map/normed_first/ppermute | solution.py:754
  178.1 19.5 %collective-permute-done.30.refs_1_ = bf16[512,1536]{1,0:T(8,128)(2,1)S(1)} collective-permute-done((bf16[512,1536]{1,0:T(8,128)(2,1)S(1)}, bf16[512,1536]{1,0:T(8,128)(2,1)S(1)}, u32[]{:S(2)}, u32[]{:S(2)}) %collective-permute-start.30) | collective-permute-done | bytes 1572896 | tf_op jit(solution)/shard_map/normed_second/ppermute | solution.py:757
  197.6 4.7 %all-gather.3.cloned.1.call-done = bf16[1536,1536]{1,0:T(8,128)(2,1)} async-done(((bf16[384,1536]{1,0:T(8,128)(2,1)}), bf16[1536,1536]{1,0:T(8,128)(2,1)}) %all-gather.3.cloned.1.call-update) | async-done | bytes 4718608 | tf_op jit(solution)/shard_map/gate_up_down_z/all_gather | solution.py:914
  202.2 17.2 %feed_forward.3 = (bf16[1024,1536]{1,0:T(8,128)(2,1)}, bf16[1024,512]{1,0:T(8,128)(2,1)}, bf16[1024,1024]{1,0:T(8,128)(2,1)}, bf16[512,1536]{1,0:T(8,128)(2,1)}, bf16[512,1536]{1,0:T(8,128)(2,1)}) custom-call(bf16[512,1536]{1,0:T(8,128)(2,1)} %collective-permute-done.31.refs_0_.refs_2_, bf16[512,1536]{1,0:T(8,128)(2,1)} %collective-permute-done.32.refs_1_.refs_3_, ...), custom_call_target="tpu_custom_call" | custom-call | flops 30000001024 | bytes 90000000 | tf_op jit(solution)/shard_map/feed_forward/pallas_call | solution.py:447
  219.5 17.4 %feed_forward.2 = (bf16[1024,1536]{1,0:T(8,128)(2,1)}, bf16[1024,512]{1,0:T(8,128)(2,1)}, bf16[1024,1024]{1,0:T(8,128)(2,1)}, bf16[512,1536]{1,0:T(8,128)(2,1)}, bf16[512,1536]{1,0:T(8,128)(2,1)}) custom-call(bf16[512,1536]{1,0:T(8,128)(2,1)} %copy-done.38, bf16[512,1536]{1,0:T(8,128)(2,1)} %copy-done.52, bf16[512,1536]{1,0:T(8,128)(2,1)} %pad_maximum_fusion.refs_2_, ...), custom_call_target="tpu_custom_call" | custom-call | flops 30000001024 | bytes 90000000 | tf_op jit(solution)/shard_map/feed_forward/pallas_call | solution.py:447
  237.0 3.0 copy-done.8
  246.5 10.2 %feed_terms.1 = (bf16[1536,1536]{1,0:T(8,128)(2,1)}, f32[8,128]{1,0:T(8,128)S(1)}) custom-call(bf16[512,1536]{1,0:T(8,128)(2,1)S(1)} %copy-done.39, bf16[512,1536]{1,0:T(8,128)(2,1)S(1)} %copy-done.53, bf16[512,1536]{1,0:T(8,128)(2,1)} %collective-permute-done.31.refs_0_.refs_2_, bf16[512,1536]{1,0:T(8,128)(2,1)} %collective-permute-done.32.refs_1_.refs_3_, ...), custom_call_target="tpu_custom_call" | custom-call | flops 15000000512 | bytes 45000000 | tf_op jit(solution)/shard_map/feed_sum_z/feed_terms/pallas_call | solution.py:519
  256.8 1.9 copy-done.7
  258.7 1.9 copy-done.9
  264.8 10.5 %collective-permute-done.37.far_ref = bf16[256,1536]{1,0:T(8,128)(2,1)} collective-permute-done((bf16[256,1536]{1,0:T(8,128)(2,1)}, bf16[256,1536]{1,0:T(8,128)(2,1)}, u32[]{:S(2)}, u32[]{:S(2)}) %collective-permute-start.37) | collective-permute-done | bytes 786464 | tf_op jit(solution)/shard_map/scaled_first/ppermute | solution.py:754
  275.3 6.2 %middle_gradient.1 = (f32[256,1536]{1,0:T(8,128)S(1)}, bf16[256,1536]{1,0:T(8,128)(2,1)S(1)}, bf16[1536,256]{1,0:T(8,128)(2,1)S(1)}) custom-call(bf16[256,1536]{1,0:T(8,128)(2,1)S(1)} %add_half.18.near_ref, bf16[256,1536]{1,0:T(8,128)(2,1)} %collective-permute-done.37.far_ref, f32[256,1536]{1,0:T(8,128)S(1)} %copy-done.17, bf16[256,1536]{1,0:T(8,128)(2,1)S(1)} %bitcast.189, ...), custom_call_target="tpu_custom_call" | custom-call | flops 100000000 | bytes 300000 | tf_op jit(solution)/shard_map/middle_gradient/pallas_call | solution.py:662
  282.7 3.6 owned_terms.2
  286.4 4.5 collective-permute-done.38
  293.7 17.8 %attention_backward.1 = (bf16[1536,256]{1,0:T(8,128)(2,1)S(1)}, bf16[2,768,1024]{2,1,0:T(8,128)(2,1)S(1)}, bf16[4,2,768,256]{3,2,1,0:T(8,128)(2,1)S(1)}) custom-call(s32[1]{0:T(128)} %bitcast.place_ref, bf16[1536,256]{1,0:T(8,128)(2,1)S(1)} %copy-done.29, bf16[768,1024]{1,0:T(8,128)(2,1)S(1)} %copy-done.19, bf16[768,1024]{1,0:T(8,128)(2,1)S(1)} %copy-done.20, ...), custom_call_target="tpu_custom_call" | custom-call | flops 100000000 | bytes 300000 | tf_op jit(solution)/shard_map/attention_backward/pallas_call | solution.py:164
  315.7 12.5 %owned_terms.3 = (bf16[4,4,48,3072]{3,2,1,0:T(8,128)(2,1)}, bf16[4,4,48,3072]{3,2,1,0:T(8,128)(2,1)}) custom-call(s32[8]{0:T(128)S(1)} %stack.179.refs_0_, bf16[1536,1024]{1,0:T(8,128)(2,1)S(1)} %copy-done.27, bf16[1536,256]{1,0:T(8,128)(2,1)S(1)} %get-tuple-element.178.refs_2_.query_ref, bf16[1536,1024]{1,0:T(8,128)(2,1)S(1)} %bitcast.190), custom_call_target="tpu_custom_call" | custom-call | flops 100000000 | bytes 300000 | tf_op jit(solution)/shard_map/projected_core/owned_terms/pallas_call | solution.py:260
  329.0 8.2 %collective-permute-done.41 = bf16[4,4,48,3072]{3,2,1,0:T(8,128)(2,1)} collective-permute-done((bf16[4,4,48,3072]{3,2,1,0:T(8,128)(2,1)}, bf16[4,4,48,3072]{3,2,1,0:T(8,128)(2,1)}, u32[]{:S(2)}, u32[]{:S(2)}) %collective-permute-start.41) | collective-permute-done | bytes 4718624 | tf_op jit(solution)/shard_map/projected_core/ppermute | solution.py:760
  337.3 3.3 convolution_convert_fusion
  340.8 2.0 add_half.24
  344.4 3.2 convolution_convert_fusion.1
  350.8 21.0 %collective-permute-done.42 = bf16[2,4,48,3072]{3,2,1,0:T(8,128)(2,1)S(1)} collective-permute-done((bf16[2,4,48,3072]{3,2,1,0:T(8,128)(2,1)S(1)}, bf16[2,4,48,3072]{3,2,1,0:T(8,128)(2,1)S(1)}, u32[]{:S(2)}, u32[]{:S(2)}) %collective-permute-start.42) | collective-permute-done | bytes 2359328 | tf_op jit(solution)/shard_map/projected_second/ppermute | solution.py:757
  373.2 1.9 add_half.23
  379.3 2.1 slice.16
  381.4 4.2 all-to-all-start.1
  388.6 2.0 collective-permute-start.48
  393.0 1.9 copy-done.3
  394.9 1.9 copy-done.5
  400.0 15.6 %collective-permute-done.47.refs_6_ = bf16[48,1536]{1,0:T(8,128)(2,1)} collective-permute-done((bf16[48,1536]{1,0:T(8,128)(2,1)}, bf16[48,1536]{1,0:T(8,128)(2,1)}, u32[]{:S(2)}, u32[]{:S(2)}) %collective-permute-start.47) | collective-permute-done | bytes 147488 | tf_op jit(solution)/shard_map/out_z/ppermute | solution.py:751
  421.8 3.1 collective-permute-start.51
  427.3 9.9 %input_gradient.1 = bf16[256,1536]{1,0:T(8,128)(2,1)} custom-call(bf16[1536,256]{1,0:T(8,128)(2,1)S(1)} %copy-done.24, bf16[1536,256]{1,0:T(8,128)(2,1)S(1)} %bitcast.196, bf16[1536,4608]{1,0:T(8,128)(2,1)} %get-tuple-element.150.weight_ref, bf16[256,1536]{1,0:T(8,128)(2,1)S(1)} %bitcast.181, f32[256,1536]{1,0:T(8,128)S(1)} %copy-done.37), custom_call_target="tpu_custom_call" | custom-call | flops 100000000 | bytes 300000 | tf_op jit(solution)/shard_map/input_gradient/pallas_call | solution.py:706
  437.2 2.8 feed_finish.1
  441.3 8.9 %collective-permute-done.51.refs_2_ = bf16[48,3072]{1,0:T(8,128)(2,1)S(1)} collective-permute-done((bf16[48,3072]{1,0:T(8,128)(2,1)S(1)}, bf16[48,3072]{1,0:T(8,128)(2,1)S(1)}, u32[]{:S(2)}, u32[]{:S(2)}) %collective-permute-start.51) | collective-permute-done | bytes 294944 | tf_op jit(solution)/shard_map/projected_z/ppermute | solution.py:751
  450.2 2.3 attention_finish.1
  (296 shorter events, 84.6 us)
Async XLA Ops:
  11.0 16.4 %collective-permute-start = (bf16[48,4608]{1,0:T(8,128)(2,1)}, bf16[48,4608]{1,0:T(8,128)(2,1)}, u32[]{:S(2)}, u32[]{:S(2)}) collective-permute-start(bf16[48,4608]{1,0:T(8,128)(2,1)} %get-tuple-element.266), channel_id=1, source_target_pairs={{0,8},{8,16},{16,24},{24,0},{1,9},{9,17},{17,25},{25,1},{2,10},{10... | collective-permute-start | bytes 1327112 | tf_op jit(solution)/shard_map/attention_weights_z/ppermute | solution.py:751
  14.0 15.1 %collective-permute-start.3 = (bf16[48,4608]{1,0:T(8,128)(2,1)}, bf16[48,4608]{1,0:T(8,128)(2,1)}, u32[]{:S(2)}, u32[]{:S(2)}) collective-permute-start(bf16[48,4608]{1,0:T(8,128)(2,1)} %get-tuple-element.266), channel_id=1, source_target_pairs={{0,2},{1,5},{2,0},{3,7},{4,6},{5,1},{6,4},{7,3},{8,10},{9,13},{10,... | collective-permute-start | bytes 1327112 | tf_op jit(solution)/shard_map/attention_weights_own/ppermute | solution.py:757
  15.5 14.3 %collective-permute-start.4 = (bf16[48,4608]{1,0:T(8,128)(2,1)}, bf16[48,4608]{1,0:T(8,128)(2,1)}, u32[]{:S(2)}, u32[]{:S(2)}) collective-permute-start(bf16[48,4608]{1,0:T(8,128)(2,1)} %get-tuple-element.266), channel_id=1, source_target_pairs={{0,4},{1,3},{2,6},{3,1},{4,0},{5,7},{6,2},{7,5},{8,12},{9,11},{10,... | collective-permute-start | bytes 1327112 | tf_op jit(solution)/shard_map/attention_weights_own/ppermute | solution.py:754
  17.0 27.2 %collective-permute-start.9 = (bf16[256,1536]{1,0:T(8,128)(2,1)S(1)}, bf16[256,1536]{1,0:T(8,128)(2,1)}, u32[]{:S(2)}, u32[]{:S(2)}) collective-permute-start(bf16[256,1536]{1,0:T(8,128)(2,1)S(1)} %bitcast.179), channel_id=1, source_target_pairs={{0,8},{8,16},{16,24},{24,0},{1,9},{9,17},{17,25},{25,1},{2,10},{10... | collective-permute-start | bytes 2359304 | tf_op jit(solution)/shard_map/tokens_z/ppermute | solution.py:751
  21.0 45.3 %all-to-all-start = ((bf16[8,48,1024]{2,1,0:T(8,128)(2,1)}), bf16[8,48,1024]{2,1,0:T(8,128)(2,1)S(1)}, u32[]{:S(2)}, u32[]{:S(2)}) async-start(bf16[8,48,1024]{2,1,0:T(8,128)(2,1)} %reshape.253), calls=%async_computation | async-start | bytes 1572864 | tf_op jit(solution)/shard_map/gate_up_f/all_to_all | solution.py:856
  24.6 177.6 %all-gather.3.cloned.1.call-start = ((), (), s32[]{:S(2)}) async-start(), calls=%async_computation.6 | async-start | bytes 5898240 | tf_op jit(solution)/shard_map/gate_up_down_z/all_gather | solution.py:914
  27.4 25.5 %collective-permute-start.1 = (bf16[48,4608]{1,0:T(8,128)(2,1)}, bf16[48,4608]{1,0:T(8,128)(2,1)}, u32[]{:S(2)}, u32[]{:S(2)}) collective-permute-start(bf16[48,4608]{1,0:T(8,128)(2,1)} %collective-permute-done), channel_id=1, source_target_pairs={{0,8},{8,16},{16,24},{24,0},{1,9},{9,17},{17,25},{25,1},{2,10},{10... | collective-permute-start | bytes 1327112 | tf_op jit(solution)/shard_map/attention_weights_z/ppermute | solution.py:751
  27.4 25.5 %collective-permute-start.7 = (bf16[48,4608]{1,0:T(8,128)(2,1)}, bf16[48,4608]{1,0:T(8,128)(2,1)}, u32[]{:S(2)}, u32[]{:S(2)}) collective-permute-start(bf16[48,4608]{1,0:T(8,128)(2,1)} %collective-permute-done), channel_id=1, source_target_pairs={{0,4},{1,3},{2,6},{3,1},{4,0},{5,7},{6,2},{7,5},{8,12},{9,11},{10,... | collective-permute-start | bytes 1327112 | tf_op jit(solution)/shard_map/attention_weights_own/ppermute | solution.py:754
  29.2 33.5 %collective-permute-start.10 = (bf16[256,1536]{1,0:T(8,128)(2,1)S(1)}, bf16[256,1536]{1,0:T(8,128)(2,1)S(1)}, u32[]{:S(2)}, u32[]{:S(2)}) collective-permute-start(bf16[256,1536]{1,0:T(8,128)(2,1)S(1)} %bitcast.187), channel_id=1, source_target_pairs={{0,4},{1,3},{2,6},{3,1},{4,0},{5,7},{6,2},{7,5},{8,12},{9,11},{10,... | collective-permute-start | bytes 2359304 | tf_op jit(solution)/shard_map/out_grad_first/ppermute | solution.py:754
  29.9 33.3 %collective-permute-start.6 = (bf16[48,4608]{1,0:T(8,128)(2,1)}, bf16[48,4608]{1,0:T(8,128)(2,1)}, u32[]{:S(2)}, u32[]{:S(2)}) collective-permute-start(bf16[48,4608]{1,0:T(8,128)(2,1)} %collective-permute-done), channel_id=1, source_target_pairs={{0,2},{1,5},{2,0},{3,7},{4,6},{5,1},{6,4},{7,3},{8,10},{9,13},{10,... | collective-permute-start | bytes 1327112 | tf_op jit(solution)/shard_map/attention_weights_own/ppermute | solution.py:757
  44.2 18.4 %collective-permute-start.5 = (bf16[48,4608]{1,0:T(8,128)(2,1)}, bf16[48,4608]{1,0:T(8,128)(2,1)}, u32[]{:S(2)}, u32[]{:S(2)}) collective-permute-start(bf16[48,4608]{1,0:T(8,128)(2,1)} %collective-permute-done.4), channel_id=1, source_target_pairs={{0,2},{1,5},{2,0},{3,7},{4,6},{5,1},{6,4},{7,3},{8,10},{9,13},{10,... | collective-permute-start | bytes 1327112 | tf_op jit(solution)/shard_map/attention_weights_own/ppermute | solution.py:757
  52.9 13.5 %collective-permute-start.2 = (bf16[48,4608]{1,0:T(8,128)(2,1)}, bf16[48,4608]{1,0:T(8,128)(2,1)}, u32[]{:S(2)}, u32[]{:S(2)}) collective-permute-start(bf16[48,4608]{1,0:T(8,128)(2,1)} %collective-permute-done.1), channel_id=1, source_target_pairs={{0,8},{8,16},{16,24},{24,0},{1,9},{9,17},{17,25},{25,1},{2,10},{10... | collective-permute-start | bytes 1327112 | tf_op jit(solution)/shard_map/attention_weights_z/ppermute | solution.py:751
  52.9 13.5 %collective-permute-start.8 = (bf16[48,4608]{1,0:T(8,128)(2,1)}, bf16[48,4608]{1,0:T(8,128)(2,1)S(1)}, u32[]{:S(2)}, u32[]{:S(2)}) collective-permute-start(bf16[48,4608]{1,0:T(8,128)(2,1)} %collective-permute-done.7), channel_id=1, source_target_pairs={{0,2},{1,5},{2,0},{3,7},{4,6},{5,1},{6,4},{7,3},{8,10},{9,13},{10,... | collective-permute-start | bytes 1327112 | tf_op jit(solution)/shard_map/attention_weights_own/ppermute | solution.py:757
  62.6 8.0 %collective-permute-start.15 = (bf16[48,4608]{1,0:T(8,128)(2,1)}, bf16[48,4608]{1,0:T(8,128)(2,1)}, u32[]{:S(2)}, u32[]{:S(2)}) collective-permute-start(bf16[48,4608]{1,0:T(8,128)(2,1)} %collective-permute-done.4), channel_id=1, source_target_pairs={{0,1},{1,0},{2,3},{3,2},{4,5},{5,4},{6,7},{7,6},{8,9},{9,8},{10,11... | collective-permute-start | bytes 1327112 | tf_op jit(solution)/shard_map/attention_weights_core/ppermute | solution.py:760
  63.1 7.5 %collective-permute-start.18 = (bf16[48,4608]{1,0:T(8,128)(2,1)}, bf16[48,4608]{1,0:T(8,128)(2,1)}, u32[]{:S(2)}, u32[]{:S(2)}) collective-permute-start(bf16[48,4608]{1,0:T(8,128)(2,1)} %collective-permute-done), channel_id=1, source_target_pairs={{0,1},{1,0},{2,3},{3,2},{4,5},{5,4},{6,7},{7,6},{8,9},{9,8},{10,11... | collective-permute-start | bytes 1327112 | tf_op jit(solution)/shard_map/attention_weights_core/ppermute | solution.py:760
  67.8 25.1 %collective-permute-start.11 = (bf16[2,48,4608]{2,1,0:T(8,128)(2,1)S(1)}, bf16[2,48,4608]{2,1,0:T(8,128)(2,1)}, u32[]{:S(2)}, u32[]{:S(2)}) collective-permute-start(bf16[2,48,4608]{2,1,0:T(8,128)(2,1)S(1)} %pad_maximum_fusion.3.refs_3_), channel_id=1, source_target_pairs={{0,4},{1,3},{2,6},{3,1},{4,0},{5,7},{6,2},{7,5},{8,12},{9,11},{10,... | collective-permute-start | bytes 2654216 | tf_op jit(solution)/shard_map/attention_weights_first/ppermute | solution.py:754
  69.1 23.7 %collective-permute-start.12 = (bf16[2,48,4608]{2,1,0:T(8,128)(2,1)S(1)}, bf16[2,48,4608]{2,1,0:T(8,128)(2,1)}, u32[]{:S(2)}, u32[]{:S(2)}) collective-permute-start(bf16[2,48,4608]{2,1,0:T(8,128)(2,1)S(1)} %pad_maximum_fusion.3.refs_3_), channel_id=1, source_target_pairs={{0,2},{1,5},{2,0},{3,7},{4,6},{5,1},{6,4},{7,3},{8,10},{9,13},{10,... | collective-permute-start | bytes 2654216 | tf_op jit(solution)/shard_map/attention_weights_second/ppermute | solution.py:757
  71.2 21.6 %collective-permute-start.13 = (bf16[256,1536]{1,0:T(8,128)(2,1)}, bf16[256,1536]{1,0:T(8,128)(2,1)}, u32[]{:S(2)}, u32[]{:S(2)}) collective-permute-start(bf16[256,1536]{1,0:T(8,128)(2,1)} %collective-permute-done.9.refs_26_), channel_id=1, source_target_pairs={{0,8},{8,16},{16,24},{24,0},{1,9},{9,17},{17,25},{25,1},{2,10},{10... | collective-permute-start | bytes 2359304 | tf_op jit(solution)/shard_map/tokens_z/ppermute | solution.py:751
  77.1 16.8 %collective-permute-start.24 = (bf16[2,48,4608]{2,1,0:T(8,128)(2,1)S(1)}, bf16[2,48,4608]{2,1,0:T(8,128)(2,1)S(1)}, u32[]{:S(2)}, u32[]{:S(2)}) collective-permute-start(bf16[2,48,4608]{2,1,0:T(8,128)(2,1)S(1)} %pad_maximum_fusion.3.refs_3_), channel_id=1, source_target_pairs={{0,1},{1,0},{2,3},{3,2},{4,5},{5,4},{6,7},{7,6},{8,9},{9,8},{10,11... | collective-permute-start | bytes 2654216 | tf_op jit(solution)/shard_map/attention_weights_core/ppermute | solution.py:760
  92.8 22.5 %collective-permute-start.22 = (bf16[2,48,4608]{2,1,0:T(8,128)(2,1)}, bf16[2,48,4608]{2,1,0:T(8,128)(2,1)}, u32[]{:S(2)}, u32[]{:S(2)}) collective-permute-start(bf16[2,48,4608]{2,1,0:T(8,128)(2,1)} %collective-permute-done.11.refs_6_), channel_id=1, source_target_pairs={{0,2},{1,5},{2,0},{3,7},{4,6},{5,1},{6,4},{7,3},{8,10},{9,13},{10,... | collective-permute-start | bytes 2654216 | tf_op jit(solution)/shard_map/attention_weights_second/ppermute | solution.py:757
  93.4 22.0 %collective-permute-start.25 = (bf16[2,48,4608]{2,1,0:T(8,128)(2,1)}, bf16[2,48,4608]{2,1,0:T(8,128)(2,1)}, u32[]{:S(2)}, u32[]{:S(2)}) collective-permute-start(bf16[2,48,4608]{2,1,0:T(8,128)(2,1)} %collective-permute-done.11.refs_6_), channel_id=1, source_target_pairs={{0,1},{1,0},{2,3},{3,2},{4,5},{5,4},{6,7},{7,6},{8,9},{9,8},{10,11... | collective-permute-start | bytes 2654216 | tf_op jit(solution)/shard_map/attention_weights_core/ppermute | solution.py:760
  93.4 22.0 %collective-permute-start.26 = (bf16[2,48,4608]{2,1,0:T(8,128)(2,1)}, bf16[2,48,4608]{2,1,0:T(8,128)(2,1)}, u32[]{:S(2)}, u32[]{:S(2)}) collective-permute-start(bf16[2,48,4608]{2,1,0:T(8,128)(2,1)} %collective-permute-done.12.refs_9_), channel_id=1, source_target_pairs={{0,1},{1,0},{2,3},{3,2},{4,5},{5,4},{6,7},{7,6},{8,9},{9,8},{10,11... | collective-permute-start | bytes 2654216 | tf_op jit(solution)/shard_map/attention_weights_core/ppermute | solution.py:760
  93.9 21.5 %collective-permute-start.23 = (bf16[256,1536]{1,0:T(8,128)(2,1)}, bf16[256,1536]{1,0:T(8,128)(2,1)S(1)}, u32[]{:S(2)}, u32[]{:S(2)}) collective-permute-start(bf16[256,1536]{1,0:T(8,128)(2,1)} %collective-permute-done.13.refs_27_), channel_id=1, source_target_pairs={{0,8},{8,16},{16,24},{24,0},{1,9},{9,17},{17,25},{25,1},{2,10},{10... | collective-permute-start | bytes 2359304 | tf_op jit(solution)/shard_map/tokens_z/ppermute | solution.py:751
  115.4 263.9 %reduce-scatter.5.cloned.1.call-start = ((), (), s32[]{:S(2)}) async-start(), calls=%async_computation.5 | async-start | bytes 5898240 | tf_op jit(solution)/shard_map/feed_sum_z/reduce_scatter | solution.py:1001
  142.2 22.7 %collective-permute-start.28 = (bf16[512,1536]{1,0:T(8,128)(2,1)}, bf16[512,1536]{1,0:T(8,128)(2,1)}, u32[]{:S(2)}, u32[]{:S(2)}) collective-permute-start(bf16[512,1536]{1,0:T(8,128)(2,1)} %pad_maximum_fusion.refs_2_), channel_id=1, source_target_pairs={{0,2},{1,5},{2,0},{3,7},{4,6},{5,1},{6,4},{7,3},{8,10},{9,13},{10,... | collective-permute-start | bytes 4718600 | tf_op jit(solution)/shard_map/out_grad_second/ppermute | solution.py:757
  164.9 12.1 %collective-permute-start.29 = (bf16[256,1536]{1,0:T(8,128)(2,1)S(1)}, bf16[256,1536]{1,0:T(8,128)(2,1)S(1)}, u32[]{:S(2)}, u32[]{:S(2)}) collective-permute-start(bf16[256,1536]{1,0:T(8,128)(2,1)S(1)} %get-tuple-element.153), channel_id=1, source_target_pairs={{0,4},{1,3},{2,6},{3,1},{4,0},{5,7},{6,2},{7,5},{8,12},{9,11},{10,... | collective-permute-start | bytes 2359304 | tf_op jit(solution)/shard_map/normed_first/ppermute | solution.py:754
  177.1 20.5 %collective-permute-start.30 = (bf16[512,1536]{1,0:T(8,128)(2,1)S(1)}, bf16[512,1536]{1,0:T(8,128)(2,1)S(1)}, u32[]{:S(2)}, u32[]{:S(2)}) collective-permute-start(bf16[512,1536]{1,0:T(8,128)(2,1)S(1)} %pad_maximum_fusion.1.refs_0_), channel_id=1, source_target_pairs={{0,2},{1,5},{2,0},{3,7},{4,6},{5,1},{6,4},{7,3},{8,10},{9,13},{10,... | collective-permute-start | bytes 4718600 | tf_op jit(solution)/shard_map/normed_second/ppermute | solution.py:757
  177.6 24.6 %collective-permute-start.33 = (bf16[512,1536]{1,0:T(8,128)(2,1)}, bf16[512,1536]{1,0:T(8,128)(2,1)}, u32[]{:S(2)}, u32[]{:S(2)}) collective-permute-start(bf16[512,1536]{1,0:T(8,128)(2,1)} %pad_maximum_fusion.refs_2_), channel_id=1, source_target_pairs={{0,1},{1,0},{2,3},{3,2},{4,5},{5,4},{6,7},{7,6},{8,9},{9,8},{10,11... | collective-permute-start | bytes 4718600 | tf_op jit(solution)/shard_map/out_grad_all/ppermute | solution.py:760
  177.6 24.6 %collective-permute-start.34 = (bf16[512,1536]{1,0:T(8,128)(2,1)}, bf16[512,1536]{1,0:T(8,128)(2,1)}, u32[]{:S(2)}, u32[]{:S(2)}) collective-permute-start(bf16[512,1536]{1,0:T(8,128)(2,1)} %collective-permute-done.28.refs_3_), channel_id=1, source_target_pairs={{0,1},{1,0},{2,3},{3,2},{4,5},{5,4},{6,7},{7,6},{8,9},{9,8},{10,11... | collective-permute-start | bytes 4718600 | tf_op jit(solution)/shard_map/out_grad_all/ppermute | solution.py:760
  178.1 24.1 %collective-permute-start.31 = (bf16[512,1536]{1,0:T(8,128)(2,1)S(1)}, bf16[512,1536]{1,0:T(8,128)(2,1)}, u32[]{:S(2)}, u32[]{:S(2)}) collective-permute-start(bf16[512,1536]{1,0:T(8,128)(2,1)S(1)} %pad_maximum_fusion.1.refs_0_), channel_id=1, source_target_pairs={{0,1},{1,0},{2,3},{3,2},{4,5},{5,4},{6,7},{7,6},{8,9},{9,8},{10,11... | collective-permute-start | bytes 4718600 | tf_op jit(solution)/shard_map/normed_second/ppermute | solution.py:760
  219.4 17.5 %collective-permute-start.35 = (bf16[1024,1536]{1,0:T(8,128)(2,1)}, bf16[1024,1536]{1,0:T(8,128)(2,1)S(1)}, u32[]{:S(2)}, u32[]{:S(2)}) collective-permute-start(bf16[1024,1536]{1,0:T(8,128)(2,1)} %get-tuple-element.159), channel_id=1, source_target_pairs={{0,1},{1,0},{2,3},{3,2},{4,5},{5,4},{6,7},{7,6},{8,9},{9,8},{10,11... | collective-permute-start | bytes 9437192 | tf_op jit(solution)/shard_map/scaled_core/ppermute | solution.py:760
  241.4 20.6 %collective-permute-start.36 = (bf16[512,1536]{1,0:T(8,128)(2,1)}, bf16[512,1536]{1,0:T(8,128)(2,1)S(1)}, u32[]{:S(2)}, u32[]{:S(2)}) collective-permute-start(bf16[512,1536]{1,0:T(8,128)(2,1)} %add_half.17), channel_id=1, source_target_pairs={{0,2},{1,5},{2,0},{3,7},{4,6},{5,1},{6,4},{7,3},{8,10},{9,13},{10,... | collective-permute-start | bytes 4718600 | tf_op jit(solution)/shard_map/scaled_second/ppermute | solution.py:757
  256.8 158.9 %reduce-scatter.3.cloned.1.call-start = ((), (), s32[]{:S(2)}) async-start(), calls=%async_computation.4 | async-start | bytes 3932160 | tf_op jit(solution)/shard_map/kv_grad_z/reduce_scatter | solution.py:1042
  263.0 12.3 %collective-permute-start.37 = (bf16[256,1536]{1,0:T(8,128)(2,1)}, bf16[256,1536]{1,0:T(8,128)(2,1)}, u32[]{:S(2)}, u32[]{:S(2)}) collective-permute-start(bf16[256,1536]{1,0:T(8,128)(2,1)} %add_half.19), channel_id=1, source_target_pairs={{0,4},{1,3},{2,6},{3,1},{4,0},{5,7},{6,2},{7,5},{8,12},{9,11},{10,... | collective-permute-start | bytes 2359304 | tf_op jit(solution)/shard_map/scaled_first/ppermute | solution.py:754
  291.3 20.3 %collective-permute-start.39 = (bf16[2,4,48,1536]{3,2,1,0:T(8,128)(2,1)S(1)}, bf16[2,4,48,1536]{3,2,1,0:T(8,128)(2,1)S(1)}, u32[]{:S(2)}, u32[]{:S(2)}) collective-permute-start(bf16[2,4,48,1536]{3,2,1,0:T(8,128)(2,1)S(1)} %bitcast.195), channel_id=1, source_target_pairs={{0,2},{1,5},{2,0},{3,7},{4,6},{5,1},{6,4},{7,3},{8,10},{9,13},{10,... | collective-permute-start | bytes 3538952 | tf_op jit(solution)/shard_map/out_second/ppermute | solution.py:757
  314.2 14.0 %collective-permute-start.40 = (bf16[1,4,48,1536]{3,2,1,0:T(8,128)(2,1)S(1)}, bf16[1,4,48,1536]{3,2,1,0:T(8,128)(2,1)S(1)}, u32[]{:S(2)}, u32[]{:S(2)}) collective-permute-start(bf16[1,4,48,1536]{3,2,1,0:T(8,128)(2,1)S(1)} %bitcast.197), channel_id=1, source_target_pairs={{0,4},{1,3},{2,6},{3,1},{4,0},{5,7},{6,2},{7,5},{8,12},{9,11},{10,... | collective-permute-start | bytes 1769480 | tf_op jit(solution)/shard_map/out_first/ppermute | solution.py:754
  329.0 8.3 %collective-permute-start.41 = (bf16[4,4,48,3072]{3,2,1,0:T(8,128)(2,1)}, bf16[4,4,48,3072]{3,2,1,0:T(8,128)(2,1)}, u32[]{:S(2)}, u32[]{:S(2)}) collective-permute-start(bf16[4,4,48,3072]{3,2,1,0:T(8,128)(2,1)} %get-tuple-element.184), channel_id=1, source_target_pairs={{0,1},{1,0},{2,3},{3,2},{4,5},{5,4},{6,7},{7,6},{8,9},{9,8},{10,11... | collective-permute-start | bytes 14155784 | tf_op jit(solution)/shard_map/projected_core/ppermute | solution.py:760
  342.9 28.9 %collective-permute-start.42 = (bf16[2,4,48,3072]{3,2,1,0:T(8,128)(2,1)S(1)}, bf16[2,4,48,3072]{3,2,1,0:T(8,128)(2,1)S(1)}, u32[]{:S(2)}, u32[]{:S(2)}) collective-permute-start(bf16[2,4,48,3072]{3,2,1,0:T(8,128)(2,1)S(1)} %bitcast.192), channel_id=1, source_target_pairs={{0,2},{1,5},{2,0},{3,7},{4,6},{5,1},{6,4},{7,3},{8,10},{9,13},{10,... | collective-permute-start | bytes 7077896 | tf_op jit(solution)/shard_map/projected_second/ppermute | solution.py:757
  371.8 43.9 %collective-permute-start.45 = (bf16[512,1536]{1,0:T(8,128)(2,1)}, bf16[512,1536]{1,0:T(8,128)(2,1)}, u32[]{:S(2)}, u32[]{:S(2)}) collective-permute-start(bf16[512,1536]{1,0:T(8,128)(2,1)} %add_half.25), channel_id=1, source_target_pairs={{0,2},{1,5},{2,0},{3,7},{4,6},{5,1},{6,4},{7,3},{8,10},{9,13},{10,... | collective-permute-start | bytes 4718600 | tf_op jit(solution)/shard_map/result_second/ppermute | solution.py:757
  376.4 39.2 %collective-permute-start.44 = (bf16[1,4,48,3072]{3,2,1,0:T(8,128)(2,1)}, bf16[1,4,48,3072]{3,2,1,0:T(8,128)(2,1)}, u32[]{:S(2)}, u32[]{:S(2)}) collective-permute-start(bf16[1,4,48,3072]{3,2,1,0:T(8,128)(2,1)} %bitcast.90), channel_id=1, source_target_pairs={{0,4},{1,3},{2,6},{3,1},{4,0},{5,7},{6,2},{7,5},{8,12},{9,11},{10,... | collective-permute-start | bytes 3538952 | tf_op jit(solution)/shard_map/projected_first/ppermute | solution.py:754
  381.4 34.2 %all-to-all-start.1 = ((bf16[8,48,1024]{2,1,0:T(8,128)(2,1)}), bf16[8,48,1024]{2,1,0:T(8,128)(2,1)}, u32[]{:S(2)}, u32[]{:S(2)}) async-start(bf16[8,48,1024]{2,1,0:T(8,128)(2,1)} %bitcast.199), calls=%async_computation.3 | async-start | bytes 1572864 | tf_op jit(solution)/shard_map/gate_up_sum_f/all_to_all | solution.py:1065
  387.7 12.3 %collective-permute-start.46 = (bf16[48,1536]{1,0:T(8,128)(2,1)}, bf16[48,1536]{1,0:T(8,128)(2,1)}, u32[]{:S(2)}, u32[]{:S(2)}) collective-permute-start(bf16[48,1536]{1,0:T(8,128)(2,1)} %get-tuple-element.264), channel_id=1, source_target_pairs={{0,24},{8,0},{16,8},{24,16},{1,25},{9,1},{17,9},{25,17},{2,26},{10... | collective-permute-start | bytes 442376 | tf_op jit(solution)/shard_map/out_z/ppermute | solution.py:751
  388.4 27.2 %collective-permute-start.47 = (bf16[48,1536]{1,0:T(8,128)(2,1)}, bf16[48,1536]{1,0:T(8,128)(2,1)}, u32[]{:S(2)}, u32[]{:S(2)}) collective-permute-start(bf16[48,1536]{1,0:T(8,128)(2,1)} %get-tuple-element.263), channel_id=1, source_target_pairs={{0,16},{8,24},{16,0},{24,8},{1,17},{9,25},{17,1},{25,9},{2,18},{10... | collective-permute-start | bytes 442376 | tf_op jit(solution)/shard_map/out_z/ppermute | solution.py:751
  388.6 27.0 %collective-permute-start.48 = (bf16[48,1536]{1,0:T(8,128)(2,1)}, bf16[48,1536]{1,0:T(8,128)(2,1)}, u32[]{:S(2)}, u32[]{:S(2)}) collective-permute-start(bf16[48,1536]{1,0:T(8,128)(2,1)} %get-tuple-element.262), channel_id=1, source_target_pairs={{0,8},{8,16},{16,24},{24,0},{1,9},{9,17},{17,25},{25,1},{2,10},{10... | collective-permute-start | bytes 442376 | tf_op jit(solution)/shard_map/out_z/ppermute | solution.py:751
  418.3 21.7 %collective-permute-start.49 = (bf16[256,1536]{1,0:T(8,128)(2,1)S(1)}, bf16[256,1536]{1,0:T(8,128)(2,1)S(1)}, u32[]{:S(2)}, u32[]{:S(2)}) collective-permute-start(bf16[256,1536]{1,0:T(8,128)(2,1)S(1)} %add_half.30), channel_id=1, source_target_pairs={{0,4},{1,3},{2,6},{3,1},{4,0},{5,7},{6,2},{7,5},{8,12},{9,11},{10,... | collective-permute-start | bytes 2359304 | tf_op jit(solution)/shard_map/result_first/ppermute | solution.py:754
  421.8 19.5 %collective-permute-start.50 = (bf16[48,3072]{1,0:T(8,128)(2,1)S(1)}, bf16[48,3072]{1,0:T(8,128)(2,1)S(1)}, u32[]{:S(2)}, u32[]{:S(2)}) collective-permute-start(bf16[48,3072]{1,0:T(8,128)(2,1)S(1)} %get-tuple-element.260), channel_id=1, source_target_pairs={{0,24},{8,0},{16,8},{24,16},{1,25},{9,1},{17,9},{25,17},{2,26},{10... | collective-permute-start | bytes 884744 | tf_op jit(solution)/shard_map/projected_z/ppermute | solution.py:751
  421.8 28.3 %collective-permute-start.51 = (bf16[48,3072]{1,0:T(8,128)(2,1)S(1)}, bf16[48,3072]{1,0:T(8,128)(2,1)S(1)}, u32[]{:S(2)}, u32[]{:S(2)}) collective-permute-start(bf16[48,3072]{1,0:T(8,128)(2,1)S(1)} %get-tuple-element.259), channel_id=1, source_target_pairs={{0,16},{8,24},{16,0},{24,8},{1,17},{9,25},{17,1},{25,9},{2,18},{10... | collective-permute-start | bytes 884744 | tf_op jit(solution)/shard_map/projected_z/ppermute | solution.py:751
  425.0 25.2 %collective-permute-start.52 = (bf16[48,3072]{1,0:T(8,128)(2,1)S(1)}, bf16[48,3072]{1,0:T(8,128)(2,1)S(1)}, u32[]{:S(2)}, u32[]{:S(2)}) collective-permute-start(bf16[48,3072]{1,0:T(8,128)(2,1)S(1)} %get-tuple-element.258), channel_id=1, source_target_pairs={{0,8},{8,16},{16,24},{24,0},{1,9},{9,17},{17,25},{25,1},{2,10},{10... | collective-permute-start | bytes 884744 | tf_op jit(solution)/shard_map/projected_z/ppermute | solution.py:751
  (84 other events, 547.3 us)
Sparse Core Ops, SparseCore 0:
  115.5 86.6 all-gather.2
  256.9 83.8 reduce-scatter.4
  343.0 70.0 reduce-scatter.2
